TPU v7x, 1024 devices: a whole 4x4x32 slice. The times are simulated.
1024 devices in a mesh: dp: 16 (over y, x), seq: 64 (over z, core).
Axes of the slice: x: 4, y: 4, z: 32, core: 2. Of those that a mesh axis runs over, the one named last changes fastest.
Arguments:
- queries: bfloat16 [16, 8192, 1024], P('dp', 'seq'), may hold values from -68 to 68
- keys: bfloat16 [16, 8192, 1024], P('dp', 'seq'), may hold values from -4 to 4
- values: bfloat16 [16, 8192, 1024], P('dp', 'seq'), may hold values from -6 to 6
- cotangent: bfloat16 [16, 8192, 1024], P('dp', 'seq'), may hold values from -6 to 6
- w_out: bfloat16 [1024, 1024], replicated, may hold values from -3 to 3
- blocks: int32 [16, 64, 4], P('dp'), may hold values from 0 to 63, as said below
- counts: int32 [16, 64], P('dp'), may hold values from 1 to 4, as said below
Outputs:
- layer_out: bfloat16 [16, 8192, 1024], P('dp', 'seq')
- value_grad: bfloat16 [16, 8192, 1024], P('dp', 'seq')
- weight_grad: float32 [1024, 1024], P('seq')
Inputs may be any that keep to these rules, and one draw needn't show every extreme that they name: blocks[g, c, 0] is c; the entries of one row are distinct clusters; only the first counts[g, c] entries are used. `counts`: every batch has at least one cluster with 4 blocks.
All inputs are finite; a program needn't handle non-finite values.
Results may differ from a plain program's by a relative error of at most 0.019.
Values may be sent and summed in bfloat16 or wider, within the bound.
No kernel may reach another device: no remote copies, remote signals or barrier semaphores. Data moves between devices by JAX's collectives and lax.ppermute only.
A program may use at most 64 MiB of HBM per device.

v0:
```python
import math

import jax
import jax.numpy as jnp
from jax import lax
from jax.sharding import PartitionSpec as P

H = 16
CSIZE = 128


def body(queries, keys, values, cotangent, w_out, blocks, counts):
    nseq = lax.axis_size("seq")
    width = w_out.shape[0]
    head_dim = width // H
    per_dev = max(H // nseq, 1)
    qsplit = max(nseq // H, 1)
    hgroups = H // per_dev
    lanes = per_dev * head_dim
    rows = queries.shape[1]
    clusters = blocks.shape[1]
    most = blocks.shape[2]
    local = rows // CSIZE
    part_rows = CSIZE // qsplit
    scale = head_dim ** (-0.5)
    node_q = queries[0]
    grad_in = cotangent[0]
    out_grad = lax.dot_general(
        grad_in, w_out, (((1,), (1,)), ((), ())), preferred_element_type=jnp.float32
    ).astype(jnp.bfloat16)

    def to_heads(field):
        shaped = field.reshape(local, qsplit, part_rows, hgroups, lanes)
        return shaped.transpose(3, 1, 0, 2, 4).reshape(nseq, local * part_rows * lanes)

    q_in, grad_heads = (
        lax.all_to_all(to_heads(node_q), "seq", split_axis=0, concat_axis=0, tiled=True),
        lax.all_to_all(to_heads(out_grad), "seq", split_axis=0, concat_axis=0, tiled=True),
    )
    packed = jnp.concatenate(
        [
            keys[0].reshape(rows, hgroups, per_dev, head_dim),
            values[0].reshape(rows, hgroups, per_dev, head_dim),
        ],
        axis=3,
    )
    packed = packed.transpose(1, 0, 2, 3)
    copies = jnp.broadcast_to(
        packed[:, None], (hgroups, qsplit, rows, per_dev, 2 * head_dim)
    ).reshape(nseq, rows * per_dev * 2 * head_dim)
    kv_in = lax.all_to_all(copies, "seq", split_axis=0, concat_axis=0, tiled=True)
    kv_heads = kv_in.reshape(clusters, CSIZE, per_dev, 2 * head_dim)
    group = math.gcd(clusters, max(1, 512 // (part_rows * per_dev)))
    steps = clusters // group
    q_groups = q_in.reshape(steps, group, part_rows, per_dev, head_dim)
    g_groups = grad_heads.reshape(steps, group, part_rows, per_dev, head_dim)
    blk_groups = blocks[0].reshape(steps, group, most)
    cnt_groups = counts[0].reshape(steps, group)

    def attend(carry, item):
        q_blk, g_blk, ids, number = item
        gathered = kv_heads[ids]
        scores = (
            jnp.einsum(
                "gqhd,gjkhd->ghqjk",
                q_blk,
                gathered[..., :head_dim],
                preferred_element_type=jnp.float32,
            )
            * scale
        )
        valid = (jnp.arange(most)[None, :] < number[:, None])[:, None, None, :, None]
        scores = jnp.where(valid, scores, -1e30)
        top = jnp.max(scores, axis=(3, 4), keepdims=True)
        expd = jnp.where(valid, jnp.exp(scores - top), 0.0)
        probs = (expd / jnp.sum(expd, axis=(3, 4), keepdims=True)).astype(jnp.bfloat16)
        attended = jnp.einsum(
            "ghqjk,gjkhd->gqhd", probs, gathered[..., head_dim:], preferred_element_type=jnp.float32
        ).astype(jnp.bfloat16)
        contrib = jnp.einsum("ghqjk,gqhd->gjkhd", probs, g_blk, preferred_element_type=jnp.float32)
        return (carry.at[ids].add(contrib), attended)

    start = jnp.zeros((clusters, CSIZE, per_dev, head_dim), jnp.float32)
    partial_value, attended = lax.scan(attend, start, (q_groups, g_groups, blk_groups, cnt_groups))
    out_send = attended.reshape(nseq, local * part_rows * lanes)
    grad_send = partial_value.astype(jnp.bfloat16).reshape(nseq, local * CSIZE * lanes)
    out_back, grad_back = (
        lax.all_to_all(out_send, "seq", split_axis=0, concat_axis=0, tiled=True),
        lax.all_to_all(grad_send, "seq", split_axis=0, concat_axis=0, tiled=True),
    )
    node_rows = (
        out_back.reshape(hgroups, qsplit, local, part_rows, per_dev, head_dim)
        .transpose(2, 1, 3, 0, 4, 5)
        .reshape(rows, width)
    )
    summed = jnp.sum(
        grad_back.reshape(hgroups, qsplit, local, CSIZE, per_dev, head_dim).astype(jnp.float32),
        axis=1,
    )
    value_grad = summed.transpose(1, 2, 0, 3, 4).reshape(rows, width).astype(jnp.bfloat16)
    layer_out = jnp.dot(node_rows, w_out, preferred_element_type=jnp.float32).astype(jnp.bfloat16)
    own_rows = lax.psum_scatter(
        lax.dot_general(
            node_rows, grad_in, (((0,), (0,)), ((), ())), preferred_element_type=jnp.float32
        ),
        "seq",
        scatter_dimension=0,
        tiled=True,
    )
    weight_grad = lax.psum(own_rows.astype(jnp.bfloat16), "dp").astype(jnp.float32)
    return (layer_out[None], value_grad[None], weight_grad)


def solution(mesh):
    return jax.shard_map(
        body,
        mesh=mesh,
        in_specs=(
            P("dp", "seq", None),
            P("dp", "seq", None),
            P("dp", "seq", None),
            P("dp", "seq", None),
            P(),
            P("dp", None, None),
            P("dp", None),
        ),
        out_specs=(P("dp", "seq", None), P("dp", "seq", None), P("seq", None)),
        check_vma=False,
    )
```

profile of v0, /device:TPU:32, one launch (start us, length us, event | category | flops | bytes accessed | tf_op | source)
XLA Modules:
  0.0 857.3 jit_solution(11158871581429233988)
XLA Ops:
  15.0 29.0 %all-to-all-start = ((bf16[64,2,1024]{2,1,0:T(2,128)(2,1)}), bf16[64,2,1024]{2,1,0:T(2,128)(2,1)S(1)}, u32[]{:S(2)}, u32[]{:S(2)}) async-start(bf16[64,2,1024]{2,1,0:T(2,128)(2,1)} %reshape.222), calls=%async_computation | async-start | bytes 524288 | tf_op jit(solution)/shard_map/all_to_all | solution.py:38
  48.9 37.4 %all-to-all-done = bf16[64,2,1024]{2,1,0:T(2,128)(2,1)S(1)} async-done(((bf16[64,2,1024]{2,1,0:T(2,128)(2,1)}), bf16[64,2,1024]{2,1,0:T(2,128)(2,1)S(1)}, u32[]{:S(2)}, u32[]{:S(2)}) %all-to-all-start) | async-done | bytes 262176 | tf_op jit(solution)/shard_map/all_to_all | solution.py:38
  86.3 6.0 all-to-all-start.1
  96.8 10.0 %all_to_all.42 = bf16[64,1,16384]{2,1,0:T(2,128)(2,1)} reshape(bf16[16,4,128,1,128]{4,2,1,0,3:T(8,128)(2,1)} %broadcast_in_dim.50) | data formatting | bytes 4194304 | tf_op jit(solution)/shard_map/all_to_all | solution.py:51
  106.8 14.5 %reduce.18 = bf16[64,16384]{1,0:T(8,128)(2,1)} reduce(bf16[64,1,16384]{2,1,0:T(2,128)(2,1)} %all_to_all.42, bf16[]{:T(256)} %broadcast.64), dimensions={1}, to_apply=%all_to_all.42.reduce_sub_computation | reduce | bytes 4194306 | tf_op jit(solution)/shard_map/all_to_all | solution.py:51
  121.3 4.5 reshape.226
  125.8 8.9 %all-to-all-done.1 = bf16[64,2,1024]{2,1,0:T(2,128)(2,1)} async-done(((bf16[64,2,1024]{2,1,0:T(2,128)(2,1)}), bf16[64,2,1024]{2,1,0:T(2,128)(2,1)}, u32[]{:S(2)}, u32[]{:S(2)}) %all-to-all-start.1) | async-done | bytes 262176 | tf_op jit(solution)/shard_map/all_to_all | solution.py:37
  134.7 13.8 %all-to-all-start.2 = ((bf16[64,2,8192]{2,1,0:T(2,128)(2,1)}), bf16[64,2,8192]{2,1,0:T(2,128)(2,1)}, u32[]{:S(2)}, u32[]{:S(2)}) async-start(bf16[64,2,8192]{2,1,0:T(2,128)(2,1)} %reshape.226), calls=%async_computation.2 | async-start | bytes 4194304 | tf_op jit(solution)/shard_map/all_to_all | solution.py:51
  156.5 188.4 %all-to-all-done.2 = bf16[64,2,8192]{2,1,0:T(2,128)(2,1)} async-done(((bf16[64,2,8192]{2,1,0:T(2,128)(2,1)}), bf16[64,2,8192]{2,1,0:T(2,128)(2,1)}, u32[]{:S(2)}, u32[]{:S(2)}) %all-to-all-start.2) | async-done | bytes 2097184 | tf_op jit(solution)/shard_map/all_to_all | solution.py:51
  345.0 10.4 %reshape.227 = bf16[64,1,16384]{2,1,0:T(2,128)(2,1)} reshape(bf16[64,2,8192]{2,1,0:T(2,128)(2,1)} %all-to-all-done.2) | data formatting | bytes 4194304
  355.4 13.8 %reduce.10 = bf16[64,16384]{1,0:T(8,128)(2,1)} reduce(bf16[64,1,16384]{2,1,0:T(2,128)(2,1)} %reshape.227, bf16[]{:T(256)} %constant.39), dimensions={1}, to_apply=%all_to_all.35.reduce_sub_computation | reduce | bytes 4194306 | tf_op jit(solution)/shard_map/all_to_all | solution.py:51
  374.4 94.5 %while.12 = (s32[]{:T(128)}, f32[64,128,1,64]{1,3,0,2:T(8,128)}, bf16[4,16,32,1,64]{4,2,1,3,0:T(8,128)(2,1)}, s32[4,16,4]{1,0,2:T(4,128)S(1)}, bf16[4,16,32,1,64...) while((s32[]{:T(128)}, f32[64,128,1,64]{1,3,0,2:T(8,128)}, ...), condition=%wide.region_4.5_spmd, body=%wide.region_0.4_spmd.sunk | while | flops 104890624 | bytes 31903940 | solution.py:84
  387.6 10.3 %scatter_fusion = f32[64,128,64]{1,2,0:T(8,128)} fusion(f32[64,128,64]{1,2,0:T(8,128)} %bitcast.145, s32[64]{0:T(128)S(1)} %reshape.241, f32[64,128,64]{1,2,0:T(8,128)} %bitcast.149), kind=kCustom, calls=%fused_computation.1.clone.1 | custom fusion | flops 524288 | bytes 6291712 | tf_op jit(solution)/shard_map/while/body/eval_jaxpr/scatter-add | solution.py:81
  411.3 10.4 %scatter_fusion = f32[64,128,64]{1,2,0:T(8,128)} fusion(f32[64,128,64]{1,2,0:T(8,128)} %bitcast.145, s32[64]{0:T(128)S(1)} %reshape.241, f32[64,128,64]{1,2,0:T(8,128)} %bitcast.149), kind=kCustom, calls=%fused_computation.1.clone.1 | custom fusion | flops 524288 | bytes 6291712 | tf_op jit(solution)/shard_map/while/body/eval_jaxpr/scatter-add | solution.py:81
  434.9 10.3 %scatter_fusion = f32[64,128,64]{1,2,0:T(8,128)} fusion(f32[64,128,64]{1,2,0:T(8,128)} %bitcast.145, s32[64]{0:T(128)S(1)} %reshape.241, f32[64,128,64]{1,2,0:T(8,128)} %bitcast.149), kind=kCustom, calls=%fused_computation.1.clone.1 | custom fusion | flops 524288 | bytes 6291712 | tf_op jit(solution)/shard_map/while/body/eval_jaxpr/scatter-add | solution.py:81
  458.5 10.3 %scatter_fusion = f32[64,128,64]{1,2,0:T(8,128)} fusion(f32[64,128,64]{1,2,0:T(8,128)} %bitcast.145, s32[64]{0:T(128)S(1)} %reshape.241, f32[64,128,64]{1,2,0:T(8,128)} %bitcast.149), kind=kCustom, calls=%fused_computation.1.clone.1 | custom fusion | flops 524288 | bytes 6291712 | tf_op jit(solution)/shard_map/while/body/eval_jaxpr/scatter-add | solution.py:81
  473.6 50.4 %all_to_all.50 = bf16[64,2,1024]{2,1,0:T(2,128)(2,1)S(1)} all-to-all(bf16[64,2,1024]{2,1,0:T(2,128)(2,1)S(1)} %reshape.228), channel_id=1, replica_groups=mesh['dp'=16,'seq'=64] {'seq'}, dimensions={0} | all-to-all | bytes 524288 | tf_op jit(solution)/shard_map/all_to_all | solution.py:88
  534.1 7.7 all_to_all.44
  541.8 8.5 reduce.20
  551.9 5.5 all-to-all-start.4
  558.6 113.4 %all-to-all-done.4 = bf16[64,2,4096]{2,1,0:T(2,128)(2,1)S(1)} async-done(((bf16[64,2,4096]{2,1,0:T(2,128)(2,1)}), bf16[64,2,4096]{2,1,0:T(2,128)(2,1)S(1)}, u32[]{:S(2)}, u32[]{:S(2)}) %all-to-all-start.4) | async-done | bytes 1048608 | tf_op jit(solution)/shard_map/all_to_all | solution.py:89
  675.5 7.9 reduce.12
  689.8 87.1 %reduce-scatter.2.cloned.1.call-done = f32[16,1024]{1,0:T(8,128)} async-done(((f32[1024,1024]{1,0:T(8,128)}), f32[16,1024]{1,0:T(8,128)}) %reduce-scatter.2.cloned.1.call-update) | async-done | bytes 65552 | tf_op jit(solution)/shard_map/reduce_scatter | solution.py:102
  777.8 71.6 %psum.7 = bf16[16,1024]{1,0:T(8,128)(2,1)S(1)} all-reduce(bf16[16,1024]{1,0:T(8,128)(2,1)S(1)} %convert_element_type.73), channel_id=1, replica_groups=mesh['dp'=16,'seq'=64] {'dp'}, use_global_device_ids=true, to_apply=%region_7.8 | all-reduce | flops 16384 | bytes 65536 | tf_op jit(solution)/shard_map/psum | solution.py:110
  (118 shorter events, 112.0 us)
Async XLA Ops:
  7.2 1.6 copy-start
  15.0 71.3 %all-to-all-start = ((bf16[64,2,1024]{2,1,0:T(2,128)(2,1)}), bf16[64,2,1024]{2,1,0:T(2,128)(2,1)S(1)}, u32[]{:S(2)}, u32[]{:S(2)}) async-start(bf16[64,2,1024]{2,1,0:T(2,128)(2,1)} %reshape.222), calls=%async_computation | async-start | bytes 524288 | tf_op jit(solution)/shard_map/all_to_all | solution.py:38
  86.3 48.4 %all-to-all-start.1 = ((bf16[64,2,1024]{2,1,0:T(2,128)(2,1)}), bf16[64,2,1024]{2,1,0:T(2,128)(2,1)}, u32[]{:S(2)}, u32[]{:S(2)}) async-start(bf16[64,2,1024]{2,1,0:T(2,128)(2,1)} %reshape.224), calls=%async_computation.1 | async-start | bytes 524288 | tf_op jit(solution)/shard_map/all_to_all | solution.py:37
  125.8 23.5 %copy-start.3 = (s32[1,64]{1,0:T(1,128)S(1)}, s32[1,64]{1,0:T(1,128)}, u32[]{:S(2)}) copy-start(s32[1,64]{1,0:T(1,128)} %param.15) | copy-start | bytes 772
  125.8 24.2 %copy-start.2 = (s32[1,64,4]{1,2,0:T(4,128)S(1)}, s32[1,64,4]{1,2,0:T(4,128)}, u32[]{:S(2)}) copy-start(s32[1,64,4]{1,2,0:T(4,128)} %param.14) | copy-start | bytes 3076
  134.7 210.3 %all-to-all-start.2 = ((bf16[64,2,8192]{2,1,0:T(2,128)(2,1)}), bf16[64,2,8192]{2,1,0:T(2,128)(2,1)}, u32[]{:S(2)}, u32[]{:S(2)}) async-start(bf16[64,2,8192]{2,1,0:T(2,128)(2,1)} %reshape.226), calls=%async_computation.2 | async-start | bytes 4194304 | tf_op jit(solution)/shard_map/all_to_all | solution.py:51
  148.5 628.4 %reduce-scatter.2.cloned.1.call-start = ((), (), s32[]{:S(2)}) async-start(), calls=%async_computation.6 | async-start | bytes 4259840 | tf_op jit(solution)/shard_map/reduce_scatter | solution.py:102
  382.3 2.2 copy-start.1
  406.0 2.2 copy-start.1
  429.6 2.2 copy-start.1
  453.2 2.2 copy-start.1
  551.9 120.1 %all-to-all-start.4 = ((bf16[64,2,4096]{2,1,0:T(2,128)(2,1)}), bf16[64,2,4096]{2,1,0:T(2,128)(2,1)S(1)}, u32[]{:S(2)}, u32[]{:S(2)}) async-start(bf16[64,2,4096]{2,1,0:T(2,128)(2,1)} %reshape.230), calls=%async_computation.4 | async-start | bytes 2097152 | tf_op jit(solution)/shard_map/all_to_all | solution.py:89
Sparse Core Ops, SparseCore 0:
  530.6 246.2 reduce-scatter.1
where the time goes:
time: 868 us; the launch traced here: 857 us
  waiting for transfers between devices  435 us (50%)
  blocking collectives  122 us (14%)
  other arithmetic  105 us (12%)
  local copies, waits for them, and re-layouts  99.8 us (11%)
  starting transfers between devices  54.6 us (6%)
  matrix products  25.6 us (3%)
  between operations  14.8 us (2%)
    all_to_all x1, waiting for transfers between devices, body(): lax.all_to_all(copies, 'seq', split_axis=0, concat_axis=0, tiled=True)  188 us
    all_to_all x1, waiting for transfers between devices, body(): lax.all_to_all(grad_send, 'seq', split_axis=0, concat_axis=0, tiled=True)  113 us
    reduce_scatter x1, waiting for transfers between devices, body(): lax.psum_scatter(lax.dot_general(node_rows, grad_in, (((0,), (0,)), ((),...  87.1 us
    psum x1, blocking collectives, body(): lax.psum(own_rows.astype(jnp.bfloat16), 'dp').astype(jnp.float32)  71.6 us
    all_to_all x1, blocking collectives, body(): lax.all_to_all(out_send, 'seq', split_axis=0, concat_axis=0, tiled=True)  50.4 us
    scatter-add x4, other arithmetic, attend(): return (carry.at[ids].add(contrib), attended)  41.4 us
    all_to_all x1, waiting for transfers between devices, body(): lax.all_to_all(to_heads(out_grad), 'seq', split_axis=0, concat_axis=0, ti...  37.4 us
    unnamed x21, local copies, waits for them, and re-layouts  33.3 us
  transfers between devices with their start and end apart: 5, of which 5 were waited for; matrix products, arithmetic and copies ran while one was open for 8% of the time, Pallas kernels for 0%

commit v1 on v0

v1 whole, which is shorter than its diff:
```python
import jax
import jax.numpy as jnp
from jax import lax
from jax.experimental import pallas as pl
from jax.experimental.pallas import tpu as pltpu
from jax.sharding import PartitionSpec as P

H = 16
HD = 64
CSIZE = 128
HALF = CSIZE // 2
MAXB = 4
SITE = 4
BATCHES = 4
BF = jnp.bfloat16
F32 = jnp.float32


def params(mib=40):
    return pltpu.CompilerParams(vmem_limit_bytes=mib * 1024 * 1024)


def pack_kernel(q_ref, k_ref, v_ref, c_ref, w_ref, out_ref):
    keys = k_ref[...]
    vals = v_ref[...].T
    qrys = q_ref[...].T
    grad = lax.dot_general(
        w_ref[...], c_ref[...], (((1,), (1,)), ((), ())), preferred_element_type=F32
    ).astype(BF)
    for i in range(2):
        part = keys[:, i * HD : (i + 1) * HD]
        out_ref[i, 0:HALF, :] = jnp.concatenate([part[:HALF], part[HALF:]], axis=1)
        out_ref[i, 64:128, :] = vals[i * HD : (i + 1) * HD]
        out_ref[i, 128:192, :] = qrys[i * HD : (i + 1) * HD]
        out_ref[i, 192:256, :] = grad[i * HD : (i + 1) * HD]


def pack(q, k, v, cot, w_out):
    rows, width = q.shape
    pair = pl.BlockSpec((rows, 2 * HD), lambda i: (0, i))
    return pl.pallas_call(
        pack_kernel,
        grid=(H // 2,),
        in_specs=[
            pair,
            pair,
            pair,
            pl.BlockSpec((rows, width), lambda i: (0, 0)),
            pl.BlockSpec((2 * HD, width), lambda i: (i, 0)),
        ],
        out_specs=pl.BlockSpec((2, 256, CSIZE), lambda i: (i, 0, 0)),
        out_shape=jax.ShapeDtypeStruct((H, 256, CSIZE), BF),
        compiler_params=params(60),
        cost_estimate=pl.CostEstimate(
            flops=2 * rows * width * width, bytes_accessed=2 * width * width + 10 * rows * width, transcendentals=0
        ),
        name="pack",
    )(q, k, v, cot, w_out)


def forward_kernel(site_ref, blk_ref, cnt_ref, q_ref, kv_ref, att_ref, prob_ref):
    cluster = SITE * pl.program_id(0) + site_ref[0]
    number = cnt_ref[cluster]
    ids = [blk_ref[MAXB * cluster + j] for j in range(MAXB)]
    q = q_ref[0]
    zero = jnp.zeros_like(q)
    both = jnp.concatenate(
        [jnp.concatenate([q, zero], axis=1), jnp.concatenate([zero, q], axis=1)], axis=0
    )
    scores = []
    for j in range(MAXB):
        keys = kv_ref[ids[j] % SITE, ids[j] // SITE, 0:64, :]
        s = jnp.dot(keys, both, preferred_element_type=F32)
        scores.append(s if j == 0 else jnp.where(j < number, s, -1e30))
    s = jnp.concatenate(scores, axis=0)
    top = jnp.max(s, axis=0, keepdims=True)
    top = jnp.maximum(top[:, :CSIZE], top[:, CSIZE:])
    e = jnp.exp((s - jnp.concatenate([top, top], axis=1)) * (HD**-0.5))
    total = jnp.sum(e, axis=0, keepdims=True)
    total = total[:, :CSIZE] + total[:, CSIZE:]
    inv = 1.0 / total
    p = (e * jnp.concatenate([inv, inv], axis=1)).astype(BF)
    att = jnp.zeros((HD, CSIZE), F32)
    for j in range(MAXB):
        part = p[j * HALF : (j + 1) * HALF]
        pj = jnp.concatenate([part[:, :CSIZE], part[:, CSIZE:]], axis=0)
        prob_ref[0, j] = pj
        vals = kv_ref[ids[j] % SITE, ids[j] // SITE, 64:128, :]
        att += jnp.dot(vals, pj, preferred_element_type=F32)
    att_ref[0] = att.astype(BF)


def forward(site, blk, cnt, recv, kv):
    n = recv.shape[0]
    return pl.pallas_call(
        forward_kernel,
        grid_spec=pltpu.PrefetchScalarGridSpec(
            num_scalar_prefetch=3,
            grid=(n,),
            in_specs=[
                pl.BlockSpec((1, 64, CSIZE), lambda i, *_: (i, 2, 0)),
                pl.BlockSpec(kv.shape, lambda i, *_: (0, 0, 0, 0)),
            ],
            out_specs=[
                pl.BlockSpec((1, HD, CSIZE), lambda i, *_: (i, 0, 0)),
                pl.BlockSpec((1, MAXB, CSIZE, CSIZE), lambda i, *_: (i, 0, 0, 0)),
            ],
        ),
        out_shape=[
            jax.ShapeDtypeStruct((n, HD, CSIZE), BF),
            jax.ShapeDtypeStruct((n, MAXB, CSIZE, CSIZE), BF),
        ],
        compiler_params=params(),
        cost_estimate=pl.CostEstimate(
            flops=n * 4 * MAXB * CSIZE * CSIZE * HD, bytes_accessed=5 << 20, transcendentals=n * MAXB * CSIZE * CSIZE
        ),
        name="attend",
    )(site, blk, cnt, recv, kv)


def backward_kernel(site_ref, blk_ref, cnt_ref, g_ref, prob_ref, out_ref, acc_ref):
    step = pl.program_id(0)

    @pl.when(step == 0)
    def _():
        acc_ref[...] = jnp.zeros_like(acc_ref)

    cluster = SITE * step + site_ref[0]
    number = cnt_ref[cluster]
    g = g_ref[0]
    for j in range(MAXB):

        @pl.when(j < number)
        def _():
            at = blk_ref[MAXB * cluster + j]
            acc_ref[at] += lax.dot_general(
                g, prob_ref[0, j], (((1,), (1,)), ((), ())), preferred_element_type=F32
            )

    @pl.when(step == pl.num_programs(0) - 1)
    def _():
        for s in range(SITE):
            out_ref[s] = acc_ref[:, 16 * s : 16 * (s + 1), :].astype(BF)


def backward(site, blk, cnt, recv, probs):
    n = recv.shape[0]
    clusters = SITE * n
    return pl.pallas_call(
        backward_kernel,
        grid_spec=pltpu.PrefetchScalarGridSpec(
            num_scalar_prefetch=3,
            grid=(n,),
            in_specs=[
                pl.BlockSpec((1, 64, CSIZE), lambda i, *_: (i, 3, 0)),
                pl.BlockSpec((1, MAXB, CSIZE, CSIZE), lambda i, *_: (i, 0, 0, 0)),
            ],
            out_specs=pl.BlockSpec((SITE, clusters, 16, CSIZE), lambda i, *_: (0, 0, 0, 0)),
            scratch_shapes=[pltpu.VMEM((clusters, HD, CSIZE), F32)],
        ),
        out_shape=jax.ShapeDtypeStruct((SITE, clusters, 16, CSIZE), BF),
        compiler_params=params(),
        cost_estimate=pl.CostEstimate(
            flops=n * 2 * MAXB * CSIZE * CSIZE * HD, bytes_accessed=3 << 20, transcendentals=0
        ),
        name="value_contrib",
    )(site, blk, cnt, recv, probs)


def split_kernel(att_ref, out_ref, wide_ref):
    wide_ref[...] = att_ref[...].astype(F32)
    n = out_ref.shape[0]
    for p in range(n):
        out_ref[p] = wide_ref[pl.ds(p, out_ref.shape[1], stride=n), :].astype(BF)


def split_rows(att_t, n):
    rows = att_t.shape[0]
    return pl.pallas_call(
        split_kernel,
        out_shape=jax.ShapeDtypeStruct((n, rows // n, CSIZE), BF),
        scratch_shapes=[pltpu.VMEM((rows, CSIZE), F32)],
        compiler_params=params(),
        cost_estimate=pl.CostEstimate(flops=0, bytes_accessed=4 * rows * CSIZE, transcendentals=0),
        name="split_rows",
    )(att_t)


def weight_kernel(att_ref, cot_ref, out_ref):
    @pl.when(pl.program_id(0) == 0)
    def _():
        out_ref[...] = jnp.zeros_like(out_ref)

    att = jnp.concatenate([att_ref[i] for i in range(BATCHES)], axis=1)
    out_ref[...] += jnp.dot(att, cot_ref[...], preferred_element_type=F32)


def weight_part(att, cots):
    n, rows, nodes = att.shape
    width = cots.shape[1]
    return pl.pallas_call(
        weight_kernel,
        grid=(n // BATCHES,),
        in_specs=[
            pl.BlockSpec((BATCHES, rows, nodes), lambda i: (i, 0, 0)),
            pl.BlockSpec((BATCHES * nodes, width), lambda i: (i, 0)),
        ],
        out_specs=pl.BlockSpec((rows, width), lambda i: (0, 0)),
        out_shape=jax.ShapeDtypeStruct((rows, width), F32),
        compiler_params=params(),
        cost_estimate=pl.CostEstimate(
            flops=2 * n * rows * nodes * width, bytes_accessed=2 * n * nodes * width, transcendentals=0
        ),
        name="weight_part",
    )(att, cots)


def flip_kernel(x_ref, out_ref):
    out_ref[...] = x_ref[...].T


def flip(x):
    rows, cols = x.shape
    return pl.pallas_call(
        flip_kernel,
        out_shape=jax.ShapeDtypeStruct((cols, rows), x.dtype),
        compiler_params=params(),
        cost_estimate=pl.CostEstimate(flops=0, bytes_accessed=4 * rows * cols, transcendentals=0),
        name="flip",
    )(x)


def body(queries, keys, values, cotangent, w_out, blocks, counts):
    nseq = lax.axis_size("seq")
    ndp = lax.axis_size("dp")
    width = w_out.shape[0]
    site = (lax.axis_index("seq") % SITE).astype(jnp.int32)[None]
    same_site = [[SITE * h + s for h in range(H)] for s in range(SITE)]
    same_head = [[SITE * h + s for s in range(SITE)] for h in range(H)]
    blk = blocks[0].reshape(-1)
    cnt = counts[0]
    cot = cotangent[0]

    sent = pack(queries[0], keys[0], values[0], cot, w_out)
    recv = lax.all_to_all(sent, "seq", split_axis=0, concat_axis=0, tiled=True, axis_index_groups=same_site)

    cots = lax.all_gather(cot, "dp", axis=0, tiled=True)

    kv, cots = lax.optimization_barrier((recv[:, :128], cots))
    kv = lax.all_gather(kv, "seq", axis_index_groups=same_head, axis=0, tiled=False)
    att, probs = forward(site, blk, cnt, recv, kv)
    att_home = lax.all_to_all(att, "seq", split_axis=0, concat_axis=0, tiled=True, axis_index_groups=same_site)
    contrib = backward(site, blk, cnt, recv, probs)
    contrib = lax.psum_scatter(contrib, "seq", axis_index_groups=same_head, scatter_dimension=0, tiled=False)

    att_t = att_home.reshape(width, CSIZE)
    pieces = lax.all_to_all(split_rows(att_t, ndp), "dp", split_axis=0, concat_axis=0, tiled=True)
    part = weight_part(pieces, cots)
    layer_out = lax.dot_general(
        att_t, w_out, (((0,), (0,)), ((), ())), preferred_element_type=F32
    ).astype(BF)

    last = jnp.concatenate([contrib, part.astype(BF).reshape(nseq, -1, CSIZE)], axis=1)
    back = lax.all_to_all(last, "seq", split_axis=0, concat_axis=0, tiled=True)
    rows = jnp.sum(back[:, 16:].astype(F32), axis=0)
    every = lax.all_to_all(
        jnp.broadcast_to(rows[None], (ndp,) + rows.shape), "dp", split_axis=0, concat_axis=0, tiled=True
    )
    value_grad = flip(back[:, :16].reshape(width, CSIZE))
    weight_grad = every.reshape(width // nseq, width)
    return (layer_out[None], value_grad[None], weight_grad)


def solution(mesh):
    return jax.shard_map(
        body,
        mesh=mesh,
        in_specs=(
            P("dp", "seq", None),
            P("dp", "seq", None),
            P("dp", "seq", None),
            P("dp", "seq", None),
            P(),
            P("dp", None, None),
            P("dp", None),
        ),
        out_specs=(P("dp", "seq", None), P("dp", "seq", None), P("seq", None)),
        check_vma=False,
    )
```

time: 868 us -> 364 us (0.42)
  the two profiles are of different devices: /device:TPU:32 before, /device:TPU:1 now
where the time goes in v1:
time: 364 us
  waiting for transfers between devices  170 us (47%)
  blocking collectives  89.1 us (24%)
  starting transfers between devices  57.2 us (16%)
  Pallas kernels  24.6 us (7%)
  between operations  13.9 us (4%)
  local copies, waits for them, and re-layouts  6.94 us (2%)
    all_to_all x1, waiting for transfers between devices, body(): lax.all_to_all(sent, 'seq', split_axis=0, concat_axis=0, tiled=True, axis...  91.7 us
    all_to_all x1, blocking collectives, body(): back = lax.all_to_all(last, 'seq', split_axis=0, concat_axis=0, tiled=True)  75.2 us
    all_gather x1, waiting for transfers between devices, body(): lax.all_gather(kv, 'seq', axis_index_groups=same_head, axis=0, tiled=False)  49.9 us
    all_to_all x1, starting transfers between devices, body(): lax.all_to_all(sent, 'seq', split_axis=0, concat_axis=0, tiled=True, axis...  29.1 us
    all_to_all x1, starting transfers between devices, body(): lax.all_to_all(att, 'seq', split_axis=0, concat_axis=0, tiled=True, axis_...  21.5 us
    all_to_all x1, waiting for transfers between devices, body(): lax.all_to_all(att, 'seq', split_axis=0, concat_axis=0, tiled=True, axis_...  18.3 us
    all_to_all x1, blocking collectives, body(): lax.all_to_all(split_rows(att_t, ndp), 'dp', split_axis=0, concat_axis=0,...  13.9 us
    pallas_call x1, Pallas kernels, backward(): pl.pallas_call(backward_kernel, grid_spec=pltpu.PrefetchScalarGridSpec(nu...  7.88 us
  transfers between devices with their start and end apart: 6, of which 6 were waited for; matrix products, arithmetic and copies ran while one was open for 1% of the time, Pallas kernels for 3%

profile of v1, /device:TPU:1, one launch (start us, length us, event | category | flops | bytes accessed | tf_op | source)
XLA Modules:
  0.0 363.6 jit_solution(10120195019264548952)
XLA Ops:
  7.2 6.7 %pack.1 = bf16[16,256,128]{2,1,0:T(8,128)(2,1)} custom-call(bf16[128,1024]{1,0:T(8,128)(2,1)} %bitcast.32, bf16[128,1024]{1,0:T(8,128)(2,1)} %bitcast.33, bf16[128,1024]{1,0:T(8,128)(2,1)} %bitcast.34, bf16[128,1024]{1,0:T(8,128)(2,1)} %bitcast.30, bf16[1024,1024]{1,0:T(8,128)(2,1)} %w_ref.1), custom_call_target="tpu_custom_call" | custom-call | flops 268435456 | bytes 3407872 | tf_op jit(solution)/shard_map/pack/pallas_call | solution.py:41
  13.8 29.1 %all-to-all-start = ((bf16[16,256,128]{2,1,0:T(8,128)(2,1)}), bf16[16,256,128]{2,1,0:T(8,128)(2,1)S(1)}, u32[]{:S(2)}, u32[]{:S(2)}) async-start(bf16[16,256,128]{2,1,0:T(8,128)(2,1)} %pack.1), calls=%async_computation | async-start | bytes 2097152 | tf_op jit(solution)/shard_map/all_to_all | solution.py:245
  43.0 0.7 all-gather.5.cloned.1.call-update
  43.8 91.7 %all-to-all-done.q_ref.g_ref = bf16[16,256,128]{2,1,0:T(8,128)(2,1)S(1)} async-done(((bf16[16,256,128]{2,1,0:T(8,128)(2,1)}), bf16[16,256,128]{2,1,0:T(8,128)(2,1)S(1)}, u32[]{:S(2)}, u32[]{:S(2)}) %all-to-all-start) | async-done | bytes 1048608 | tf_op jit(solution)/shard_map/all_to_all | solution.py:245
  135.5 0.8 slice.12
  136.7 49.9 %all-gather.7.cloned.1.call-done = bf16[64,128,128]{2,1,0:T(8,128)(2,1)} async-done(((bf16[16,128,128]{2,1,0:T(8,128)(2,1)}), bf16[64,128,128]{2,1,0:T(8,128)(2,1)}) %all-gather.7.cloned.1.call-update) | async-done | bytes 2097168 | tf_op jit(solution)/shard_map/all_gather | solution.py:250
  186.5 1.6 copy-done.1
  188.1 7.8 %attend.1 = (bf16[16,64,128]{2,1,0:T(8,128)(2,1)S(1)}, bf16[16,4,128,128]{3,2,1,0:T(8,128)(2,1)S(1)}) custom-call(s32[1]{0:T(128)} %bitcast.site_ref, s32[256]{0:T(256)S(1)} %reshape_squeeze.3.blk_ref, s32[64]{0:T(128)S(1)} %bitcast.28, bf16[16,256,128]{2,1,0:T(8,128)(2,1)S(1)} %all-to-all-done.q_ref.g_ref, bf16[4,16,128,128]{3,2,1,0:T(8,128)(2,1)S(1)} %bitcast.26), custom_call_target="tpu_custom_call" | custom-call | flops 268435456 | bytes 5242880 | tf_op jit(solution)/shard_map/attend/pallas_call | solution.py:95
  195.9 0.7 copy-done.2
  196.6 21.5 %all-to-all-start.1 = ((bf16[16,64,128]{2,1,0:T(8,128)(2,1)}), bf16[16,64,128]{2,1,0:T(8,128)(2,1)S(1)}, u32[]{:S(2)}, u32[]{:S(2)}) async-start(bf16[16,64,128]{2,1,0:T(8,128)(2,1)} %copy-done.2), calls=%async_computation.1 | async-start | bytes 524288 | tf_op jit(solution)/shard_map/all_to_all | solution.py:252
  218.1 7.9 %value_contrib.1 = bf16[4,64,16,128]{3,2,1,0:T(8,128)(2,1)} custom-call(s32[1]{0:T(128)} %bitcast.site_ref, s32[256]{0:T(256)S(1)} %reshape_squeeze.3.blk_ref, s32[64]{0:T(128)S(1)} %bitcast.29, bf16[16,256,128]{2,1,0:T(8,128)(2,1)S(1)} %all-to-all-done.q_ref.g_ref, bf16[16,4,128,128]{3,2,1,0:T(8,128)(2,1)S(1)} %get-tuple-element.9.prob_ref), custom_call_target="tpu_custom_call" | custom-call | flops 134217728 | bytes 3145728 | tf_op jit(solution)/shard_map/value_contrib/pallas_call | solution.py:149
  226.0 18.3 %all-to-all-done.1 = bf16[16,64,128]{2,1,0:T(8,128)(2,1)S(1)} async-done(((bf16[16,64,128]{2,1,0:T(8,128)(2,1)}), bf16[16,64,128]{2,1,0:T(8,128)(2,1)S(1)}, u32[]{:S(2)}, u32[]{:S(2)}) %all-to-all-start.1) | async-done | bytes 262176 | tf_op jit(solution)/shard_map/all_to_all | solution.py:252
  244.5 13.9 %all_to_all.25.att_ref = bf16[16,64,128]{2,1,0:T(8,128)(2,1)S(1)} all-to-all(bf16[16,64,128]{2,1,0:T(8,128)(2,1)S(1)} %split_rows.1), channel_id=1, replica_groups=mesh['dp'=16,'seq'=64] {'dp'}, dimensions={0} | all-to-all | bytes 524288 | tf_op jit(solution)/shard_map/all_to_all | solution.py:257
  258.4 2.3 copy-done
  260.7 1.3 weight_part.1
  262.0 4.4 %reduce-scatter.2.cloned.1.call-done = bf16[1,64,16,128]{3,2,1,0:T(8,128)(2,1)} async-done(((bf16[4,64,16,128]{3,2,1,0:T(8,128)(2,1)}), bf16[1,64,16,128]{3,2,1,0:T(8,128)(2,1)}) %reduce-scatter.2.cloned.1.call-update) | async-done | bytes 262160 | tf_op jit(solution)/shard_map/reduce_scatter | solution.py:254
  266.4 1.0 pad_maximum_fusion
  267.4 75.2 %all_to_all.26 = bf16[64,24,128]{2,1,0:T(8,128)(2,1)S(1)} all-to-all(bf16[64,24,128]{2,1,0:T(8,128)(2,1)S(1)} %pad_maximum_fusion), channel_id=1, replica_groups=mesh['dp'=16,'seq'=64] {'seq'}, dimensions={0} | all-to-all | bytes 786432 | tf_op jit(solution)/shard_map/all_to_all | solution.py:264
  342.8 0.6 broadcast_in_dim.18
  343.4 6.5 %all-to-all-start.4 = ((f32[16,8,128]{2,1,0:T(8,128)}), f32[16,8,128]{2,1,0:T(8,128)S(1)}, u32[]{:S(2)}, u32[]{:S(2)}) async-start(f32[16,8,128]{2,1,0:T(8,128)} %broadcast_in_dim.18), calls=%async_computation.5 | async-start | bytes 131072 | tf_op jit(solution)/shard_map/all_to_all | solution.py:266
  349.9 1.2 fusion
  351.1 0.8 flip.1
  351.9 4.5 %all-to-all-done.4 = f32[16,8,128]{2,1,0:T(8,128)S(1)} async-done(((f32[16,8,128]{2,1,0:T(8,128)}), f32[16,8,128]{2,1,0:T(8,128)S(1)}, u32[]{:S(2)}, u32[]{:S(2)}) %all-to-all-start.4) | async-done | bytes 65568 | tf_op jit(solution)/shard_map/all_to_all | solution.py:266
  356.4 0.6 copy.15
  (22 shorter events, 0.8 us)
Async XLA Ops:
  13.8 122.6 %copy-start.5 = (s32[1,64,4]{1,2,0:T(4,128)S(1)}, s32[1,64,4]{1,2,0:T(4,128)}, u32[]{:S(2)}) copy-start(s32[1,64,4]{1,2,0:T(4,128)} %param.12) | copy-start | bytes 3076
  13.8 172.7 %copy-start.3 = (s32[1,64]{1,0:T(1,128)S(1)}, s32[1,64]{1,0:T(1,128)}, u32[]{:S(2)}) copy-start(s32[1,64]{1,0:T(1,128)} %param.13) | copy-start | bytes 772
  13.8 121.7 %all-to-all-start = ((bf16[16,256,128]{2,1,0:T(8,128)(2,1)}), bf16[16,256,128]{2,1,0:T(8,128)(2,1)S(1)}, u32[]{:S(2)}, u32[]{:S(2)}) async-start(bf16[16,256,128]{2,1,0:T(8,128)(2,1)} %pack.1), calls=%async_computation | async-start | bytes 2097152 | tf_op jit(solution)/shard_map/all_to_all | solution.py:245
  43.0 93.4 %all-gather.5.cloned.1.call-start = ((), (), s32[]{:S(2)}) async-start(), calls=%async_computation.7 | async-start | bytes 4456448 | tf_op jit(solution)/shard_map/all_gather | solution.py:247
  43.7 142.8 %all-gather.7.cloned.1.call-start = ((), (), s32[]{:S(2)}) async-start(), calls=%async_computation.8 | async-start | bytes 2621440 | tf_op jit(solution)/shard_map/all_gather | solution.py:250
  186.5 1.6 copy-start.1
  195.9 0.7 copy-start.2
  196.6 47.7 %all-to-all-start.1 = ((bf16[16,64,128]{2,1,0:T(8,128)(2,1)}), bf16[16,64,128]{2,1,0:T(8,128)(2,1)S(1)}, u32[]{:S(2)}, u32[]{:S(2)}) async-start(bf16[16,64,128]{2,1,0:T(8,128)(2,1)} %copy-done.2), calls=%async_computation.1 | async-start | bytes 524288 | tf_op jit(solution)/shard_map/all_to_all | solution.py:252
  218.1 48.4 %reduce-scatter.2.cloned.1.call-start = ((), (), s32[]{:S(2)}) async-start(), calls=%async_computation.6 | async-start | bytes 1310720 | tf_op jit(solution)/shard_map/reduce_scatter | solution.py:254
  258.4 2.3 copy-start
  261.9 87.9 %copy-start.4 = (bf16[1024,1024]{1,0:T(8,128)(2,1)S(1)}, bf16[1024,1024]{1,0:T(8,128)(2,1)}, u32[]{:S(2)}) copy-start(bf16[1024,1024]{1,0:T(8,128)(2,1)} %w_ref.1) | copy-start | bytes 6291460
  343.4 13.0 %all-to-all-start.4 = ((f32[16,8,128]{2,1,0:T(8,128)}), f32[16,8,128]{2,1,0:T(8,128)S(1)}, u32[]{:S(2)}, u32[]{:S(2)}) async-start(f32[16,8,128]{2,1,0:T(8,128)} %broadcast_in_dim.18), calls=%async_computation.5 | async-start | bytes 131072 | tf_op jit(solution)/shard_map/all_to_all | solution.py:266
Sparse Core Ops, SparseCore 0:
  48.0 88.3 all-gather.4
  139.1 47.3 all-gather.6
  226.2 40.2 reduce-scatter.1

commit v2 on v1

--- a/solution.py
+++ b/solution.py
@@ -11,7 +11,9 @@
 HALF = CSIZE // 2
 MAXB = 4
 SITE = 4
-BATCHES = 4
+BATCHES = 8
+ROWS = 8
+PAIR = 8
 BF = jnp.bfloat16
 F32 = jnp.float32
 
@@ -20,14 +22,16 @@
     return pltpu.CompilerParams(vmem_limit_bytes=mib * 1024 * 1024)
 
 
-def pack_kernel(q_ref, k_ref, v_ref, c_ref, w_ref, out_ref):
+def pack_kernel(q_ref, k_ref, v_ref, c_ref, w_ref, out_ref, ct_ref):
+    @pl.when(pl.program_id(0) == 0)
+    def _():
+        ct_ref[...] = c_ref[...].T
+
     keys = k_ref[...]
     vals = v_ref[...].T
     qrys = q_ref[...].T
-    grad = lax.dot_general(
-        w_ref[...], c_ref[...], (((1,), (1,)), ((), ())), preferred_element_type=F32
-    ).astype(BF)
-    for i in range(2):
+    grad = jnp.dot(w_ref[...], ct_ref[...], preferred_element_type=F32).astype(BF)
+    for i in range(PAIR):
         part = keys[:, i * HD : (i + 1) * HD]
         out_ref[i, 0:HALF, :] = jnp.concatenate([part[:HALF], part[HALF:]], axis=1)
         out_ref[i, 64:128, :] = vals[i * HD : (i + 1) * HD]
@@ -37,18 +41,19 @@
 
 def pack(q, k, v, cot, w_out):
     rows, width = q.shape
-    pair = pl.BlockSpec((rows, 2 * HD), lambda i: (0, i))
+    pair = pl.BlockSpec((rows, PAIR * HD), lambda i: (0, i))
     return pl.pallas_call(
         pack_kernel,
-        grid=(H // 2,),
+        grid=(H // PAIR,),
         in_specs=[
             pair,
             pair,
             pair,
             pl.BlockSpec((rows, width), lambda i: (0, 0)),
-            pl.BlockSpec((2 * HD, width), lambda i: (i, 0)),
+            pl.BlockSpec((PAIR * HD, width), lambda i: (i, 0)),
         ],
-        out_specs=pl.BlockSpec((2, 256, CSIZE), lambda i: (i, 0, 0)),
+        out_specs=pl.BlockSpec((PAIR, 256, CSIZE), lambda i: (i, 0, 0)),
+        scratch_shapes=[pltpu.VMEM((width, rows), BF)],
         out_shape=jax.ShapeDtypeStruct((H, 256, CSIZE), BF),
         compiler_params=params(60),
         cost_estimate=pl.CostEstimate(
@@ -58,67 +63,83 @@
     )(q, k, v, cot, w_out)
 
 
-def forward_kernel(site_ref, blk_ref, cnt_ref, q_ref, kv_ref, att_ref, prob_ref):
-    cluster = SITE * pl.program_id(0) + site_ref[0]
-    number = cnt_ref[cluster]
-    ids = [blk_ref[MAXB * cluster + j] for j in range(MAXB)]
-    q = q_ref[0]
-    zero = jnp.zeros_like(q)
-    both = jnp.concatenate(
-        [jnp.concatenate([q, zero], axis=1), jnp.concatenate([zero, q], axis=1)], axis=0
-    )
-    scores = []
-    for j in range(MAXB):
-        keys = kv_ref[ids[j] % SITE, ids[j] // SITE, 0:64, :]
-        s = jnp.dot(keys, both, preferred_element_type=F32)
-        scores.append(s if j == 0 else jnp.where(j < number, s, -1e30))
-    s = jnp.concatenate(scores, axis=0)
-    top = jnp.max(s, axis=0, keepdims=True)
-    top = jnp.maximum(top[:, :CSIZE], top[:, CSIZE:])
-    e = jnp.exp((s - jnp.concatenate([top, top], axis=1)) * (HD**-0.5))
-    total = jnp.sum(e, axis=0, keepdims=True)
-    total = total[:, :CSIZE] + total[:, CSIZE:]
-    inv = 1.0 / total
-    p = (e * jnp.concatenate([inv, inv], axis=1)).astype(BF)
-    att = jnp.zeros((HD, CSIZE), F32)
-    for j in range(MAXB):
-        part = p[j * HALF : (j + 1) * HALF]
-        pj = jnp.concatenate([part[:, :CSIZE], part[:, CSIZE:]], axis=0)
-        prob_ref[0, j] = pj
-        vals = kv_ref[ids[j] % SITE, ids[j] // SITE, 64:128, :]
-        att += jnp.dot(vals, pj, preferred_element_type=F32)
-    att_ref[0] = att.astype(BF)
-
-
-def forward(site, blk, cnt, recv, kv):
+def forward_kernel(site_ref, blk_ref, cnt_ref, q_ref, kv0, kv1, kv2, kv3, att_ref, prob_ref, kv_ref, sems):
+    @pl.when(pl.program_id(0) == 0)
+    def _():
+        copies = [
+            pltpu.make_async_copy(part, kv_ref.at[t], sems.at[t])
+            for t, part in enumerate((kv0, kv1, kv2, kv3))
+        ]
+        for copy in copies:
+            copy.start()
+        for copy in copies:
+            copy.wait()
+
+    count = q_ref.shape[0]
+    ids, slots, scores = [], [], []
+    for u in range(count):
+        cluster = SITE * (count * pl.program_id(0) + u) + site_ref[0]
+        number = cnt_ref[cluster]
+        q = q_ref[u]
+        zero = jnp.zeros_like(q)
+        both = jnp.concatenate(
+            [jnp.concatenate([q, zero], axis=1), jnp.concatenate([zero, q], axis=1)], axis=0
+        )
+        at = [blk_ref[MAXB * cluster + j] for j in range(MAXB)]
+        ids.append([i // SITE for i in at])
+        slots.append([(i % SITE) ^ site_ref[0] for i in at])
+        mine = []
+        for j in range(MAXB):
+            keys = kv_ref[slots[u][j], ids[u][j], 0:64, :]
+            s = jnp.dot(keys, both, preferred_element_type=F32)
+            mine.append(s if j == 0 else jnp.where(j < number, s, -1e30))
+        scores.append(jnp.concatenate(mine, axis=0))
+    for u in range(count):
+        s = scores[u]
+        top = jnp.max(s, axis=0, keepdims=True)
+        top = jnp.maximum(top[:, :CSIZE], top[:, CSIZE:])
+        e = jnp.exp((s - jnp.concatenate([top, top], axis=1)) * (HD**-0.5))
+        total = jnp.sum(e, axis=0, keepdims=True)
+        inv = 1.0 / (total[:, :CSIZE] + total[:, CSIZE:])
+        p = (e * jnp.concatenate([inv, inv], axis=1)).astype(BF)
+        halves = [p[i * HALF : (i + 1) * HALF, h : h + CSIZE] for i in range(MAXB) for h in (0, CSIZE)]
+        for j in range(MAXB):
+            prob_ref[u, j] = jnp.concatenate(halves[2 * j : 2 * j + 2], axis=0)
+        vals = jnp.concatenate([kv_ref[slots[u][j], ids[u][j], 64:128, :] for j in range(MAXB)], axis=1)
+        att = jnp.dot(vals, jnp.concatenate(halves, axis=0), preferred_element_type=F32)
+        att_ref[u] = att.astype(BF)
+
+
+def forward(site, blk, cnt, recv, kvs):
     n = recv.shape[0]
     return pl.pallas_call(
         forward_kernel,
         grid_spec=pltpu.PrefetchScalarGridSpec(
             num_scalar_prefetch=3,
-            grid=(n,),
+            grid=(n // ROWS,),
             in_specs=[
-                pl.BlockSpec((1, 64, CSIZE), lambda i, *_: (i, 2, 0)),
-                pl.BlockSpec(kv.shape, lambda i, *_: (0, 0, 0, 0)),
+                pl.BlockSpec((ROWS, 64, CSIZE), lambda i, *_: (i, 2, 0)),
+            ]
+            + [pl.BlockSpec(memory_space=pl.ANY)] * SITE,
+            out_specs=[
+                pl.BlockSpec((ROWS, HD, CSIZE), lambda i, *_: (i, 0, 0)),
+                pl.BlockSpec((ROWS, MAXB, CSIZE, CSIZE), lambda i, *_: (i, 0, 0, 0)),
             ],
-            out_specs=[
-                pl.BlockSpec((1, HD, CSIZE), lambda i, *_: (i, 0, 0)),
-                pl.BlockSpec((1, MAXB, CSIZE, CSIZE), lambda i, *_: (i, 0, 0, 0)),
-            ],
+            scratch_shapes=[pltpu.VMEM((SITE,) + kvs[0].shape, BF), pltpu.SemaphoreType.DMA((SITE,))],
         ),
         out_shape=[
             jax.ShapeDtypeStruct((n, HD, CSIZE), BF),
             jax.ShapeDtypeStruct((n, MAXB, CSIZE, CSIZE), BF),
         ],
-        compiler_params=params(),
+        compiler_params=params(60),
         cost_estimate=pl.CostEstimate(
             flops=n * 4 * MAXB * CSIZE * CSIZE * HD, bytes_accessed=5 << 20, transcendentals=n * MAXB * CSIZE * CSIZE
         ),
         name="attend",
-    )(site, blk, cnt, recv, kv)
-
-
-def backward_kernel(site_ref, blk_ref, cnt_ref, g_ref, prob_ref, out_ref, acc_ref):
+    )(site, blk, cnt, recv, *kvs)
+
+
+def backward_kernel(site_ref, blk_ref, cnt_ref, g_ref, prob_ref, keep_ref, swap_ref, acc_ref):
     step = pl.program_id(0)
 
     @pl.when(step == 0)
@@ -139,8 +160,9 @@
 
     @pl.when(step == pl.num_programs(0) - 1)
     def _():
-        for s in range(SITE):
-            out_ref[s] = acc_ref[:, 16 * s : 16 * (s + 1), :].astype(BF)
+        for t in range(SITE):
+            first = pl.multiple_of(16 * (site_ref[0] ^ t), 16)
+            (swap_ref if t % 2 else keep_ref)[t // 2] = acc_ref[:, pl.ds(first, 16), :].astype(BF)
 
 
 def backward(site, blk, cnt, recv, probs):
@@ -155,10 +177,10 @@
                 pl.BlockSpec((1, 64, CSIZE), lambda i, *_: (i, 3, 0)),
                 pl.BlockSpec((1, MAXB, CSIZE, CSIZE), lambda i, *_: (i, 0, 0, 0)),
             ],
-            out_specs=pl.BlockSpec((SITE, clusters, 16, CSIZE), lambda i, *_: (0, 0, 0, 0)),
+            out_specs=[pl.BlockSpec((2, clusters, 16, CSIZE), lambda i, *_: (0, 0, 0, 0))] * 2,
             scratch_shapes=[pltpu.VMEM((clusters, HD, CSIZE), F32)],
         ),
-        out_shape=jax.ShapeDtypeStruct((SITE, clusters, 16, CSIZE), BF),
+        out_shape=[jax.ShapeDtypeStruct((2, clusters, 16, CSIZE), BF)] * 2,
         compiler_params=params(),
         cost_estimate=pl.CostEstimate(
             flops=n * 2 * MAXB * CSIZE * CSIZE * HD, bytes_accessed=3 << 20, transcendentals=0
@@ -191,23 +213,24 @@
     def _():
         out_ref[...] = jnp.zeros_like(out_ref)
 
-    att = jnp.concatenate([att_ref[i] for i in range(BATCHES)], axis=1)
+    att = jnp.concatenate([att_ref[i] for i in range(att_ref.shape[0])], axis=1)
     out_ref[...] += jnp.dot(att, cot_ref[...], preferred_element_type=F32)
 
 
 def weight_part(att, cots):
     n, rows, nodes = att.shape
     width = cots.shape[1]
+    batches = min(BATCHES, n)
     return pl.pallas_call(
         weight_kernel,
-        grid=(n // BATCHES,),
+        grid=(n // batches,),
         in_specs=[
-            pl.BlockSpec((BATCHES, rows, nodes), lambda i: (i, 0, 0)),
-            pl.BlockSpec((BATCHES * nodes, width), lambda i: (i, 0)),
+            pl.BlockSpec((batches, rows, nodes), lambda i: (i, 0, 0)),
+            pl.BlockSpec((batches * nodes, width), lambda i: (i, 0)),
         ],
         out_specs=pl.BlockSpec((rows, width), lambda i: (0, 0)),
         out_shape=jax.ShapeDtypeStruct((rows, width), F32),
-        compiler_params=params(),
+        compiler_params=params(60),
         cost_estimate=pl.CostEstimate(
             flops=2 * n * rows * nodes * width, bytes_accessed=2 * n * nodes * width, transcendentals=0
         ),
@@ -236,7 +259,10 @@
     width = w_out.shape[0]
     site = (lax.axis_index("seq") % SITE).astype(jnp.int32)[None]
     same_site = [[SITE * h + s for h in range(H)] for s in range(SITE)]
-    same_head = [[SITE * h + s for s in range(SITE)] for h in range(H)]
+
+    def swap(x, bit):
+        return lax.ppermute(x, "seq", [(i, i ^ bit) for i in range(nseq)])
+
     blk = blocks[0].reshape(-1)
     cnt = counts[0]
     cot = cotangent[0]
@@ -247,11 +273,13 @@
     cots = lax.all_gather(cot, "dp", axis=0, tiled=True)
 
     kv, cots = lax.optimization_barrier((recv[:, :128], cots))
-    kv = lax.all_gather(kv, "seq", axis_index_groups=same_head, axis=0, tiled=False)
-    att, probs = forward(site, blk, cnt, recv, kv)
+    kv_z = swap(kv, 2)
+    kvs = [kv, swap(kv, 1), kv_z, swap(kv_z, 1)]
+    att, probs = forward(site, blk, cnt, recv, kvs)
     att_home = lax.all_to_all(att, "seq", split_axis=0, concat_axis=0, tiled=True, axis_index_groups=same_site)
-    contrib = backward(site, blk, cnt, recv, probs)
-    contrib = lax.psum_scatter(contrib, "seq", axis_index_groups=same_head, scatter_dimension=0, tiled=False)
+    keep, give = backward(site, blk, cnt, recv, probs)
+    chip = (keep.astype(F32) + swap(give, 1).astype(F32)).astype(BF)
+    contrib = (chip[0].astype(F32) + swap(chip[1], 2).astype(F32)).astype(BF)
 
     att_t = att_home.reshape(width, CSIZE)
     pieces = lax.all_to_all(split_rows(att_t, ndp), "dp", split_axis=0, concat_axis=0, tiled=True)

time: 364 us -> 321 us (0.88)
  waiting for transfers between devices: 170 us -> 119 us
  starting transfers between devices: 57.2 us -> 82.8 us
  blocking collectives: 89.1 us -> 73 us
    all_gather x1 -> x0, waiting for transfers between devices: 49.9 us -> none  [body(): lax.all_gather(kv, 'seq', axis_index_groups=same_head, axis=0, tiled=False)]
    ppermute x0 -> x5, starting transfers between devices: none -> 26.1 us  [swap(): return lax.ppermute(x, 'seq', [(i, i ^ bit) for i in range(nseq)])]
    all_to_all x1 -> x0, blocking collectives: 13.9 us -> none  [body(): lax.all_to_all(split_rows(att_t, ndp), 'dp', split_axis=0, concat_axis=0,...]
    all_to_all x0 -> x1, waiting for transfers between devices: none -> 7.45 us  [body(): lax.all_to_all(split_rows(att_t, ndp), 'dp', split_axis=0, concat_axis=0,...]
    all_to_all x1, waiting for transfers between devices: 18.3 us -> 11.5 us  [body(): lax.all_to_all(att, 'seq', split_axis=0, concat_axis=0, tiled=True, axis_...]
    all_to_all x0 -> x1, starting transfers between devices: none -> 5.03 us  [body(): lax.all_to_all(split_rows(att_t, ndp), 'dp', split_axis=0, concat_axis=0,...]
    reduce_scatter x1 -> x0, waiting for transfers between devices: 4.43 us -> none  [body(): lax.psum_scatter(contrib, 'seq', axis_index_groups=same_head, scatter_dim...]
  transfers between devices with their start and end apart: 6 -> 10, of which waited for: 6 -> 7; matrix products, arithmetic and copies ran while one was open for 1% -> 1% of each run, Pallas kernels for 3% -> 3%
where the time goes in v2:
time: 321 us
  waiting for transfers between devices  119 us (37%)
  starting transfers between devices  82.8 us (26%)
  blocking collectives  73 us (23%)
  Pallas kernels  22.1 us (7%)
  between operations  14.3 us (4%)
  local copies, waits for them, and re-layouts  6.47 us (2%)
    all_to_all x1, waiting for transfers between devices, body(): lax.all_to_all(sent, 'seq', split_axis=0, concat_axis=0, tiled=True, axis...  91.8 us
    all_to_all x1, blocking collectives, body(): back = lax.all_to_all(last, 'seq', split_axis=0, concat_axis=0, tiled=True)  73 us
    all_to_all x1, starting transfers between devices, body(): lax.all_to_all(sent, 'seq', split_axis=0, concat_axis=0, tiled=True, axis...  29.1 us
    ppermute x5, starting transfers between devices, swap(): return lax.ppermute(x, 'seq', [(i, i ^ bit) for i in range(nseq)])  26.1 us
    all_to_all x1, starting transfers between devices, body(): lax.all_to_all(att, 'seq', split_axis=0, concat_axis=0, tiled=True, axis_...  19 us
    all_to_all x1, waiting for transfers between devices, body(): lax.all_to_all(att, 'seq', split_axis=0, concat_axis=0, tiled=True, axis_...  11.5 us
    all_to_all x1, waiting for transfers between devices, body(): lax.all_to_all(split_rows(att_t, ndp), 'dp', split_axis=0, concat_axis=0,...  7.45 us
    pallas_call x1, Pallas kernels, backward(): pl.pallas_call(backward_kernel, grid_spec=pltpu.PrefetchScalarGridSpec(nu...  7.06 us
  transfers between devices with their start and end apart: 10, of which 7 were waited for; matrix products, arithmetic and copies ran while one was open for 1% of the time, Pallas kernels for 3%

profile of v2, /device:TPU:1, one launch (start us, length us, event | category | flops | bytes accessed | tf_op | source)
XLA Modules:
  0.0 320.6 jit_solution(290198908121227245)
XLA Ops:
  7.2 3.4 %pack.1 = bf16[16,256,128]{2,1,0:T(8,128)(2,1)} custom-call(bf16[128,1024]{1,0:T(8,128)(2,1)} %bitcast.36, bf16[128,1024]{1,0:T(8,128)(2,1)} %bitcast.37, bf16[128,1024]{1,0:T(8,128)(2,1)} %bitcast.38, bf16[128,1024]{1,0:T(8,128)(2,1)} %bitcast.34, bf16[1024,1024]{1,0:T(8,128)(2,1)} %w_ref.1), custom_call_target="tpu_custom_call" | custom-call | flops 268435456 | bytes 3407872 | tf_op jit(solution)/shard_map/pack/pallas_call | solution.py:45
  10.6 29.1 %all-to-all-start = ((bf16[16,256,128]{2,1,0:T(8,128)(2,1)}), bf16[16,256,128]{2,1,0:T(8,128)(2,1)S(1)}, u32[]{:S(2)}, u32[]{:S(2)}) async-start(bf16[16,256,128]{2,1,0:T(8,128)(2,1)} %pack.1), calls=%async_computation | async-start | bytes 2097152 | tf_op jit(solution)/shard_map/all_to_all | solution.py:271
  40.4 91.8 %all-to-all-done.q_ref.g_ref = bf16[16,256,128]{2,1,0:T(8,128)(2,1)S(1)} async-done(((bf16[16,256,128]{2,1,0:T(8,128)(2,1)}), bf16[16,256,128]{2,1,0:T(8,128)(2,1)S(1)}, u32[]{:S(2)}, u32[]{:S(2)}) %all-to-all-start) | async-done | bytes 1048608 | tf_op jit(solution)/shard_map/all_to_all | solution.py:271
  133.1 5.6 %collective-permute-start.1 = (bf16[16,128,128]{2,1,0:T(8,128)(2,1)S(1)}, bf16[16,128,128]{2,1,0:T(8,128)(2,1)S(1)}, u32[]{:S(2)}, u32[]{:S(2)}) collective-permute-start(bf16[16,128,128]{2,1,0:T(8,128)(2,1)S(1)} %slice.20.kv0), channel_id=1, source_target_pairs={{0,2},{1,3},{2,0},{3,1},{4,6},{5,7},{6,4},{7,5},{8,10},{9,11},{10,... | collective-permute-start | bytes 1572872 | tf_op jit(solution)/shard_map/ppermute | solution.py:264
  138.7 8.7 %collective-permute-start = (bf16[16,128,128]{2,1,0:T(8,128)(2,1)S(1)}, bf16[16,128,128]{2,1,0:T(8,128)(2,1)S(1)}, u32[]{:S(2)}, u32[]{:S(2)}) collective-permute-start(bf16[16,128,128]{2,1,0:T(8,128)(2,1)S(1)} %slice.20.kv0), channel_id=1, source_target_pairs={{0,1},{1,0},{2,3},{3,2},{4,5},{5,4},{6,7},{7,6},{8,9},{9,8},{10,11... | collective-permute-start | bytes 1572872 | tf_op jit(solution)/shard_map/ppermute | solution.py:264
  147.5 7.1 %collective-permute-start.2 = (bf16[16,128,128]{2,1,0:T(8,128)(2,1)S(1)}, bf16[16,128,128]{2,1,0:T(8,128)(2,1)S(1)}, u32[]{:S(2)}, u32[]{:S(2)}) collective-permute-start(bf16[16,128,128]{2,1,0:T(8,128)(2,1)S(1)} %collective-permute-done.1.kv2), channel_id=1, source_target_pairs={{0,1},{1,0},{2,3},{3,2},{4,5},{5,4},{6,7},{7,6},{8,9},{9,8},{10,11... | collective-permute-start | bytes 1572872 | tf_op jit(solution)/shard_map/ppermute | solution.py:264
  156.9 6.4 %attend.1 = (bf16[16,64,128]{2,1,0:T(8,128)(2,1)}, bf16[16,4,128,128]{3,2,1,0:T(8,128)(2,1)}) custom-call(s32[1]{0:T(128)} %bitcast.site_ref, s32[256]{0:T(256)} %reshape_squeeze.3.blk_ref, s32[64]{0:T(128)} %bitcast.31, bf16[16,256,128]{2,1,0:T(8,128)(2,1)} %copy-done, bf16[16,128,128]{2,1,0:T(8,128)(2,1)} %copy-done.6, bf16[16,128,128]{2,1,0:T(8,128)(2,1)} %copy-done.9, ...), custom_call_target="tpu_custom_call" | custom-call | flops 268435456 | bytes 5242880 | tf_op jit(solution)/shard_map/attend/pallas_call | solution.py:115
  163.3 19.0 %all-to-all-start.1 = ((bf16[16,64,128]{2,1,0:T(8,128)(2,1)}), bf16[16,64,128]{2,1,0:T(8,128)(2,1)S(1)}, u32[]{:S(2)}, u32[]{:S(2)}) async-start(bf16[16,64,128]{2,1,0:T(8,128)(2,1)} %get-tuple-element.10), calls=%async_computation.1 | async-start | bytes 524288 | tf_op jit(solution)/shard_map/all_to_all | solution.py:279
  182.4 1.2 copy-done.1
  183.6 1.6 copy-done.2
  185.2 7.1 %value_contrib.1 = (bf16[2,64,16,128]{3,2,1,0:T(8,128)(2,1)S(1)}, bf16[2,64,16,128]{3,2,1,0:T(8,128)(2,1)S(1)}) custom-call(s32[1]{0:T(128)} %bitcast.site_ref, s32[256]{0:T(256)S(1)} %copy-done.3, s32[64]{0:T(128)S(1)} %bitcast.32, bf16[16,256,128]{2,1,0:T(8,128)(2,1)S(1)} %copy-done.1, bf16[16,4,128,128]{3,2,1,0:T(8,128)(2,1)S(1)} %copy-done.2), custom_call_target="tpu_custom_call" | custom-call | flops 134217728 | bytes 3145728 | tf_op jit(solution)/shard_map/value_contrib/pallas_call | solution.py:171
  192.2 2.0 collective-permute-start.3
  194.2 1.8 collective-permute-done.3
  196.2 2.7 collective-permute-start.4
  199.0 11.5 %all-to-all-done.1 = bf16[16,64,128]{2,1,0:T(8,128)(2,1)S(1)} async-done(((bf16[16,64,128]{2,1,0:T(8,128)(2,1)}), bf16[16,64,128]{2,1,0:T(8,128)(2,1)S(1)}, u32[]{:S(2)}, u32[]{:S(2)}) %all-to-all-start.1) | async-done | bytes 262176 | tf_op jit(solution)/shard_map/all_to_all | solution.py:279
  210.5 0.9 split_rows.1
  211.4 5.0 %all-to-all-start.2 = ((bf16[16,64,128]{2,1,0:T(8,128)(2,1)}), bf16[16,64,128]{2,1,0:T(8,128)(2,1)S(1)}, u32[]{:S(2)}, u32[]{:S(2)}) async-start(bf16[16,64,128]{2,1,0:T(8,128)(2,1)} %split_rows.1), calls=%async_computation.2 | async-start | bytes 524288 | tf_op jit(solution)/shard_map/all_to_all | solution.py:285
  216.5 7.5 %all-to-all-done.2.att_ref = bf16[16,64,128]{2,1,0:T(8,128)(2,1)S(1)} async-done(((bf16[16,64,128]{2,1,0:T(8,128)(2,1)}), bf16[16,64,128]{2,1,0:T(8,128)(2,1)S(1)}, u32[]{:S(2)}, u32[]{:S(2)}) %all-to-all-start.2) | async-done | bytes 262176 | tf_op jit(solution)/shard_map/all_to_all | solution.py:285
  224.7 3.5 %weight_part.1 = f32[64,1024]{1,0:T(8,128)} custom-call(bf16[16,64,128]{2,1,0:T(8,128)(2,1)} %copy-done.7, bf16[2048,1024]{1,0:T(8,128)(2,1)} %bitcast.33), custom_call_target="tpu_custom_call" | custom-call | flops 268435456 | bytes 4194304 | tf_op jit(solution)/shard_map/weight_part/pallas_call | solution.py:224
  228.2 1.1 convert_bitcast_fusion
  229.4 73.0 %all_to_all.25 = bf16[64,24,128]{2,1,0:T(8,128)(2,1)S(1)} all-to-all(bf16[64,24,128]{2,1,0:T(8,128)(2,1)S(1)} %pad_maximum_fusion), channel_id=1, replica_groups=mesh['dp'=16,'seq'=64] {'seq'}, dimensions={0} | all-to-all | bytes 786432 | tf_op jit(solution)/shard_map/all_to_all | solution.py:292
  303.1 3.5 %all-to-all-start.4 = ((f32[16,8,128]{2,1,0:T(8,128)}), f32[16,8,128]{2,1,0:T(8,128)S(1)}, u32[]{:S(2)}, u32[]{:S(2)}) async-start(f32[16,8,128]{2,1,0:T(8,128)} %broadcast_in_dim.18), calls=%async_computation.4 | async-start | bytes 131072 | tf_op jit(solution)/shard_map/all_to_all | solution.py:294
  306.6 1.2 fusion
  308.7 4.4 %all-to-all-done.4 = f32[16,8,128]{2,1,0:T(8,128)S(1)} async-done(((f32[16,8,128]{2,1,0:T(8,128)}), f32[16,8,128]{2,1,0:T(8,128)S(1)}, u32[]{:S(2)}, u32[]{:S(2)}) %all-to-all-start.4) | async-done | bytes 65568 | tf_op jit(solution)/shard_map/all_to_all | solution.py:294
  (42 shorter events, 7.1 us)
Async XLA Ops:
  10.6 144.0 %copy-start.11 = (s32[1,64,4]{1,2,0:T(4,128)S(1)}, s32[1,64,4]{1,2,0:T(4,128)}, u32[]{:S(2)}) copy-start(s32[1,64,4]{1,2,0:T(4,128)} %param.12) | copy-start | bytes 3076
  10.6 121.7 %all-to-all-start = ((bf16[16,256,128]{2,1,0:T(8,128)(2,1)}), bf16[16,256,128]{2,1,0:T(8,128)(2,1)S(1)}, u32[]{:S(2)}, u32[]{:S(2)}) async-start(bf16[16,256,128]{2,1,0:T(8,128)(2,1)} %pack.1), calls=%async_computation | async-start | bytes 2097152 | tf_op jit(solution)/shard_map/all_to_all | solution.py:271
  39.7 93.4 %all-gather.3.cloned.1.call-start = ((), (), s32[]{:S(2)}) async-start(), calls=%async_computation.5 | async-start | bytes 4456448 | tf_op jit(solution)/shard_map/all_gather | solution.py:273
  132.2 23.9 %copy-start = (bf16[16,256,128]{2,1,0:T(8,128)(2,1)}, bf16[16,256,128]{2,1,0:T(8,128)(2,1)S(1)}, u32[]{:S(2)}) copy-start(bf16[16,256,128]{2,1,0:T(8,128)(2,1)S(1)} %all-to-all-done.q_ref.g_ref) | copy-start | bytes 3145732
  132.3 23.8 %copy-start.6 = (bf16[16,128,128]{2,1,0:T(8,128)(2,1)}, bf16[16,128,128]{2,1,0:T(8,128)(2,1)S(1)}, u32[]{:S(2)}) copy-start(bf16[16,128,128]{2,1,0:T(8,128)(2,1)S(1)} %slice.20.kv0) | copy-start | bytes 1572868
  132.3 50.0 %copy-start.4 = (s32[1,64]{1,0:T(1,128)S(1)}, s32[1,64]{1,0:T(1,128)}, u32[]{:S(2)}) copy-start(s32[1,64]{1,0:T(1,128)} %param.13) | copy-start | bytes 772
  133.1 14.3 %collective-permute-start.1 = (bf16[16,128,128]{2,1,0:T(8,128)(2,1)S(1)}, bf16[16,128,128]{2,1,0:T(8,128)(2,1)S(1)}, u32[]{:S(2)}, u32[]{:S(2)}) collective-permute-start(bf16[16,128,128]{2,1,0:T(8,128)(2,1)S(1)} %slice.20.kv0), channel_id=1, source_target_pairs={{0,2},{1,3},{2,0},{3,1},{4,6},{5,7},{6,4},{7,5},{8,10},{9,11},{10,... | collective-permute-start | bytes 1572872 | tf_op jit(solution)/shard_map/ppermute | solution.py:264
  138.7 16.6 %collective-permute-start = (bf16[16,128,128]{2,1,0:T(8,128)(2,1)S(1)}, bf16[16,128,128]{2,1,0:T(8,128)(2,1)S(1)}, u32[]{:S(2)}, u32[]{:S(2)}) collective-permute-start(bf16[16,128,128]{2,1,0:T(8,128)(2,1)S(1)} %slice.20.kv0), channel_id=1, source_target_pairs={{0,1},{1,0},{2,3},{3,2},{4,5},{5,4},{6,7},{7,6},{8,9},{9,8},{10,11... | collective-permute-start | bytes 1572872 | tf_op jit(solution)/shard_map/ppermute | solution.py:264
  147.5 8.7 %copy-start.8 = (bf16[16,128,128]{2,1,0:T(8,128)(2,1)}, bf16[16,128,128]{2,1,0:T(8,128)(2,1)S(1)}, u32[]{:S(2)}) copy-start(bf16[16,128,128]{2,1,0:T(8,128)(2,1)S(1)} %collective-permute-done.1.kv2) | copy-start | bytes 1572868
  147.5 8.6 %collective-permute-start.2 = (bf16[16,128,128]{2,1,0:T(8,128)(2,1)S(1)}, bf16[16,128,128]{2,1,0:T(8,128)(2,1)S(1)}, u32[]{:S(2)}, u32[]{:S(2)}) collective-permute-start(bf16[16,128,128]{2,1,0:T(8,128)(2,1)S(1)} %collective-permute-done.1.kv2), channel_id=1, source_target_pairs={{0,1},{1,0},{2,3},{3,2},{4,5},{5,4},{6,7},{7,6},{8,9},{9,8},{10,11... | collective-permute-start | bytes 1572872 | tf_op jit(solution)/shard_map/ppermute | solution.py:264
  155.4 27.0 %copy-start.3 = (s32[256]{0:T(256)S(1)}, s32[256]{0:T(256)}, u32[]{:S(2)}) copy-start(s32[256]{0:T(256)} %reshape_squeeze.3.blk_ref) | copy-start | bytes 3076
  155.4 0.9 copy-start.9
  156.1 0.8 copy-start.10
  163.3 47.2 %all-to-all-start.1 = ((bf16[16,64,128]{2,1,0:T(8,128)(2,1)}), bf16[16,64,128]{2,1,0:T(8,128)(2,1)S(1)}, u32[]{:S(2)}, u32[]{:S(2)}) async-start(bf16[16,64,128]{2,1,0:T(8,128)(2,1)} %get-tuple-element.10), calls=%async_computation.1 | async-start | bytes 524288 | tf_op jit(solution)/shard_map/all_to_all | solution.py:279
  182.4 1.2 copy-start.1
  183.6 1.6 copy-start.2
  192.2 3.8 %collective-permute-start.3 = (bf16[2,64,16,128]{3,2,1,0:T(8,128)(2,1)S(1)}, bf16[2,64,16,128]{3,2,1,0:T(8,128)(2,1)S(1)}, u32[]{:S(2)}, u32[]{:S(2)}) collective-permute-start(bf16[2,64,16,128]{3,2,1,0:T(8,128)(2,1)S(1)} %get-tuple-element.13), channel_id=1, source_target_pairs={{0,1},{1,0},{2,3},{3,2},{4,5},{5,4},{6,7},{7,6},{8,9},{9,8},{10,11... | collective-permute-start | bytes 1572872 | tf_op jit(solution)/shard_map/ppermute | solution.py:264
  196.2 20.2 %collective-permute-start.4 = (bf16[64,16,128]{2,1,0:T(8,128)(2,1)S(1)}, bf16[64,16,128]{2,1,0:T(8,128)(2,1)S(1)}, u32[]{:S(2)}, u32[]{:S(2)}) collective-permute-start(bf16[64,16,128]{2,1,0:T(8,128)(2,1)S(1)} %slice_bitcast_fusion), channel_id=1, source_target_pairs={{0,2},{1,3},{2,0},{3,1},{4,6},{5,7},{6,4},{7,5},{8,10},{9,11},{10,... | collective-permute-start | bytes 786440 | tf_op jit(solution)/shard_map/ppermute | solution.py:264
  211.4 12.6 %all-to-all-start.2 = ((bf16[16,64,128]{2,1,0:T(8,128)(2,1)}), bf16[16,64,128]{2,1,0:T(8,128)(2,1)S(1)}, u32[]{:S(2)}, u32[]{:S(2)}) async-start(bf16[16,64,128]{2,1,0:T(8,128)(2,1)} %split_rows.1), calls=%async_computation.2 | async-start | bytes 524288 | tf_op jit(solution)/shard_map/all_to_all | solution.py:285
  224.0 0.7 copy-start.7
  228.2 78.4 %copy-start.5 = (bf16[1024,1024]{1,0:T(8,128)(2,1)S(1)}, bf16[1024,1024]{1,0:T(8,128)(2,1)}, u32[]{:S(2)}) copy-start(bf16[1024,1024]{1,0:T(8,128)(2,1)} %w_ref.1) | copy-start | bytes 6291460
  303.1 10.0 %all-to-all-start.4 = ((f32[16,8,128]{2,1,0:T(8,128)}), f32[16,8,128]{2,1,0:T(8,128)S(1)}, u32[]{:S(2)}, u32[]{:S(2)}) async-start(f32[16,8,128]{2,1,0:T(8,128)} %broadcast_in_dim.18), calls=%async_computation.4 | async-start | bytes 131072 | tf_op jit(solution)/shard_map/all_to_all | solution.py:294
Sparse Core Ops, SparseCore 0:
  44.7 88.3 all-gather.2

commit v3 on v2

--- a/solution.py
+++ b/solution.py
@@ -63,7 +63,7 @@
     )(q, k, v, cot, w_out)
 
 
-def forward_kernel(site_ref, blk_ref, cnt_ref, q_ref, kv0, kv1, kv2, kv3, att_ref, prob_ref, kv_ref, sems):
+def forward_kernel(site_ref, blk_ref, cnt_ref, q_ref, kv0, kv1, kv2, kv3, att_ref, prob_ref, kv_ref, wide_ref, sems):
     @pl.when(pl.program_id(0) == 0)
     def _():
         copies = [
@@ -107,10 +107,13 @@
             prob_ref[u, j] = jnp.concatenate(halves[2 * j : 2 * j + 2], axis=0)
         vals = jnp.concatenate([kv_ref[slots[u][j], ids[u][j], 64:128, :] for j in range(MAXB)], axis=1)
         att = jnp.dot(vals, jnp.concatenate(halves, axis=0), preferred_element_type=F32)
-        att_ref[u] = att.astype(BF)
-
-
-def forward(site, blk, cnt, recv, kvs):
+        wide_ref[u * HD : (u + 1) * HD, :] = att
+    split = att_ref.shape[0]
+    for p in range(split):
+        att_ref[p] = wide_ref[pl.ds(p, att_ref.shape[1], stride=split), :].astype(BF)
+
+
+def forward(site, blk, cnt, recv, kvs, split):
     n = recv.shape[0]
     return pl.pallas_call(
         forward_kernel,
@@ -122,13 +125,17 @@
             ]
             + [pl.BlockSpec(memory_space=pl.ANY)] * SITE,
             out_specs=[
-                pl.BlockSpec((ROWS, HD, CSIZE), lambda i, *_: (i, 0, 0)),
+                pl.BlockSpec((split, ROWS * HD // split, CSIZE), lambda i, *_: (0, i, 0)),
                 pl.BlockSpec((ROWS, MAXB, CSIZE, CSIZE), lambda i, *_: (i, 0, 0, 0)),
             ],
-            scratch_shapes=[pltpu.VMEM((SITE,) + kvs[0].shape, BF), pltpu.SemaphoreType.DMA((SITE,))],
+            scratch_shapes=[
+                pltpu.VMEM((SITE,) + kvs[0].shape, BF),
+                pltpu.VMEM((ROWS * HD, CSIZE), F32),
+                pltpu.SemaphoreType.DMA((SITE,)),
+            ],
         ),
         out_shape=[
-            jax.ShapeDtypeStruct((n, HD, CSIZE), BF),
+            jax.ShapeDtypeStruct((split, n * HD // split, CSIZE), BF),
             jax.ShapeDtypeStruct((n, MAXB, CSIZE, CSIZE), BF),
         ],
         compiler_params=params(60),
@@ -189,32 +196,20 @@
     )(site, blk, cnt, recv, probs)
 
 
-def split_kernel(att_ref, out_ref, wide_ref):
-    wide_ref[...] = att_ref[...].astype(F32)
-    n = out_ref.shape[0]
-    for p in range(n):
-        out_ref[p] = wide_ref[pl.ds(p, out_ref.shape[1], stride=n), :].astype(BF)
-
-
-def split_rows(att_t, n):
-    rows = att_t.shape[0]
-    return pl.pallas_call(
-        split_kernel,
-        out_shape=jax.ShapeDtypeStruct((n, rows // n, CSIZE), BF),
-        scratch_shapes=[pltpu.VMEM((rows, CSIZE), F32)],
-        compiler_params=params(),
-        cost_estimate=pl.CostEstimate(flops=0, bytes_accessed=4 * rows * CSIZE, transcendentals=0),
-        name="split_rows",
-    )(att_t)
-
-
-def weight_kernel(att_ref, cot_ref, out_ref):
-    @pl.when(pl.program_id(0) == 0)
-    def _():
-        out_ref[...] = jnp.zeros_like(out_ref)
+def weight_kernel(att_ref, cot_ref, out_ref, acc_ref):
+    step = pl.program_id(0)
+
+    @pl.when(step == 0)
+    def _():
+        acc_ref[...] = jnp.zeros_like(acc_ref)
 
     att = jnp.concatenate([att_ref[i] for i in range(att_ref.shape[0])], axis=1)
-    out_ref[...] += jnp.dot(att, cot_ref[...], preferred_element_type=F32)
+    acc_ref[...] += jnp.dot(att, cot_ref[...], preferred_element_type=F32)
+
+    @pl.when(step == pl.num_programs(0) - 1)
+    def _():
+        for i in range(out_ref.shape[1]):
+            out_ref[:, i, :] = acc_ref[:, CSIZE * i : CSIZE * (i + 1)]
 
 
 def weight_part(att, cots):
@@ -228,14 +223,70 @@
             pl.BlockSpec((batches, rows, nodes), lambda i: (i, 0, 0)),
             pl.BlockSpec((batches * nodes, width), lambda i: (i, 0)),
         ],
-        out_specs=pl.BlockSpec((rows, width), lambda i: (0, 0)),
-        out_shape=jax.ShapeDtypeStruct((rows, width), F32),
+        out_specs=pl.BlockSpec((rows, width // CSIZE, CSIZE), lambda i: (0, 0, 0)),
+        out_shape=jax.ShapeDtypeStruct((rows, width // CSIZE, CSIZE), F32),
+        scratch_shapes=[pltpu.VMEM((rows, width), F32)],
         compiler_params=params(60),
         cost_estimate=pl.CostEstimate(
             flops=2 * n * rows * nodes * width, bytes_accessed=2 * n * nodes * width, transcendentals=0
         ),
         name="weight_part",
     )(att, cots)
+
+
+def gather_kernel(back_ref, att_ref, out_ref):
+    n, rows, _ = att_ref.shape
+    total = jnp.sum(back_ref[...].astype(F32), axis=0)[16:]
+    high = total.astype(BF).astype(F32)
+    both = jnp.concatenate([high, total - high], axis=0).astype(BF)
+    for p in range(n):
+        out_ref[p, :rows, :] = att_ref[p]
+        out_ref[p, rows:, :] = both
+
+
+def gather_send(back, att):
+    n, rows, nodes = att.shape
+    more = 2 * (back.shape[1] - 16)
+    return pl.pallas_call(
+        gather_kernel,
+        out_shape=jax.ShapeDtypeStruct((n, rows + more, nodes), BF),
+        compiler_params=params(),
+        cost_estimate=pl.CostEstimate(flops=back.size, bytes_accessed=2 * back.size + 4 * att.size, transcendentals=0),
+        name="gather_send",
+    )(back, att)
+
+
+def finish_kernel(got_ref, w_ref, layer_ref, weight_ref, wide_ref, rows_ref):
+    n, total, nodes = got_ref.shape
+    rows = w_ref.shape[0] // n
+    more = (total - rows) // 2
+    for p in range(n):
+        wide_ref[pl.ds(p, rows, stride=n), :] = got_ref[p, :rows, :].astype(F32)
+        both = got_ref[p, rows:, :].astype(F32)
+        rows_ref[p * more : (p + 1) * more, :] = both[:more] + both[more:]
+    layer_ref[...] = jnp.dot(
+        wide_ref[...].T.astype(BF), w_ref[...], preferred_element_type=F32
+    ).astype(BF)
+    pieces = weight_ref.shape[1] // nodes
+    for i in range(pieces):
+        weight_ref[:, i * nodes : (i + 1) * nodes] = rows_ref[pl.ds(i, weight_ref.shape[0], stride=pieces), :]
+
+
+def finish(got, w_out, own):
+    nodes = got.shape[2]
+    width = w_out.shape[0]
+    more = (got.shape[1] - width // got.shape[0]) // 2
+    return pl.pallas_call(
+        finish_kernel,
+        out_shape=[
+            jax.ShapeDtypeStruct((nodes, width), BF),
+            jax.ShapeDtypeStruct((own, width), F32),
+        ],
+        scratch_shapes=[pltpu.VMEM((width, nodes), F32), pltpu.VMEM((got.shape[0] * more, nodes), F32)],
+        compiler_params=params(),
+        cost_estimate=pl.CostEstimate(flops=2 * nodes * width * width, bytes_accessed=2 * width * width, transcendentals=0),
+        name="finish",
+    )(got, w_out)
 
 
 def flip_kernel(x_ref, out_ref):
@@ -259,6 +310,7 @@
     width = w_out.shape[0]
     site = (lax.axis_index("seq") % SITE).astype(jnp.int32)[None]
     same_site = [[SITE * h + s for h in range(H)] for s in range(SITE)]
+    same_site_dp = [[p * nseq + i for p in range(ndp) for i in group] for group in same_site]
 
     def swap(x, bit):
         return lax.ppermute(x, "seq", [(i, i ^ bit) for i in range(nseq)])
@@ -275,27 +327,22 @@
     kv, cots = lax.optimization_barrier((recv[:, :128], cots))
     kv_z = swap(kv, 2)
     kvs = [kv, swap(kv, 1), kv_z, swap(kv_z, 1)]
-    att, probs = forward(site, blk, cnt, recv, kvs)
-    att_home = lax.all_to_all(att, "seq", split_axis=0, concat_axis=0, tiled=True, axis_index_groups=same_site)
+    att, probs = forward(site, blk, cnt, recv, kvs, ndp)
+    sent_att = att.reshape(ndp * H, HD // ndp, CSIZE)
+    pieces = lax.all_to_all(
+        sent_att, ("dp", "seq"), split_axis=0, concat_axis=0, tiled=True, axis_index_groups=same_site_dp
+    ).reshape(ndp, width // ndp, CSIZE)
     keep, give = backward(site, blk, cnt, recv, probs)
     chip = (keep.astype(F32) + swap(give, 1).astype(F32)).astype(BF)
     contrib = (chip[0].astype(F32) + swap(chip[1], 2).astype(F32)).astype(BF)
 
-    att_t = att_home.reshape(width, CSIZE)
-    pieces = lax.all_to_all(split_rows(att_t, ndp), "dp", split_axis=0, concat_axis=0, tiled=True)
-    part = weight_part(pieces, cots)
-    layer_out = lax.dot_general(
-        att_t, w_out, (((0,), (0,)), ((), ())), preferred_element_type=F32
-    ).astype(BF)
-
-    last = jnp.concatenate([contrib, part.astype(BF).reshape(nseq, -1, CSIZE)], axis=1)
-    back = lax.all_to_all(last, "seq", split_axis=0, concat_axis=0, tiled=True)
-    rows = jnp.sum(back[:, 16:].astype(F32), axis=0)
-    every = lax.all_to_all(
-        jnp.broadcast_to(rows[None], (ndp,) + rows.shape), "dp", split_axis=0, concat_axis=0, tiled=True
+    part = weight_part(pieces, cots).astype(BF).reshape(nseq, -1, CSIZE)
+    back = lax.all_to_all(
+        jnp.concatenate([contrib, part], axis=1), "seq", split_axis=0, concat_axis=0, tiled=True
     )
+    got = lax.all_to_all(gather_send(back, pieces), "dp", split_axis=0, concat_axis=0, tiled=True)
     value_grad = flip(back[:, :16].reshape(width, CSIZE))
-    weight_grad = every.reshape(width // nseq, width)
+    layer_out, weight_grad = finish(got, w_out, width // nseq)
     return (layer_out[None], value_grad[None], weight_grad)
 
 

time: 321 us -> 323 us (level)
  blocking collectives: 73 us -> 63.4 us
  starting transfers between devices: 82.8 us -> 90.1 us
  waiting for transfers between devices: 119 us -> 126 us
    ppermute x5, waiting for transfers between devices: 2.54 us -> 14.2 us  [swap(): return lax.ppermute(x, 'seq', [(i, i ^ bit) for i in range(nseq)])]
    all_to_all x1, blocking collectives: 73 us -> 63.4 us  [body(): lax.all_to_all(jnp.concatenate([contrib, part], axis=1), 'seq', split_axi...]
    all_to_all x3 -> x2, starting transfers between devices: 27.6 us -> 34.2 us  [the longest x1 26.9 us: body(): lax.all_to_all(sent_att, ('dp', 'seq'), split_axis=0, concat_axis=0, tile...]
    all_to_all x3 -> x2, waiting for transfers between devices: 23.4 us -> 18 us  [the longest x1 10.8 us: body(): lax.all_to_all(sent_att, ('dp', 'seq'), split_axis=0, concat_axis=0, tile...]
  transfers between devices with their start and end apart: 10 -> 9, of which waited for: 7 -> 7; matrix products, arithmetic and copies ran while one was open for 1% -> 0% of each run, Pallas kernels for 3% -> 2%
where the time goes in v3:
time: 323 us
  waiting for transfers between devices  126 us (39%)
  starting transfers between devices  90.1 us (28%)
  blocking collectives  63.4 us (20%)
  Pallas kernels  22.7 us (7%)
  between operations  14.2 us (4%)
  local copies, waits for them, and re-layouts  5.17 us (2%)
    all_to_all x1, waiting for transfers between devices, body(): lax.all_to_all(sent, 'seq', split_axis=0, concat_axis=0, tiled=True, axis...  91.8 us
    all_to_all x1, blocking collectives, body(): lax.all_to_all(jnp.concatenate([contrib, part], axis=1), 'seq', split_axi...  63.4 us
    all_to_all x1, starting transfers between devices, body(): lax.all_to_all(sent, 'seq', split_axis=0, concat_axis=0, tiled=True, axis...  29.1 us
    all_to_all x1, starting transfers between devices, body(): lax.all_to_all(sent_att, ('dp', 'seq'), split_axis=0, concat_axis=0, tile...  26.9 us
    ppermute x5, starting transfers between devices, swap(): return lax.ppermute(x, 'seq', [(i, i ^ bit) for i in range(nseq)])  26.8 us
    ppermute x5, waiting for transfers between devices, swap(): return lax.ppermute(x, 'seq', [(i, i ^ bit) for i in range(nseq)])  14.2 us
    all_to_all x1, waiting for transfers between devices, body(): lax.all_to_all(sent_att, ('dp', 'seq'), split_axis=0, concat_axis=0, tile...  10.8 us
    all_to_all x1, starting transfers between devices, body(): lax.all_to_all(gather_send(back, pieces), 'dp', split_axis=0, concat_axis...  7.31 us
  transfers between devices with their start and end apart: 9, of which 7 were waited for; matrix products, arithmetic and copies ran while one was open for 0% of the time, Pallas kernels for 2%

profile of v3, /device:TPU:1, one launch (start us, length us, event | category | flops | bytes accessed | tf_op | source)
XLA Modules:
  0.0 322.5 jit_solution(6156614562399440204)
XLA Ops:
  7.2 3.4 %pack.1 = bf16[16,256,128]{2,1,0:T(8,128)(2,1)} custom-call(bf16[128,1024]{1,0:T(8,128)(2,1)} %bitcast.26, bf16[128,1024]{1,0:T(8,128)(2,1)} %bitcast.27, bf16[128,1024]{1,0:T(8,128)(2,1)} %bitcast.28, bf16[128,1024]{1,0:T(8,128)(2,1)} %bitcast.25, bf16[1024,1024]{1,0:T(8,128)(2,1)} %w_ref.3), custom_call_target="tpu_custom_call" | custom-call | flops 268435456 | bytes 3407872 | tf_op jit(solution)/shard_map/pack/pallas_call | solution.py:45
  10.6 29.1 %all-to-all-start = ((bf16[16,256,128]{2,1,0:T(8,128)(2,1)}), bf16[16,256,128]{2,1,0:T(8,128)(2,1)S(1)}, u32[]{:S(2)}, u32[]{:S(2)}) async-start(bf16[16,256,128]{2,1,0:T(8,128)(2,1)} %pack.1), calls=%async_computation | async-start | bytes 2097152 | tf_op jit(solution)/shard_map/all_to_all | solution.py:323
  40.4 91.8 %all-to-all-done.q_ref.g_ref = bf16[16,256,128]{2,1,0:T(8,128)(2,1)S(1)} async-done(((bf16[16,256,128]{2,1,0:T(8,128)(2,1)}), bf16[16,256,128]{2,1,0:T(8,128)(2,1)S(1)}, u32[]{:S(2)}, u32[]{:S(2)}) %all-to-all-start) | async-done | bytes 1048608 | tf_op jit(solution)/shard_map/all_to_all | solution.py:323
  132.3 0.8 all-gather.3.cloned.1.call-done
  133.1 5.6 %collective-permute-start.1 = (bf16[16,128,128]{2,1,0:T(8,128)(2,1)S(1)}, bf16[16,128,128]{2,1,0:T(8,128)(2,1)S(1)}, u32[]{:S(2)}, u32[]{:S(2)}) collective-permute-start(bf16[16,128,128]{2,1,0:T(8,128)(2,1)S(1)} %slice.16.kv0), channel_id=1, source_target_pairs={{0,2},{1,3},{2,0},{3,1},{4,6},{5,7},{6,4},{7,5},{8,10},{9,11},{10,... | collective-permute-start | bytes 1572872 | tf_op jit(solution)/shard_map/ppermute | solution.py:316
  138.7 8.7 %collective-permute-start = (bf16[16,128,128]{2,1,0:T(8,128)(2,1)S(1)}, bf16[16,128,128]{2,1,0:T(8,128)(2,1)S(1)}, u32[]{:S(2)}, u32[]{:S(2)}) collective-permute-start(bf16[16,128,128]{2,1,0:T(8,128)(2,1)S(1)} %slice.16.kv0), channel_id=1, source_target_pairs={{0,1},{1,0},{2,3},{3,2},{4,5},{5,4},{6,7},{7,6},{8,9},{9,8},{10,11... | collective-permute-start | bytes 1572872 | tf_op jit(solution)/shard_map/ppermute | solution.py:316
  147.5 7.1 %collective-permute-start.2 = (bf16[16,128,128]{2,1,0:T(8,128)(2,1)S(1)}, bf16[16,128,128]{2,1,0:T(8,128)(2,1)S(1)}, u32[]{:S(2)}, u32[]{:S(2)}) collective-permute-start(bf16[16,128,128]{2,1,0:T(8,128)(2,1)S(1)} %collective-permute-done.1.kv2), channel_id=1, source_target_pairs={{0,1},{1,0},{2,3},{3,2},{4,5},{5,4},{6,7},{7,6},{8,9},{9,8},{10,11... | collective-permute-start | bytes 1572872 | tf_op jit(solution)/shard_map/ppermute | solution.py:316
  156.9 6.7 %attend.1 = (bf16[16,64,128]{2,1,0:T(8,128)(2,1)}, bf16[16,4,128,128]{3,2,1,0:T(8,128)(2,1)}) custom-call(s32[1]{0:T(128)} %bitcast.site_ref, s32[256]{0:T(256)} %reshape_squeeze.3.blk_ref, s32[64]{0:T(128)} %bitcast.22, bf16[16,256,128]{2,1,0:T(8,128)(2,1)} %copy-done, bf16[16,128,128]{2,1,0:T(8,128)(2,1)} %copy-done.8, bf16[16,128,128]{2,1,0:T(8,128)(2,1)} %copy-done.10, ...), custom_call_target="tpu_custom_call" | custom-call | flops 268435456 | bytes 5242880 | tf_op jit(solution)/shard_map/attend/pallas_call | solution.py:118
  163.6 26.9 %all-to-all-start.1 = ((bf16[256,4,128]{2,1,0:T(4,128)(2,1)}), bf16[256,4,128]{2,1,0:T(4,128)(2,1)S(1)}, u32[]{:S(2)}, u32[]{:S(2)}) async-start(bf16[256,4,128]{2,1,0:T(4,128)(2,1)} %bitcast.29), calls=%async_computation.1 | async-start | bytes 524288 | tf_op jit(solution)/shard_map/all_to_all | solution.py:332
  190.5 1.2 copy-done.1
  191.7 1.6 copy-done.5
  193.3 6.0 %value_contrib.1 = (bf16[2,64,16,128]{3,2,1,0:T(8,128)(2,1)S(1)}, bf16[2,64,16,128]{3,2,1,0:T(8,128)(2,1)S(1)}) custom-call(s32[1]{0:T(128)} %bitcast.site_ref, s32[256]{0:T(256)S(1)} %copy-done.6, s32[64]{0:T(128)S(1)} %bitcast.23, bf16[16,256,128]{2,1,0:T(8,128)(2,1)S(1)} %copy-done.1, bf16[16,4,128,128]{3,2,1,0:T(8,128)(2,1)S(1)} %copy-done.5), custom_call_target="tpu_custom_call" | custom-call | flops 134217728 | bytes 3145728 | tf_op jit(solution)/shard_map/value_contrib/pallas_call | solution.py:178
  199.3 3.5 %collective-permute-start.3 = (bf16[2,64,16,128]{3,2,1,0:T(8,128)(2,1)S(1)}, bf16[2,64,16,128]{3,2,1,0:T(8,128)(2,1)S(1)}, u32[]{:S(2)}, u32[]{:S(2)}) collective-permute-start(bf16[2,64,16,128]{3,2,1,0:T(8,128)(2,1)S(1)} %get-tuple-element.14), channel_id=1, source_target_pairs={{0,1},{1,0},{2,3},{3,2},{4,5},{5,4},{6,7},{7,6},{8,9},{9,8},{10,11... | collective-permute-start | bytes 1572872 | tf_op jit(solution)/shard_map/ppermute | solution.py:316
  202.8 1.5 collective-permute-done.3
  204.5 1.9 collective-permute-start.4
  206.4 12.0 %collective-permute-done.4 = bf16[64,16,128]{2,1,0:T(8,128)(2,1)S(1)} collective-permute-done((bf16[64,16,128]{2,1,0:T(8,128)(2,1)S(1)}, bf16[64,16,128]{2,1,0:T(8,128)(2,1)S(1)}, u32[]{:S(2)}, u32[]{:S(2)}) %collective-permute-start.4) | collective-permute-done | bytes 262176 | tf_op jit(solution)/shard_map/ppermute | solution.py:316
  218.4 10.8 %all-to-all-done.1 = bf16[256,4,128]{2,1,0:T(4,128)(2,1)S(1)} async-done(((bf16[256,4,128]{2,1,0:T(4,128)(2,1)}), bf16[256,4,128]{2,1,0:T(4,128)(2,1)S(1)}, u32[]{:S(2)}, u32[]{:S(2)}) %all-to-all-start.1) | async-done | bytes 262176 | tf_op jit(solution)/shard_map/all_to_all | solution.py:332
  229.9 3.7 %weight_part.1 = f32[64,8,128]{2,1,0:T(8,128)} custom-call(bf16[16,64,128]{2,1,0:T(8,128)(2,1)} %bitcast.19, bf16[2048,1024]{1,0:T(8,128)(2,1)} %bitcast.24), custom_call_target="tpu_custom_call" | custom-call | flops 268435456 | bytes 4194304 | tf_op jit(solution)/shard_map/weight_part/pallas_call | solution.py:219
  233.6 1.0 convert_element_type.31
  234.7 63.4 %all_to_all.20.back_ref = bf16[64,24,128]{2,1,0:T(8,128)(2,1)S(1)} all-to-all(bf16[64,24,128]{2,1,0:T(8,128)(2,1)S(1)} %pad_maximum_fusion), channel_id=1, replica_groups=mesh['dp'=16,'seq'=64] {'seq'}, dimensions={0} | all-to-all | bytes 786432 | tf_op jit(solution)/shard_map/all_to_all | solution.py:340
  298.9 7.3 %all-to-all-start.3 = ((bf16[16,80,128]{2,1,0:T(8,128)(2,1)}), bf16[16,80,128]{2,1,0:T(8,128)(2,1)S(1)}, u32[]{:S(2)}, u32[]{:S(2)}) async-start(bf16[16,80,128]{2,1,0:T(8,128)(2,1)} %gather_send.1), calls=%async_computation.3 | async-start | bytes 655360 | tf_op jit(solution)/shard_map/all_to_all | solution.py:343
  306.2 0.8 flip.1
  307.1 7.3 %all-to-all-done.3.got_ref = bf16[16,80,128]{2,1,0:T(8,128)(2,1)S(1)} async-done(((bf16[16,80,128]{2,1,0:T(8,128)(2,1)}), bf16[16,80,128]{2,1,0:T(8,128)(2,1)S(1)}, u32[]{:S(2)}, u32[]{:S(2)}) %all-to-all-start.3) | async-done | bytes 327712 | tf_op jit(solution)/shard_map/all_to_all | solution.py:343
  314.3 1.3 finish.1
  (38 shorter events, 4.9 us)
Async XLA Ops:
  10.6 144.0 %copy-start.12 = (s32[1,64,4]{1,2,0:T(4,128)S(1)}, s32[1,64,4]{1,2,0:T(4,128)}, u32[]{:S(2)}) copy-start(s32[1,64,4]{1,2,0:T(4,128)} %param.12) | copy-start | bytes 3076
  10.6 121.7 %all-to-all-start = ((bf16[16,256,128]{2,1,0:T(8,128)(2,1)}), bf16[16,256,128]{2,1,0:T(8,128)(2,1)S(1)}, u32[]{:S(2)}, u32[]{:S(2)}) async-start(bf16[16,256,128]{2,1,0:T(8,128)(2,1)} %pack.1), calls=%async_computation | async-start | bytes 2097152 | tf_op jit(solution)/shard_map/all_to_all | solution.py:323
  39.7 93.4 %all-gather.3.cloned.1.call-start = ((), (), s32[]{:S(2)}) async-start(), calls=%async_computation.4 | async-start | bytes 4456448 | tf_op jit(solution)/shard_map/all_gather | solution.py:325
  132.3 23.9 %copy-start = (bf16[16,256,128]{2,1,0:T(8,128)(2,1)}, bf16[16,256,128]{2,1,0:T(8,128)(2,1)S(1)}, u32[]{:S(2)}) copy-start(bf16[16,256,128]{2,1,0:T(8,128)(2,1)S(1)} %all-to-all-done.q_ref.g_ref) | copy-start | bytes 3145732
  132.3 23.8 %copy-start.8 = (bf16[16,128,128]{2,1,0:T(8,128)(2,1)}, bf16[16,128,128]{2,1,0:T(8,128)(2,1)S(1)}, u32[]{:S(2)}) copy-start(bf16[16,128,128]{2,1,0:T(8,128)(2,1)S(1)} %slice.16.kv0) | copy-start | bytes 1572868
  132.3 58.1 %copy-start.7 = (s32[1,64]{1,0:T(1,128)S(1)}, s32[1,64]{1,0:T(1,128)}, u32[]{:S(2)}) copy-start(s32[1,64]{1,0:T(1,128)} %param.13) | copy-start | bytes 772
  133.1 14.3 %collective-permute-start.1 = (bf16[16,128,128]{2,1,0:T(8,128)(2,1)S(1)}, bf16[16,128,128]{2,1,0:T(8,128)(2,1)S(1)}, u32[]{:S(2)}, u32[]{:S(2)}) collective-permute-start(bf16[16,128,128]{2,1,0:T(8,128)(2,1)S(1)} %slice.16.kv0), channel_id=1, source_target_pairs={{0,2},{1,3},{2,0},{3,1},{4,6},{5,7},{6,4},{7,5},{8,10},{9,11},{10,... | collective-permute-start | bytes 1572872 | tf_op jit(solution)/shard_map/ppermute | solution.py:316
  138.7 16.6 %collective-permute-start = (bf16[16,128,128]{2,1,0:T(8,128)(2,1)S(1)}, bf16[16,128,128]{2,1,0:T(8,128)(2,1)S(1)}, u32[]{:S(2)}, u32[]{:S(2)}) collective-permute-start(bf16[16,128,128]{2,1,0:T(8,128)(2,1)S(1)} %slice.16.kv0), channel_id=1, source_target_pairs={{0,1},{1,0},{2,3},{3,2},{4,5},{5,4},{6,7},{7,6},{8,9},{9,8},{10,11... | collective-permute-start | bytes 1572872 | tf_op jit(solution)/shard_map/ppermute | solution.py:316
  147.5 8.7 %copy-start.9 = (bf16[16,128,128]{2,1,0:T(8,128)(2,1)}, bf16[16,128,128]{2,1,0:T(8,128)(2,1)S(1)}, u32[]{:S(2)}) copy-start(bf16[16,128,128]{2,1,0:T(8,128)(2,1)S(1)} %collective-permute-done.1.kv2) | copy-start | bytes 1572868
  147.5 8.6 %collective-permute-start.2 = (bf16[16,128,128]{2,1,0:T(8,128)(2,1)S(1)}, bf16[16,128,128]{2,1,0:T(8,128)(2,1)S(1)}, u32[]{:S(2)}, u32[]{:S(2)}) collective-permute-start(bf16[16,128,128]{2,1,0:T(8,128)(2,1)S(1)} %collective-permute-done.1.kv2), channel_id=1, source_target_pairs={{0,1},{1,0},{2,3},{3,2},{4,5},{5,4},{6,7},{7,6},{8,9},{9,8},{10,11... | collective-permute-start | bytes 1572872 | tf_op jit(solution)/shard_map/ppermute | solution.py:316
  155.4 35.1 %copy-start.6 = (s32[256]{0:T(256)S(1)}, s32[256]{0:T(256)}, u32[]{:S(2)}) copy-start(s32[256]{0:T(256)} %reshape_squeeze.3.blk_ref) | copy-start | bytes 3076
  155.4 0.9 copy-start.10
  156.1 0.8 copy-start.11
  163.6 65.6 %all-to-all-start.1 = ((bf16[256,4,128]{2,1,0:T(4,128)(2,1)}), bf16[256,4,128]{2,1,0:T(4,128)(2,1)S(1)}, u32[]{:S(2)}, u32[]{:S(2)}) async-start(bf16[256,4,128]{2,1,0:T(4,128)(2,1)} %bitcast.29), calls=%async_computation.1 | async-start | bytes 524288 | tf_op jit(solution)/shard_map/all_to_all | solution.py:332
  190.5 1.2 copy-start.1
  191.7 1.6 copy-start.5
  199.3 5.0 %collective-permute-start.3 = (bf16[2,64,16,128]{3,2,1,0:T(8,128)(2,1)S(1)}, bf16[2,64,16,128]{3,2,1,0:T(8,128)(2,1)S(1)}, u32[]{:S(2)}, u32[]{:S(2)}) collective-permute-start(bf16[2,64,16,128]{3,2,1,0:T(8,128)(2,1)S(1)} %get-tuple-element.14), channel_id=1, source_target_pairs={{0,1},{1,0},{2,3},{3,2},{4,5},{5,4},{6,7},{7,6},{8,9},{9,8},{10,11... | collective-permute-start | bytes 1572872 | tf_op jit(solution)/shard_map/ppermute | solution.py:316
  204.5 13.9 %collective-permute-start.4 = (bf16[64,16,128]{2,1,0:T(8,128)(2,1)S(1)}, bf16[64,16,128]{2,1,0:T(8,128)(2,1)S(1)}, u32[]{:S(2)}, u32[]{:S(2)}) collective-permute-start(bf16[64,16,128]{2,1,0:T(8,128)(2,1)S(1)} %slice_bitcast_fusion), channel_id=1, source_target_pairs={{0,2},{1,3},{2,0},{3,1},{4,6},{5,7},{6,4},{7,5},{8,10},{9,11},{10,... | collective-permute-start | bytes 786440 | tf_op jit(solution)/shard_map/ppermute | solution.py:316
  229.2 0.7 copy-start.3
  233.6 64.5 %copy-start.4 = (bf16[256,4,128]{2,1,0:T(4,128)(2,1)S(1)}, bf16[256,4,128]{2,1,0:T(4,128)(2,1)}, u32[]{:S(2)}) copy-start(bf16[256,4,128]{2,1,0:T(4,128)(2,1)} %copy-done.3) | copy-start | bytes 786436
  234.6 79.7 %copy-start.2 = (bf16[1024,1024]{1,0:T(8,128)(2,1)S(1)}, bf16[1024,1024]{1,0:T(8,128)(2,1)}, u32[]{:S(2)}) copy-start(bf16[1024,1024]{1,0:T(8,128)(2,1)} %w_ref.3) | copy-start | bytes 6291460
  298.9 15.4 %all-to-all-start.3 = ((bf16[16,80,128]{2,1,0:T(8,128)(2,1)}), bf16[16,80,128]{2,1,0:T(8,128)(2,1)S(1)}, u32[]{:S(2)}, u32[]{:S(2)}) async-start(bf16[16,80,128]{2,1,0:T(8,128)(2,1)} %gather_send.1), calls=%async_computation.3 | async-start | bytes 655360 | tf_op jit(solution)/shard_map/all_to_all | solution.py:343
Sparse Core Ops, SparseCore 0:
  44.7 88.3 all-gather.2

commit v4 on v3

--- a/solution.py
+++ b/solution.py
@@ -14,6 +14,7 @@
 BATCHES = 8
 ROWS = 8
 PAIR = 8
+BROWS = 8
 BF = jnp.bfloat16
 F32 = jnp.float32
 
@@ -146,24 +147,22 @@
     )(site, blk, cnt, recv, *kvs)
 
 
-def backward_kernel(site_ref, blk_ref, cnt_ref, g_ref, prob_ref, keep_ref, swap_ref, acc_ref):
+def backward_kernel(site_ref, blk_ref, g_ref, prob_ref, keep_ref, swap_ref, acc_ref):
     step = pl.program_id(0)
 
     @pl.when(step == 0)
     def _():
         acc_ref[...] = jnp.zeros_like(acc_ref)
 
-    cluster = SITE * step + site_ref[0]
-    number = cnt_ref[cluster]
-    g = g_ref[0]
-    for j in range(MAXB):
-
-        @pl.when(j < number)
-        def _():
-            at = blk_ref[MAXB * cluster + j]
-            acc_ref[at] += lax.dot_general(
-                g, prob_ref[0, j], (((1,), (1,)), ((), ())), preferred_element_type=F32
-            )
+    count = g_ref.shape[0]
+    for u in range(count):
+        cluster = SITE * (count * step + u) + site_ref[0]
+        terms = [
+            lax.dot_general(g_ref[u], prob_ref[u, j], (((1,), (1,)), ((), ())), preferred_element_type=F32)
+            for j in range(MAXB)
+        ]
+        for j in range(MAXB):
+            acc_ref[blk_ref[MAXB * cluster + j]] += terms[j]
 
     @pl.when(step == pl.num_programs(0) - 1)
     def _():
@@ -172,28 +171,44 @@
             (swap_ref if t % 2 else keep_ref)[t // 2] = acc_ref[:, pl.ds(first, 16), :].astype(BF)
 
 
-def backward(site, blk, cnt, recv, probs):
+def backward(site, blk, recv, probs):
     n = recv.shape[0]
     clusters = SITE * n
     return pl.pallas_call(
         backward_kernel,
         grid_spec=pltpu.PrefetchScalarGridSpec(
-            num_scalar_prefetch=3,
-            grid=(n,),
+            num_scalar_prefetch=2,
+            grid=(n // BROWS,),
             in_specs=[
-                pl.BlockSpec((1, 64, CSIZE), lambda i, *_: (i, 3, 0)),
-                pl.BlockSpec((1, MAXB, CSIZE, CSIZE), lambda i, *_: (i, 0, 0, 0)),
+                pl.BlockSpec((BROWS, 64, CSIZE), lambda i, *_: (i, 3, 0)),
+                pl.BlockSpec((BROWS, MAXB, CSIZE, CSIZE), lambda i, *_: (i, 0, 0, 0)),
             ],
             out_specs=[pl.BlockSpec((2, clusters, 16, CSIZE), lambda i, *_: (0, 0, 0, 0))] * 2,
             scratch_shapes=[pltpu.VMEM((clusters, HD, CSIZE), F32)],
         ),
         out_shape=[jax.ShapeDtypeStruct((2, clusters, 16, CSIZE), BF)] * 2,
-        compiler_params=params(),
+        compiler_params=params(60),
         cost_estimate=pl.CostEstimate(
             flops=n * 2 * MAXB * CSIZE * CSIZE * HD, bytes_accessed=3 << 20, transcendentals=0
         ),
         name="value_contrib",
-    )(site, blk, cnt, recv, probs)
+    )(site, blk, recv, probs)
+
+
+def merge_kernel(own_ref, other_ref, part_ref, out_ref):
+    total = own_ref[...].astype(F32) + other_ref[...].astype(F32)
+    out_ref[...] = jnp.concatenate([total, part_ref[...]], axis=1).astype(BF)
+
+
+def merge(own, other, part):
+    n, rows, nodes = own.shape
+    return pl.pallas_call(
+        merge_kernel,
+        out_shape=jax.ShapeDtypeStruct((n, rows + part.shape[1], nodes), BF),
+        compiler_params=params(),
+        cost_estimate=pl.CostEstimate(flops=own.size, bytes_accessed=6 * own.size + 6 * part.size, transcendentals=0),
+        name="merge",
+    )(own, other, part)
 
 
 def weight_kernel(att_ref, cot_ref, out_ref, acc_ref):
@@ -332,13 +347,11 @@
     pieces = lax.all_to_all(
         sent_att, ("dp", "seq"), split_axis=0, concat_axis=0, tiled=True, axis_index_groups=same_site_dp
     ).reshape(ndp, width // ndp, CSIZE)
-    keep, give = backward(site, blk, cnt, recv, probs)
+    keep, give = backward(site, blk, recv, probs)
     chip = (keep.astype(F32) + swap(give, 1).astype(F32)).astype(BF)
-    contrib = (chip[0].astype(F32) + swap(chip[1], 2).astype(F32)).astype(BF)
-
-    part = weight_part(pieces, cots).astype(BF).reshape(nseq, -1, CSIZE)
+    part = weight_part(pieces, cots).reshape(nseq, -1, CSIZE)
     back = lax.all_to_all(
-        jnp.concatenate([contrib, part], axis=1), "seq", split_axis=0, concat_axis=0, tiled=True
+        merge(chip[0], swap(chip[1], 2), part), "seq", split_axis=0, concat_axis=0, tiled=True
     )
     got = lax.all_to_all(gather_send(back, pieces), "dp", split_axis=0, concat_axis=0, tiled=True)
     value_grad = flip(back[:, :16].reshape(width, CSIZE))

time: 323 us -> 320 us (level)
  starting transfers between devices: 90.1 us -> 85.8 us
    all_to_all x1, waiting for transfers between devices: 10.8 us -> 25.9 us  [body(): lax.all_to_all(sent_att, ('dp', 'seq'), split_axis=0, concat_axis=0, tile...]
    ppermute x5, waiting for transfers between devices: 14.2 us -> 2.45 us  [swap(): return lax.ppermute(x, 'seq', [(i, i ^ bit) for i in range(nseq)])]
    all_to_all x1, starting transfers between devices: 7.31 us -> 3.54 us  [body(): lax.all_to_all(gather_send(back, pieces), 'dp', split_axis=0, concat_axis...]
  transfers between devices with their start and end apart: 9 -> 9, of which waited for: 7 -> 6; matrix products, arithmetic and copies ran while one was open for 0% -> 1% of each run, Pallas kernels for 2% -> 3%
where the time goes in v4:
time: 320 us; the launch traced here: 319 us
  waiting for transfers between devices  129 us (40%)
  starting transfers between devices  85.8 us (27%)
  blocking collectives  63.6 us (20%)
  Pallas kernels  21.8 us (7%)
  between operations  14.2 us (4%)
  local copies, waits for them, and re-layouts  3.36 us (1%)
    all_to_all x1, waiting for transfers between devices, body(): lax.all_to_all(sent, 'seq', split_axis=0, concat_axis=0, tiled=True, axis...  91.8 us
    all_to_all x1, blocking collectives, body(): lax.all_to_all(merge(chip[0], swap(chip[1], 2), part), 'seq', split_axis=...  63.6 us
    all_to_all x1, starting transfers between devices, body(): lax.all_to_all(sent, 'seq', split_axis=0, concat_axis=0, tiled=True, axis...  29.1 us
    all_to_all x1, starting transfers between devices, body(): lax.all_to_all(sent_att, ('dp', 'seq'), split_axis=0, concat_axis=0, tile...  26.9 us
    ppermute x5, starting transfers between devices, swap(): return lax.ppermute(x, 'seq', [(i, i ^ bit) for i in range(nseq)])  26.2 us
    all_to_all x1, waiting for transfers between devices, body(): lax.all_to_all(sent_att, ('dp', 'seq'), split_axis=0, concat_axis=0, tile...  25.9 us
    all_to_all x1, waiting for transfers between devices, body(): lax.all_to_all(gather_send(back, pieces), 'dp', split_axis=0, concat_axis...  7.62 us
    pallas_call x1, Pallas kernels, forward(): pl.pallas_call(forward_kernel, grid_spec=pltpu.PrefetchScalarGridSpec(num...  6.67 us
  transfers between devices with their start and end apart: 9, of which 6 were waited for; matrix products, arithmetic and copies ran while one was open for 1% of the time, Pallas kernels for 3%

profile of v4, /device:TPU:1, one launch (start us, length us, event | category | flops | bytes accessed | tf_op | source)
XLA Modules:
  0.0 319.2 jit_solution(17333611232772134085)
XLA Ops:
  7.2 3.4 %pack.1 = bf16[16,256,128]{2,1,0:T(8,128)(2,1)} custom-call(bf16[128,1024]{1,0:T(8,128)(2,1)} %bitcast.21, bf16[128,1024]{1,0:T(8,128)(2,1)} %bitcast.22, bf16[128,1024]{1,0:T(8,128)(2,1)} %bitcast.23, bf16[128,1024]{1,0:T(8,128)(2,1)} %bitcast.20, bf16[1024,1024]{1,0:T(8,128)(2,1)} %w_ref.3), custom_call_target="tpu_custom_call" | custom-call | flops 268435456 | bytes 3407872 | tf_op jit(solution)/shard_map/pack/pallas_call | solution.py:46
  10.6 29.1 %all-to-all-start = ((bf16[16,256,128]{2,1,0:T(8,128)(2,1)}), bf16[16,256,128]{2,1,0:T(8,128)(2,1)S(1)}, u32[]{:S(2)}, u32[]{:S(2)}) async-start(bf16[16,256,128]{2,1,0:T(8,128)(2,1)} %pack.1), calls=%async_computation | async-start | bytes 2097152 | tf_op jit(solution)/shard_map/all_to_all | solution.py:338
  40.4 91.8 %all-to-all-done.q_ref.g_ref = bf16[16,256,128]{2,1,0:T(8,128)(2,1)S(1)} async-done(((bf16[16,256,128]{2,1,0:T(8,128)(2,1)}), bf16[16,256,128]{2,1,0:T(8,128)(2,1)S(1)}, u32[]{:S(2)}, u32[]{:S(2)}) %all-to-all-start) | async-done | bytes 1048608 | tf_op jit(solution)/shard_map/all_to_all | solution.py:338
  132.3 0.8 all-gather.3.cloned.1.call-done
  133.1 5.6 %collective-permute-start.1 = (bf16[16,128,128]{2,1,0:T(8,128)(2,1)S(1)}, bf16[16,128,128]{2,1,0:T(8,128)(2,1)S(1)}, u32[]{:S(2)}, u32[]{:S(2)}) collective-permute-start(bf16[16,128,128]{2,1,0:T(8,128)(2,1)S(1)} %slice.16.kv0), channel_id=1, source_target_pairs={{0,2},{1,3},{2,0},{3,1},{4,6},{5,7},{6,4},{7,5},{8,10},{9,11},{10,... | collective-permute-start | bytes 1572872 | tf_op jit(solution)/shard_map/ppermute | solution.py:331
  138.7 8.7 %collective-permute-start = (bf16[16,128,128]{2,1,0:T(8,128)(2,1)S(1)}, bf16[16,128,128]{2,1,0:T(8,128)(2,1)S(1)}, u32[]{:S(2)}, u32[]{:S(2)}) collective-permute-start(bf16[16,128,128]{2,1,0:T(8,128)(2,1)S(1)} %slice.16.kv0), channel_id=1, source_target_pairs={{0,1},{1,0},{2,3},{3,2},{4,5},{5,4},{6,7},{7,6},{8,9},{9,8},{10,11... | collective-permute-start | bytes 1572872 | tf_op jit(solution)/shard_map/ppermute | solution.py:331
  147.5 7.1 %collective-permute-start.2 = (bf16[16,128,128]{2,1,0:T(8,128)(2,1)S(1)}, bf16[16,128,128]{2,1,0:T(8,128)(2,1)S(1)}, u32[]{:S(2)}, u32[]{:S(2)}) collective-permute-start(bf16[16,128,128]{2,1,0:T(8,128)(2,1)S(1)} %collective-permute-done.1.kv2), channel_id=1, source_target_pairs={{0,1},{1,0},{2,3},{3,2},{4,5},{5,4},{6,7},{7,6},{8,9},{9,8},{10,11... | collective-permute-start | bytes 1572872 | tf_op jit(solution)/shard_map/ppermute | solution.py:331
  155.4 0.7 collective-permute-done.2.kv3
  156.9 6.7 %attend.1 = (bf16[16,64,128]{2,1,0:T(8,128)(2,1)}, bf16[16,4,128,128]{3,2,1,0:T(8,128)(2,1)}) custom-call(s32[1]{0:T(128)} %bitcast.site_ref, s32[256]{0:T(256)} %reshape_squeeze.3.blk_ref, s32[64]{0:T(128)} %bitcast.26, bf16[16,256,128]{2,1,0:T(8,128)(2,1)} %copy-done.4, bf16[16,128,128]{2,1,0:T(8,128)(2,1)} %copy-done.5, bf16[16,128,128]{2,1,0:T(8,128)(2,1)} %copy-done.7, ...), custom_call_target="tpu_custom_call" | custom-call | flops 268435456 | bytes 5242880 | tf_op jit(solution)/shard_map/attend/pallas_call | solution.py:119
  163.6 26.9 %all-to-all-start.1 = ((bf16[256,4,128]{2,1,0:T(4,128)(2,1)}), bf16[256,4,128]{2,1,0:T(4,128)(2,1)S(1)}, u32[]{:S(2)}, u32[]{:S(2)}) async-start(bf16[256,4,128]{2,1,0:T(4,128)(2,1)} %bitcast.24), calls=%async_computation.1 | async-start | bytes 524288 | tf_op jit(solution)/shard_map/all_to_all | solution.py:347
  190.4 5.0 %value_contrib.1 = (bf16[2,64,16,128]{3,2,1,0:T(8,128)(2,1)}, bf16[2,64,16,128]{3,2,1,0:T(8,128)(2,1)}) custom-call(s32[1]{0:T(128)} %bitcast.site_ref, s32[256]{0:T(256)} %reshape_squeeze.3.blk_ref, bf16[16,256,128]{2,1,0:T(8,128)(2,1)} %copy-done.4, bf16[16,4,128,128]{3,2,1,0:T(8,128)(2,1)} %get-tuple-element.12.prob_ref), custom_call_target="tpu_custom_call" | custom-call | flops 134217728 | bytes 3145728 | tf_op jit(solution)/shard_map/value_contrib/pallas_call | solution.py:177
  195.5 2.6 collective-permute-start.3
  198.0 1.7 collective-permute-done.3
  199.8 1.2 add_convert_fusion
  201.0 2.3 collective-permute-start.4
  203.3 25.9 %all-to-all-done.1 = bf16[256,4,128]{2,1,0:T(4,128)(2,1)S(1)} async-done(((bf16[256,4,128]{2,1,0:T(4,128)(2,1)}), bf16[256,4,128]{2,1,0:T(4,128)(2,1)S(1)}, u32[]{:S(2)}, u32[]{:S(2)}) %all-to-all-start.1) | async-done | bytes 262176 | tf_op jit(solution)/shard_map/all_to_all | solution.py:347
  229.9 3.7 %weight_part.1.part_ref = f32[64,8,128]{2,1,0:T(8,128)} custom-call(bf16[16,64,128]{2,1,0:T(8,128)(2,1)} %bitcast.16, bf16[2048,1024]{1,0:T(8,128)(2,1)} %bitcast.19), custom_call_target="tpu_custom_call" | custom-call | flops 268435456 | bytes 4194304 | tf_op jit(solution)/shard_map/weight_part/pallas_call | solution.py:234
  233.6 1.0 copy-done.3
  234.7 63.6 %all_to_all.20.back_ref = bf16[64,24,128]{2,1,0:T(8,128)(2,1)S(1)} all-to-all(bf16[64,24,128]{2,1,0:T(8,128)(2,1)S(1)} %merge.1), channel_id=1, replica_groups=mesh['dp'=16,'seq'=64] {'seq'}, dimensions={0} | all-to-all | bytes 786432 | tf_op jit(solution)/shard_map/all_to_all | solution.py:353
  298.2 0.8 gather_send.1
  299.0 3.5 %all-to-all-start.3 = ((bf16[16,80,128]{2,1,0:T(8,128)(2,1)}), bf16[16,80,128]{2,1,0:T(8,128)(2,1)S(1)}, u32[]{:S(2)}, u32[]{:S(2)}) async-start(bf16[16,80,128]{2,1,0:T(8,128)(2,1)} %gather_send.1), calls=%async_computation.3 | async-start | bytes 655360 | tf_op jit(solution)/shard_map/all_to_all | solution.py:356
  302.6 0.8 flip.1
  303.4 7.6 %all-to-all-done.3.got_ref = bf16[16,80,128]{2,1,0:T(8,128)(2,1)S(1)} async-done(((bf16[16,80,128]{2,1,0:T(8,128)(2,1)}), bf16[16,80,128]{2,1,0:T(8,128)(2,1)S(1)}, u32[]{:S(2)}, u32[]{:S(2)}) %all-to-all-start.3) | async-done | bytes 327712 | tf_op jit(solution)/shard_map/all_to_all | solution.py:356
  311.1 1.3 finish.1
  (30 shorter events, 3.2 us)
Async XLA Ops:
  10.6 144.0 %copy-start.9 = (s32[1,64,4]{1,2,0:T(4,128)S(1)}, s32[1,64,4]{1,2,0:T(4,128)}, u32[]{:S(2)}) copy-start(s32[1,64,4]{1,2,0:T(4,128)} %param.12) | copy-start | bytes 3076
  10.6 121.7 %all-to-all-start = ((bf16[16,256,128]{2,1,0:T(8,128)(2,1)}), bf16[16,256,128]{2,1,0:T(8,128)(2,1)S(1)}, u32[]{:S(2)}, u32[]{:S(2)}) async-start(bf16[16,256,128]{2,1,0:T(8,128)(2,1)} %pack.1), calls=%async_computation | async-start | bytes 2097152 | tf_op jit(solution)/shard_map/all_to_all | solution.py:338
  39.7 93.4 %all-gather.3.cloned.1.call-start = ((), (), s32[]{:S(2)}) async-start(), calls=%async_computation.4 | async-start | bytes 4456448 | tf_op jit(solution)/shard_map/all_gather | solution.py:340
  132.2 23.8 %copy-start.4 = (bf16[16,256,128]{2,1,0:T(8,128)(2,1)}, bf16[16,256,128]{2,1,0:T(8,128)(2,1)S(1)}, u32[]{:S(2)}) copy-start(bf16[16,256,128]{2,1,0:T(8,128)(2,1)S(1)} %all-to-all-done.q_ref.g_ref) | copy-start | bytes 3145732
  132.3 23.8 %copy-start.5 = (bf16[16,128,128]{2,1,0:T(8,128)(2,1)}, bf16[16,128,128]{2,1,0:T(8,128)(2,1)S(1)}, u32[]{:S(2)}) copy-start(bf16[16,128,128]{2,1,0:T(8,128)(2,1)S(1)} %slice.16.kv0) | copy-start | bytes 1572868
  133.1 14.3 %collective-permute-start.1 = (bf16[16,128,128]{2,1,0:T(8,128)(2,1)S(1)}, bf16[16,128,128]{2,1,0:T(8,128)(2,1)S(1)}, u32[]{:S(2)}, u32[]{:S(2)}) collective-permute-start(bf16[16,128,128]{2,1,0:T(8,128)(2,1)S(1)} %slice.16.kv0), channel_id=1, source_target_pairs={{0,2},{1,3},{2,0},{3,1},{4,6},{5,7},{6,4},{7,5},{8,10},{9,11},{10,... | collective-permute-start | bytes 1572872 | tf_op jit(solution)/shard_map/ppermute | solution.py:331
  138.7 16.6 %collective-permute-start = (bf16[16,128,128]{2,1,0:T(8,128)(2,1)S(1)}, bf16[16,128,128]{2,1,0:T(8,128)(2,1)S(1)}, u32[]{:S(2)}, u32[]{:S(2)}) collective-permute-start(bf16[16,128,128]{2,1,0:T(8,128)(2,1)S(1)} %slice.16.kv0), channel_id=1, source_target_pairs={{0,1},{1,0},{2,3},{3,2},{4,5},{5,4},{6,7},{7,6},{8,9},{9,8},{10,11... | collective-permute-start | bytes 1572872 | tf_op jit(solution)/shard_map/ppermute | solution.py:331
  147.4 8.7 %copy-start.6 = (bf16[16,128,128]{2,1,0:T(8,128)(2,1)}, bf16[16,128,128]{2,1,0:T(8,128)(2,1)S(1)}, u32[]{:S(2)}) copy-start(bf16[16,128,128]{2,1,0:T(8,128)(2,1)S(1)} %collective-permute-done.1.kv2) | copy-start | bytes 1572868
  147.5 8.6 %collective-permute-start.2 = (bf16[16,128,128]{2,1,0:T(8,128)(2,1)S(1)}, bf16[16,128,128]{2,1,0:T(8,128)(2,1)S(1)}, u32[]{:S(2)}, u32[]{:S(2)}) collective-permute-start(bf16[16,128,128]{2,1,0:T(8,128)(2,1)S(1)} %collective-permute-done.1.kv2), channel_id=1, source_target_pairs={{0,1},{1,0},{2,3},{3,2},{4,5},{5,4},{6,7},{7,6},{8,9},{9,8},{10,11... | collective-permute-start | bytes 1572872 | tf_op jit(solution)/shard_map/ppermute | solution.py:331
  155.4 0.9 copy-start.7
  156.1 0.8 copy-start.8
  163.6 65.7 %all-to-all-start.1 = ((bf16[256,4,128]{2,1,0:T(4,128)(2,1)}), bf16[256,4,128]{2,1,0:T(4,128)(2,1)S(1)}, u32[]{:S(2)}, u32[]{:S(2)}) async-start(bf16[256,4,128]{2,1,0:T(4,128)(2,1)} %bitcast.24), calls=%async_computation.1 | async-start | bytes 524288 | tf_op jit(solution)/shard_map/all_to_all | solution.py:347
  195.5 4.3 %collective-permute-start.3 = (bf16[2,64,16,128]{3,2,1,0:T(8,128)(2,1)}, bf16[2,64,16,128]{3,2,1,0:T(8,128)(2,1)S(1)}, u32[]{:S(2)}, u32[]{:S(2)}) collective-permute-start(bf16[2,64,16,128]{3,2,1,0:T(8,128)(2,1)} %get-tuple-element.14), channel_id=1, source_target_pairs={{0,1},{1,0},{2,3},{3,2},{4,5},{5,4},{6,7},{7,6},{8,9},{9,8},{10,11... | collective-permute-start | bytes 1572872 | tf_op jit(solution)/shard_map/ppermute | solution.py:331
  201.0 32.6 %collective-permute-start.4 = (bf16[64,16,128]{2,1,0:T(8,128)(2,1)S(1)}, bf16[64,16,128]{2,1,0:T(8,128)(2,1)S(1)}, u32[]{:S(2)}, u32[]{:S(2)}) collective-permute-start(bf16[64,16,128]{2,1,0:T(8,128)(2,1)S(1)} %get-tuple-element.19), channel_id=1, source_target_pairs={{0,2},{1,3},{2,0},{3,1},{4,6},{5,7},{6,4},{7,5},{8,10},{9,11},{10,... | collective-permute-start | bytes 786440 | tf_op jit(solution)/shard_map/ppermute | solution.py:331
  229.2 0.7 copy-start.1
  233.6 64.6 %copy-start.2 = (bf16[256,4,128]{2,1,0:T(4,128)(2,1)S(1)}, bf16[256,4,128]{2,1,0:T(4,128)(2,1)}, u32[]{:S(2)}) copy-start(bf16[256,4,128]{2,1,0:T(4,128)(2,1)} %copy-done.1) | copy-start | bytes 786436
  233.6 1.0 copy-start.3
  234.6 76.5 %copy-start = (bf16[1024,1024]{1,0:T(8,128)(2,1)S(1)}, bf16[1024,1024]{1,0:T(8,128)(2,1)}, u32[]{:S(2)}) copy-start(bf16[1024,1024]{1,0:T(8,128)(2,1)} %w_ref.3) | copy-start | bytes 6291460
  299.0 12.0 %all-to-all-start.3 = ((bf16[16,80,128]{2,1,0:T(8,128)(2,1)}), bf16[16,80,128]{2,1,0:T(8,128)(2,1)S(1)}, u32[]{:S(2)}, u32[]{:S(2)}) async-start(bf16[16,80,128]{2,1,0:T(8,128)(2,1)} %gather_send.1), calls=%async_computation.3 | async-start | bytes 655360 | tf_op jit(solution)/shard_map/all_to_all | solution.py:356
Sparse Core Ops, SparseCore 0:
  44.7 88.3 all-gather.2

commit v5 on v4

--- a/solution.py
+++ b/solution.py
@@ -11,7 +11,6 @@
 HALF = CSIZE // 2
 MAXB = 4
 SITE = 4
-BATCHES = 8
 ROWS = 8
 PAIR = 8
 BROWS = 8
@@ -211,42 +210,48 @@
     )(own, other, part)
 
 
-def weight_kernel(att_ref, cot_ref, out_ref, acc_ref):
-    step = pl.program_id(0)
-
-    @pl.when(step == 0)
-    def _():
-        acc_ref[...] = jnp.zeros_like(acc_ref)
-
-    att = jnp.concatenate([att_ref[i] for i in range(att_ref.shape[0])], axis=1)
-    acc_ref[...] += jnp.dot(att, cot_ref[...], preferred_element_type=F32)
-
-    @pl.when(step == pl.num_programs(0) - 1)
-    def _():
-        for i in range(out_ref.shape[1]):
-            out_ref[:, i, :] = acc_ref[:, CSIZE * i : CSIZE * (i + 1)]
-
-
-def weight_part(att, cots):
+def weight_kernel(me_ref, att_ref, *refs):
+    n = att_ref.shape[0]
+    cots, (out_ref, cot_ref, acc_ref, sems) = refs[:n], refs[n:]
+    copies = [pltpu.make_async_copy(cots[t], cot_ref.at[t], sems.at[t]) for t in range(n)]
+    for copy in copies:
+        copy.start()
+    step = min(2, n)
+    for t in range(0, n, step):
+        for i in range(step):
+            copies[t + i].wait()
+        att = jnp.concatenate([att_ref[me_ref[0] ^ (t + i)] for i in range(step)], axis=1)
+        cot = jnp.concatenate([cot_ref[t + i] for i in range(step)], axis=0)
+        term = jnp.dot(att, cot, preferred_element_type=F32)
+        acc_ref[...] = term if t == 0 else acc_ref[...] + term
+    for i in range(out_ref.shape[1]):
+        out_ref[:, i, :] = acc_ref[:, CSIZE * i : CSIZE * (i + 1)]
+
+
+def weight_part(me, att, cots):
     n, rows, nodes = att.shape
-    width = cots.shape[1]
-    batches = min(BATCHES, n)
+    width = cots[0].shape[1]
     return pl.pallas_call(
         weight_kernel,
-        grid=(n // batches,),
-        in_specs=[
-            pl.BlockSpec((batches, rows, nodes), lambda i: (i, 0, 0)),
-            pl.BlockSpec((batches * nodes, width), lambda i: (i, 0)),
-        ],
-        out_specs=pl.BlockSpec((rows, width // CSIZE, CSIZE), lambda i: (0, 0, 0)),
+        grid_spec=pltpu.PrefetchScalarGridSpec(
+            num_scalar_prefetch=1,
+            grid=(1,),
+            in_specs=[pl.BlockSpec(att.shape, lambda i, *_: (0, 0, 0))]
+            + [pl.BlockSpec(memory_space=pl.ANY)] * n,
+            out_specs=pl.BlockSpec((rows, width // CSIZE, CSIZE), lambda i, *_: (0, 0, 0)),
+            scratch_shapes=[
+                pltpu.VMEM((n, nodes, width), BF),
+                pltpu.VMEM((rows, width), F32),
+                pltpu.SemaphoreType.DMA((n,)),
+            ],
+        ),
         out_shape=jax.ShapeDtypeStruct((rows, width // CSIZE, CSIZE), F32),
-        scratch_shapes=[pltpu.VMEM((rows, width), F32)],
         compiler_params=params(60),
         cost_estimate=pl.CostEstimate(
             flops=2 * n * rows * nodes * width, bytes_accessed=2 * n * nodes * width, transcendentals=0
         ),
         name="weight_part",
-    )(att, cots)
+    )(me, att, *cots)
 
 
 def gather_kernel(back_ref, att_ref, out_ref):
@@ -323,6 +328,7 @@
     nseq = lax.axis_size("seq")
     ndp = lax.axis_size("dp")
     width = w_out.shape[0]
+    me = lax.axis_index("dp").astype(jnp.int32)[None]
     site = (lax.axis_index("seq") % SITE).astype(jnp.int32)[None]
     same_site = [[SITE * h + s for h in range(H)] for s in range(SITE)]
     same_site_dp = [[p * nseq + i for p in range(ndp) for i in group] for group in same_site]
@@ -335,10 +341,9 @@
     cot = cotangent[0]
 
     sent = pack(queries[0], keys[0], values[0], cot, w_out)
+    sent, cot = lax.optimization_barrier((sent, cot))
+    cots = [cot] + [lax.ppermute(cot, "dp", [(i, i ^ t) for i in range(ndp)]) for t in range(1, ndp)]
     recv = lax.all_to_all(sent, "seq", split_axis=0, concat_axis=0, tiled=True, axis_index_groups=same_site)
-
-    cots = lax.all_gather(cot, "dp", axis=0, tiled=True)
-
     kv, cots = lax.optimization_barrier((recv[:, :128], cots))
     kv_z = swap(kv, 2)
     kvs = [kv, swap(kv, 1), kv_z, swap(kv_z, 1)]
@@ -349,7 +354,7 @@
     ).reshape(ndp, width // ndp, CSIZE)
     keep, give = backward(site, blk, recv, probs)
     chip = (keep.astype(F32) + swap(give, 1).astype(F32)).astype(BF)
-    part = weight_part(pieces, cots).reshape(nseq, -1, CSIZE)
+    part = weight_part(me, pieces, cots).reshape(nseq, -1, CSIZE)
     back = lax.all_to_all(
         merge(chip[0], swap(chip[1], 2), part), "seq", split_axis=0, concat_axis=0, tiled=True
     )

time: 320 us -> 307 us (0.959)
  waiting for transfers between devices: 129 us -> 75.3 us
  starting transfers between devices: 85.8 us -> 138 us
  between operations: 14.2 us -> 1.19 us
    all_to_all x1, waiting for transfers between devices: 91.8 us -> 13.2 us  [body(): lax.all_to_all(sent, 'seq', split_axis=0, concat_axis=0, tiled=True, axis...]
    ppermute x0 -> x15, starting transfers between devices: none -> 52.5 us  [body(): lax.ppermute(cot, 'dp', [(i, i ^ t) for i in range(ndp)])]
    ppermute x0 -> x15, waiting for transfers between devices: none -> 25.8 us  [body(): lax.ppermute(cot, 'dp', [(i, i ^ t) for i in range(ndp)])]
  transfers between devices with their start and end apart: 9 -> 23, of which waited for: 6 -> 7; matrix products, arithmetic and copies ran while one was open for 1% -> 1% of each run, Pallas kernels for 3% -> 3%
where the time goes in v5:
time: 307 us; the launch traced here: 306 us
  starting transfers between devices  138 us (45%)
  waiting for transfers between devices  75.3 us (25%)
  blocking collectives  63.4 us (21%)
  Pallas kernels  22.3 us (7%)
  local copies, waits for them, and re-layouts  4.13 us (1%)
    all_to_all x1, blocking collectives, body(): lax.all_to_all(merge(chip[0], swap(chip[1], 2), part), 'seq', split_axis=...  63.4 us
    ppermute x15, starting transfers between devices, body(): lax.ppermute(cot, 'dp', [(i, i ^ t) for i in range(ndp)])  52.5 us
    all_to_all x1, starting transfers between devices, body(): lax.all_to_all(sent, 'seq', split_axis=0, concat_axis=0, tiled=True, axis...  29.1 us
    ppermute x5, starting transfers between devices, swap(): return lax.ppermute(x, 'seq', [(i, i ^ bit) for i in range(nseq)])  27 us
    all_to_all x1, waiting for transfers between devices, body(): lax.all_to_all(sent_att, ('dp', 'seq'), split_axis=0, concat_axis=0, tile...  26.2 us
    all_to_all x1, starting transfers between devices, body(): lax.all_to_all(sent_att, ('dp', 'seq'), split_axis=0, concat_axis=0, tile...  26 us
    ppermute x15, waiting for transfers between devices, body(): lax.ppermute(cot, 'dp', [(i, i ^ t) for i in range(ndp)])  25.8 us
    all_to_all x1, waiting for transfers between devices, body(): lax.all_to_all(sent, 'seq', split_axis=0, concat_axis=0, tiled=True, axis...  13.2 us
  transfers between devices with their start and end apart: 23, of which 7 were waited for; matrix products, arithmetic and copies ran while one was open for 1% of the time, Pallas kernels for 3%

profile of v5, /device:TPU:1, one launch (start us, length us, event | category | flops | bytes accessed | tf_op | source)
XLA Modules:
  0.0 305.7 jit_solution(11869249623593899385)
XLA Ops:
  0.6 3.5 %pack.1 = bf16[16,256,128]{2,1,0:T(8,128)(2,1)} custom-call(bf16[128,1024]{1,0:T(8,128)(2,1)} %bitcast.36, bf16[128,1024]{1,0:T(8,128)(2,1)} %bitcast.37, bf16[128,1024]{1,0:T(8,128)(2,1)} %bitcast.38, bf16[128,1024]{1,0:T(8,128)(2,1)} %bitcast.19, bf16[1024,1024]{1,0:T(8,128)(2,1)} %w_ref.3), custom_call_target="tpu_custom_call" | custom-call | flops 268435456 | bytes 3407872 | tf_op jit(solution)/shard_map/pack/pallas_call | solution.py:45
  4.1 29.1 %all-to-all-start = ((bf16[16,256,128]{2,1,0:T(8,128)(2,1)}), bf16[16,256,128]{2,1,0:T(8,128)(2,1)S(1)}, u32[]{:S(2)}, u32[]{:S(2)}) async-start(bf16[16,256,128]{2,1,0:T(8,128)(2,1)} %pack.1), calls=%async_computation | async-start | bytes 2097152 | tf_op jit(solution)/shard_map/all_to_all | solution.py:346
  33.2 6.8 %collective-permute-start.14 = (bf16[128,1024]{1,0:T(8,128)(2,1)S(1)}, bf16[128,1024]{1,0:T(8,128)(2,1)S(1)}, u32[]{:S(2)}, u32[]{:S(2)}) collective-permute-start(bf16[128,1024]{1,0:T(8,128)(2,1)S(1)} %bitcast.21), channel_id=1, source_target_pairs={{0,960},{64,896},{128,832},{192,768},{256,704},{320,640},{384,576}... | collective-permute-start | bytes 786440 | tf_op jit(solution)/shard_map/ppermute | solution.py:345
  42.3 4.5 %collective-permute-start.12 = (bf16[128,1024]{1,0:T(8,128)(2,1)S(1)}, bf16[128,1024]{1,0:T(8,128)(2,1)S(1)}, u32[]{:S(2)}, u32[]{:S(2)}) collective-permute-start(bf16[128,1024]{1,0:T(8,128)(2,1)S(1)} %bitcast.23), channel_id=1, source_target_pairs={{0,832},{64,768},{128,960},{192,896},{256,576},{320,512},{384,704}... | collective-permute-start | bytes 786440 | tf_op jit(solution)/shard_map/ppermute | solution.py:345
  48.8 4.4 %collective-permute-start.10 = (bf16[128,1024]{1,0:T(8,128)(2,1)S(1)}, bf16[128,1024]{1,0:T(8,128)(2,1)S(1)}, u32[]{:S(2)}, u32[]{:S(2)}) collective-permute-start(bf16[128,1024]{1,0:T(8,128)(2,1)S(1)} %bitcast.25), channel_id=1, source_target_pairs={{0,704},{64,640},{128,576},{192,512},{256,960},{320,896},{384,832}... | collective-permute-start | bytes 786440 | tf_op jit(solution)/shard_map/ppermute | solution.py:345
  53.3 4.7 %collective-permute-start.9 = (bf16[128,1024]{1,0:T(8,128)(2,1)S(1)}, bf16[128,1024]{1,0:T(8,128)(2,1)S(1)}, u32[]{:S(2)}, u32[]{:S(2)}) collective-permute-start(bf16[128,1024]{1,0:T(8,128)(2,1)S(1)} %bitcast.26), channel_id=1, source_target_pairs={{0,640},{64,704},{128,512},{192,576},{256,896},{320,960},{384,768}... | collective-permute-start | bytes 786440 | tf_op jit(solution)/shard_map/ppermute | solution.py:345
  60.3 5.3 %collective-permute-start.7 = (bf16[128,1024]{1,0:T(8,128)(2,1)S(1)}, bf16[128,1024]{1,0:T(8,128)(2,1)S(1)}, u32[]{:S(2)}, u32[]{:S(2)}) collective-permute-start(bf16[128,1024]{1,0:T(8,128)(2,1)S(1)} %bitcast.28), channel_id=1, source_target_pairs={{0,512},{64,576},{128,640},{192,704},{256,768},{320,832},{384,896}... | collective-permute-start | bytes 786440 | tf_op jit(solution)/shard_map/ppermute | solution.py:345
  65.7 21.9 %collective-permute-done.11.refs_12_ = bf16[128,1024]{1,0:T(8,128)(2,1)S(1)} collective-permute-done((bf16[128,1024]{1,0:T(8,128)(2,1)S(1)}, bf16[128,1024]{1,0:T(8,128)(2,1)S(1)}, u32[]{:S(2)}, u32[]{:S(2)}) %collective-permute-start.11) | collective-permute-done | bytes 262176 | tf_op jit(solution)/shard_map/ppermute | solution.py:345
  90.2 3.8 %collective-permute-start.5 = (bf16[128,1024]{1,0:T(8,128)(2,1)S(1)}, bf16[128,1024]{1,0:T(8,128)(2,1)S(1)}, u32[]{:S(2)}, u32[]{:S(2)}) collective-permute-start(bf16[128,1024]{1,0:T(8,128)(2,1)S(1)} %bitcast.30), channel_id=1, source_target_pairs={{0,384},{64,448},{128,256},{192,320},{256,128},{320,192},{384,0},{... | collective-permute-start | bytes 786440 | tf_op jit(solution)/shard_map/ppermute | solution.py:345
  96.0 4.6 %collective-permute-start.3 = (bf16[128,1024]{1,0:T(8,128)(2,1)S(1)}, bf16[128,1024]{1,0:T(8,128)(2,1)}, u32[]{:S(2)}, u32[]{:S(2)}) collective-permute-start(bf16[128,1024]{1,0:T(8,128)(2,1)S(1)} %bitcast.32), channel_id=1, source_target_pairs={{0,256},{64,320},{128,384},{192,448},{256,0},{320,64},{384,128},{4... | collective-permute-start | bytes 786440 | tf_op jit(solution)/shard_map/ppermute | solution.py:345
  100.6 2.9 collective-permute-start.2
  103.5 3.9 %collective-permute-done.6.refs_7_ = bf16[128,1024]{1,0:T(8,128)(2,1)S(1)} collective-permute-done((bf16[128,1024]{1,0:T(8,128)(2,1)S(1)}, bf16[128,1024]{1,0:T(8,128)(2,1)S(1)}, u32[]{:S(2)}, u32[]{:S(2)}) %collective-permute-start.6) | collective-permute-done | bytes 262176 | tf_op jit(solution)/shard_map/ppermute | solution.py:345
  112.5 13.2 %all-to-all-done.q_ref.g_ref = bf16[16,256,128]{2,1,0:T(8,128)(2,1)S(1)} async-done(((bf16[16,256,128]{2,1,0:T(8,128)(2,1)}), bf16[16,256,128]{2,1,0:T(8,128)(2,1)S(1)}, u32[]{:S(2)}, u32[]{:S(2)}) %all-to-all-start) | async-done | bytes 1048608 | tf_op jit(solution)/shard_map/all_to_all | solution.py:346
  125.8 6.5 %collective-permute-start.16 = (bf16[16,128,128]{2,1,0:T(8,128)(2,1)S(1)}, bf16[16,128,128]{2,1,0:T(8,128)(2,1)S(1)}, u32[]{:S(2)}, u32[]{:S(2)}) collective-permute-start(bf16[16,128,128]{2,1,0:T(8,128)(2,1)S(1)} %slice.16.kv0), channel_id=1, source_target_pairs={{0,2},{1,3},{2,0},{3,1},{4,6},{5,7},{6,4},{7,5},{8,10},{9,11},{10,... | collective-permute-start | bytes 1572872 | tf_op jit(solution)/shard_map/ppermute | solution.py:337
  132.3 8.7 %collective-permute-start.15 = (bf16[16,128,128]{2,1,0:T(8,128)(2,1)S(1)}, bf16[16,128,128]{2,1,0:T(8,128)(2,1)S(1)}, u32[]{:S(2)}, u32[]{:S(2)}) collective-permute-start(bf16[16,128,128]{2,1,0:T(8,128)(2,1)S(1)} %slice.16.kv0), channel_id=1, source_target_pairs={{0,1},{1,0},{2,3},{3,2},{4,5},{5,4},{6,7},{7,6},{8,9},{9,8},{10,11... | collective-permute-start | bytes 1572872 | tf_op jit(solution)/shard_map/ppermute | solution.py:337
  141.1 7.1 %collective-permute-start.17 = (bf16[16,128,128]{2,1,0:T(8,128)(2,1)S(1)}, bf16[16,128,128]{2,1,0:T(8,128)(2,1)S(1)}, u32[]{:S(2)}, u32[]{:S(2)}) collective-permute-start(bf16[16,128,128]{2,1,0:T(8,128)(2,1)S(1)} %collective-permute-done.16.kv2), channel_id=1, source_target_pairs={{0,1},{1,0},{2,3},{3,2},{4,5},{5,4},{6,7},{7,6},{8,9},{9,8},{10,11... | collective-permute-start | bytes 1572872 | tf_op jit(solution)/shard_map/ppermute | solution.py:337
  150.5 6.7 %attend.1 = (bf16[16,64,128]{2,1,0:T(8,128)(2,1)}, bf16[16,4,128,128]{3,2,1,0:T(8,128)(2,1)}) custom-call(s32[1]{0:T(128)} %bitcast.site_ref, s32[256]{0:T(256)} %reshape_squeeze.3.blk_ref, s32[64]{0:T(128)} %bitcast.41, bf16[16,256,128]{2,1,0:T(8,128)(2,1)} %copy-done.4, bf16[16,128,128]{2,1,0:T(8,128)(2,1)} %copy-done.5, bf16[16,128,128]{2,1,0:T(8,128)(2,1)} %copy-done.8, ...), custom_call_target="tpu_custom_call" | custom-call | flops 268435456 | bytes 5242880 | tf_op jit(solution)/shard_map/attend/pallas_call | solution.py:118
  157.2 26.0 %all-to-all-start.1 = ((bf16[256,4,128]{2,1,0:T(4,128)(2,1)}), bf16[256,4,128]{2,1,0:T(4,128)(2,1)S(1)}, u32[]{:S(2)}, u32[]{:S(2)}) async-start(bf16[256,4,128]{2,1,0:T(4,128)(2,1)} %bitcast.39), calls=%async_computation.1 | async-start | bytes 524288 | tf_op jit(solution)/shard_map/all_to_all | solution.py:352
  183.2 4.9 %value_contrib.1 = (bf16[2,64,16,128]{3,2,1,0:T(8,128)(2,1)}, bf16[2,64,16,128]{3,2,1,0:T(8,128)(2,1)}) custom-call(s32[1]{0:T(128)} %bitcast.site_ref, s32[256]{0:T(256)} %reshape_squeeze.3.blk_ref, bf16[16,256,128]{2,1,0:T(8,128)(2,1)} %copy-done.4, bf16[16,4,128,128]{3,2,1,0:T(8,128)(2,1)} %get-tuple-element.31.prob_ref), custom_call_target="tpu_custom_call" | custom-call | flops 134217728 | bytes 3145728 | tf_op jit(solution)/shard_map/value_contrib/pallas_call | solution.py:176
  195.9 26.2 %all-to-all-done.1 = bf16[256,4,128]{2,1,0:T(4,128)(2,1)S(1)} async-done(((bf16[256,4,128]{2,1,0:T(4,128)(2,1)}), bf16[256,4,128]{2,1,0:T(4,128)(2,1)S(1)}, u32[]{:S(2)}, u32[]{:S(2)}) %all-to-all-start.1) | async-done | bytes 262176 | tf_op jit(solution)/shard_map/all_to_all | solution.py:352
  222.8 4.2 %weight_part.1.part_ref = f32[64,8,128]{2,1,0:T(8,128)} custom-call(s32[1]{0:T(128)} %bitcast.8.me_ref, bf16[16,64,128]{2,1,0:T(8,128)(2,1)} %bitcast.16, bf16[128,1024]{1,0:T(8,128)(2,1)} %bitcast.20, bf16[128,1024]{1,0:T(8,128)(2,1)} %collective-permute-done.refs_1_, bf16[128,1024]{1,0:T(8,128)(2,1)} %collective-permute-done.1.refs_2_, ...), custom_call_target="tpu_custom_call" | custom-call | flops 268435456 | bytes 4194304 | tf_op jit(solution)/shard_map/weight_part/pallas_call | solution.py:234
  228.1 63.4 %all_to_all.20.back_ref = bf16[64,24,128]{2,1,0:T(8,128)(2,1)S(1)} all-to-all(bf16[64,24,128]{2,1,0:T(8,128)(2,1)S(1)} %merge.1), channel_id=1, replica_groups=mesh['dp'=16,'seq'=64] {'seq'}, dimensions={0} | all-to-all | bytes 786432 | tf_op jit(solution)/shard_map/all_to_all | solution.py:358
  292.4 3.5 %all-to-all-start.3 = ((bf16[16,80,128]{2,1,0:T(8,128)(2,1)}), bf16[16,80,128]{2,1,0:T(8,128)(2,1)S(1)}, u32[]{:S(2)}, u32[]{:S(2)}) async-start(bf16[16,80,128]{2,1,0:T(8,128)(2,1)} %gather_send.1), calls=%async_computation.3 | async-start | bytes 655360 | tf_op jit(solution)/shard_map/all_to_all | solution.py:361
  296.8 7.6 %all-to-all-done.3.got_ref = bf16[16,80,128]{2,1,0:T(8,128)(2,1)S(1)} async-done(((bf16[16,80,128]{2,1,0:T(8,128)(2,1)}), bf16[16,80,128]{2,1,0:T(8,128)(2,1)S(1)}, u32[]{:S(2)}, u32[]{:S(2)}) %all-to-all-start.3) | async-done | bytes 327712 | tf_op jit(solution)/shard_map/all_to_all | solution.py:361
  (79 shorter events, 31.0 us)
Async XLA Ops:
  4.1 121.6 %all-to-all-start = ((bf16[16,256,128]{2,1,0:T(8,128)(2,1)}), bf16[16,256,128]{2,1,0:T(8,128)(2,1)S(1)}, u32[]{:S(2)}, u32[]{:S(2)}) async-start(bf16[16,256,128]{2,1,0:T(8,128)(2,1)} %pack.1), calls=%async_computation | async-start | bytes 2097152 | tf_op jit(solution)/shard_map/all_to_all | solution.py:346
  33.2 20.0 %collective-permute-start.14 = (bf16[128,1024]{1,0:T(8,128)(2,1)S(1)}, bf16[128,1024]{1,0:T(8,128)(2,1)S(1)}, u32[]{:S(2)}, u32[]{:S(2)}) collective-permute-start(bf16[128,1024]{1,0:T(8,128)(2,1)S(1)} %bitcast.21), channel_id=1, source_target_pairs={{0,960},{64,896},{128,832},{192,768},{256,704},{320,640},{384,576}... | collective-permute-start | bytes 786440 | tf_op jit(solution)/shard_map/ppermute | solution.py:345
  40.1 17.9 %collective-permute-start.13 = (bf16[128,1024]{1,0:T(8,128)(2,1)S(1)}, bf16[128,1024]{1,0:T(8,128)(2,1)S(1)}, u32[]{:S(2)}, u32[]{:S(2)}) collective-permute-start(bf16[128,1024]{1,0:T(8,128)(2,1)S(1)} %bitcast.22), channel_id=1, source_target_pairs={{0,896},{64,960},{128,768},{192,832},{256,640},{320,704},{384,512}... | collective-permute-start | bytes 786440 | tf_op jit(solution)/shard_map/ppermute | solution.py:345
  42.3 18.0 %collective-permute-start.12 = (bf16[128,1024]{1,0:T(8,128)(2,1)S(1)}, bf16[128,1024]{1,0:T(8,128)(2,1)S(1)}, u32[]{:S(2)}, u32[]{:S(2)}) collective-permute-start(bf16[128,1024]{1,0:T(8,128)(2,1)S(1)} %bitcast.23), channel_id=1, source_target_pairs={{0,832},{64,768},{128,960},{192,896},{256,576},{320,512},{384,704}... | collective-permute-start | bytes 786440 | tf_op jit(solution)/shard_map/ppermute | solution.py:345
  46.8 40.7 %collective-permute-start.11 = (bf16[128,1024]{1,0:T(8,128)(2,1)S(1)}, bf16[128,1024]{1,0:T(8,128)(2,1)S(1)}, u32[]{:S(2)}, u32[]{:S(2)}) collective-permute-start(bf16[128,1024]{1,0:T(8,128)(2,1)S(1)} %bitcast.24), channel_id=1, source_target_pairs={{0,768},{64,832},{128,896},{192,960},{256,512},{320,576},{384,640}... | collective-permute-start | bytes 786440 | tf_op jit(solution)/shard_map/ppermute | solution.py:345
  48.8 41.4 %collective-permute-start.10 = (bf16[128,1024]{1,0:T(8,128)(2,1)S(1)}, bf16[128,1024]{1,0:T(8,128)(2,1)S(1)}, u32[]{:S(2)}, u32[]{:S(2)}) collective-permute-start(bf16[128,1024]{1,0:T(8,128)(2,1)S(1)} %bitcast.25), channel_id=1, source_target_pairs={{0,704},{64,640},{128,576},{192,512},{256,960},{320,896},{384,832}... | collective-permute-start | bytes 786440 | tf_op jit(solution)/shard_map/ppermute | solution.py:345
  53.3 168.8 %copy-start.10 = (bf16[128,1024]{1,0:T(8,128)(2,1)}, bf16[128,1024]{1,0:T(8,128)(2,1)S(1)}, u32[]{:S(2)}) copy-start(bf16[128,1024]{1,0:T(8,128)(2,1)S(1)} %collective-permute-done.14.refs_15_) | copy-start | bytes 786436
  53.3 40.7 %collective-permute-start.9 = (bf16[128,1024]{1,0:T(8,128)(2,1)S(1)}, bf16[128,1024]{1,0:T(8,128)(2,1)S(1)}, u32[]{:S(2)}, u32[]{:S(2)}) collective-permute-start(bf16[128,1024]{1,0:T(8,128)(2,1)S(1)} %bitcast.26), channel_id=1, source_target_pairs={{0,640},{64,704},{128,512},{192,576},{256,896},{320,960},{384,768}... | collective-permute-start | bytes 786440 | tf_op jit(solution)/shard_map/ppermute | solution.py:345
  58.0 37.9 %collective-permute-start.8 = (bf16[128,1024]{1,0:T(8,128)(2,1)S(1)}, bf16[128,1024]{1,0:T(8,128)(2,1)S(1)}, u32[]{:S(2)}, u32[]{:S(2)}) collective-permute-start(bf16[128,1024]{1,0:T(8,128)(2,1)S(1)} %bitcast.27), channel_id=1, source_target_pairs={{0,576},{64,512},{128,704},{192,640},{256,832},{320,768},{384,960}... | collective-permute-start | bytes 786440 | tf_op jit(solution)/shard_map/ppermute | solution.py:345
  60.3 40.2 %collective-permute-start.7 = (bf16[128,1024]{1,0:T(8,128)(2,1)S(1)}, bf16[128,1024]{1,0:T(8,128)(2,1)S(1)}, u32[]{:S(2)}, u32[]{:S(2)}) collective-permute-start(bf16[128,1024]{1,0:T(8,128)(2,1)S(1)} %bitcast.28), channel_id=1, source_target_pairs={{0,512},{64,576},{128,640},{192,704},{256,768},{320,832},{384,896}... | collective-permute-start | bytes 786440 | tf_op jit(solution)/shard_map/ppermute | solution.py:345
  87.5 19.8 %collective-permute-start.6 = (bf16[128,1024]{1,0:T(8,128)(2,1)S(1)}, bf16[128,1024]{1,0:T(8,128)(2,1)S(1)}, u32[]{:S(2)}, u32[]{:S(2)}) collective-permute-start(bf16[128,1024]{1,0:T(8,128)(2,1)S(1)} %bitcast.29), channel_id=1, source_target_pairs={{0,448},{64,384},{128,320},{192,256},{256,192},{320,128},{384,64},... | collective-permute-start | bytes 786440 | tf_op jit(solution)/shard_map/ppermute | solution.py:345
  90.2 19.0 %collective-permute-start.5 = (bf16[128,1024]{1,0:T(8,128)(2,1)S(1)}, bf16[128,1024]{1,0:T(8,128)(2,1)S(1)}, u32[]{:S(2)}, u32[]{:S(2)}) collective-permute-start(bf16[128,1024]{1,0:T(8,128)(2,1)S(1)} %bitcast.30), channel_id=1, source_target_pairs={{0,384},{64,448},{128,256},{192,320},{256,128},{320,192},{384,0},{... | collective-permute-start | bytes 786440 | tf_op jit(solution)/shard_map/ppermute | solution.py:345
  94.0 31.7 %collective-permute-start.4 = (bf16[128,1024]{1,0:T(8,128)(2,1)S(1)}, bf16[128,1024]{1,0:T(8,128)(2,1)}, u32[]{:S(2)}, u32[]{:S(2)}) collective-permute-start(bf16[128,1024]{1,0:T(8,128)(2,1)S(1)} %bitcast.31), channel_id=1, source_target_pairs={{0,320},{64,256},{128,448},{192,384},{256,64},{320,0},{384,192},{4... | collective-permute-start | bytes 786440 | tf_op jit(solution)/shard_map/ppermute | solution.py:345
  96.0 29.8 %collective-permute-start.3 = (bf16[128,1024]{1,0:T(8,128)(2,1)S(1)}, bf16[128,1024]{1,0:T(8,128)(2,1)}, u32[]{:S(2)}, u32[]{:S(2)}) collective-permute-start(bf16[128,1024]{1,0:T(8,128)(2,1)S(1)} %bitcast.32), channel_id=1, source_target_pairs={{0,256},{64,320},{128,384},{192,448},{256,0},{320,64},{384,128},{4... | collective-permute-start | bytes 786440 | tf_op jit(solution)/shard_map/ppermute | solution.py:345
  100.6 25.1 %collective-permute-start.2 = (bf16[128,1024]{1,0:T(8,128)(2,1)S(1)}, bf16[128,1024]{1,0:T(8,128)(2,1)}, u32[]{:S(2)}, u32[]{:S(2)}) collective-permute-start(bf16[128,1024]{1,0:T(8,128)(2,1)S(1)} %bitcast.33), channel_id=1, source_target_pairs={{0,192},{64,128},{128,64},{192,0},{256,448},{320,384},{384,320},{4... | collective-permute-start | bytes 786440 | tf_op jit(solution)/shard_map/ppermute | solution.py:345
  107.3 18.4 %collective-permute-start.1 = (bf16[128,1024]{1,0:T(8,128)(2,1)S(1)}, bf16[128,1024]{1,0:T(8,128)(2,1)}, u32[]{:S(2)}, u32[]{:S(2)}) collective-permute-start(bf16[128,1024]{1,0:T(8,128)(2,1)S(1)} %bitcast.34), channel_id=1, source_target_pairs={{0,128},{64,192},{128,0},{192,64},{256,384},{320,448},{384,256},{4... | collective-permute-start | bytes 786440 | tf_op jit(solution)/shard_map/ppermute | solution.py:345
  110.0 15.8 %collective-permute-start = (bf16[128,1024]{1,0:T(8,128)(2,1)S(1)}, bf16[128,1024]{1,0:T(8,128)(2,1)}, u32[]{:S(2)}, u32[]{:S(2)}) collective-permute-start(bf16[128,1024]{1,0:T(8,128)(2,1)S(1)} %bitcast.35), channel_id=1, source_target_pairs={{0,64},{64,0},{128,192},{192,128},{256,320},{320,256},{384,448},{4... | collective-permute-start | bytes 786440 | tf_op jit(solution)/shard_map/ppermute | solution.py:345
  125.8 15.2 %collective-permute-start.16 = (bf16[16,128,128]{2,1,0:T(8,128)(2,1)S(1)}, bf16[16,128,128]{2,1,0:T(8,128)(2,1)S(1)}, u32[]{:S(2)}, u32[]{:S(2)}) collective-permute-start(bf16[16,128,128]{2,1,0:T(8,128)(2,1)S(1)} %slice.16.kv0), channel_id=1, source_target_pairs={{0,2},{1,3},{2,0},{3,1},{4,6},{5,7},{6,4},{7,5},{8,10},{9,11},{10,... | collective-permute-start | bytes 1572872 | tf_op jit(solution)/shard_map/ppermute | solution.py:337
  132.3 16.6 %collective-permute-start.15 = (bf16[16,128,128]{2,1,0:T(8,128)(2,1)S(1)}, bf16[16,128,128]{2,1,0:T(8,128)(2,1)S(1)}, u32[]{:S(2)}, u32[]{:S(2)}) collective-permute-start(bf16[16,128,128]{2,1,0:T(8,128)(2,1)S(1)} %slice.16.kv0), channel_id=1, source_target_pairs={{0,1},{1,0},{2,3},{3,2},{4,5},{5,4},{6,7},{7,6},{8,9},{9,8},{10,11... | collective-permute-start | bytes 1572872 | tf_op jit(solution)/shard_map/ppermute | solution.py:337
  141.1 8.6 %collective-permute-start.17 = (bf16[16,128,128]{2,1,0:T(8,128)(2,1)S(1)}, bf16[16,128,128]{2,1,0:T(8,128)(2,1)S(1)}, u32[]{:S(2)}, u32[]{:S(2)}) collective-permute-start(bf16[16,128,128]{2,1,0:T(8,128)(2,1)S(1)} %collective-permute-done.16.kv2), channel_id=1, source_target_pairs={{0,1},{1,0},{2,3},{3,2},{4,5},{5,4},{6,7},{7,6},{8,9},{9,8},{10,11... | collective-permute-start | bytes 1572872 | tf_op jit(solution)/shard_map/ppermute | solution.py:337
  157.2 64.9 %all-to-all-start.1 = ((bf16[256,4,128]{2,1,0:T(4,128)(2,1)}), bf16[256,4,128]{2,1,0:T(4,128)(2,1)S(1)}, u32[]{:S(2)}, u32[]{:S(2)}) async-start(bf16[256,4,128]{2,1,0:T(4,128)(2,1)} %bitcast.39), calls=%async_computation.1 | async-start | bytes 524288 | tf_op jit(solution)/shard_map/all_to_all | solution.py:352
  188.2 4.3 %collective-permute-start.18 = (bf16[2,64,16,128]{3,2,1,0:T(8,128)(2,1)}, bf16[2,64,16,128]{3,2,1,0:T(8,128)(2,1)S(1)}, u32[]{:S(2)}, u32[]{:S(2)}) collective-permute-start(bf16[2,64,16,128]{3,2,1,0:T(8,128)(2,1)} %get-tuple-element.33), channel_id=1, source_target_pairs={{0,1},{1,0},{2,3},{3,2},{4,5},{5,4},{6,7},{7,6},{8,9},{9,8},{10,11... | collective-permute-start | bytes 1572872 | tf_op jit(solution)/shard_map/ppermute | solution.py:337
  193.7 33.4 %collective-permute-start.19 = (bf16[64,16,128]{2,1,0:T(8,128)(2,1)S(1)}, bf16[64,16,128]{2,1,0:T(8,128)(2,1)S(1)}, u32[]{:S(2)}, u32[]{:S(2)}) collective-permute-start(bf16[64,16,128]{2,1,0:T(8,128)(2,1)S(1)} %get-tuple-element.53), channel_id=1, source_target_pairs={{0,2},{1,3},{2,0},{3,1},{4,6},{5,7},{6,4},{7,5},{8,10},{9,11},{10,... | collective-permute-start | bytes 786440 | tf_op jit(solution)/shard_map/ppermute | solution.py:337
  292.4 12.0 %all-to-all-start.3 = ((bf16[16,80,128]{2,1,0:T(8,128)(2,1)}), bf16[16,80,128]{2,1,0:T(8,128)(2,1)S(1)}, u32[]{:S(2)}, u32[]{:S(2)}) async-start(bf16[16,80,128]{2,1,0:T(8,128)(2,1)} %gather_send.1), calls=%async_computation.3 | async-start | bytes 655360 | tf_op jit(solution)/shard_map/all_to_all | solution.py:361
  (20 other events, 671.4 us)

commit v6 on v5

--- a/solution.py
+++ b/solution.py
@@ -1,3 +1,5 @@
+import math
+
 import jax
 import jax.numpy as jnp
 from jax import lax
@@ -8,7 +10,7 @@
 H = 16
 HD = 64
 CSIZE = 128
-HALF = CSIZE // 2
+HALF = HD // 2
 MAXB = 4
 SITE = 4
 ROWS = 8
@@ -33,7 +35,7 @@
     grad = jnp.dot(w_ref[...], ct_ref[...], preferred_element_type=F32).astype(BF)
     for i in range(PAIR):
         part = keys[:, i * HD : (i + 1) * HD]
-        out_ref[i, 0:HALF, :] = jnp.concatenate([part[:HALF], part[HALF:]], axis=1)
+        out_ref[i, 0:64, :] = jnp.concatenate([part[:64], part[64:]], axis=1)
         out_ref[i, 64:128, :] = vals[i * HD : (i + 1) * HD]
         out_ref[i, 128:192, :] = qrys[i * HD : (i + 1) * HD]
         out_ref[i, 192:256, :] = grad[i * HD : (i + 1) * HD]
@@ -98,11 +100,11 @@
         s = scores[u]
         top = jnp.max(s, axis=0, keepdims=True)
         top = jnp.maximum(top[:, :CSIZE], top[:, CSIZE:])
-        e = jnp.exp((s - jnp.concatenate([top, top], axis=1)) * (HD**-0.5))
+        e = jnp.exp2((s - jnp.concatenate([top, top], axis=1)) * (HD**-0.5 * math.log2(math.e)))
         total = jnp.sum(e, axis=0, keepdims=True)
         inv = 1.0 / (total[:, :CSIZE] + total[:, CSIZE:])
         p = (e * jnp.concatenate([inv, inv], axis=1)).astype(BF)
-        halves = [p[i * HALF : (i + 1) * HALF, h : h + CSIZE] for i in range(MAXB) for h in (0, CSIZE)]
+        halves = [p[i * 64 : (i + 1) * 64, h : h + CSIZE] for i in range(MAXB) for h in (0, CSIZE)]
         for j in range(MAXB):
             prob_ref[u, j] = jnp.concatenate(halves[2 * j : 2 * j + 2], axis=0)
         vals = jnp.concatenate([kv_ref[slots[u][j], ids[u][j], 64:128, :] for j in range(MAXB)], axis=1)
@@ -165,9 +167,12 @@
 
     @pl.when(step == pl.num_programs(0) - 1)
     def _():
-        for t in range(SITE):
-            first = pl.multiple_of(16 * (site_ref[0] ^ t), 16)
-            (swap_ref if t % 2 else keep_ref)[t // 2] = acc_ref[:, pl.ds(first, 16), :].astype(BF)
+        core = site_ref[0] % 2
+        for t in range(2):
+            rows = pl.ds(pl.multiple_of(HALF * ((site_ref[0] // 2) ^ t), HALF), HALF)
+            for k in range(keep_ref.shape[1]):
+                keep_ref[t, k] = acc_ref[2 * k + core, rows, :].astype(BF)
+                swap_ref[t, k] = acc_ref[2 * k + 1 - core, rows, :].astype(BF)
 
 
 def backward(site, blk, recv, probs):
@@ -182,10 +187,10 @@
                 pl.BlockSpec((BROWS, 64, CSIZE), lambda i, *_: (i, 3, 0)),
                 pl.BlockSpec((BROWS, MAXB, CSIZE, CSIZE), lambda i, *_: (i, 0, 0, 0)),
             ],
-            out_specs=[pl.BlockSpec((2, clusters, 16, CSIZE), lambda i, *_: (0, 0, 0, 0))] * 2,
+            out_specs=[pl.BlockSpec((2, clusters // 2, HALF, CSIZE), lambda i, *_: (0, 0, 0, 0))] * 2,
             scratch_shapes=[pltpu.VMEM((clusters, HD, CSIZE), F32)],
         ),
-        out_shape=[jax.ShapeDtypeStruct((2, clusters, 16, CSIZE), BF)] * 2,
+        out_shape=[jax.ShapeDtypeStruct((2, clusters // 2, HALF, CSIZE), BF)] * 2,
         compiler_params=params(60),
         cost_estimate=pl.CostEstimate(
             flops=n * 2 * MAXB * CSIZE * CSIZE * HD, bytes_accessed=3 << 20, transcendentals=0
@@ -194,25 +199,25 @@
     )(site, blk, recv, probs)
 
 
-def merge_kernel(own_ref, other_ref, part_ref, out_ref):
-    total = own_ref[...].astype(F32) + other_ref[...].astype(F32)
-    out_ref[...] = jnp.concatenate([total, part_ref[...]], axis=1).astype(BF)
-
-
-def merge(own, other, part):
+def merge_kernel(own_ref, other_ref, part_ref, more_ref, out_ref):
+    value = own_ref[...].astype(F32) + other_ref[...].astype(F32)
+    out_ref[...] = jnp.concatenate([value, part_ref[...] + more_ref[...]], axis=1).astype(BF)
+
+
+def merge(own, other, part, more):
     n, rows, nodes = own.shape
     return pl.pallas_call(
         merge_kernel,
         out_shape=jax.ShapeDtypeStruct((n, rows + part.shape[1], nodes), BF),
         compiler_params=params(),
-        cost_estimate=pl.CostEstimate(flops=own.size, bytes_accessed=6 * own.size + 6 * part.size, transcendentals=0),
+        cost_estimate=pl.CostEstimate(flops=own.size, bytes_accessed=6 * own.size + 10 * part.size, transcendentals=0),
         name="merge",
-    )(own, other, part)
-
-
-def weight_kernel(me_ref, att_ref, *refs):
+    )(own, other, part, more)
+
+
+def weight_kernel(me_ref, site_ref, att_ref, *refs):
     n = att_ref.shape[0]
-    cots, (out_ref, cot_ref, acc_ref, sems) = refs[:n], refs[n:]
+    cots, (keep_ref, swap_ref, cot_ref, acc_ref, wide_ref, sems) = refs[:n], refs[n:]
     copies = [pltpu.make_async_copy(cots[t], cot_ref.at[t], sems.at[t]) for t in range(n)]
     for copy in copies:
         copy.start()
@@ -224,39 +229,47 @@
         cot = jnp.concatenate([cot_ref[t + i] for i in range(step)], axis=0)
         term = jnp.dot(att, cot, preferred_element_type=F32)
         acc_ref[...] = term if t == 0 else acc_ref[...] + term
-    for i in range(out_ref.shape[1]):
-        out_ref[:, i, :] = acc_ref[:, CSIZE * i : CSIZE * (i + 1)]
-
-
-def weight_part(me, att, cots):
+    for i in range(wide_ref.shape[1]):
+        wide_ref[:, i, :] = acc_ref[:, CSIZE * i : CSIZE * (i + 1)]
+    core = site_ref[0] % 2
+    half, piece, _ = keep_ref.shape
+    rows = wide_ref.shape[0] // half // 2
+    for k in range(half):
+        for to_ref, parity in ((keep_ref, core), (swap_ref, 1 - core)):
+            to_ref[k] = wide_ref[pl.ds((2 * k + parity) * rows, rows)].reshape(piece, CSIZE)
+
+
+def weight_part(me, site, att, cots, targets):
     n, rows, nodes = att.shape
     width = cots[0].shape[1]
+    piece = (targets // 2, rows * width // CSIZE // targets, CSIZE)
     return pl.pallas_call(
         weight_kernel,
         grid_spec=pltpu.PrefetchScalarGridSpec(
-            num_scalar_prefetch=1,
+            num_scalar_prefetch=2,
             grid=(1,),
             in_specs=[pl.BlockSpec(att.shape, lambda i, *_: (0, 0, 0))]
             + [pl.BlockSpec(memory_space=pl.ANY)] * n,
-            out_specs=pl.BlockSpec((rows, width // CSIZE, CSIZE), lambda i, *_: (0, 0, 0)),
+            out_specs=[pl.BlockSpec(piece, lambda i, *_: (0, 0, 0))] * 2,
             scratch_shapes=[
                 pltpu.VMEM((n, nodes, width), BF),
                 pltpu.VMEM((rows, width), F32),
+                pltpu.VMEM((rows, width // CSIZE, CSIZE), F32),
                 pltpu.SemaphoreType.DMA((n,)),
             ],
         ),
-        out_shape=jax.ShapeDtypeStruct((rows, width // CSIZE, CSIZE), F32),
+        out_shape=[jax.ShapeDtypeStruct(piece, F32)] * 2,
         compiler_params=params(60),
         cost_estimate=pl.CostEstimate(
             flops=2 * n * rows * nodes * width, bytes_accessed=2 * n * nodes * width, transcendentals=0
         ),
         name="weight_part",
-    )(me, att, *cots)
+    )(me, site, att, *cots)
 
 
 def gather_kernel(back_ref, att_ref, out_ref):
     n, rows, _ = att_ref.shape
-    total = jnp.sum(back_ref[...].astype(F32), axis=0)[16:]
+    total = jnp.sum(back_ref[...].astype(F32), axis=0)[HALF:]
     high = total.astype(BF).astype(F32)
     both = jnp.concatenate([high, total - high], axis=0).astype(BF)
     for p in range(n):
@@ -266,7 +279,7 @@
 
 def gather_send(back, att):
     n, rows, nodes = att.shape
-    more = 2 * (back.shape[1] - 16)
+    more = 2 * (back.shape[1] - HALF)
     return pl.pallas_call(
         gather_kernel,
         out_shape=jax.ShapeDtypeStruct((n, rows + more, nodes), BF),
@@ -331,6 +344,7 @@
     me = lax.axis_index("dp").astype(jnp.int32)[None]
     site = (lax.axis_index("seq") % SITE).astype(jnp.int32)[None]
     same_site = [[SITE * h + s for h in range(H)] for s in range(SITE)]
+    same_core = [list(range(c, nseq, 2)) for c in range(2)]
     same_site_dp = [[p * nseq + i for p in range(ndp) for i in group] for group in same_site]
 
     def swap(x, bit):
@@ -354,12 +368,12 @@
     ).reshape(ndp, width // ndp, CSIZE)
     keep, give = backward(site, blk, recv, probs)
     chip = (keep.astype(F32) + swap(give, 1).astype(F32)).astype(BF)
-    part = weight_part(me, pieces, cots).reshape(nseq, -1, CSIZE)
-    back = lax.all_to_all(
-        merge(chip[0], swap(chip[1], 2), part), "seq", split_axis=0, concat_axis=0, tiled=True
-    )
+    pieces, _ = lax.optimization_barrier((pieces, chip))
+    part, more = weight_part(me, site, pieces, cots, nseq)
+    last = merge(chip[0], swap(chip[1], 2), part, swap(more, 1))
+    back = lax.all_to_all(last, "seq", split_axis=0, concat_axis=0, tiled=True, axis_index_groups=same_core)
     got = lax.all_to_all(gather_send(back, pieces), "dp", split_axis=0, concat_axis=0, tiled=True)
-    value_grad = flip(back[:, :16].reshape(width, CSIZE))
+    value_grad = flip(back[:, :HALF].reshape(width, CSIZE))
     layer_out, weight_grad = finish(got, w_out, width // nseq)
     return (layer_out[None], value_grad[None], weight_grad)
 

time: 307 us -> 304 us (level)
  blocking collectives: 63.4 us -> 51.5 us
  starting transfers between devices: 138 us -> 146 us
    all_to_all x1, blocking collectives: 63.4 us -> 51.5 us  [body(): lax.all_to_all(last, 'seq', split_axis=0, concat_axis=0, tiled=True, axis...]
    ppermute x5 -> x6, starting transfers between devices: 27 us -> 34.4 us  [swap(): return lax.ppermute(x, 'seq', [(i, i ^ bit) for i in range(nseq)])]
  transfers between devices with their start and end apart: 23 -> 24, of which waited for: 7 -> 8; matrix products, arithmetic and copies ran while one was open for 1% -> 1% of each run, Pallas kernels for 3% -> 3%
where the time goes in v6:
time: 304 us; the launch traced here: 302 us
  starting transfers between devices  146 us (48%)
  waiting for transfers between devices  75.9 us (25%)
  blocking collectives  51.5 us (17%)
  Pallas kernels  22.2 us (7%)
  local copies, waits for them, and re-layouts  4.97 us (2%)
    ppermute x15, starting transfers between devices, body(): lax.ppermute(cot, 'dp', [(i, i ^ t) for i in range(ndp)])  52.5 us
    all_to_all x1, blocking collectives, body(): lax.all_to_all(last, 'seq', split_axis=0, concat_axis=0, tiled=True, axis...  51.5 us
    ppermute x6, starting transfers between devices, swap(): return lax.ppermute(x, 'seq', [(i, i ^ bit) for i in range(nseq)])  34.4 us
    all_to_all x1, starting transfers between devices, body(): lax.all_to_all(sent, 'seq', split_axis=0, concat_axis=0, tiled=True, axis...  29.1 us
    all_to_all x1, waiting for transfers between devices, body(): lax.all_to_all(sent_att, ('dp', 'seq'), split_axis=0, concat_axis=0, tile...  26.2 us
    all_to_all x1, starting transfers between devices, body(): lax.all_to_all(sent_att, ('dp', 'seq'), split_axis=0, concat_axis=0, tile...  26 us
    ppermute x15, waiting for transfers between devices, body(): lax.ppermute(cot, 'dp', [(i, i ^ t) for i in range(ndp)])  25.8 us
    all_to_all x1, waiting for transfers between devices, body(): lax.all_to_all(sent, 'seq', split_axis=0, concat_axis=0, tiled=True, axis...  13.2 us
  transfers between devices with their start and end apart: 24, of which 8 were waited for; matrix products, arithmetic and copies ran while one was open for 1% of the time, Pallas kernels for 3%

profile of v6, /device:TPU:1, one launch (start us, length us, event | category | flops | bytes accessed | tf_op | source)
XLA Modules:
  0.0 302.5 jit_solution(6399243214140800557)
XLA Ops:
  0.6 3.4 %pack.1 = bf16[16,256,128]{2,1,0:T(8,128)(2,1)} custom-call(bf16[128,1024]{1,0:T(8,128)(2,1)} %bitcast.36, bf16[128,1024]{1,0:T(8,128)(2,1)} %bitcast.37, bf16[128,1024]{1,0:T(8,128)(2,1)} %bitcast.38, bf16[128,1024]{1,0:T(8,128)(2,1)} %bitcast.19, bf16[1024,1024]{1,0:T(8,128)(2,1)} %w_ref.3), custom_call_target="tpu_custom_call" | custom-call | flops 268435456 | bytes 3407872 | tf_op jit(solution)/shard_map/pack/pallas_call | solution.py:47
  4.1 29.1 %all-to-all-start = ((bf16[16,256,128]{2,1,0:T(8,128)(2,1)}), bf16[16,256,128]{2,1,0:T(8,128)(2,1)S(1)}, u32[]{:S(2)}, u32[]{:S(2)}) async-start(bf16[16,256,128]{2,1,0:T(8,128)(2,1)} %pack.1), calls=%async_computation | async-start | bytes 2097152 | tf_op jit(solution)/shard_map/all_to_all | solution.py:360
  33.2 6.8 %collective-permute-start.14 = (bf16[128,1024]{1,0:T(8,128)(2,1)S(1)}, bf16[128,1024]{1,0:T(8,128)(2,1)S(1)}, u32[]{:S(2)}, u32[]{:S(2)}) collective-permute-start(bf16[128,1024]{1,0:T(8,128)(2,1)S(1)} %bitcast.21), channel_id=1, source_target_pairs={{0,960},{64,896},{128,832},{192,768},{256,704},{320,640},{384,576}... | collective-permute-start | bytes 786440 | tf_op jit(solution)/shard_map/ppermute | solution.py:359
  42.3 4.5 %collective-permute-start.12 = (bf16[128,1024]{1,0:T(8,128)(2,1)S(1)}, bf16[128,1024]{1,0:T(8,128)(2,1)S(1)}, u32[]{:S(2)}, u32[]{:S(2)}) collective-permute-start(bf16[128,1024]{1,0:T(8,128)(2,1)S(1)} %bitcast.23), channel_id=1, source_target_pairs={{0,832},{64,768},{128,960},{192,896},{256,576},{320,512},{384,704}... | collective-permute-start | bytes 786440 | tf_op jit(solution)/shard_map/ppermute | solution.py:359
  48.8 4.4 %collective-permute-start.10 = (bf16[128,1024]{1,0:T(8,128)(2,1)S(1)}, bf16[128,1024]{1,0:T(8,128)(2,1)S(1)}, u32[]{:S(2)}, u32[]{:S(2)}) collective-permute-start(bf16[128,1024]{1,0:T(8,128)(2,1)S(1)} %bitcast.25), channel_id=1, source_target_pairs={{0,704},{64,640},{128,576},{192,512},{256,960},{320,896},{384,832}... | collective-permute-start | bytes 786440 | tf_op jit(solution)/shard_map/ppermute | solution.py:359
  53.3 4.7 %collective-permute-start.9 = (bf16[128,1024]{1,0:T(8,128)(2,1)S(1)}, bf16[128,1024]{1,0:T(8,128)(2,1)S(1)}, u32[]{:S(2)}, u32[]{:S(2)}) collective-permute-start(bf16[128,1024]{1,0:T(8,128)(2,1)S(1)} %bitcast.26), channel_id=1, source_target_pairs={{0,640},{64,704},{128,512},{192,576},{256,896},{320,960},{384,768}... | collective-permute-start | bytes 786440 | tf_op jit(solution)/shard_map/ppermute | solution.py:359
  60.3 5.3 %collective-permute-start.7 = (bf16[128,1024]{1,0:T(8,128)(2,1)S(1)}, bf16[128,1024]{1,0:T(8,128)(2,1)S(1)}, u32[]{:S(2)}, u32[]{:S(2)}) collective-permute-start(bf16[128,1024]{1,0:T(8,128)(2,1)S(1)} %bitcast.28), channel_id=1, source_target_pairs={{0,512},{64,576},{128,640},{192,704},{256,768},{320,832},{384,896}... | collective-permute-start | bytes 786440 | tf_op jit(solution)/shard_map/ppermute | solution.py:359
  65.7 21.9 %collective-permute-done.11.refs_12_ = bf16[128,1024]{1,0:T(8,128)(2,1)S(1)} collective-permute-done((bf16[128,1024]{1,0:T(8,128)(2,1)S(1)}, bf16[128,1024]{1,0:T(8,128)(2,1)S(1)}, u32[]{:S(2)}, u32[]{:S(2)}) %collective-permute-start.11) | collective-permute-done | bytes 262176 | tf_op jit(solution)/shard_map/ppermute | solution.py:359
  90.2 3.8 %collective-permute-start.5 = (bf16[128,1024]{1,0:T(8,128)(2,1)S(1)}, bf16[128,1024]{1,0:T(8,128)(2,1)S(1)}, u32[]{:S(2)}, u32[]{:S(2)}) collective-permute-start(bf16[128,1024]{1,0:T(8,128)(2,1)S(1)} %bitcast.30), channel_id=1, source_target_pairs={{0,384},{64,448},{128,256},{192,320},{256,128},{320,192},{384,0},{... | collective-permute-start | bytes 786440 | tf_op jit(solution)/shard_map/ppermute | solution.py:359
  96.0 4.6 %collective-permute-start.3 = (bf16[128,1024]{1,0:T(8,128)(2,1)S(1)}, bf16[128,1024]{1,0:T(8,128)(2,1)}, u32[]{:S(2)}, u32[]{:S(2)}) collective-permute-start(bf16[128,1024]{1,0:T(8,128)(2,1)S(1)} %bitcast.32), channel_id=1, source_target_pairs={{0,256},{64,320},{128,384},{192,448},{256,0},{320,64},{384,128},{4... | collective-permute-start | bytes 786440 | tf_op jit(solution)/shard_map/ppermute | solution.py:359
  103.5 3.9 %collective-permute-done.6.refs_7_ = bf16[128,1024]{1,0:T(8,128)(2,1)S(1)} collective-permute-done((bf16[128,1024]{1,0:T(8,128)(2,1)S(1)}, bf16[128,1024]{1,0:T(8,128)(2,1)S(1)}, u32[]{:S(2)}, u32[]{:S(2)}) %collective-permute-start.6) | collective-permute-done | bytes 262176 | tf_op jit(solution)/shard_map/ppermute | solution.py:359
  112.5 13.2 %all-to-all-done.q_ref.g_ref = bf16[16,256,128]{2,1,0:T(8,128)(2,1)S(1)} async-done(((bf16[16,256,128]{2,1,0:T(8,128)(2,1)}), bf16[16,256,128]{2,1,0:T(8,128)(2,1)S(1)}, u32[]{:S(2)}, u32[]{:S(2)}) %all-to-all-start) | async-done | bytes 1048608 | tf_op jit(solution)/shard_map/all_to_all | solution.py:360
  125.8 6.5 %collective-permute-start.16 = (bf16[16,128,128]{2,1,0:T(8,128)(2,1)S(1)}, bf16[16,128,128]{2,1,0:T(8,128)(2,1)S(1)}, u32[]{:S(2)}, u32[]{:S(2)}) collective-permute-start(bf16[16,128,128]{2,1,0:T(8,128)(2,1)S(1)} %slice.16.kv0), channel_id=1, source_target_pairs={{0,2},{1,3},{2,0},{3,1},{4,6},{5,7},{6,4},{7,5},{8,10},{9,11},{10,... | collective-permute-start | bytes 1572872 | tf_op jit(solution)/shard_map/ppermute | solution.py:351
  132.3 8.7 %collective-permute-start.15 = (bf16[16,128,128]{2,1,0:T(8,128)(2,1)S(1)}, bf16[16,128,128]{2,1,0:T(8,128)(2,1)S(1)}, u32[]{:S(2)}, u32[]{:S(2)}) collective-permute-start(bf16[16,128,128]{2,1,0:T(8,128)(2,1)S(1)} %slice.16.kv0), channel_id=1, source_target_pairs={{0,1},{1,0},{2,3},{3,2},{4,5},{5,4},{6,7},{7,6},{8,9},{9,8},{10,11... | collective-permute-start | bytes 1572872 | tf_op jit(solution)/shard_map/ppermute | solution.py:351
  141.0 7.1 %collective-permute-start.17 = (bf16[16,128,128]{2,1,0:T(8,128)(2,1)S(1)}, bf16[16,128,128]{2,1,0:T(8,128)(2,1)S(1)}, u32[]{:S(2)}, u32[]{:S(2)}) collective-permute-start(bf16[16,128,128]{2,1,0:T(8,128)(2,1)S(1)} %collective-permute-done.16.kv2), channel_id=1, source_target_pairs={{0,1},{1,0},{2,3},{3,2},{4,5},{5,4},{6,7},{7,6},{8,9},{9,8},{10,11... | collective-permute-start | bytes 1572872 | tf_op jit(solution)/shard_map/ppermute | solution.py:351
  150.5 6.5 %attend.1 = (bf16[16,64,128]{2,1,0:T(8,128)(2,1)}, bf16[16,4,128,128]{3,2,1,0:T(8,128)(2,1)}) custom-call(s32[1]{0:T(128)} %bitcast.site_ref, s32[256]{0:T(256)} %reshape_squeeze.3.blk_ref, s32[64]{0:T(128)} %bitcast.41, bf16[16,256,128]{2,1,0:T(8,128)(2,1)} %copy-done.4, bf16[16,128,128]{2,1,0:T(8,128)(2,1)} %copy-done.5, bf16[16,128,128]{2,1,0:T(8,128)(2,1)} %copy-done.8, ...), custom_call_target="tpu_custom_call" | custom-call | flops 268435456 | bytes 5242880 | tf_op jit(solution)/shard_map/attend/pallas_call | solution.py:120
  157.0 26.0 %all-to-all-start.1 = ((bf16[256,4,128]{2,1,0:T(4,128)(2,1)}), bf16[256,4,128]{2,1,0:T(4,128)(2,1)S(1)}, u32[]{:S(2)}, u32[]{:S(2)}) async-start(bf16[256,4,128]{2,1,0:T(4,128)(2,1)} %bitcast.39), calls=%async_computation.1 | async-start | bytes 524288 | tf_op jit(solution)/shard_map/all_to_all | solution.py:366
  183.0 4.9 %value_contrib.1 = (bf16[2,32,32,128]{3,2,1,0:T(8,128)(2,1)}, bf16[2,32,32,128]{3,2,1,0:T(8,128)(2,1)}) custom-call(s32[1]{0:T(128)} %bitcast.site_ref, s32[256]{0:T(256)} %reshape_squeeze.3.blk_ref, bf16[16,256,128]{2,1,0:T(8,128)(2,1)} %copy-done.4, bf16[16,4,128,128]{3,2,1,0:T(8,128)(2,1)} %get-tuple-element.34.prob_ref), custom_call_target="tpu_custom_call" | custom-call | flops 134217728 | bytes 3145728 | tf_op jit(solution)/shard_map/value_contrib/pallas_call | solution.py:181
  195.7 26.2 %all-to-all-done.1 = bf16[256,4,128]{2,1,0:T(4,128)(2,1)S(1)} async-done(((bf16[256,4,128]{2,1,0:T(4,128)(2,1)}), bf16[256,4,128]{2,1,0:T(4,128)(2,1)S(1)}, u32[]{:S(2)}, u32[]{:S(2)}) %all-to-all-start.1) | async-done | bytes 262176 | tf_op jit(solution)/shard_map/all_to_all | solution.py:366
  222.6 4.3 %weight_part.1 = (f32[32,8,128]{2,1,0:T(8,128)}, f32[32,8,128]{2,1,0:T(8,128)}) custom-call(s32[1]{0:T(128)} %bitcast.8.me_ref, s32[1]{0:T(128)} %bitcast.site_ref, bf16[16,64,128]{2,1,0:T(8,128)(2,1)} %bitcast.16, bf16[128,1024]{1,0:T(8,128)(2,1)} %bitcast.20, bf16[128,1024]{1,0:T(8,128)(2,1)} %collective-permute-done.refs_1_, ...), custom_call_target="tpu_custom_call" | custom-call | flops 268435456 | bytes 4194304 | tf_op jit(solution)/shard_map/weight_part/pallas_call | solution.py:246
  226.9 7.3 %collective-permute-start.20 = (f32[32,8,128]{2,1,0:T(8,128)}, f32[32,8,128]{2,1,0:T(8,128)S(1)}, u32[]{:S(2)}, u32[]{:S(2)}) collective-permute-start(f32[32,8,128]{2,1,0:T(8,128)} %get-tuple-element.56), channel_id=1, source_target_pairs={{0,1},{1,0},{2,3},{3,2},{4,5},{5,4},{6,7},{7,6},{8,9},{9,8},{10,11... | collective-permute-start | bytes 393224 | tf_op jit(solution)/shard_map/ppermute | solution.py:351
  236.4 51.5 %all_to_all.20.back_ref = bf16[32,40,128]{2,1,0:T(8,128)(2,1)S(1)} all-to-all(bf16[32,40,128]{2,1,0:T(8,128)(2,1)S(1)} %merge.1), channel_id=1, replica_groups={{0,2,4,6,8,10,12,14,16,18,20,22,24,26,28,30,32,34,36,38,40,42,44,46,48,..., dimensions={0} | all-to-all | bytes 655360 | tf_op jit(solution)/shard_map/all_to_all | solution.py:374
  289.7 3.5 %all-to-all-start.3 = ((bf16[16,80,128]{2,1,0:T(8,128)(2,1)}), bf16[16,80,128]{2,1,0:T(8,128)(2,1)S(1)}, u32[]{:S(2)}, u32[]{:S(2)}) async-start(bf16[16,80,128]{2,1,0:T(8,128)(2,1)} %gather_send.1), calls=%async_computation.3 | async-start | bytes 655360 | tf_op jit(solution)/shard_map/all_to_all | solution.py:375
  294.1 7.1 %all-to-all-done.3.got_ref = bf16[16,80,128]{2,1,0:T(8,128)(2,1)S(1)} async-done(((bf16[16,80,128]{2,1,0:T(8,128)(2,1)}), bf16[16,80,128]{2,1,0:T(8,128)(2,1)S(1)}, u32[]{:S(2)}, u32[]{:S(2)}) %all-to-all-start.3) | async-done | bytes 327712 | tf_op jit(solution)/shard_map/all_to_all | solution.py:375
  (81 shorter events, 35.8 us)
Async XLA Ops:
  4.1 121.6 %all-to-all-start = ((bf16[16,256,128]{2,1,0:T(8,128)(2,1)}), bf16[16,256,128]{2,1,0:T(8,128)(2,1)S(1)}, u32[]{:S(2)}, u32[]{:S(2)}) async-start(bf16[16,256,128]{2,1,0:T(8,128)(2,1)} %pack.1), calls=%async_computation | async-start | bytes 2097152 | tf_op jit(solution)/shard_map/all_to_all | solution.py:360
  33.2 20.0 %collective-permute-start.14 = (bf16[128,1024]{1,0:T(8,128)(2,1)S(1)}, bf16[128,1024]{1,0:T(8,128)(2,1)S(1)}, u32[]{:S(2)}, u32[]{:S(2)}) collective-permute-start(bf16[128,1024]{1,0:T(8,128)(2,1)S(1)} %bitcast.21), channel_id=1, source_target_pairs={{0,960},{64,896},{128,832},{192,768},{256,704},{320,640},{384,576}... | collective-permute-start | bytes 786440 | tf_op jit(solution)/shard_map/ppermute | solution.py:359
  40.1 17.9 %collective-permute-start.13 = (bf16[128,1024]{1,0:T(8,128)(2,1)S(1)}, bf16[128,1024]{1,0:T(8,128)(2,1)S(1)}, u32[]{:S(2)}, u32[]{:S(2)}) collective-permute-start(bf16[128,1024]{1,0:T(8,128)(2,1)S(1)} %bitcast.22), channel_id=1, source_target_pairs={{0,896},{64,960},{128,768},{192,832},{256,640},{320,704},{384,512}... | collective-permute-start | bytes 786440 | tf_op jit(solution)/shard_map/ppermute | solution.py:359
  42.3 18.0 %collective-permute-start.12 = (bf16[128,1024]{1,0:T(8,128)(2,1)S(1)}, bf16[128,1024]{1,0:T(8,128)(2,1)S(1)}, u32[]{:S(2)}, u32[]{:S(2)}) collective-permute-start(bf16[128,1024]{1,0:T(8,128)(2,1)S(1)} %bitcast.23), channel_id=1, source_target_pairs={{0,832},{64,768},{128,960},{192,896},{256,576},{320,512},{384,704}... | collective-permute-start | bytes 786440 | tf_op jit(solution)/shard_map/ppermute | solution.py:359
  46.8 40.7 %collective-permute-start.11 = (bf16[128,1024]{1,0:T(8,128)(2,1)S(1)}, bf16[128,1024]{1,0:T(8,128)(2,1)S(1)}, u32[]{:S(2)}, u32[]{:S(2)}) collective-permute-start(bf16[128,1024]{1,0:T(8,128)(2,1)S(1)} %bitcast.24), channel_id=1, source_target_pairs={{0,768},{64,832},{128,896},{192,960},{256,512},{320,576},{384,640}... | collective-permute-start | bytes 786440 | tf_op jit(solution)/shard_map/ppermute | solution.py:359
  48.8 41.4 %collective-permute-start.10 = (bf16[128,1024]{1,0:T(8,128)(2,1)S(1)}, bf16[128,1024]{1,0:T(8,128)(2,1)S(1)}, u32[]{:S(2)}, u32[]{:S(2)}) collective-permute-start(bf16[128,1024]{1,0:T(8,128)(2,1)S(1)} %bitcast.25), channel_id=1, source_target_pairs={{0,704},{64,640},{128,576},{192,512},{256,960},{320,896},{384,832}... | collective-permute-start | bytes 786440 | tf_op jit(solution)/shard_map/ppermute | solution.py:359
  53.3 40.7 %collective-permute-start.9 = (bf16[128,1024]{1,0:T(8,128)(2,1)S(1)}, bf16[128,1024]{1,0:T(8,128)(2,1)S(1)}, u32[]{:S(2)}, u32[]{:S(2)}) collective-permute-start(bf16[128,1024]{1,0:T(8,128)(2,1)S(1)} %bitcast.26), channel_id=1, source_target_pairs={{0,640},{64,704},{128,512},{192,576},{256,896},{320,960},{384,768}... | collective-permute-start | bytes 786440 | tf_op jit(solution)/shard_map/ppermute | solution.py:359
  58.0 37.9 %collective-permute-start.8 = (bf16[128,1024]{1,0:T(8,128)(2,1)S(1)}, bf16[128,1024]{1,0:T(8,128)(2,1)S(1)}, u32[]{:S(2)}, u32[]{:S(2)}) collective-permute-start(bf16[128,1024]{1,0:T(8,128)(2,1)S(1)} %bitcast.27), channel_id=1, source_target_pairs={{0,576},{64,512},{128,704},{192,640},{256,832},{320,768},{384,960}... | collective-permute-start | bytes 786440 | tf_op jit(solution)/shard_map/ppermute | solution.py:359
  60.3 40.2 %collective-permute-start.7 = (bf16[128,1024]{1,0:T(8,128)(2,1)S(1)}, bf16[128,1024]{1,0:T(8,128)(2,1)S(1)}, u32[]{:S(2)}, u32[]{:S(2)}) collective-permute-start(bf16[128,1024]{1,0:T(8,128)(2,1)S(1)} %bitcast.28), channel_id=1, source_target_pairs={{0,512},{64,576},{128,640},{192,704},{256,768},{320,832},{384,896}... | collective-permute-start | bytes 786440 | tf_op jit(solution)/shard_map/ppermute | solution.py:359
  87.5 19.8 %collective-permute-start.6 = (bf16[128,1024]{1,0:T(8,128)(2,1)S(1)}, bf16[128,1024]{1,0:T(8,128)(2,1)S(1)}, u32[]{:S(2)}, u32[]{:S(2)}) collective-permute-start(bf16[128,1024]{1,0:T(8,128)(2,1)S(1)} %bitcast.29), channel_id=1, source_target_pairs={{0,448},{64,384},{128,320},{192,256},{256,192},{320,128},{384,64},... | collective-permute-start | bytes 786440 | tf_op jit(solution)/shard_map/ppermute | solution.py:359
  90.2 19.0 %collective-permute-start.5 = (bf16[128,1024]{1,0:T(8,128)(2,1)S(1)}, bf16[128,1024]{1,0:T(8,128)(2,1)S(1)}, u32[]{:S(2)}, u32[]{:S(2)}) collective-permute-start(bf16[128,1024]{1,0:T(8,128)(2,1)S(1)} %bitcast.30), channel_id=1, source_target_pairs={{0,384},{64,448},{128,256},{192,320},{256,128},{320,192},{384,0},{... | collective-permute-start | bytes 786440 | tf_op jit(solution)/shard_map/ppermute | solution.py:359
  94.0 31.7 %collective-permute-start.4 = (bf16[128,1024]{1,0:T(8,128)(2,1)S(1)}, bf16[128,1024]{1,0:T(8,128)(2,1)}, u32[]{:S(2)}, u32[]{:S(2)}) collective-permute-start(bf16[128,1024]{1,0:T(8,128)(2,1)S(1)} %bitcast.31), channel_id=1, source_target_pairs={{0,320},{64,256},{128,448},{192,384},{256,64},{320,0},{384,192},{4... | collective-permute-start | bytes 786440 | tf_op jit(solution)/shard_map/ppermute | solution.py:359
  96.0 29.8 %collective-permute-start.3 = (bf16[128,1024]{1,0:T(8,128)(2,1)S(1)}, bf16[128,1024]{1,0:T(8,128)(2,1)}, u32[]{:S(2)}, u32[]{:S(2)}) collective-permute-start(bf16[128,1024]{1,0:T(8,128)(2,1)S(1)} %bitcast.32), channel_id=1, source_target_pairs={{0,256},{64,320},{128,384},{192,448},{256,0},{320,64},{384,128},{4... | collective-permute-start | bytes 786440 | tf_op jit(solution)/shard_map/ppermute | solution.py:359
  100.6 25.1 %collective-permute-start.2 = (bf16[128,1024]{1,0:T(8,128)(2,1)S(1)}, bf16[128,1024]{1,0:T(8,128)(2,1)}, u32[]{:S(2)}, u32[]{:S(2)}) collective-permute-start(bf16[128,1024]{1,0:T(8,128)(2,1)S(1)} %bitcast.33), channel_id=1, source_target_pairs={{0,192},{64,128},{128,64},{192,0},{256,448},{320,384},{384,320},{4... | collective-permute-start | bytes 786440 | tf_op jit(solution)/shard_map/ppermute | solution.py:359
  107.3 18.4 %collective-permute-start.1 = (bf16[128,1024]{1,0:T(8,128)(2,1)S(1)}, bf16[128,1024]{1,0:T(8,128)(2,1)}, u32[]{:S(2)}, u32[]{:S(2)}) collective-permute-start(bf16[128,1024]{1,0:T(8,128)(2,1)S(1)} %bitcast.34), channel_id=1, source_target_pairs={{0,128},{64,192},{128,0},{192,64},{256,384},{320,448},{384,256},{4... | collective-permute-start | bytes 786440 | tf_op jit(solution)/shard_map/ppermute | solution.py:359
  110.0 15.8 %collective-permute-start = (bf16[128,1024]{1,0:T(8,128)(2,1)S(1)}, bf16[128,1024]{1,0:T(8,128)(2,1)}, u32[]{:S(2)}, u32[]{:S(2)}) collective-permute-start(bf16[128,1024]{1,0:T(8,128)(2,1)S(1)} %bitcast.35), channel_id=1, source_target_pairs={{0,64},{64,0},{128,192},{192,128},{256,320},{320,256},{384,448},{4... | collective-permute-start | bytes 786440 | tf_op jit(solution)/shard_map/ppermute | solution.py:359
  125.8 15.2 %collective-permute-start.16 = (bf16[16,128,128]{2,1,0:T(8,128)(2,1)S(1)}, bf16[16,128,128]{2,1,0:T(8,128)(2,1)S(1)}, u32[]{:S(2)}, u32[]{:S(2)}) collective-permute-start(bf16[16,128,128]{2,1,0:T(8,128)(2,1)S(1)} %slice.16.kv0), channel_id=1, source_target_pairs={{0,2},{1,3},{2,0},{3,1},{4,6},{5,7},{6,4},{7,5},{8,10},{9,11},{10,... | collective-permute-start | bytes 1572872 | tf_op jit(solution)/shard_map/ppermute | solution.py:351
  132.3 16.6 %collective-permute-start.15 = (bf16[16,128,128]{2,1,0:T(8,128)(2,1)S(1)}, bf16[16,128,128]{2,1,0:T(8,128)(2,1)S(1)}, u32[]{:S(2)}, u32[]{:S(2)}) collective-permute-start(bf16[16,128,128]{2,1,0:T(8,128)(2,1)S(1)} %slice.16.kv0), channel_id=1, source_target_pairs={{0,1},{1,0},{2,3},{3,2},{4,5},{5,4},{6,7},{7,6},{8,9},{9,8},{10,11... | collective-permute-start | bytes 1572872 | tf_op jit(solution)/shard_map/ppermute | solution.py:351
  141.0 8.6 %collective-permute-start.17 = (bf16[16,128,128]{2,1,0:T(8,128)(2,1)S(1)}, bf16[16,128,128]{2,1,0:T(8,128)(2,1)S(1)}, u32[]{:S(2)}, u32[]{:S(2)}) collective-permute-start(bf16[16,128,128]{2,1,0:T(8,128)(2,1)S(1)} %collective-permute-done.16.kv2), channel_id=1, source_target_pairs={{0,1},{1,0},{2,3},{3,2},{4,5},{5,4},{6,7},{7,6},{8,9},{9,8},{10,11... | collective-permute-start | bytes 1572872 | tf_op jit(solution)/shard_map/ppermute | solution.py:351
  157.0 64.9 %all-to-all-start.1 = ((bf16[256,4,128]{2,1,0:T(4,128)(2,1)}), bf16[256,4,128]{2,1,0:T(4,128)(2,1)S(1)}, u32[]{:S(2)}, u32[]{:S(2)}) async-start(bf16[256,4,128]{2,1,0:T(4,128)(2,1)} %bitcast.39), calls=%async_computation.1 | async-start | bytes 524288 | tf_op jit(solution)/shard_map/all_to_all | solution.py:366
  187.9 4.3 %collective-permute-start.18 = (bf16[2,32,32,128]{3,2,1,0:T(8,128)(2,1)}, bf16[2,32,32,128]{3,2,1,0:T(8,128)(2,1)S(1)}, u32[]{:S(2)}, u32[]{:S(2)}) collective-permute-start(bf16[2,32,32,128]{3,2,1,0:T(8,128)(2,1)} %get-tuple-element.36), channel_id=1, source_target_pairs={{0,1},{1,0},{2,3},{3,2},{4,5},{5,4},{6,7},{7,6},{8,9},{9,8},{10,11... | collective-permute-start | bytes 1572872 | tf_op jit(solution)/shard_map/ppermute | solution.py:351
  193.4 40.9 %collective-permute-start.19 = (bf16[32,32,128]{2,1,0:T(8,128)(2,1)S(1)}, bf16[32,32,128]{2,1,0:T(8,128)(2,1)S(1)}, u32[]{:S(2)}, u32[]{:S(2)}) collective-permute-start(bf16[32,32,128]{2,1,0:T(8,128)(2,1)S(1)} %get-tuple-element.59), channel_id=1, source_target_pairs={{0,2},{1,3},{2,0},{3,1},{4,6},{5,7},{6,4},{7,5},{8,10},{9,11},{10,... | collective-permute-start | bytes 786440 | tf_op jit(solution)/shard_map/ppermute | solution.py:351
  226.9 8.5 %collective-permute-start.20 = (f32[32,8,128]{2,1,0:T(8,128)}, f32[32,8,128]{2,1,0:T(8,128)S(1)}, u32[]{:S(2)}, u32[]{:S(2)}) collective-permute-start(f32[32,8,128]{2,1,0:T(8,128)} %get-tuple-element.56), channel_id=1, source_target_pairs={{0,1},{1,0},{2,3},{3,2},{4,5},{5,4},{6,7},{7,6},{8,9},{9,8},{10,11... | collective-permute-start | bytes 393224 | tf_op jit(solution)/shard_map/ppermute | solution.py:351
  289.7 11.5 %all-to-all-start.3 = ((bf16[16,80,128]{2,1,0:T(8,128)(2,1)}), bf16[16,80,128]{2,1,0:T(8,128)(2,1)S(1)}, u32[]{:S(2)}, u32[]{:S(2)}) async-start(bf16[16,80,128]{2,1,0:T(8,128)(2,1)} %gather_send.1), calls=%async_computation.3 | async-start | bytes 655360 | tf_op jit(solution)/shard_map/all_to_all | solution.py:375
  (21 other events, 764.7 us)

commit v7 on v6

--- a/solution.py
+++ b/solution.py
@@ -216,18 +216,11 @@
 
 
 def weight_kernel(me_ref, site_ref, att_ref, *refs):
-    n = att_ref.shape[0]
-    cots, (keep_ref, swap_ref, cot_ref, acc_ref, wide_ref, sems) = refs[:n], refs[n:]
-    copies = [pltpu.make_async_copy(cots[t], cot_ref.at[t], sems.at[t]) for t in range(n)]
-    for copy in copies:
-        copy.start()
-    step = min(2, n)
-    for t in range(0, n, step):
-        for i in range(step):
-            copies[t + i].wait()
-        att = jnp.concatenate([att_ref[me_ref[0] ^ (t + i)] for i in range(step)], axis=1)
-        cot = jnp.concatenate([cot_ref[t + i] for i in range(step)], axis=0)
-        term = jnp.dot(att, cot, preferred_element_type=F32)
+    cots, (keep_ref, swap_ref, acc_ref, wide_ref) = refs[:-4], refs[-4:]
+    each = att_ref.shape[0] // len(cots)
+    for t, cot_ref in enumerate(cots):
+        att = jnp.concatenate([att_ref[me_ref[0] ^ (each * t + i)] for i in range(each)], axis=1)
+        term = jnp.dot(att, cot_ref[...], preferred_element_type=F32)
         acc_ref[...] = term if t == 0 else acc_ref[...] + term
     for i in range(wide_ref.shape[1]):
         wide_ref[:, i, :] = acc_ref[:, CSIZE * i : CSIZE * (i + 1)]
@@ -245,21 +238,10 @@
     piece = (targets // 2, rows * width // CSIZE // targets, CSIZE)
     return pl.pallas_call(
         weight_kernel,
-        grid_spec=pltpu.PrefetchScalarGridSpec(
-            num_scalar_prefetch=2,
-            grid=(1,),
-            in_specs=[pl.BlockSpec(att.shape, lambda i, *_: (0, 0, 0))]
-            + [pl.BlockSpec(memory_space=pl.ANY)] * n,
-            out_specs=[pl.BlockSpec(piece, lambda i, *_: (0, 0, 0))] * 2,
-            scratch_shapes=[
-                pltpu.VMEM((n, nodes, width), BF),
-                pltpu.VMEM((rows, width), F32),
-                pltpu.VMEM((rows, width // CSIZE, CSIZE), F32),
-                pltpu.SemaphoreType.DMA((n,)),
-            ],
-        ),
+        in_specs=[pl.BlockSpec(memory_space=pltpu.SMEM)] * 2 + [pl.BlockSpec(memory_space=pltpu.VMEM)] * (1 + len(cots)),
         out_shape=[jax.ShapeDtypeStruct(piece, F32)] * 2,
-        compiler_params=params(60),
+        scratch_shapes=[pltpu.VMEM((rows, width), F32), pltpu.VMEM((rows, width // CSIZE, CSIZE), F32)],
+        compiler_params=params(16),
         cost_estimate=pl.CostEstimate(
             flops=2 * n * rows * nodes * width, bytes_accessed=2 * n * nodes * width, transcendentals=0
         ),
@@ -356,7 +338,10 @@
 
     sent = pack(queries[0], keys[0], values[0], cot, w_out)
     sent, cot = lax.optimization_barrier((sent, cot))
-    cots = [cot] + [lax.ppermute(cot, "dp", [(i, i ^ t) for i in range(ndp)]) for t in range(1, ndp)]
+    cots = [cot]
+    if ndp > 1:
+        cot = jnp.concatenate([cot, lax.ppermute(cot, "dp", [(i, i ^ 1) for i in range(ndp)])], axis=0)
+        cots = [cot] + [lax.ppermute(cot, "dp", [(i, i ^ t) for i in range(ndp)]) for t in range(2, ndp, 2)]
     recv = lax.all_to_all(sent, "seq", split_axis=0, concat_axis=0, tiled=True, axis_index_groups=same_site)
     kv, cots = lax.optimization_barrier((recv[:, :128], cots))
     kv_z = swap(kv, 2)

time: 304 us -> 302 us (level)
  waiting for transfers between devices: 75.9 us -> 97.6 us
  starting transfers between devices: 146 us -> 125 us
    ppermute x15 -> x7, starting transfers between devices: 52.5 us -> 28 us  [body(): lax.ppermute(cot, 'dp', [(i, i ^ t) for i in range(ndp)])]
    all_to_all x1, waiting for transfers between devices: 13.2 us -> 36.3 us  [body(): lax.all_to_all(sent, 'seq', split_axis=0, concat_axis=0, tiled=True, axis...]
    ppermute x15 -> x7, waiting for transfers between devices: 25.8 us -> 19.3 us  [body(): lax.ppermute(cot, 'dp', [(i, i ^ t) for i in range(ndp)])]
    ppermute x0 -> x1, waiting for transfers between devices: none -> 5.6 us  [body(): lax.ppermute(cot, 'dp', [(i, i ^ 1) for i in range(ndp)])]
    ppermute x0 -> x1, starting transfers between devices: none -> 3.12 us  [body(): lax.ppermute(cot, 'dp', [(i, i ^ 1) for i in range(ndp)])]
    unnamed x43 -> x12, local copies, waits for them, and re-layouts: 4.21 us -> 1.17 us
  transfers between devices with their start and end apart: 24 -> 17, of which waited for: 8 -> 8; matrix products, arithmetic and copies ran while one was open for 1% -> 2% of each run, Pallas kernels for 3% -> 3%
where the time goes in v7:
time: 302 us; the launch traced here: 300 us
  starting transfers between devices  125 us (41%)
  waiting for transfers between devices  97.6 us (32%)
  blocking collectives  51.2 us (17%)
  Pallas kernels  20.1 us (7%)
  local copies, waits for them, and re-layouts  4.52 us (1%)
    all_to_all x1, blocking collectives, body(): lax.all_to_all(last, 'seq', split_axis=0, concat_axis=0, tiled=True, axis...  51.2 us
    all_to_all x1, waiting for transfers between devices, body(): lax.all_to_all(sent, 'seq', split_axis=0, concat_axis=0, tiled=True, axis...  36.3 us
    ppermute x6, starting transfers between devices, swap(): return lax.ppermute(x, 'seq', [(i, i ^ bit) for i in range(nseq)])  35 us
    all_to_all x1, starting transfers between devices, body(): lax.all_to_all(sent, 'seq', split_axis=0, concat_axis=0, tiled=True, axis...  29.2 us
    ppermute x7, starting transfers between devices, body(): lax.ppermute(cot, 'dp', [(i, i ^ t) for i in range(ndp)])  28 us
    all_to_all x1, starting transfers between devices, body(): lax.all_to_all(sent_att, ('dp', 'seq'), split_axis=0, concat_axis=0, tile...  26 us
    all_to_all x1, waiting for transfers between devices, body(): lax.all_to_all(sent_att, ('dp', 'seq'), split_axis=0, concat_axis=0, tile...  25.5 us
    ppermute x7, waiting for transfers between devices, body(): lax.ppermute(cot, 'dp', [(i, i ^ t) for i in range(ndp)])  19.3 us
  transfers between devices with their start and end apart: 17, of which 8 were waited for; matrix products, arithmetic and copies ran while one was open for 2% of the time, Pallas kernels for 3%

profile of v7, /device:TPU:1, one launch (start us, length us, event | category | flops | bytes accessed | tf_op | source)
XLA Modules:
  0.0 300.4 jit_solution(11001022199380405032)
XLA Ops:
  0.6 3.4 %pack.1 = bf16[16,256,128]{2,1,0:T(8,128)(2,1)} custom-call(bf16[128,1024]{1,0:T(8,128)(2,1)} %bitcast.22, bf16[128,1024]{1,0:T(8,128)(2,1)} %bitcast.23, bf16[128,1024]{1,0:T(8,128)(2,1)} %bitcast.24, bf16[128,1024]{1,0:T(8,128)(2,1)} %bitcast.19, bf16[1024,1024]{1,0:T(8,128)(2,1)} %w_ref.3), custom_call_target="tpu_custom_call" | custom-call | flops 268435456 | bytes 3407872 | tf_op jit(solution)/shard_map/pack/pallas_call | solution.py:47
  4.1 29.2 %all-to-all-start = ((bf16[16,256,128]{2,1,0:T(8,128)(2,1)}), bf16[16,256,128]{2,1,0:T(8,128)(2,1)}, u32[]{:S(2)}, u32[]{:S(2)}) async-start(bf16[16,256,128]{2,1,0:T(8,128)(2,1)} %pack.1), calls=%async_computation | async-start | bytes 2097152 | tf_op jit(solution)/shard_map/all_to_all | solution.py:345
  33.3 3.1 %collective-permute-start = (bf16[128,1024]{1,0:T(8,128)(2,1)S(1)}, bf16[128,1024]{1,0:T(8,128)(2,1)S(1)}, u32[]{:S(2)}, u32[]{:S(2)}) collective-permute-start(bf16[128,1024]{1,0:T(8,128)(2,1)S(1)} %bitcast.20), channel_id=1, source_target_pairs={{0,64},{64,0},{128,192},{192,128},{256,320},{320,256},{384,448},{4... | collective-permute-start | bytes 786440 | tf_op jit(solution)/shard_map/ppermute | solution.py:343
  36.4 5.6 %collective-permute-done = bf16[128,1024]{1,0:T(8,128)(2,1)S(1)} collective-permute-done((bf16[128,1024]{1,0:T(8,128)(2,1)S(1)}, bf16[128,1024]{1,0:T(8,128)(2,1)S(1)}, u32[]{:S(2)}, u32[]{:S(2)}) %collective-permute-start) | collective-permute-done | bytes 262176 | tf_op jit(solution)/shard_map/ppermute | solution.py:343
  42.1 7.1 %collective-permute-start.7 = (bf16[256,1024]{1,0:T(8,128)(2,1)S(1)}, bf16[256,1024]{1,0:T(8,128)(2,1)S(1)}, u32[]{:S(2)}, u32[]{:S(2)}) collective-permute-start(bf16[256,1024]{1,0:T(8,128)(2,1)S(1)} %constant_dynamic-update-slice_fusion.refs_0_), channel_id=1, source_target_pairs={{0,896},{64,960},{128,768},{192,832},{256,640},{320,704},{384,512}... | collective-permute-start | bytes 1572872 | tf_op jit(solution)/shard_map/ppermute | solution.py:344
  51.1 3.5 %collective-permute-start.5 = (bf16[256,1024]{1,0:T(8,128)(2,1)S(1)}, bf16[256,1024]{1,0:T(8,128)(2,1)S(1)}, u32[]{:S(2)}, u32[]{:S(2)}) collective-permute-start(bf16[256,1024]{1,0:T(8,128)(2,1)S(1)} %constant_dynamic-update-slice_fusion.refs_0_), channel_id=1, source_target_pairs={{0,640},{64,704},{128,512},{192,576},{256,896},{320,960},{384,768}... | collective-permute-start | bytes 1572872 | tf_op jit(solution)/shard_map/ppermute | solution.py:344
  54.6 3.3 %collective-permute-start.4 = (bf16[256,1024]{1,0:T(8,128)(2,1)S(1)}, bf16[256,1024]{1,0:T(8,128)(2,1)S(1)}, u32[]{:S(2)}, u32[]{:S(2)}) collective-permute-start(bf16[256,1024]{1,0:T(8,128)(2,1)S(1)} %constant_dynamic-update-slice_fusion.refs_0_), channel_id=1, source_target_pairs={{0,512},{64,576},{128,640},{192,704},{256,768},{320,832},{384,896}... | collective-permute-start | bytes 1572872 | tf_op jit(solution)/shard_map/ppermute | solution.py:344
  57.9 4.6 %collective-permute-start.3 = (bf16[256,1024]{1,0:T(8,128)(2,1)S(1)}, bf16[256,1024]{1,0:T(8,128)(2,1)S(1)}, u32[]{:S(2)}, u32[]{:S(2)}) collective-permute-start(bf16[256,1024]{1,0:T(8,128)(2,1)S(1)} %constant_dynamic-update-slice_fusion.refs_0_), channel_id=1, source_target_pairs={{0,384},{64,448},{128,256},{192,320},{256,128},{320,192},{384,0},{... | collective-permute-start | bytes 1572872 | tf_op jit(solution)/shard_map/ppermute | solution.py:344
  62.5 3.1 %collective-permute-start.2 = (bf16[256,1024]{1,0:T(8,128)(2,1)S(1)}, bf16[256,1024]{1,0:T(8,128)(2,1)}, u32[]{:S(2)}, u32[]{:S(2)}) collective-permute-start(bf16[256,1024]{1,0:T(8,128)(2,1)S(1)} %constant_dynamic-update-slice_fusion.refs_0_), channel_id=1, source_target_pairs={{0,256},{64,320},{128,384},{192,448},{256,0},{320,64},{384,128},{4... | collective-permute-start | bytes 1572872 | tf_op jit(solution)/shard_map/ppermute | solution.py:344
  65.6 19.3 %collective-permute-done.6.refs_6_ = bf16[256,1024]{1,0:T(8,128)(2,1)S(1)} collective-permute-done((bf16[256,1024]{1,0:T(8,128)(2,1)S(1)}, bf16[256,1024]{1,0:T(8,128)(2,1)S(1)}, u32[]{:S(2)}, u32[]{:S(2)}) %collective-permute-start.6) | collective-permute-done | bytes 524320 | tf_op jit(solution)/shard_map/ppermute | solution.py:344
  84.9 4.5 %collective-permute-start.1 = (bf16[256,1024]{1,0:T(8,128)(2,1)S(1)}, bf16[256,1024]{1,0:T(8,128)(2,1)}, u32[]{:S(2)}, u32[]{:S(2)}) collective-permute-start(bf16[256,1024]{1,0:T(8,128)(2,1)S(1)} %constant_dynamic-update-slice_fusion.refs_0_), channel_id=1, source_target_pairs={{0,128},{64,192},{128,0},{192,64},{256,384},{320,448},{384,256},{4... | collective-permute-start | bytes 1572872 | tf_op jit(solution)/shard_map/ppermute | solution.py:344
  89.4 36.3 %all-to-all-done.q_ref.g_ref = bf16[16,256,128]{2,1,0:T(8,128)(2,1)} async-done(((bf16[16,256,128]{2,1,0:T(8,128)(2,1)}), bf16[16,256,128]{2,1,0:T(8,128)(2,1)}, u32[]{:S(2)}, u32[]{:S(2)}) %all-to-all-start) | async-done | bytes 1048608 | tf_op jit(solution)/shard_map/all_to_all | solution.py:345
  127.7 6.8 %collective-permute-start.9 = (bf16[16,128,128]{2,1,0:T(8,128)(2,1)}, bf16[16,128,128]{2,1,0:T(8,128)(2,1)}, u32[]{:S(2)}, u32[]{:S(2)}) collective-permute-start(bf16[16,128,128]{2,1,0:T(8,128)(2,1)} %slice.16.kv0), channel_id=1, source_target_pairs={{0,2},{1,3},{2,0},{3,1},{4,6},{5,7},{6,4},{7,5},{8,10},{9,11},{10,... | collective-permute-start | bytes 1572872 | tf_op jit(solution)/shard_map/ppermute | solution.py:333
  134.5 8.5 %collective-permute-start.8 = (bf16[16,128,128]{2,1,0:T(8,128)(2,1)}, bf16[16,128,128]{2,1,0:T(8,128)(2,1)}, u32[]{:S(2)}, u32[]{:S(2)}) collective-permute-start(bf16[16,128,128]{2,1,0:T(8,128)(2,1)} %slice.16.kv0), channel_id=1, source_target_pairs={{0,1},{1,0},{2,3},{3,2},{4,5},{5,4},{6,7},{7,6},{8,9},{9,8},{10,11... | collective-permute-start | bytes 1572872 | tf_op jit(solution)/shard_map/ppermute | solution.py:333
  143.0 7.4 %collective-permute-start.10 = (bf16[16,128,128]{2,1,0:T(8,128)(2,1)}, bf16[16,128,128]{2,1,0:T(8,128)(2,1)}, u32[]{:S(2)}, u32[]{:S(2)}) collective-permute-start(bf16[16,128,128]{2,1,0:T(8,128)(2,1)} %collective-permute-done.9.kv2), channel_id=1, source_target_pairs={{0,1},{1,0},{2,3},{3,2},{4,5},{5,4},{6,7},{7,6},{8,9},{9,8},{10,11... | collective-permute-start | bytes 1572872 | tf_op jit(solution)/shard_map/ppermute | solution.py:333
  152.2 6.5 %attend.1 = (bf16[16,64,128]{2,1,0:T(8,128)(2,1)}, bf16[16,4,128,128]{3,2,1,0:T(8,128)(2,1)}) custom-call(s32[1]{0:T(128)} %bitcast.site_ref, s32[256]{0:T(256)} %reshape_squeeze.3.blk_ref, s32[64]{0:T(128)} %bitcast.27, bf16[16,256,128]{2,1,0:T(8,128)(2,1)} %all-to-all-done.q_ref.g_ref, bf16[16,128,128]{2,1,0:T(8,128)(2,1)} %slice.16.kv0, ...), custom_call_target="tpu_custom_call" | custom-call | flops 268435456 | bytes 5242880 | tf_op jit(solution)/shard_map/attend/pallas_call | solution.py:120
  158.7 26.0 %all-to-all-start.1 = ((bf16[256,4,128]{2,1,0:T(4,128)(2,1)}), bf16[256,4,128]{2,1,0:T(4,128)(2,1)S(1)}, u32[]{:S(2)}, u32[]{:S(2)}) async-start(bf16[256,4,128]{2,1,0:T(4,128)(2,1)} %bitcast.25), calls=%async_computation.1 | async-start | bytes 524288 | tf_op jit(solution)/shard_map/all_to_all | solution.py:351
  184.8 4.9 %value_contrib.1 = (bf16[2,32,32,128]{3,2,1,0:T(8,128)(2,1)}, bf16[2,32,32,128]{3,2,1,0:T(8,128)(2,1)}) custom-call(s32[1]{0:T(128)} %bitcast.site_ref, s32[256]{0:T(256)} %reshape_squeeze.3.blk_ref, bf16[16,256,128]{2,1,0:T(8,128)(2,1)} %all-to-all-done.q_ref.g_ref, bf16[16,4,128,128]{3,2,1,0:T(8,128)(2,1)} %get-tuple-element.26.prob_ref), custom_call_target="tpu_custom_call" | custom-call | flops 134217728 | bytes 3145728 | tf_op jit(solution)/shard_map/value_contrib/pallas_call | solution.py:181
  189.7 2.6 collective-permute-start.11
  198.1 25.5 %all-to-all-done.1 = bf16[256,4,128]{2,1,0:T(4,128)(2,1)S(1)} async-done(((bf16[256,4,128]{2,1,0:T(4,128)(2,1)}), bf16[256,4,128]{2,1,0:T(4,128)(2,1)S(1)}, u32[]{:S(2)}, u32[]{:S(2)}) %all-to-all-start.1) | async-done | bytes 262176 | tf_op jit(solution)/shard_map/all_to_all | solution.py:351
  226.9 7.6 %collective-permute-start.13 = (f32[32,8,128]{2,1,0:T(8,128)S(1)}, f32[32,8,128]{2,1,0:T(8,128)S(1)}, u32[]{:S(2)}, u32[]{:S(2)}) collective-permute-start(f32[32,8,128]{2,1,0:T(8,128)S(1)} %get-tuple-element.40), channel_id=1, source_target_pairs={{0,1},{1,0},{2,3},{3,2},{4,5},{5,4},{6,7},{7,6},{8,9},{9,8},{10,11... | collective-permute-start | bytes 393224 | tf_op jit(solution)/shard_map/ppermute | solution.py:333
  235.6 51.2 %all_to_all.20.back_ref = bf16[32,40,128]{2,1,0:T(8,128)(2,1)S(1)} all-to-all(bf16[32,40,128]{2,1,0:T(8,128)(2,1)S(1)} %merge.1), channel_id=1, replica_groups={{0,2,4,6,8,10,12,14,16,18,20,22,24,26,28,30,32,34,36,38,40,42,44,46,48,..., dimensions={0} | all-to-all | bytes 655360 | tf_op jit(solution)/shard_map/all_to_all | solution.py:359
  287.6 3.5 %all-to-all-start.3 = ((bf16[16,80,128]{2,1,0:T(8,128)(2,1)}), bf16[16,80,128]{2,1,0:T(8,128)(2,1)S(1)}, u32[]{:S(2)}, u32[]{:S(2)}) async-start(bf16[16,80,128]{2,1,0:T(8,128)(2,1)} %gather_send.1), calls=%async_computation.3 | async-start | bytes 655360 | tf_op jit(solution)/shard_map/all_to_all | solution.py:360
  292.0 7.1 %all-to-all-done.3.got_ref = bf16[16,80,128]{2,1,0:T(8,128)(2,1)S(1)} async-done(((bf16[16,80,128]{2,1,0:T(8,128)(2,1)}), bf16[16,80,128]{2,1,0:T(8,128)(2,1)S(1)}, u32[]{:S(2)}, u32[]{:S(2)}) %all-to-all-start.3) | async-done | bytes 327712 | tf_op jit(solution)/shard_map/all_to_all | solution.py:360
  (37 shorter events, 18.8 us)
Async XLA Ops:
  0.6 32.6 %copy-start.3 = (bf16[1,128,1024]{2,1,0:T(8,128)(2,1)S(1)}, bf16[1,128,1024]{2,1,0:T(8,128)(2,1)}, u32[]{:S(2)}) copy-start(bf16[1,128,1024]{2,1,0:T(8,128)(2,1)} %param.10) | copy-start | bytes 786436
  4.1 146.3 %copy-start.4 = (s32[1,64,4]{1,2,0:T(4,128)S(1)}, s32[1,64,4]{1,2,0:T(4,128)}, u32[]{:S(2)}) copy-start(s32[1,64,4]{1,2,0:T(4,128)} %param.12) | copy-start | bytes 3076
  4.1 121.7 %all-to-all-start = ((bf16[16,256,128]{2,1,0:T(8,128)(2,1)}), bf16[16,256,128]{2,1,0:T(8,128)(2,1)}, u32[]{:S(2)}, u32[]{:S(2)}) async-start(bf16[16,256,128]{2,1,0:T(8,128)(2,1)} %pack.1), calls=%async_computation | async-start | bytes 2097152 | tf_op jit(solution)/shard_map/all_to_all | solution.py:345
  33.3 8.8 %collective-permute-start = (bf16[128,1024]{1,0:T(8,128)(2,1)S(1)}, bf16[128,1024]{1,0:T(8,128)(2,1)S(1)}, u32[]{:S(2)}, u32[]{:S(2)}) collective-permute-start(bf16[128,1024]{1,0:T(8,128)(2,1)S(1)} %bitcast.20), channel_id=1, source_target_pairs={{0,64},{64,0},{128,192},{192,128},{256,320},{320,256},{384,448},{4... | collective-permute-start | bytes 786440 | tf_op jit(solution)/shard_map/ppermute | solution.py:343
  42.1 20.4 %collective-permute-start.7 = (bf16[256,1024]{1,0:T(8,128)(2,1)S(1)}, bf16[256,1024]{1,0:T(8,128)(2,1)S(1)}, u32[]{:S(2)}, u32[]{:S(2)}) collective-permute-start(bf16[256,1024]{1,0:T(8,128)(2,1)S(1)} %constant_dynamic-update-slice_fusion.refs_0_), channel_id=1, source_target_pairs={{0,896},{64,960},{128,768},{192,832},{256,640},{320,704},{384,512}... | collective-permute-start | bytes 1572872 | tf_op jit(solution)/shard_map/ppermute | solution.py:344
  49.2 35.7 %collective-permute-start.6 = (bf16[256,1024]{1,0:T(8,128)(2,1)S(1)}, bf16[256,1024]{1,0:T(8,128)(2,1)S(1)}, u32[]{:S(2)}, u32[]{:S(2)}) collective-permute-start(bf16[256,1024]{1,0:T(8,128)(2,1)S(1)} %constant_dynamic-update-slice_fusion.refs_0_), channel_id=1, source_target_pairs={{0,768},{64,832},{128,896},{192,960},{256,512},{320,576},{384,640}... | collective-permute-start | bytes 1572872 | tf_op jit(solution)/shard_map/ppermute | solution.py:344
  51.1 76.6 %collective-permute-start.5 = (bf16[256,1024]{1,0:T(8,128)(2,1)S(1)}, bf16[256,1024]{1,0:T(8,128)(2,1)S(1)}, u32[]{:S(2)}, u32[]{:S(2)}) collective-permute-start(bf16[256,1024]{1,0:T(8,128)(2,1)S(1)} %constant_dynamic-update-slice_fusion.refs_0_), channel_id=1, source_target_pairs={{0,640},{64,704},{128,512},{192,576},{256,896},{320,960},{384,768}... | collective-permute-start | bytes 1572872 | tf_op jit(solution)/shard_map/ppermute | solution.py:344
  54.6 73.1 %collective-permute-start.4 = (bf16[256,1024]{1,0:T(8,128)(2,1)S(1)}, bf16[256,1024]{1,0:T(8,128)(2,1)S(1)}, u32[]{:S(2)}, u32[]{:S(2)}) collective-permute-start(bf16[256,1024]{1,0:T(8,128)(2,1)S(1)} %constant_dynamic-update-slice_fusion.refs_0_), channel_id=1, source_target_pairs={{0,512},{64,576},{128,640},{192,704},{256,768},{320,832},{384,896}... | collective-permute-start | bytes 1572872 | tf_op jit(solution)/shard_map/ppermute | solution.py:344
  57.9 69.8 %collective-permute-start.3 = (bf16[256,1024]{1,0:T(8,128)(2,1)S(1)}, bf16[256,1024]{1,0:T(8,128)(2,1)S(1)}, u32[]{:S(2)}, u32[]{:S(2)}) collective-permute-start(bf16[256,1024]{1,0:T(8,128)(2,1)S(1)} %constant_dynamic-update-slice_fusion.refs_0_), channel_id=1, source_target_pairs={{0,384},{64,448},{128,256},{192,320},{256,128},{320,192},{384,0},{... | collective-permute-start | bytes 1572872 | tf_op jit(solution)/shard_map/ppermute | solution.py:344
  62.5 65.2 %collective-permute-start.2 = (bf16[256,1024]{1,0:T(8,128)(2,1)S(1)}, bf16[256,1024]{1,0:T(8,128)(2,1)}, u32[]{:S(2)}, u32[]{:S(2)}) collective-permute-start(bf16[256,1024]{1,0:T(8,128)(2,1)S(1)} %constant_dynamic-update-slice_fusion.refs_0_), channel_id=1, source_target_pairs={{0,256},{64,320},{128,384},{192,448},{256,0},{320,64},{384,128},{4... | collective-permute-start | bytes 1572872 | tf_op jit(solution)/shard_map/ppermute | solution.py:344
  84.9 42.8 %collective-permute-start.1 = (bf16[256,1024]{1,0:T(8,128)(2,1)S(1)}, bf16[256,1024]{1,0:T(8,128)(2,1)}, u32[]{:S(2)}, u32[]{:S(2)}) collective-permute-start(bf16[256,1024]{1,0:T(8,128)(2,1)S(1)} %constant_dynamic-update-slice_fusion.refs_0_), channel_id=1, source_target_pairs={{0,128},{64,192},{128,0},{192,64},{256,384},{320,448},{384,256},{4... | collective-permute-start | bytes 1572872 | tf_op jit(solution)/shard_map/ppermute | solution.py:344
  127.7 31.1 %copy-start.1 = (bf16[256,1024]{1,0:T(8,128)(2,1)}, bf16[256,1024]{1,0:T(8,128)(2,1)S(1)}, u32[]{:S(2)}) copy-start(bf16[256,1024]{1,0:T(8,128)(2,1)S(1)} %collective-permute-done.3.refs_3_) | copy-start | bytes 1572868
  127.7 15.2 %collective-permute-start.9 = (bf16[16,128,128]{2,1,0:T(8,128)(2,1)}, bf16[16,128,128]{2,1,0:T(8,128)(2,1)}, u32[]{:S(2)}, u32[]{:S(2)}) collective-permute-start(bf16[16,128,128]{2,1,0:T(8,128)(2,1)} %slice.16.kv0), channel_id=1, source_target_pairs={{0,2},{1,3},{2,0},{3,1},{4,6},{5,7},{6,4},{7,5},{8,10},{9,11},{10,... | collective-permute-start | bytes 1572872 | tf_op jit(solution)/shard_map/ppermute | solution.py:333
  134.5 16.7 %collective-permute-start.8 = (bf16[16,128,128]{2,1,0:T(8,128)(2,1)}, bf16[16,128,128]{2,1,0:T(8,128)(2,1)}, u32[]{:S(2)}, u32[]{:S(2)}) collective-permute-start(bf16[16,128,128]{2,1,0:T(8,128)(2,1)} %slice.16.kv0), channel_id=1, source_target_pairs={{0,1},{1,0},{2,3},{3,2},{4,5},{5,4},{6,7},{7,6},{8,9},{9,8},{10,11... | collective-permute-start | bytes 1572872 | tf_op jit(solution)/shard_map/ppermute | solution.py:333
  143.0 9.3 %collective-permute-start.10 = (bf16[16,128,128]{2,1,0:T(8,128)(2,1)}, bf16[16,128,128]{2,1,0:T(8,128)(2,1)}, u32[]{:S(2)}, u32[]{:S(2)}) collective-permute-start(bf16[16,128,128]{2,1,0:T(8,128)(2,1)} %collective-permute-done.9.kv2), channel_id=1, source_target_pairs={{0,1},{1,0},{2,3},{3,2},{4,5},{5,4},{6,7},{7,6},{8,9},{9,8},{10,11... | collective-permute-start | bytes 1572872 | tf_op jit(solution)/shard_map/ppermute | solution.py:333
  158.7 64.9 %all-to-all-start.1 = ((bf16[256,4,128]{2,1,0:T(4,128)(2,1)}), bf16[256,4,128]{2,1,0:T(4,128)(2,1)S(1)}, u32[]{:S(2)}, u32[]{:S(2)}) async-start(bf16[256,4,128]{2,1,0:T(4,128)(2,1)} %bitcast.25), calls=%async_computation.1 | async-start | bytes 524288 | tf_op jit(solution)/shard_map/all_to_all | solution.py:351
  189.7 4.3 %collective-permute-start.11 = (bf16[2,32,32,128]{3,2,1,0:T(8,128)(2,1)}, bf16[2,32,32,128]{3,2,1,0:T(8,128)(2,1)S(1)}, u32[]{:S(2)}, u32[]{:S(2)}) collective-permute-start(bf16[2,32,32,128]{3,2,1,0:T(8,128)(2,1)} %get-tuple-element.28), channel_id=1, source_target_pairs={{0,1},{1,0},{2,3},{3,2},{4,5},{5,4},{6,7},{7,6},{8,9},{9,8},{10,11... | collective-permute-start | bytes 1572872 | tf_op jit(solution)/shard_map/ppermute | solution.py:333
  195.9 38.7 %collective-permute-start.12 = (bf16[32,32,128]{2,1,0:T(8,128)(2,1)}, bf16[32,32,128]{2,1,0:T(8,128)(2,1)S(1)}, u32[]{:S(2)}, u32[]{:S(2)}) collective-permute-start(bf16[32,32,128]{2,1,0:T(8,128)(2,1)} %get-tuple-element.43), channel_id=1, source_target_pairs={{0,2},{1,3},{2,0},{3,1},{4,6},{5,7},{6,4},{7,5},{8,10},{9,11},{10,... | collective-permute-start | bytes 786440 | tf_op jit(solution)/shard_map/ppermute | solution.py:333
  223.7 1.0 copy-start.2
  226.9 8.6 %collective-permute-start.13 = (f32[32,8,128]{2,1,0:T(8,128)S(1)}, f32[32,8,128]{2,1,0:T(8,128)S(1)}, u32[]{:S(2)}, u32[]{:S(2)}) collective-permute-start(f32[32,8,128]{2,1,0:T(8,128)S(1)} %get-tuple-element.40), channel_id=1, source_target_pairs={{0,1},{1,0},{2,3},{3,2},{4,5},{5,4},{6,7},{7,6},{8,9},{9,8},{10,11... | collective-permute-start | bytes 393224 | tf_op jit(solution)/shard_map/ppermute | solution.py:333
  235.5 63.5 %copy-start = (bf16[1024,1024]{1,0:T(8,128)(2,1)S(1)}, bf16[1024,1024]{1,0:T(8,128)(2,1)}, u32[]{:S(2)}) copy-start(bf16[1024,1024]{1,0:T(8,128)(2,1)} %w_ref.3) | copy-start | bytes 6291460
  287.6 11.5 %all-to-all-start.3 = ((bf16[16,80,128]{2,1,0:T(8,128)(2,1)}), bf16[16,80,128]{2,1,0:T(8,128)(2,1)S(1)}, u32[]{:S(2)}, u32[]{:S(2)}) async-start(bf16[16,80,128]{2,1,0:T(8,128)(2,1)} %gather_send.1), calls=%async_computation.3 | async-start | bytes 655360 | tf_op jit(solution)/shard_map/all_to_all | solution.py:360

commit v8 on v7

--- a/solution.py
+++ b/solution.py
@@ -137,10 +137,10 @@
             ],
         ),
         out_shape=[
-            jax.ShapeDtypeStruct((split, n * HD // split, CSIZE), BF),
-            jax.ShapeDtypeStruct((n, MAXB, CSIZE, CSIZE), BF),
+            pltpu.HBM((split, n * HD // split, CSIZE), BF),
+            pltpu.HBM((n, MAXB, CSIZE, CSIZE), BF),
         ],
-        compiler_params=params(60),
+        compiler_params=params(24),
         cost_estimate=pl.CostEstimate(
             flops=n * 4 * MAXB * CSIZE * CSIZE * HD, bytes_accessed=5 << 20, transcendentals=n * MAXB * CSIZE * CSIZE
         ),
@@ -191,7 +191,7 @@
             scratch_shapes=[pltpu.VMEM((clusters, HD, CSIZE), F32)],
         ),
         out_shape=[jax.ShapeDtypeStruct((2, clusters // 2, HALF, CSIZE), BF)] * 2,
-        compiler_params=params(60),
+        compiler_params=params(24),
         cost_estimate=pl.CostEstimate(
             flops=n * 2 * MAXB * CSIZE * CSIZE * HD, bytes_accessed=3 << 20, transcendentals=0
         ),

time: 302 us -> 298 us (0.987)
  Pallas kernels: 20.1 us -> 16.9 us
  transfers between devices with their start and end apart: 17 -> 17, of which waited for: 8 -> 8; matrix products, arithmetic and copies ran while one was open for 2% -> 0% of each run, Pallas kernels for 3% -> 2%
where the time goes in v8:
time: 298 us; the launch traced here: 296 us
  starting transfers between devices  125 us (42%)
  waiting for transfers between devices  99.6 us (33%)
  blocking collectives  51.3 us (17%)
  Pallas kernels  16.9 us (6%)
    all_to_all x1, blocking collectives, body(): lax.all_to_all(last, 'seq', split_axis=0, concat_axis=0, tiled=True, axis...  51.3 us
    all_to_all x1, waiting for transfers between devices, body(): lax.all_to_all(sent, 'seq', split_axis=0, concat_axis=0, tiled=True, axis...  35.5 us
    ppermute x6, starting transfers between devices, swap(): return lax.ppermute(x, 'seq', [(i, i ^ bit) for i in range(nseq)])  35 us
    all_to_all x1, starting transfers between devices, body(): lax.all_to_all(sent, 'seq', split_axis=0, concat_axis=0, tiled=True, axis...  29.1 us
    all_to_all x1, waiting for transfers between devices, body(): lax.all_to_all(sent_att, ('dp', 'seq'), split_axis=0, concat_axis=0, tile...  28.1 us
    ppermute x7, starting transfers between devices, body(): lax.ppermute(cot, 'dp', [(i, i ^ t) for i in range(ndp)])  28 us
    all_to_all x1, starting transfers between devices, body(): lax.all_to_all(sent_att, ('dp', 'seq'), split_axis=0, concat_axis=0, tile...  26 us
    ppermute x7, waiting for transfers between devices, body(): lax.ppermute(cot, 'dp', [(i, i ^ t) for i in range(ndp)])  19.3 us
  transfers between devices with their start and end apart: 17, of which 8 were waited for; matrix products, arithmetic and copies ran while one was open for 0% of the time, Pallas kernels for 2%

profile of v8, /device:TPU:1, one launch (start us, length us, event | category | flops | bytes accessed | tf_op | source)
XLA Modules:
  0.0 296.5 jit_solution(553926826067471870)
XLA Ops:
  0.6 3.4 %pack.1 = bf16[16,256,128]{2,1,0:T(8,128)(2,1)} custom-call(bf16[128,1024]{1,0:T(8,128)(2,1)} %bitcast.23, bf16[128,1024]{1,0:T(8,128)(2,1)} %bitcast.24, bf16[128,1024]{1,0:T(8,128)(2,1)} %bitcast.25, bf16[128,1024]{1,0:T(8,128)(2,1)} %bitcast.20, bf16[1024,1024]{1,0:T(8,128)(2,1)} %w_ref.3), custom_call_target="tpu_custom_call" | custom-call | flops 268435456 | bytes 3407872 | tf_op jit(solution)/shard_map/pack/pallas_call | solution.py:47
  4.1 29.1 %all-to-all-start = ((bf16[16,256,128]{2,1,0:T(8,128)(2,1)}), bf16[16,256,128]{2,1,0:T(8,128)(2,1)S(1)}, u32[]{:S(2)}, u32[]{:S(2)}) async-start(bf16[16,256,128]{2,1,0:T(8,128)(2,1)} %pack.1), calls=%async_computation | async-start | bytes 2097152 | tf_op jit(solution)/shard_map/all_to_all | solution.py:345
  33.2 3.1 %collective-permute-start = (bf16[128,1024]{1,0:T(8,128)(2,1)S(1)}, bf16[128,1024]{1,0:T(8,128)(2,1)S(1)}, u32[]{:S(2)}, u32[]{:S(2)}) collective-permute-start(bf16[128,1024]{1,0:T(8,128)(2,1)S(1)} %bitcast.21), channel_id=1, source_target_pairs={{0,64},{64,0},{128,192},{192,128},{256,320},{320,256},{384,448},{4... | collective-permute-start | bytes 786440 | tf_op jit(solution)/shard_map/ppermute | solution.py:343
  36.4 5.6 %collective-permute-done = bf16[128,1024]{1,0:T(8,128)(2,1)S(1)} collective-permute-done((bf16[128,1024]{1,0:T(8,128)(2,1)S(1)}, bf16[128,1024]{1,0:T(8,128)(2,1)S(1)}, u32[]{:S(2)}, u32[]{:S(2)}) %collective-permute-start) | collective-permute-done | bytes 262176 | tf_op jit(solution)/shard_map/ppermute | solution.py:343
  42.0 7.1 %collective-permute-start.7 = (bf16[256,1024]{1,0:T(8,128)(2,1)S(1)}, bf16[256,1024]{1,0:T(8,128)(2,1)S(1)}, u32[]{:S(2)}, u32[]{:S(2)}) collective-permute-start(bf16[256,1024]{1,0:T(8,128)(2,1)S(1)} %constant_dynamic-update-slice_fusion.refs_0_), channel_id=1, source_target_pairs={{0,896},{64,960},{128,768},{192,832},{256,640},{320,704},{384,512}... | collective-permute-start | bytes 1572872 | tf_op jit(solution)/shard_map/ppermute | solution.py:344
  51.1 3.5 %collective-permute-start.5 = (bf16[256,1024]{1,0:T(8,128)(2,1)S(1)}, bf16[256,1024]{1,0:T(8,128)(2,1)S(1)}, u32[]{:S(2)}, u32[]{:S(2)}) collective-permute-start(bf16[256,1024]{1,0:T(8,128)(2,1)S(1)} %constant_dynamic-update-slice_fusion.refs_0_), channel_id=1, source_target_pairs={{0,640},{64,704},{128,512},{192,576},{256,896},{320,960},{384,768}... | collective-permute-start | bytes 1572872 | tf_op jit(solution)/shard_map/ppermute | solution.py:344
  54.6 3.3 %collective-permute-start.4 = (bf16[256,1024]{1,0:T(8,128)(2,1)S(1)}, bf16[256,1024]{1,0:T(8,128)(2,1)}, u32[]{:S(2)}, u32[]{:S(2)}) collective-permute-start(bf16[256,1024]{1,0:T(8,128)(2,1)S(1)} %constant_dynamic-update-slice_fusion.refs_0_), channel_id=1, source_target_pairs={{0,512},{64,576},{128,640},{192,704},{256,768},{320,832},{384,896}... | collective-permute-start | bytes 1572872 | tf_op jit(solution)/shard_map/ppermute | solution.py:344
  57.9 4.6 %collective-permute-start.3 = (bf16[256,1024]{1,0:T(8,128)(2,1)S(1)}, bf16[256,1024]{1,0:T(8,128)(2,1)}, u32[]{:S(2)}, u32[]{:S(2)}) collective-permute-start(bf16[256,1024]{1,0:T(8,128)(2,1)S(1)} %constant_dynamic-update-slice_fusion.refs_0_), channel_id=1, source_target_pairs={{0,384},{64,448},{128,256},{192,320},{256,128},{320,192},{384,0},{... | collective-permute-start | bytes 1572872 | tf_op jit(solution)/shard_map/ppermute | solution.py:344
  62.5 3.1 %collective-permute-start.2 = (bf16[256,1024]{1,0:T(8,128)(2,1)S(1)}, bf16[256,1024]{1,0:T(8,128)(2,1)}, u32[]{:S(2)}, u32[]{:S(2)}) collective-permute-start(bf16[256,1024]{1,0:T(8,128)(2,1)S(1)} %constant_dynamic-update-slice_fusion.refs_0_), channel_id=1, source_target_pairs={{0,256},{64,320},{128,384},{192,448},{256,0},{320,64},{384,128},{4... | collective-permute-start | bytes 1572872 | tf_op jit(solution)/shard_map/ppermute | solution.py:344
  65.6 19.3 %collective-permute-done.6.refs_6_ = bf16[256,1024]{1,0:T(8,128)(2,1)S(1)} collective-permute-done((bf16[256,1024]{1,0:T(8,128)(2,1)S(1)}, bf16[256,1024]{1,0:T(8,128)(2,1)S(1)}, u32[]{:S(2)}, u32[]{:S(2)}) %collective-permute-start.6) | collective-permute-done | bytes 524320 | tf_op jit(solution)/shard_map/ppermute | solution.py:344
  85.7 4.5 %collective-permute-start.1 = (bf16[256,1024]{1,0:T(8,128)(2,1)S(1)}, bf16[256,1024]{1,0:T(8,128)(2,1)}, u32[]{:S(2)}, u32[]{:S(2)}) collective-permute-start(bf16[256,1024]{1,0:T(8,128)(2,1)S(1)} %constant_dynamic-update-slice_fusion.refs_0_), channel_id=1, source_target_pairs={{0,128},{64,192},{128,0},{192,64},{256,384},{320,448},{384,256},{4... | collective-permute-start | bytes 1572872 | tf_op jit(solution)/shard_map/ppermute | solution.py:344
  90.2 35.5 %all-to-all-done.q_ref.g_ref = bf16[16,256,128]{2,1,0:T(8,128)(2,1)S(1)} async-done(((bf16[16,256,128]{2,1,0:T(8,128)(2,1)}), bf16[16,256,128]{2,1,0:T(8,128)(2,1)S(1)}, u32[]{:S(2)}, u32[]{:S(2)}) %all-to-all-start) | async-done | bytes 1048608 | tf_op jit(solution)/shard_map/all_to_all | solution.py:345
  125.8 6.8 %collective-permute-start.9 = (bf16[16,128,128]{2,1,0:T(8,128)(2,1)S(1)}, bf16[16,128,128]{2,1,0:T(8,128)(2,1)}, u32[]{:S(2)}, u32[]{:S(2)}) collective-permute-start(bf16[16,128,128]{2,1,0:T(8,128)(2,1)S(1)} %slice.16.kv0), channel_id=1, source_target_pairs={{0,2},{1,3},{2,0},{3,1},{4,6},{5,7},{6,4},{7,5},{8,10},{9,11},{10,... | collective-permute-start | bytes 1572872 | tf_op jit(solution)/shard_map/ppermute | solution.py:333
  132.6 8.5 %collective-permute-start.8 = (bf16[16,128,128]{2,1,0:T(8,128)(2,1)S(1)}, bf16[16,128,128]{2,1,0:T(8,128)(2,1)}, u32[]{:S(2)}, u32[]{:S(2)}) collective-permute-start(bf16[16,128,128]{2,1,0:T(8,128)(2,1)S(1)} %slice.16.kv0), channel_id=1, source_target_pairs={{0,1},{1,0},{2,3},{3,2},{4,5},{5,4},{6,7},{7,6},{8,9},{9,8},{10,11... | collective-permute-start | bytes 1572872 | tf_op jit(solution)/shard_map/ppermute | solution.py:333
  141.0 7.2 %collective-permute-start.10 = (bf16[16,128,128]{2,1,0:T(8,128)(2,1)}, bf16[16,128,128]{2,1,0:T(8,128)(2,1)}, u32[]{:S(2)}, u32[]{:S(2)}) collective-permute-start(bf16[16,128,128]{2,1,0:T(8,128)(2,1)} %collective-permute-done.9.kv2), channel_id=1, source_target_pairs={{0,1},{1,0},{2,3},{3,2},{4,5},{5,4},{6,7},{7,6},{8,9},{9,8},{10,11... | collective-permute-start | bytes 1572872 | tf_op jit(solution)/shard_map/ppermute | solution.py:333
  150.1 5.4 %attend.1 = (bf16[16,64,128]{2,1,0:T(8,128)(2,1)}, bf16[16,4,128,128]{3,2,1,0:T(8,128)(2,1)}) custom-call(s32[1]{0:T(128)} %bitcast.site_ref, s32[256]{0:T(256)S(1)} %reshape_squeeze.3.blk_ref, s32[64]{0:T(128)S(1)} %bitcast.19, bf16[16,256,128]{2,1,0:T(8,128)(2,1)S(1)} %all-to-all-done.q_ref.g_ref, bf16[16,128,128]{2,1,0:T(8,128)(2,1)S(1)} %slice.16.kv0, ...), custom_call_target="tpu_custom_call" | custom-call | flops 268435456 | bytes 5242880 | tf_op jit(solution)/shard_map/attend/pallas_call | solution.py:120
  155.5 26.0 %all-to-all-start.1 = ((bf16[256,4,128]{2,1,0:T(4,128)(2,1)}), bf16[256,4,128]{2,1,0:T(4,128)(2,1)S(1)}, u32[]{:S(2)}, u32[]{:S(2)}) async-start(bf16[256,4,128]{2,1,0:T(4,128)(2,1)} %bitcast.26), calls=%async_computation.1 | async-start | bytes 524288 | tf_op jit(solution)/shard_map/all_to_all | solution.py:351
  185.7 2.7 collective-permute-start.11
  192.3 28.1 %all-to-all-done.1 = bf16[256,4,128]{2,1,0:T(4,128)(2,1)S(1)} async-done(((bf16[256,4,128]{2,1,0:T(4,128)(2,1)}), bf16[256,4,128]{2,1,0:T(4,128)(2,1)S(1)}, u32[]{:S(2)}, u32[]{:S(2)}) %all-to-all-start.1) | async-done | bytes 262176 | tf_op jit(solution)/shard_map/all_to_all | solution.py:351
  220.4 2.5 weight_part.1
  223.0 7.6 %collective-permute-start.13 = (f32[32,8,128]{2,1,0:T(8,128)S(1)}, f32[32,8,128]{2,1,0:T(8,128)S(1)}, u32[]{:S(2)}, u32[]{:S(2)}) collective-permute-start(f32[32,8,128]{2,1,0:T(8,128)S(1)} %get-tuple-element.40), channel_id=1, source_target_pairs={{0,1},{1,0},{2,3},{3,2},{4,5},{5,4},{6,7},{7,6},{8,9},{9,8},{10,11... | collective-permute-start | bytes 393224 | tf_op jit(solution)/shard_map/ppermute | solution.py:333
  231.6 51.3 %all_to_all.20.back_ref = bf16[32,40,128]{2,1,0:T(8,128)(2,1)S(1)} all-to-all(bf16[32,40,128]{2,1,0:T(8,128)(2,1)S(1)} %merge.1), channel_id=1, replica_groups={{0,2,4,6,8,10,12,14,16,18,20,22,24,26,28,30,32,34,36,38,40,42,44,46,48,..., dimensions={0} | all-to-all | bytes 655360 | tf_op jit(solution)/shard_map/all_to_all | solution.py:359
  283.6 3.5 %all-to-all-start.3 = ((bf16[16,80,128]{2,1,0:T(8,128)(2,1)}), bf16[16,80,128]{2,1,0:T(8,128)(2,1)S(1)}, u32[]{:S(2)}, u32[]{:S(2)}) async-start(bf16[16,80,128]{2,1,0:T(8,128)(2,1)} %gather_send.1), calls=%async_computation.3 | async-start | bytes 655360 | tf_op jit(solution)/shard_map/all_to_all | solution.py:360
  288.0 7.1 %all-to-all-done.3.got_ref = bf16[16,80,128]{2,1,0:T(8,128)(2,1)S(1)} async-done(((bf16[16,80,128]{2,1,0:T(8,128)(2,1)}), bf16[16,80,128]{2,1,0:T(8,128)(2,1)S(1)}, u32[]{:S(2)}, u32[]{:S(2)}) %all-to-all-start.3) | async-done | bytes 327712 | tf_op jit(solution)/shard_map/all_to_all | solution.py:360
  (45 shorter events, 16.7 us)
Async XLA Ops:
  0.6 32.6 %copy-start.7 = (bf16[1,128,1024]{2,1,0:T(8,128)(2,1)S(1)}, bf16[1,128,1024]{2,1,0:T(8,128)(2,1)}, u32[]{:S(2)}) copy-start(bf16[1,128,1024]{2,1,0:T(8,128)(2,1)} %param.10) | copy-start | bytes 786436
  4.1 144.2 %copy-start.8 = (s32[1,64,4]{1,2,0:T(4,128)S(1)}, s32[1,64,4]{1,2,0:T(4,128)}, u32[]{:S(2)}) copy-start(s32[1,64,4]{1,2,0:T(4,128)} %param.12) | copy-start | bytes 3076
  4.1 146.0 %copy-start.6 = (s32[1,64]{1,0:T(1,128)S(1)}, s32[1,64]{1,0:T(1,128)}, u32[]{:S(2)}) copy-start(s32[1,64]{1,0:T(1,128)} %param.13) | copy-start | bytes 772
  4.1 121.6 %all-to-all-start = ((bf16[16,256,128]{2,1,0:T(8,128)(2,1)}), bf16[16,256,128]{2,1,0:T(8,128)(2,1)S(1)}, u32[]{:S(2)}, u32[]{:S(2)}) async-start(bf16[16,256,128]{2,1,0:T(8,128)(2,1)} %pack.1), calls=%async_computation | async-start | bytes 2097152 | tf_op jit(solution)/shard_map/all_to_all | solution.py:345
  33.2 8.8 %collective-permute-start = (bf16[128,1024]{1,0:T(8,128)(2,1)S(1)}, bf16[128,1024]{1,0:T(8,128)(2,1)S(1)}, u32[]{:S(2)}, u32[]{:S(2)}) collective-permute-start(bf16[128,1024]{1,0:T(8,128)(2,1)S(1)} %bitcast.21), channel_id=1, source_target_pairs={{0,64},{64,0},{128,192},{192,128},{256,320},{320,256},{384,448},{4... | collective-permute-start | bytes 786440 | tf_op jit(solution)/shard_map/ppermute | solution.py:343
  42.0 20.4 %collective-permute-start.7 = (bf16[256,1024]{1,0:T(8,128)(2,1)S(1)}, bf16[256,1024]{1,0:T(8,128)(2,1)S(1)}, u32[]{:S(2)}, u32[]{:S(2)}) collective-permute-start(bf16[256,1024]{1,0:T(8,128)(2,1)S(1)} %constant_dynamic-update-slice_fusion.refs_0_), channel_id=1, source_target_pairs={{0,896},{64,960},{128,768},{192,832},{256,640},{320,704},{384,512}... | collective-permute-start | bytes 1572872 | tf_op jit(solution)/shard_map/ppermute | solution.py:344
  49.1 35.7 %collective-permute-start.6 = (bf16[256,1024]{1,0:T(8,128)(2,1)S(1)}, bf16[256,1024]{1,0:T(8,128)(2,1)S(1)}, u32[]{:S(2)}, u32[]{:S(2)}) collective-permute-start(bf16[256,1024]{1,0:T(8,128)(2,1)S(1)} %constant_dynamic-update-slice_fusion.refs_0_), channel_id=1, source_target_pairs={{0,768},{64,832},{128,896},{192,960},{256,512},{320,576},{384,640}... | collective-permute-start | bytes 1572872 | tf_op jit(solution)/shard_map/ppermute | solution.py:344
  51.1 74.7 %collective-permute-start.5 = (bf16[256,1024]{1,0:T(8,128)(2,1)S(1)}, bf16[256,1024]{1,0:T(8,128)(2,1)S(1)}, u32[]{:S(2)}, u32[]{:S(2)}) collective-permute-start(bf16[256,1024]{1,0:T(8,128)(2,1)S(1)} %constant_dynamic-update-slice_fusion.refs_0_), channel_id=1, source_target_pairs={{0,640},{64,704},{128,512},{192,576},{256,896},{320,960},{384,768}... | collective-permute-start | bytes 1572872 | tf_op jit(solution)/shard_map/ppermute | solution.py:344
  54.6 71.2 %collective-permute-start.4 = (bf16[256,1024]{1,0:T(8,128)(2,1)S(1)}, bf16[256,1024]{1,0:T(8,128)(2,1)}, u32[]{:S(2)}, u32[]{:S(2)}) collective-permute-start(bf16[256,1024]{1,0:T(8,128)(2,1)S(1)} %constant_dynamic-update-slice_fusion.refs_0_), channel_id=1, source_target_pairs={{0,512},{64,576},{128,640},{192,704},{256,768},{320,832},{384,896}... | collective-permute-start | bytes 1572872 | tf_op jit(solution)/shard_map/ppermute | solution.py:344
  57.9 67.9 %collective-permute-start.3 = (bf16[256,1024]{1,0:T(8,128)(2,1)S(1)}, bf16[256,1024]{1,0:T(8,128)(2,1)}, u32[]{:S(2)}, u32[]{:S(2)}) collective-permute-start(bf16[256,1024]{1,0:T(8,128)(2,1)S(1)} %constant_dynamic-update-slice_fusion.refs_0_), channel_id=1, source_target_pairs={{0,384},{64,448},{128,256},{192,320},{256,128},{320,192},{384,0},{... | collective-permute-start | bytes 1572872 | tf_op jit(solution)/shard_map/ppermute | solution.py:344
  62.5 63.3 %collective-permute-start.2 = (bf16[256,1024]{1,0:T(8,128)(2,1)S(1)}, bf16[256,1024]{1,0:T(8,128)(2,1)}, u32[]{:S(2)}, u32[]{:S(2)}) collective-permute-start(bf16[256,1024]{1,0:T(8,128)(2,1)S(1)} %constant_dynamic-update-slice_fusion.refs_0_), channel_id=1, source_target_pairs={{0,256},{64,320},{128,384},{192,448},{256,0},{320,64},{384,128},{4... | collective-permute-start | bytes 1572872 | tf_op jit(solution)/shard_map/ppermute | solution.py:344
  85.7 40.1 %collective-permute-start.1 = (bf16[256,1024]{1,0:T(8,128)(2,1)S(1)}, bf16[256,1024]{1,0:T(8,128)(2,1)}, u32[]{:S(2)}, u32[]{:S(2)}) collective-permute-start(bf16[256,1024]{1,0:T(8,128)(2,1)S(1)} %constant_dynamic-update-slice_fusion.refs_0_), channel_id=1, source_target_pairs={{0,128},{64,192},{128,0},{192,64},{256,384},{320,448},{384,256},{4... | collective-permute-start | bytes 1572872 | tf_op jit(solution)/shard_map/ppermute | solution.py:344
  125.7 29.8 %copy-start.4 = (bf16[256,1024]{1,0:T(8,128)(2,1)}, bf16[256,1024]{1,0:T(8,128)(2,1)S(1)}, u32[]{:S(2)}) copy-start(bf16[256,1024]{1,0:T(8,128)(2,1)S(1)} %collective-permute-done.5.refs_5_) | copy-start | bytes 1572868
  125.8 15.2 %collective-permute-start.9 = (bf16[16,128,128]{2,1,0:T(8,128)(2,1)S(1)}, bf16[16,128,128]{2,1,0:T(8,128)(2,1)}, u32[]{:S(2)}, u32[]{:S(2)}) collective-permute-start(bf16[16,128,128]{2,1,0:T(8,128)(2,1)S(1)} %slice.16.kv0), channel_id=1, source_target_pairs={{0,2},{1,3},{2,0},{3,1},{4,6},{5,7},{6,4},{7,5},{8,10},{9,11},{10,... | collective-permute-start | bytes 1572872 | tf_op jit(solution)/shard_map/ppermute | solution.py:333
  132.6 15.9 %collective-permute-start.8 = (bf16[16,128,128]{2,1,0:T(8,128)(2,1)S(1)}, bf16[16,128,128]{2,1,0:T(8,128)(2,1)}, u32[]{:S(2)}, u32[]{:S(2)}) collective-permute-start(bf16[16,128,128]{2,1,0:T(8,128)(2,1)S(1)} %slice.16.kv0), channel_id=1, source_target_pairs={{0,1},{1,0},{2,3},{3,2},{4,5},{5,4},{6,7},{7,6},{8,9},{9,8},{10,11... | collective-permute-start | bytes 1572872 | tf_op jit(solution)/shard_map/ppermute | solution.py:333
  141.0 9.1 %collective-permute-start.10 = (bf16[16,128,128]{2,1,0:T(8,128)(2,1)}, bf16[16,128,128]{2,1,0:T(8,128)(2,1)}, u32[]{:S(2)}, u32[]{:S(2)}) collective-permute-start(bf16[16,128,128]{2,1,0:T(8,128)(2,1)} %collective-permute-done.9.kv2), channel_id=1, source_target_pairs={{0,1},{1,0},{2,3},{3,2},{4,5},{5,4},{6,7},{7,6},{8,9},{9,8},{10,11... | collective-permute-start | bytes 1572872 | tf_op jit(solution)/shard_map/ppermute | solution.py:333
  155.5 64.9 %all-to-all-start.1 = ((bf16[256,4,128]{2,1,0:T(4,128)(2,1)}), bf16[256,4,128]{2,1,0:T(4,128)(2,1)S(1)}, u32[]{:S(2)}, u32[]{:S(2)}) async-start(bf16[256,4,128]{2,1,0:T(4,128)(2,1)} %bitcast.26), calls=%async_computation.1 | async-start | bytes 524288 | tf_op jit(solution)/shard_map/all_to_all | solution.py:351
  185.7 34.8 %copy-start.3 = (bf16[256,1024]{1,0:T(8,128)(2,1)S(1)}, bf16[256,1024]{1,0:T(8,128)(2,1)}, u32[]{:S(2)}) copy-start(bf16[256,1024]{1,0:T(8,128)(2,1)} %copy-done.2) | copy-start | bytes 1572868
  185.7 34.7 %copy-start.5 = (bf16[256,1024]{1,0:T(8,128)(2,1)S(1)}, bf16[256,1024]{1,0:T(8,128)(2,1)}, u32[]{:S(2)}) copy-start(bf16[256,1024]{1,0:T(8,128)(2,1)} %copy-done.4) | copy-start | bytes 1572868
  185.7 4.2 %collective-permute-start.11 = (bf16[2,32,32,128]{3,2,1,0:T(8,128)(2,1)S(1)}, bf16[2,32,32,128]{3,2,1,0:T(8,128)(2,1)S(1)}, u32[]{:S(2)}, u32[]{:S(2)}) collective-permute-start(bf16[2,32,32,128]{3,2,1,0:T(8,128)(2,1)S(1)} %get-tuple-element.28), channel_id=1, source_target_pairs={{0,1},{1,0},{2,3},{3,2},{4,5},{5,4},{6,7},{7,6},{8,9},{9,8},{10,11... | collective-permute-start | bytes 1572872 | tf_op jit(solution)/shard_map/ppermute | solution.py:333
  190.1 40.5 %collective-permute-start.12 = (bf16[32,32,128]{2,1,0:T(8,128)(2,1)S(1)}, bf16[32,32,128]{2,1,0:T(8,128)(2,1)S(1)}, u32[]{:S(2)}, u32[]{:S(2)}) collective-permute-start(bf16[32,32,128]{2,1,0:T(8,128)(2,1)S(1)} %get-tuple-element.43), channel_id=1, source_target_pairs={{0,2},{1,3},{2,0},{3,1},{4,6},{5,7},{6,4},{7,5},{8,10},{9,11},{10,... | collective-permute-start | bytes 786440 | tf_op jit(solution)/shard_map/ppermute | solution.py:333
  223.0 8.6 %collective-permute-start.13 = (f32[32,8,128]{2,1,0:T(8,128)S(1)}, f32[32,8,128]{2,1,0:T(8,128)S(1)}, u32[]{:S(2)}, u32[]{:S(2)}) collective-permute-start(f32[32,8,128]{2,1,0:T(8,128)S(1)} %get-tuple-element.40), channel_id=1, source_target_pairs={{0,1},{1,0},{2,3},{3,2},{4,5},{5,4},{6,7},{7,6},{8,9},{9,8},{10,11... | collective-permute-start | bytes 393224 | tf_op jit(solution)/shard_map/ppermute | solution.py:333
  231.5 63.6 %copy-start = (bf16[1024,1024]{1,0:T(8,128)(2,1)S(1)}, bf16[1024,1024]{1,0:T(8,128)(2,1)}, u32[]{:S(2)}) copy-start(bf16[1024,1024]{1,0:T(8,128)(2,1)} %w_ref.3) | copy-start | bytes 6291460
  283.6 11.5 %all-to-all-start.3 = ((bf16[16,80,128]{2,1,0:T(8,128)(2,1)}), bf16[16,80,128]{2,1,0:T(8,128)(2,1)S(1)}, u32[]{:S(2)}, u32[]{:S(2)}) async-start(bf16[16,80,128]{2,1,0:T(8,128)(2,1)} %gather_send.1), calls=%async_computation.3 | async-start | bytes 655360 | tf_op jit(solution)/shard_map/all_to_all | solution.py:360
  (2 other events, 2.4 us)

commit v9 on v8

--- a/solution.py
+++ b/solution.py
@@ -65,12 +65,16 @@
     )(q, k, v, cot, w_out)
 
 
-def forward_kernel(site_ref, blk_ref, cnt_ref, q_ref, kv0, kv1, kv2, kv3, att_ref, prob_ref, kv_ref, wide_ref, sems):
+def forward_kernel(site_ref, blk_ref, cnt_ref, q_ref, *refs):
+    parts, (att_ref, prob_ref, kv_ref, wide_ref, sems) = refs[:-5], refs[-5:]
+    each = parts[0].shape[0]
+    pieces = len(parts) // SITE
+
     @pl.when(pl.program_id(0) == 0)
     def _():
         copies = [
-            pltpu.make_async_copy(part, kv_ref.at[t], sems.at[t])
-            for t, part in enumerate((kv0, kv1, kv2, kv3))
+            pltpu.make_async_copy(part, kv_ref.at[t // pieces, pl.ds(t % pieces * each, each)], sems.at[t])
+            for t, part in enumerate(parts)
         ]
         for copy in copies:
             copy.start()
@@ -116,6 +120,7 @@
 
 
 def forward(site, blk, cnt, recv, kvs, split):
+    parts = [part for member in kvs for part in member]
     n = recv.shape[0]
     return pl.pallas_call(
         forward_kernel,
@@ -125,15 +130,15 @@
             in_specs=[
                 pl.BlockSpec((ROWS, 64, CSIZE), lambda i, *_: (i, 2, 0)),
             ]
-            + [pl.BlockSpec(memory_space=pl.ANY)] * SITE,
+            + [pl.BlockSpec(memory_space=pl.ANY)] * len(parts),
             out_specs=[
                 pl.BlockSpec((split, ROWS * HD // split, CSIZE), lambda i, *_: (0, i, 0)),
                 pl.BlockSpec((ROWS, MAXB, CSIZE, CSIZE), lambda i, *_: (i, 0, 0, 0)),
             ],
             scratch_shapes=[
-                pltpu.VMEM((SITE,) + kvs[0].shape, BF),
+                pltpu.VMEM((SITE, n) + parts[0].shape[1:], BF),
                 pltpu.VMEM((ROWS * HD, CSIZE), F32),
-                pltpu.SemaphoreType.DMA((SITE,)),
+                pltpu.SemaphoreType.DMA((len(parts),)),
             ],
         ),
         out_shape=[
@@ -145,7 +150,7 @@
             flops=n * 4 * MAXB * CSIZE * CSIZE * HD, bytes_accessed=5 << 20, transcendentals=n * MAXB * CSIZE * CSIZE
         ),
         name="attend",
-    )(site, blk, cnt, recv, *kvs)
+    )(site, blk, cnt, recv, *parts)
 
 
 def backward_kernel(site_ref, blk_ref, g_ref, prob_ref, keep_ref, swap_ref, acc_ref):
@@ -343,9 +348,10 @@
         cot = jnp.concatenate([cot, lax.ppermute(cot, "dp", [(i, i ^ 1) for i in range(ndp)])], axis=0)
         cots = [cot] + [lax.ppermute(cot, "dp", [(i, i ^ t) for i in range(ndp)]) for t in range(2, ndp, 2)]
     recv = lax.all_to_all(sent, "seq", split_axis=0, concat_axis=0, tiled=True, axis_index_groups=same_site)
-    kv, cots = lax.optimization_barrier((recv[:, :128], cots))
-    kv_z = swap(kv, 2)
-    kvs = [kv, swap(kv, 1), kv_z, swap(kv_z, 1)]
+    half = H // 2
+    kv, cots = lax.optimization_barrier(([recv[:half, :128], recv[half:, :128]], cots))
+    kv_z = [swap(x, 2) for x in kv]
+    kvs = [kv, [swap(x, 1) for x in kv], kv_z, [swap(x, 1) for x in kv_z]]
     att, probs = forward(site, blk, cnt, recv, kvs, ndp)
     sent_att = att.reshape(ndp * H, HD // ndp, CSIZE)
     pieces = lax.all_to_all(

time: 298 us -> 297 us (level)
    ppermute x6 -> x9, starting transfers between devices: 35 us -> 36.1 us  [swap(): return lax.ppermute(x, 'seq', [(i, i ^ bit) for i in range(nseq)])]
  transfers between devices with their start and end apart: 17 -> 20, of which waited for: 8 -> 8; matrix products, arithmetic and copies ran while one was open for 0% -> 0% of each run, Pallas kernels for 2% -> 2%
where the time goes in v9:
time: 297 us; the launch traced here: 296 us
  starting transfers between devices  125 us (42%)
  waiting for transfers between devices  98.8 us (33%)
  blocking collectives  51.2 us (17%)
  Pallas kernels  16.8 us (6%)
  local copies, waits for them, and re-layouts  3.45 us (1%)
    all_to_all x1, blocking collectives, body(): lax.all_to_all(last, 'seq', split_axis=0, concat_axis=0, tiled=True, axis...  51.2 us
    ppermute x9, starting transfers between devices, swap(): return lax.ppermute(x, 'seq', [(i, i ^ bit) for i in range(nseq)])  36.1 us
    all_to_all x1, waiting for transfers between devices, body(): lax.all_to_all(sent, 'seq', split_axis=0, concat_axis=0, tiled=True, axis...  35.5 us
    all_to_all x1, starting transfers between devices, body(): lax.all_to_all(sent, 'seq', split_axis=0, concat_axis=0, tiled=True, axis...  29.1 us
    ppermute x7, starting transfers between devices, body(): lax.ppermute(cot, 'dp', [(i, i ^ t) for i in range(ndp)])  28 us
    all_to_all x1, waiting for transfers between devices, body(): lax.all_to_all(sent_att, ('dp', 'seq'), split_axis=0, concat_axis=0, tile...  27.4 us
    all_to_all x1, starting transfers between devices, body(): lax.all_to_all(sent_att, ('dp', 'seq'), split_axis=0, concat_axis=0, tile...  24.7 us
    ppermute x7, waiting for transfers between devices, body(): lax.ppermute(cot, 'dp', [(i, i ^ t) for i in range(ndp)])  19.3 us
  transfers between devices with their start and end apart: 20, of which 8 were waited for; matrix products, arithmetic and copies ran while one was open for 0% of the time, Pallas kernels for 2%

profile of v9, /device:TPU:1, one launch (start us, length us, event | category | flops | bytes accessed | tf_op | source)
XLA Modules:
  0.0 296.0 jit_solution(18204441488895798841)
XLA Ops:
  0.6 3.4 %pack.1 = bf16[16,256,128]{2,1,0:T(8,128)(2,1)} custom-call(bf16[128,1024]{1,0:T(8,128)(2,1)} %bitcast.23, bf16[128,1024]{1,0:T(8,128)(2,1)} %bitcast.24, bf16[128,1024]{1,0:T(8,128)(2,1)} %bitcast.25, bf16[128,1024]{1,0:T(8,128)(2,1)} %bitcast.20, bf16[1024,1024]{1,0:T(8,128)(2,1)} %w_ref.3), custom_call_target="tpu_custom_call" | custom-call | flops 268435456 | bytes 3407872 | tf_op jit(solution)/shard_map/pack/pallas_call | solution.py:47
  4.1 29.1 %all-to-all-start = ((bf16[16,256,128]{2,1,0:T(8,128)(2,1)}), bf16[16,256,128]{2,1,0:T(8,128)(2,1)S(1)}, u32[]{:S(2)}, u32[]{:S(2)}) async-start(bf16[16,256,128]{2,1,0:T(8,128)(2,1)} %pack.1), calls=%async_computation | async-start | bytes 2097152 | tf_op jit(solution)/shard_map/all_to_all | solution.py:350
  33.2 3.1 %collective-permute-start = (bf16[128,1024]{1,0:T(8,128)(2,1)S(1)}, bf16[128,1024]{1,0:T(8,128)(2,1)S(1)}, u32[]{:S(2)}, u32[]{:S(2)}) collective-permute-start(bf16[128,1024]{1,0:T(8,128)(2,1)S(1)} %bitcast.21), channel_id=1, source_target_pairs={{0,64},{64,0},{128,192},{192,128},{256,320},{320,256},{384,448},{4... | collective-permute-start | bytes 786440 | tf_op jit(solution)/shard_map/ppermute | solution.py:348
  36.4 5.6 %collective-permute-done = bf16[128,1024]{1,0:T(8,128)(2,1)S(1)} collective-permute-done((bf16[128,1024]{1,0:T(8,128)(2,1)S(1)}, bf16[128,1024]{1,0:T(8,128)(2,1)S(1)}, u32[]{:S(2)}, u32[]{:S(2)}) %collective-permute-start) | collective-permute-done | bytes 262176 | tf_op jit(solution)/shard_map/ppermute | solution.py:348
  42.0 7.1 %collective-permute-start.7 = (bf16[256,1024]{1,0:T(8,128)(2,1)S(1)}, bf16[256,1024]{1,0:T(8,128)(2,1)S(1)}, u32[]{:S(2)}, u32[]{:S(2)}) collective-permute-start(bf16[256,1024]{1,0:T(8,128)(2,1)S(1)} %constant_dynamic-update-slice_fusion.refs_0_), channel_id=1, source_target_pairs={{0,896},{64,960},{128,768},{192,832},{256,640},{320,704},{384,512}... | collective-permute-start | bytes 1572872 | tf_op jit(solution)/shard_map/ppermute | solution.py:349
  51.1 3.5 %collective-permute-start.5 = (bf16[256,1024]{1,0:T(8,128)(2,1)S(1)}, bf16[256,1024]{1,0:T(8,128)(2,1)S(1)}, u32[]{:S(2)}, u32[]{:S(2)}) collective-permute-start(bf16[256,1024]{1,0:T(8,128)(2,1)S(1)} %constant_dynamic-update-slice_fusion.refs_0_), channel_id=1, source_target_pairs={{0,640},{64,704},{128,512},{192,576},{256,896},{320,960},{384,768}... | collective-permute-start | bytes 1572872 | tf_op jit(solution)/shard_map/ppermute | solution.py:349
  54.5 3.3 %collective-permute-start.4 = (bf16[256,1024]{1,0:T(8,128)(2,1)S(1)}, bf16[256,1024]{1,0:T(8,128)(2,1)}, u32[]{:S(2)}, u32[]{:S(2)}) collective-permute-start(bf16[256,1024]{1,0:T(8,128)(2,1)S(1)} %constant_dynamic-update-slice_fusion.refs_0_), channel_id=1, source_target_pairs={{0,512},{64,576},{128,640},{192,704},{256,768},{320,832},{384,896}... | collective-permute-start | bytes 1572872 | tf_op jit(solution)/shard_map/ppermute | solution.py:349
  57.9 4.6 %collective-permute-start.3 = (bf16[256,1024]{1,0:T(8,128)(2,1)S(1)}, bf16[256,1024]{1,0:T(8,128)(2,1)}, u32[]{:S(2)}, u32[]{:S(2)}) collective-permute-start(bf16[256,1024]{1,0:T(8,128)(2,1)S(1)} %constant_dynamic-update-slice_fusion.refs_0_), channel_id=1, source_target_pairs={{0,384},{64,448},{128,256},{192,320},{256,128},{320,192},{384,0},{... | collective-permute-start | bytes 1572872 | tf_op jit(solution)/shard_map/ppermute | solution.py:349
  62.5 3.1 %collective-permute-start.2 = (bf16[256,1024]{1,0:T(8,128)(2,1)S(1)}, bf16[256,1024]{1,0:T(8,128)(2,1)}, u32[]{:S(2)}, u32[]{:S(2)}) collective-permute-start(bf16[256,1024]{1,0:T(8,128)(2,1)S(1)} %constant_dynamic-update-slice_fusion.refs_0_), channel_id=1, source_target_pairs={{0,256},{64,320},{128,384},{192,448},{256,0},{320,64},{384,128},{4... | collective-permute-start | bytes 1572872 | tf_op jit(solution)/shard_map/ppermute | solution.py:349
  65.6 19.3 %collective-permute-done.6.refs_6_ = bf16[256,1024]{1,0:T(8,128)(2,1)S(1)} collective-permute-done((bf16[256,1024]{1,0:T(8,128)(2,1)S(1)}, bf16[256,1024]{1,0:T(8,128)(2,1)S(1)}, u32[]{:S(2)}, u32[]{:S(2)}) %collective-permute-start.6) | collective-permute-done | bytes 524320 | tf_op jit(solution)/shard_map/ppermute | solution.py:349
  85.7 4.5 %collective-permute-start.1 = (bf16[256,1024]{1,0:T(8,128)(2,1)S(1)}, bf16[256,1024]{1,0:T(8,128)(2,1)}, u32[]{:S(2)}, u32[]{:S(2)}) collective-permute-start(bf16[256,1024]{1,0:T(8,128)(2,1)S(1)} %constant_dynamic-update-slice_fusion.refs_0_), channel_id=1, source_target_pairs={{0,128},{64,192},{128,0},{192,64},{256,384},{320,448},{384,256},{4... | collective-permute-start | bytes 1572872 | tf_op jit(solution)/shard_map/ppermute | solution.py:349
  90.2 35.5 %all-to-all-done.q_ref.g_ref = bf16[16,256,128]{2,1,0:T(8,128)(2,1)S(1)} async-done(((bf16[16,256,128]{2,1,0:T(8,128)(2,1)}), bf16[16,256,128]{2,1,0:T(8,128)(2,1)S(1)}, u32[]{:S(2)}, u32[]{:S(2)}) %all-to-all-start) | async-done | bytes 1048608 | tf_op jit(solution)/shard_map/all_to_all | solution.py:350
  125.8 6.8 %collective-permute-start.10 = (bf16[8,128,128]{2,1,0:T(8,128)(2,1)S(1)}, bf16[8,128,128]{2,1,0:T(8,128)(2,1)S(1)}, u32[]{:S(2)}, u32[]{:S(2)}) collective-permute-start(bf16[8,128,128]{2,1,0:T(8,128)(2,1)S(1)} %get-tuple-element.26.refs_0_), channel_id=1, source_target_pairs={{0,2},{1,3},{2,0},{3,1},{4,6},{5,7},{6,4},{7,5},{8,10},{9,11},{10,... | collective-permute-start | bytes 786440 | tf_op jit(solution)/shard_map/ppermute | solution.py:338
  134.5 8.5 %collective-permute-start.8 = (bf16[8,128,128]{2,1,0:T(8,128)(2,1)S(1)}, bf16[8,128,128]{2,1,0:T(8,128)(2,1)}, u32[]{:S(2)}, u32[]{:S(2)}) collective-permute-start(bf16[8,128,128]{2,1,0:T(8,128)(2,1)S(1)} %get-tuple-element.26.refs_0_), channel_id=1, source_target_pairs={{0,1},{1,0},{2,3},{3,2},{4,5},{5,4},{6,7},{7,6},{8,9},{9,8},{10,11... | collective-permute-start | bytes 786440 | tf_op jit(solution)/shard_map/ppermute | solution.py:338
  151.1 5.3 %attend.1 = (bf16[16,64,128]{2,1,0:T(8,128)(2,1)}, bf16[16,4,128,128]{3,2,1,0:T(8,128)(2,1)}) custom-call(s32[1]{0:T(128)} %bitcast.site_ref, s32[256]{0:T(256)S(1)} %reshape_squeeze.3.blk_ref, s32[64]{0:T(128)S(1)} %bitcast.19, bf16[16,256,128]{2,1,0:T(8,128)(2,1)S(1)} %all-to-all-done.q_ref.g_ref, bf16[8,128,128]{2,1,0:T(8,128)(2,1)S(1)} %get-tuple-element.26.refs_0_, ...), custom_call_target="tpu_custom_call" | custom-call | flops 268435456 | bytes 5242880 | tf_op jit(solution)/shard_map/attend/pallas_call | solution.py:125
  156.4 24.7 %all-to-all-start.1 = ((bf16[256,4,128]{2,1,0:T(4,128)(2,1)}), bf16[256,4,128]{2,1,0:T(4,128)(2,1)S(1)}, u32[]{:S(2)}, u32[]{:S(2)}) async-start(bf16[256,4,128]{2,1,0:T(4,128)(2,1)} %bitcast.26), calls=%async_computation.1 | async-start | bytes 524288 | tf_op jit(solution)/shard_map/all_to_all | solution.py:357
  182.7 2.5 value_contrib.1
  185.2 2.7 collective-permute-start.14
  192.6 27.4 %all-to-all-done.1 = bf16[256,4,128]{2,1,0:T(4,128)(2,1)S(1)} async-done(((bf16[256,4,128]{2,1,0:T(4,128)(2,1)}), bf16[256,4,128]{2,1,0:T(4,128)(2,1)S(1)}, u32[]{:S(2)}, u32[]{:S(2)}) %all-to-all-start.1) | async-done | bytes 262176 | tf_op jit(solution)/shard_map/all_to_all | solution.py:357
  220.0 2.5 weight_part.1
  222.5 7.6 %collective-permute-start.16 = (f32[32,8,128]{2,1,0:T(8,128)S(1)}, f32[32,8,128]{2,1,0:T(8,128)S(1)}, u32[]{:S(2)}, u32[]{:S(2)}) collective-permute-start(f32[32,8,128]{2,1,0:T(8,128)S(1)} %get-tuple-element.42), channel_id=1, source_target_pairs={{0,1},{1,0},{2,3},{3,2},{4,5},{5,4},{6,7},{7,6},{8,9},{9,8},{10,11... | collective-permute-start | bytes 393224 | tf_op jit(solution)/shard_map/ppermute | solution.py:338
  231.2 51.2 %all_to_all.20.back_ref = bf16[32,40,128]{2,1,0:T(8,128)(2,1)S(1)} all-to-all(bf16[32,40,128]{2,1,0:T(8,128)(2,1)S(1)} %merge.1), channel_id=1, replica_groups={{0,2,4,6,8,10,12,14,16,18,20,22,24,26,28,30,32,34,36,38,40,42,44,46,48,..., dimensions={0} | all-to-all | bytes 655360 | tf_op jit(solution)/shard_map/all_to_all | solution.py:365
  283.2 3.5 %all-to-all-start.3 = ((bf16[16,80,128]{2,1,0:T(8,128)(2,1)}), bf16[16,80,128]{2,1,0:T(8,128)(2,1)S(1)}, u32[]{:S(2)}, u32[]{:S(2)}) async-start(bf16[16,80,128]{2,1,0:T(8,128)(2,1)} %gather_send.1), calls=%async_computation.3 | async-start | bytes 655360 | tf_op jit(solution)/shard_map/all_to_all | solution.py:366
  287.6 7.1 %all-to-all-done.3.got_ref = bf16[16,80,128]{2,1,0:T(8,128)(2,1)S(1)} async-done(((bf16[16,80,128]{2,1,0:T(8,128)(2,1)}), bf16[16,80,128]{2,1,0:T(8,128)(2,1)S(1)}, u32[]{:S(2)}, u32[]{:S(2)}) %all-to-all-start.3) | async-done | bytes 327712 | tf_op jit(solution)/shard_map/all_to_all | solution.py:366
  (51 shorter events, 23.0 us)
Async XLA Ops:
  4.1 145.3 %copy-start.8 = (s32[1,64,4]{1,2,0:T(4,128)S(1)}, s32[1,64,4]{1,2,0:T(4,128)}, u32[]{:S(2)}) copy-start(s32[1,64,4]{1,2,0:T(4,128)} %param.12) | copy-start | bytes 3076
  4.1 147.0 %copy-start.6 = (s32[1,64]{1,0:T(1,128)S(1)}, s32[1,64]{1,0:T(1,128)}, u32[]{:S(2)}) copy-start(s32[1,64]{1,0:T(1,128)} %param.13) | copy-start | bytes 772
  4.1 121.6 %all-to-all-start = ((bf16[16,256,128]{2,1,0:T(8,128)(2,1)}), bf16[16,256,128]{2,1,0:T(8,128)(2,1)S(1)}, u32[]{:S(2)}, u32[]{:S(2)}) async-start(bf16[16,256,128]{2,1,0:T(8,128)(2,1)} %pack.1), calls=%async_computation | async-start | bytes 2097152 | tf_op jit(solution)/shard_map/all_to_all | solution.py:350
  33.2 8.8 %collective-permute-start = (bf16[128,1024]{1,0:T(8,128)(2,1)S(1)}, bf16[128,1024]{1,0:T(8,128)(2,1)S(1)}, u32[]{:S(2)}, u32[]{:S(2)}) collective-permute-start(bf16[128,1024]{1,0:T(8,128)(2,1)S(1)} %bitcast.21), channel_id=1, source_target_pairs={{0,64},{64,0},{128,192},{192,128},{256,320},{320,256},{384,448},{4... | collective-permute-start | bytes 786440 | tf_op jit(solution)/shard_map/ppermute | solution.py:348
  42.0 20.4 %collective-permute-start.7 = (bf16[256,1024]{1,0:T(8,128)(2,1)S(1)}, bf16[256,1024]{1,0:T(8,128)(2,1)S(1)}, u32[]{:S(2)}, u32[]{:S(2)}) collective-permute-start(bf16[256,1024]{1,0:T(8,128)(2,1)S(1)} %constant_dynamic-update-slice_fusion.refs_0_), channel_id=1, source_target_pairs={{0,896},{64,960},{128,768},{192,832},{256,640},{320,704},{384,512}... | collective-permute-start | bytes 1572872 | tf_op jit(solution)/shard_map/ppermute | solution.py:349
  49.1 35.7 %collective-permute-start.6 = (bf16[256,1024]{1,0:T(8,128)(2,1)S(1)}, bf16[256,1024]{1,0:T(8,128)(2,1)S(1)}, u32[]{:S(2)}, u32[]{:S(2)}) collective-permute-start(bf16[256,1024]{1,0:T(8,128)(2,1)S(1)} %constant_dynamic-update-slice_fusion.refs_0_), channel_id=1, source_target_pairs={{0,768},{64,832},{128,896},{192,960},{256,512},{320,576},{384,640}... | collective-permute-start | bytes 1572872 | tf_op jit(solution)/shard_map/ppermute | solution.py:349
  51.1 74.7 %collective-permute-start.5 = (bf16[256,1024]{1,0:T(8,128)(2,1)S(1)}, bf16[256,1024]{1,0:T(8,128)(2,1)S(1)}, u32[]{:S(2)}, u32[]{:S(2)}) collective-permute-start(bf16[256,1024]{1,0:T(8,128)(2,1)S(1)} %constant_dynamic-update-slice_fusion.refs_0_), channel_id=1, source_target_pairs={{0,640},{64,704},{128,512},{192,576},{256,896},{320,960},{384,768}... | collective-permute-start | bytes 1572872 | tf_op jit(solution)/shard_map/ppermute | solution.py:349
  54.5 71.2 %collective-permute-start.4 = (bf16[256,1024]{1,0:T(8,128)(2,1)S(1)}, bf16[256,1024]{1,0:T(8,128)(2,1)}, u32[]{:S(2)}, u32[]{:S(2)}) collective-permute-start(bf16[256,1024]{1,0:T(8,128)(2,1)S(1)} %constant_dynamic-update-slice_fusion.refs_0_), channel_id=1, source_target_pairs={{0,512},{64,576},{128,640},{192,704},{256,768},{320,832},{384,896}... | collective-permute-start | bytes 1572872 | tf_op jit(solution)/shard_map/ppermute | solution.py:349
  57.9 67.9 %collective-permute-start.3 = (bf16[256,1024]{1,0:T(8,128)(2,1)S(1)}, bf16[256,1024]{1,0:T(8,128)(2,1)}, u32[]{:S(2)}, u32[]{:S(2)}) collective-permute-start(bf16[256,1024]{1,0:T(8,128)(2,1)S(1)} %constant_dynamic-update-slice_fusion.refs_0_), channel_id=1, source_target_pairs={{0,384},{64,448},{128,256},{192,320},{256,128},{320,192},{384,0},{... | collective-permute-start | bytes 1572872 | tf_op jit(solution)/shard_map/ppermute | solution.py:349
  62.5 63.3 %collective-permute-start.2 = (bf16[256,1024]{1,0:T(8,128)(2,1)S(1)}, bf16[256,1024]{1,0:T(8,128)(2,1)}, u32[]{:S(2)}, u32[]{:S(2)}) collective-permute-start(bf16[256,1024]{1,0:T(8,128)(2,1)S(1)} %constant_dynamic-update-slice_fusion.refs_0_), channel_id=1, source_target_pairs={{0,256},{64,320},{128,384},{192,448},{256,0},{320,64},{384,128},{4... | collective-permute-start | bytes 1572872 | tf_op jit(solution)/shard_map/ppermute | solution.py:349
  85.7 40.1 %collective-permute-start.1 = (bf16[256,1024]{1,0:T(8,128)(2,1)S(1)}, bf16[256,1024]{1,0:T(8,128)(2,1)}, u32[]{:S(2)}, u32[]{:S(2)}) collective-permute-start(bf16[256,1024]{1,0:T(8,128)(2,1)S(1)} %constant_dynamic-update-slice_fusion.refs_0_), channel_id=1, source_target_pairs={{0,128},{64,192},{128,0},{192,64},{256,384},{320,448},{384,256},{4... | collective-permute-start | bytes 1572872 | tf_op jit(solution)/shard_map/ppermute | solution.py:349
  125.8 19.1 %collective-permute-start.10 = (bf16[8,128,128]{2,1,0:T(8,128)(2,1)S(1)}, bf16[8,128,128]{2,1,0:T(8,128)(2,1)S(1)}, u32[]{:S(2)}, u32[]{:S(2)}) collective-permute-start(bf16[8,128,128]{2,1,0:T(8,128)(2,1)S(1)} %get-tuple-element.26.refs_0_), channel_id=1, source_target_pairs={{0,2},{1,3},{2,0},{3,1},{4,6},{5,7},{6,4},{7,5},{8,10},{9,11},{10,... | collective-permute-start | bytes 786440 | tf_op jit(solution)/shard_map/ppermute | solution.py:338
  132.6 14.8 %collective-permute-start.11 = (bf16[8,128,128]{2,1,0:T(8,128)(2,1)S(1)}, bf16[8,128,128]{2,1,0:T(8,128)(2,1)}, u32[]{:S(2)}, u32[]{:S(2)}) collective-permute-start(bf16[8,128,128]{2,1,0:T(8,128)(2,1)S(1)} %get-tuple-element.27.refs_1_), channel_id=1, source_target_pairs={{0,2},{1,3},{2,0},{3,1},{4,6},{5,7},{6,4},{7,5},{8,10},{9,11},{10,... | collective-permute-start | bytes 786440 | tf_op jit(solution)/shard_map/ppermute | solution.py:338
  134.5 15.1 %collective-permute-start.8 = (bf16[8,128,128]{2,1,0:T(8,128)(2,1)S(1)}, bf16[8,128,128]{2,1,0:T(8,128)(2,1)}, u32[]{:S(2)}, u32[]{:S(2)}) collective-permute-start(bf16[8,128,128]{2,1,0:T(8,128)(2,1)S(1)} %get-tuple-element.26.refs_0_), channel_id=1, source_target_pairs={{0,1},{1,0},{2,3},{3,2},{4,5},{5,4},{6,7},{7,6},{8,9},{9,8},{10,11... | collective-permute-start | bytes 786440 | tf_op jit(solution)/shard_map/ppermute | solution.py:338
  142.9 6.7 %collective-permute-start.9 = (bf16[8,128,128]{2,1,0:T(8,128)(2,1)S(1)}, bf16[8,128,128]{2,1,0:T(8,128)(2,1)}, u32[]{:S(2)}, u32[]{:S(2)}) collective-permute-start(bf16[8,128,128]{2,1,0:T(8,128)(2,1)S(1)} %get-tuple-element.27.refs_1_), channel_id=1, source_target_pairs={{0,1},{1,0},{2,3},{3,2},{4,5},{5,4},{6,7},{7,6},{8,9},{9,8},{10,11... | collective-permute-start | bytes 786440 | tf_op jit(solution)/shard_map/ppermute | solution.py:338
  144.9 4.7 %collective-permute-start.12 = (bf16[8,128,128]{2,1,0:T(8,128)(2,1)S(1)}, bf16[8,128,128]{2,1,0:T(8,128)(2,1)}, u32[]{:S(2)}, u32[]{:S(2)}) collective-permute-start(bf16[8,128,128]{2,1,0:T(8,128)(2,1)S(1)} %collective-permute-done.10.refs_4_), channel_id=1, source_target_pairs={{0,1},{1,0},{2,3},{3,2},{4,5},{5,4},{6,7},{7,6},{8,9},{9,8},{10,11... | collective-permute-start | bytes 786440 | tf_op jit(solution)/shard_map/ppermute | solution.py:338
  147.3 3.8 %collective-permute-start.13 = (bf16[8,128,128]{2,1,0:T(8,128)(2,1)}, bf16[8,128,128]{2,1,0:T(8,128)(2,1)}, u32[]{:S(2)}, u32[]{:S(2)}) collective-permute-start(bf16[8,128,128]{2,1,0:T(8,128)(2,1)} %collective-permute-done.11.refs_5_), channel_id=1, source_target_pairs={{0,1},{1,0},{2,3},{3,2},{4,5},{5,4},{6,7},{7,6},{8,9},{9,8},{10,11... | collective-permute-start | bytes 786440 | tf_op jit(solution)/shard_map/ppermute | solution.py:338
  156.4 63.6 %all-to-all-start.1 = ((bf16[256,4,128]{2,1,0:T(4,128)(2,1)}), bf16[256,4,128]{2,1,0:T(4,128)(2,1)S(1)}, u32[]{:S(2)}, u32[]{:S(2)}) async-start(bf16[256,4,128]{2,1,0:T(4,128)(2,1)} %bitcast.26), calls=%async_computation.1 | async-start | bytes 524288 | tf_op jit(solution)/shard_map/all_to_all | solution.py:357
  185.2 34.8 %copy-start.3 = (bf16[256,1024]{1,0:T(8,128)(2,1)S(1)}, bf16[256,1024]{1,0:T(8,128)(2,1)}, u32[]{:S(2)}) copy-start(bf16[256,1024]{1,0:T(8,128)(2,1)} %copy-done.2) | copy-start | bytes 1572868
  185.2 4.2 %collective-permute-start.14 = (bf16[2,32,32,128]{3,2,1,0:T(8,128)(2,1)S(1)}, bf16[2,32,32,128]{3,2,1,0:T(8,128)(2,1)S(1)}, u32[]{:S(2)}, u32[]{:S(2)}) collective-permute-start(bf16[2,32,32,128]{3,2,1,0:T(8,128)(2,1)S(1)} %get-tuple-element.30), channel_id=1, source_target_pairs={{0,1},{1,0},{2,3},{3,2},{4,5},{5,4},{6,7},{7,6},{8,9},{9,8},{10,11... | collective-permute-start | bytes 1572872 | tf_op jit(solution)/shard_map/ppermute | solution.py:338
  190.3 39.8 %collective-permute-start.15 = (bf16[32,32,128]{2,1,0:T(8,128)(2,1)}, bf16[32,32,128]{2,1,0:T(8,128)(2,1)S(1)}, u32[]{:S(2)}, u32[]{:S(2)}) collective-permute-start(bf16[32,32,128]{2,1,0:T(8,128)(2,1)} %get-tuple-element.47), channel_id=1, source_target_pairs={{0,2},{1,3},{2,0},{3,1},{4,6},{5,7},{6,4},{7,5},{8,10},{9,11},{10,... | collective-permute-start | bytes 786440 | tf_op jit(solution)/shard_map/ppermute | solution.py:338
  222.5 8.6 %collective-permute-start.16 = (f32[32,8,128]{2,1,0:T(8,128)S(1)}, f32[32,8,128]{2,1,0:T(8,128)S(1)}, u32[]{:S(2)}, u32[]{:S(2)}) collective-permute-start(f32[32,8,128]{2,1,0:T(8,128)S(1)} %get-tuple-element.42), channel_id=1, source_target_pairs={{0,1},{1,0},{2,3},{3,2},{4,5},{5,4},{6,7},{7,6},{8,9},{9,8},{10,11... | collective-permute-start | bytes 393224 | tf_op jit(solution)/shard_map/ppermute | solution.py:338
  231.1 63.5 %copy-start = (bf16[1024,1024]{1,0:T(8,128)(2,1)S(1)}, bf16[1024,1024]{1,0:T(8,128)(2,1)}, u32[]{:S(2)}) copy-start(bf16[1024,1024]{1,0:T(8,128)(2,1)} %w_ref.3) | copy-start | bytes 6291460
  283.2 11.5 %all-to-all-start.3 = ((bf16[16,80,128]{2,1,0:T(8,128)(2,1)}), bf16[16,80,128]{2,1,0:T(8,128)(2,1)S(1)}, u32[]{:S(2)}, u32[]{:S(2)}) async-start(bf16[16,80,128]{2,1,0:T(8,128)(2,1)} %gather_send.1), calls=%async_computation.3 | async-start | bytes 655360 | tf_op jit(solution)/shard_map/all_to_all | solution.py:366
  (5 other events, 100.4 us)

commit v10 on v9

--- a/solution.py
+++ b/solution.py
@@ -67,15 +67,16 @@
 
 def forward_kernel(site_ref, blk_ref, cnt_ref, q_ref, *refs):
     parts, (att_ref, prob_ref, kv_ref, wide_ref, sems) = refs[:-5], refs[-5:]
-    each = parts[0].shape[0]
-    pieces = len(parts) // SITE
 
     @pl.when(pl.program_id(0) == 0)
     def _():
-        copies = [
-            pltpu.make_async_copy(part, kv_ref.at[t // pieces, pl.ds(t % pieces * each, each)], sems.at[t])
-            for t, part in enumerate(parts)
-        ]
+        copies = []
+        row = 0
+        for t, part in enumerate(parts):
+            member, first = divmod(row, kv_ref.shape[1])
+            to = kv_ref.at[member, pl.ds(first, part.shape[0])]
+            copies.append(pltpu.make_async_copy(part, to, sems.at[t]))
+            row += part.shape[0]
         for copy in copies:
             copy.start()
         for copy in copies:
@@ -349,9 +350,9 @@
         cots = [cot] + [lax.ppermute(cot, "dp", [(i, i ^ t) for i in range(ndp)]) for t in range(2, ndp, 2)]
     recv = lax.all_to_all(sent, "seq", split_axis=0, concat_axis=0, tiled=True, axis_index_groups=same_site)
     half = H // 2
-    kv, cots = lax.optimization_barrier(([recv[:half, :128], recv[half:, :128]], cots))
-    kv_z = [swap(x, 2) for x in kv]
-    kvs = [kv, [swap(x, 1) for x in kv], kv_z, [swap(x, 1) for x in kv_z]]
+    kv, cots = lax.optimization_barrier((recv[:, :128], cots))
+    kv_z = [swap(x, 2) for x in (kv[:half], kv[half:])]
+    kvs = [[kv], [swap(kv, 1)], kv_z, [swap(x, 1) for x in kv_z]]
     att, probs = forward(site, blk, cnt, recv, kvs, ndp)
     sent_att = att.reshape(ndp * H, HD // ndp, CSIZE)
     pieces = lax.all_to_all(

time: 297 us -> 297 us (level)
    ppermute x9 -> x8, starting transfers between devices: 36.1 us -> 35.9 us  [swap(): return lax.ppermute(x, 'seq', [(i, i ^ bit) for i in range(nseq)])]
  transfers between devices with their start and end apart: 20 -> 19, of which waited for: 8 -> 8; matrix products, arithmetic and copies ran while one was open for 0% -> 0% of each run, Pallas kernels for 2% -> 2%
where the time goes in v10:
time: 297 us; the launch traced here: 296 us
  starting transfers between devices  124 us (42%)
  waiting for transfers between devices  99.3 us (33%)
  blocking collectives  51.4 us (17%)
  Pallas kernels  16.8 us (6%)
    all_to_all x1, blocking collectives, body(): lax.all_to_all(last, 'seq', split_axis=0, concat_axis=0, tiled=True, axis...  51.4 us
    ppermute x8, starting transfers between devices, swap(): return lax.ppermute(x, 'seq', [(i, i ^ bit) for i in range(nseq)])  35.9 us
    all_to_all x1, waiting for transfers between devices, body(): lax.all_to_all(sent, 'seq', split_axis=0, concat_axis=0, tiled=True, axis...  35.4 us
    all_to_all x1, starting transfers between devices, body(): lax.all_to_all(sent, 'seq', split_axis=0, concat_axis=0, tiled=True, axis...  29 us
    all_to_all x1, waiting for transfers between devices, body(): lax.all_to_all(sent_att, ('dp', 'seq'), split_axis=0, concat_axis=0, tile...  28.1 us
    ppermute x7, starting transfers between devices, body(): lax.ppermute(cot, 'dp', [(i, i ^ t) for i in range(ndp)])  28 us
    all_to_all x1, starting transfers between devices, body(): lax.all_to_all(sent_att, ('dp', 'seq'), split_axis=0, concat_axis=0, tile...  24.9 us
    ppermute x7, waiting for transfers between devices, body(): lax.ppermute(cot, 'dp', [(i, i ^ t) for i in range(ndp)])  19.3 us
  transfers between devices with their start and end apart: 19, of which 8 were waited for; matrix products, arithmetic and copies ran while one was open for 0% of the time, Pallas kernels for 2%

profile of v10, /device:TPU:1, one launch (start us, length us, event | category | flops | bytes accessed | tf_op | source)
XLA Modules:
  0.0 295.9 jit_solution(690535647939586283)
XLA Ops:
  0.6 3.4 %pack.1 = bf16[16,256,128]{2,1,0:T(8,128)(2,1)} custom-call(bf16[128,1024]{1,0:T(8,128)(2,1)} %bitcast.23, bf16[128,1024]{1,0:T(8,128)(2,1)} %bitcast.24, bf16[128,1024]{1,0:T(8,128)(2,1)} %bitcast.25, bf16[128,1024]{1,0:T(8,128)(2,1)} %bitcast.20, bf16[1024,1024]{1,0:T(8,128)(2,1)} %w_ref.3), custom_call_target="tpu_custom_call" | custom-call | flops 268435456 | bytes 3407872 | tf_op jit(solution)/shard_map/pack/pallas_call | solution.py:47
  4.1 29.0 %all-to-all-start = ((bf16[16,256,128]{2,1,0:T(8,128)(2,1)}), bf16[16,256,128]{2,1,0:T(8,128)(2,1)S(1)}, u32[]{:S(2)}, u32[]{:S(2)}) async-start(bf16[16,256,128]{2,1,0:T(8,128)(2,1)} %pack.1), calls=%async_computation | async-start | bytes 2097152 | tf_op jit(solution)/shard_map/all_to_all | solution.py:351
  33.1 3.1 %collective-permute-start = (bf16[128,1024]{1,0:T(8,128)(2,1)S(1)}, bf16[128,1024]{1,0:T(8,128)(2,1)S(1)}, u32[]{:S(2)}, u32[]{:S(2)}) collective-permute-start(bf16[128,1024]{1,0:T(8,128)(2,1)S(1)} %bitcast.21), channel_id=1, source_target_pairs={{0,64},{64,0},{128,192},{192,128},{256,320},{320,256},{384,448},{4... | collective-permute-start | bytes 786440 | tf_op jit(solution)/shard_map/ppermute | solution.py:349
  36.3 5.6 %collective-permute-done = bf16[128,1024]{1,0:T(8,128)(2,1)S(1)} collective-permute-done((bf16[128,1024]{1,0:T(8,128)(2,1)S(1)}, bf16[128,1024]{1,0:T(8,128)(2,1)S(1)}, u32[]{:S(2)}, u32[]{:S(2)}) %collective-permute-start) | collective-permute-done | bytes 262176 | tf_op jit(solution)/shard_map/ppermute | solution.py:349
  41.9 7.1 %collective-permute-start.7 = (bf16[256,1024]{1,0:T(8,128)(2,1)S(1)}, bf16[256,1024]{1,0:T(8,128)(2,1)S(1)}, u32[]{:S(2)}, u32[]{:S(2)}) collective-permute-start(bf16[256,1024]{1,0:T(8,128)(2,1)S(1)} %constant_dynamic-update-slice_fusion.refs_0_), channel_id=1, source_target_pairs={{0,896},{64,960},{128,768},{192,832},{256,640},{320,704},{384,512}... | collective-permute-start | bytes 1572872 | tf_op jit(solution)/shard_map/ppermute | solution.py:350
  50.9 3.5 %collective-permute-start.5 = (bf16[256,1024]{1,0:T(8,128)(2,1)S(1)}, bf16[256,1024]{1,0:T(8,128)(2,1)S(1)}, u32[]{:S(2)}, u32[]{:S(2)}) collective-permute-start(bf16[256,1024]{1,0:T(8,128)(2,1)S(1)} %constant_dynamic-update-slice_fusion.refs_0_), channel_id=1, source_target_pairs={{0,640},{64,704},{128,512},{192,576},{256,896},{320,960},{384,768}... | collective-permute-start | bytes 1572872 | tf_op jit(solution)/shard_map/ppermute | solution.py:350
  54.4 3.3 %collective-permute-start.4 = (bf16[256,1024]{1,0:T(8,128)(2,1)S(1)}, bf16[256,1024]{1,0:T(8,128)(2,1)}, u32[]{:S(2)}, u32[]{:S(2)}) collective-permute-start(bf16[256,1024]{1,0:T(8,128)(2,1)S(1)} %constant_dynamic-update-slice_fusion.refs_0_), channel_id=1, source_target_pairs={{0,512},{64,576},{128,640},{192,704},{256,768},{320,832},{384,896}... | collective-permute-start | bytes 1572872 | tf_op jit(solution)/shard_map/ppermute | solution.py:350
  57.7 4.6 %collective-permute-start.3 = (bf16[256,1024]{1,0:T(8,128)(2,1)S(1)}, bf16[256,1024]{1,0:T(8,128)(2,1)}, u32[]{:S(2)}, u32[]{:S(2)}) collective-permute-start(bf16[256,1024]{1,0:T(8,128)(2,1)S(1)} %constant_dynamic-update-slice_fusion.refs_0_), channel_id=1, source_target_pairs={{0,384},{64,448},{128,256},{192,320},{256,128},{320,192},{384,0},{... | collective-permute-start | bytes 1572872 | tf_op jit(solution)/shard_map/ppermute | solution.py:350
  62.4 3.1 %collective-permute-start.2 = (bf16[256,1024]{1,0:T(8,128)(2,1)S(1)}, bf16[256,1024]{1,0:T(8,128)(2,1)}, u32[]{:S(2)}, u32[]{:S(2)}) collective-permute-start(bf16[256,1024]{1,0:T(8,128)(2,1)S(1)} %constant_dynamic-update-slice_fusion.refs_0_), channel_id=1, source_target_pairs={{0,256},{64,320},{128,384},{192,448},{256,0},{320,64},{384,128},{4... | collective-permute-start | bytes 1572872 | tf_op jit(solution)/shard_map/ppermute | solution.py:350
  65.5 19.3 %collective-permute-done.6.refs_6_ = bf16[256,1024]{1,0:T(8,128)(2,1)S(1)} collective-permute-done((bf16[256,1024]{1,0:T(8,128)(2,1)S(1)}, bf16[256,1024]{1,0:T(8,128)(2,1)S(1)}, u32[]{:S(2)}, u32[]{:S(2)}) %collective-permute-start.6) | collective-permute-done | bytes 524320 | tf_op jit(solution)/shard_map/ppermute | solution.py:350
  85.6 4.5 %collective-permute-start.1 = (bf16[256,1024]{1,0:T(8,128)(2,1)S(1)}, bf16[256,1024]{1,0:T(8,128)(2,1)}, u32[]{:S(2)}, u32[]{:S(2)}) collective-permute-start(bf16[256,1024]{1,0:T(8,128)(2,1)S(1)} %constant_dynamic-update-slice_fusion.refs_0_), channel_id=1, source_target_pairs={{0,128},{64,192},{128,0},{192,64},{256,384},{320,448},{384,256},{4... | collective-permute-start | bytes 1572872 | tf_op jit(solution)/shard_map/ppermute | solution.py:350
  90.1 35.4 %all-to-all-done.q_ref.g_ref = bf16[16,256,128]{2,1,0:T(8,128)(2,1)S(1)} async-done(((bf16[16,256,128]{2,1,0:T(8,128)(2,1)}), bf16[16,256,128]{2,1,0:T(8,128)(2,1)S(1)}, u32[]{:S(2)}, u32[]{:S(2)}) %all-to-all-start) | async-done | bytes 1048608 | tf_op jit(solution)/shard_map/all_to_all | solution.py:351
  125.7 6.8 %collective-permute-start.10 = (bf16[8,128,128]{2,1,0:T(8,128)(2,1)S(1)}, bf16[8,128,128]{2,1,0:T(8,128)(2,1)S(1)}, u32[]{:S(2)}, u32[]{:S(2)}) collective-permute-start(bf16[8,128,128]{2,1,0:T(8,128)(2,1)S(1)} %get-tuple-element.45), channel_id=1, source_target_pairs={{0,2},{1,3},{2,0},{3,1},{4,6},{5,7},{6,4},{7,5},{8,10},{9,11},{10,... | collective-permute-start | bytes 786440 | tf_op jit(solution)/shard_map/ppermute | solution.py:339
  134.4 8.5 %collective-permute-start.8 = (bf16[16,128,128]{2,1,0:T(8,128)(2,1)S(1)}, bf16[16,128,128]{2,1,0:T(8,128)(2,1)}, u32[]{:S(2)}, u32[]{:S(2)}) collective-permute-start(bf16[16,128,128]{2,1,0:T(8,128)(2,1)S(1)} %slice.24.refs_0_), channel_id=1, source_target_pairs={{0,1},{1,0},{2,3},{3,2},{4,5},{5,4},{6,7},{7,6},{8,9},{9,8},{10,11... | collective-permute-start | bytes 1572872 | tf_op jit(solution)/shard_map/ppermute | solution.py:339
  145.3 4.0 %collective-permute-start.11 = (bf16[8,128,128]{2,1,0:T(8,128)(2,1)}, bf16[8,128,128]{2,1,0:T(8,128)(2,1)}, u32[]{:S(2)}, u32[]{:S(2)}) collective-permute-start(bf16[8,128,128]{2,1,0:T(8,128)(2,1)} %collective-permute-done.9.refs_2_), channel_id=1, source_target_pairs={{0,1},{1,0},{2,3},{3,2},{4,5},{5,4},{6,7},{7,6},{8,9},{9,8},{10,11... | collective-permute-start | bytes 786440 | tf_op jit(solution)/shard_map/ppermute | solution.py:339
  150.8 5.3 %attend.1 = (bf16[16,64,128]{2,1,0:T(8,128)(2,1)}, bf16[16,4,128,128]{3,2,1,0:T(8,128)(2,1)}) custom-call(s32[1]{0:T(128)} %bitcast.site_ref, s32[256]{0:T(256)S(1)} %reshape_squeeze.3.blk_ref, s32[64]{0:T(128)S(1)} %bitcast.19, bf16[16,256,128]{2,1,0:T(8,128)(2,1)S(1)} %all-to-all-done.q_ref.g_ref, bf16[16,128,128]{2,1,0:T(8,128)(2,1)S(1)} %slice.24.refs_0_, ...), custom_call_target="tpu_custom_call" | custom-call | flops 268435456 | bytes 5242880 | tf_op jit(solution)/shard_map/attend/pallas_call | solution.py:126
  156.1 24.9 %all-to-all-start.1 = ((bf16[256,4,128]{2,1,0:T(4,128)(2,1)}), bf16[256,4,128]{2,1,0:T(4,128)(2,1)S(1)}, u32[]{:S(2)}, u32[]{:S(2)}) async-start(bf16[256,4,128]{2,1,0:T(4,128)(2,1)} %bitcast.26), calls=%async_computation.1 | async-start | bytes 524288 | tf_op jit(solution)/shard_map/all_to_all | solution.py:358
  185.1 2.7 collective-permute-start.13
  191.7 28.1 %all-to-all-done.1 = bf16[256,4,128]{2,1,0:T(4,128)(2,1)S(1)} async-done(((bf16[256,4,128]{2,1,0:T(4,128)(2,1)}), bf16[256,4,128]{2,1,0:T(4,128)(2,1)S(1)}, u32[]{:S(2)}, u32[]{:S(2)}) %all-to-all-start.1) | async-done | bytes 262176 | tf_op jit(solution)/shard_map/all_to_all | solution.py:358
  219.9 2.5 weight_part.1
  222.4 7.5 %collective-permute-start.15 = (f32[32,8,128]{2,1,0:T(8,128)S(1)}, f32[32,8,128]{2,1,0:T(8,128)S(1)}, u32[]{:S(2)}, u32[]{:S(2)}) collective-permute-start(f32[32,8,128]{2,1,0:T(8,128)S(1)} %get-tuple-element.40), channel_id=1, source_target_pairs={{0,1},{1,0},{2,3},{3,2},{4,5},{5,4},{6,7},{7,6},{8,9},{9,8},{10,11... | collective-permute-start | bytes 393224 | tf_op jit(solution)/shard_map/ppermute | solution.py:339
  230.9 51.4 %all_to_all.20.back_ref = bf16[32,40,128]{2,1,0:T(8,128)(2,1)S(1)} all-to-all(bf16[32,40,128]{2,1,0:T(8,128)(2,1)S(1)} %merge.1), channel_id=1, replica_groups={{0,2,4,6,8,10,12,14,16,18,20,22,24,26,28,30,32,34,36,38,40,42,44,46,48,..., dimensions={0} | all-to-all | bytes 655360 | tf_op jit(solution)/shard_map/all_to_all | solution.py:366
  283.1 3.5 %all-to-all-start.3 = ((bf16[16,80,128]{2,1,0:T(8,128)(2,1)}), bf16[16,80,128]{2,1,0:T(8,128)(2,1)S(1)}, u32[]{:S(2)}, u32[]{:S(2)}) async-start(bf16[16,80,128]{2,1,0:T(8,128)(2,1)} %gather_send.1), calls=%async_computation.3 | async-start | bytes 655360 | tf_op jit(solution)/shard_map/all_to_all | solution.py:367
  287.5 7.1 %all-to-all-done.3.got_ref = bf16[16,80,128]{2,1,0:T(8,128)(2,1)S(1)} async-done(((bf16[16,80,128]{2,1,0:T(8,128)(2,1)}), bf16[16,80,128]{2,1,0:T(8,128)(2,1)S(1)}, u32[]{:S(2)}, u32[]{:S(2)}) %all-to-all-start.3) | async-done | bytes 327712 | tf_op jit(solution)/shard_map/all_to_all | solution.py:367
  (50 shorter events, 20.6 us)
Async XLA Ops:
  4.1 121.4 %all-to-all-start = ((bf16[16,256,128]{2,1,0:T(8,128)(2,1)}), bf16[16,256,128]{2,1,0:T(8,128)(2,1)S(1)}, u32[]{:S(2)}, u32[]{:S(2)}) async-start(bf16[16,256,128]{2,1,0:T(8,128)(2,1)} %pack.1), calls=%async_computation | async-start | bytes 2097152 | tf_op jit(solution)/shard_map/all_to_all | solution.py:351
  33.1 116.2 %copy-start.8 = (s32[1,64,4]{1,2,0:T(4,128)S(1)}, s32[1,64,4]{1,2,0:T(4,128)}, u32[]{:S(2)}) copy-start(s32[1,64,4]{1,2,0:T(4,128)} %param.12) | copy-start | bytes 3076
  33.1 117.7 %copy-start.6 = (s32[1,64]{1,0:T(1,128)S(1)}, s32[1,64]{1,0:T(1,128)}, u32[]{:S(2)}) copy-start(s32[1,64]{1,0:T(1,128)} %param.13) | copy-start | bytes 772
  33.1 8.8 %collective-permute-start = (bf16[128,1024]{1,0:T(8,128)(2,1)S(1)}, bf16[128,1024]{1,0:T(8,128)(2,1)S(1)}, u32[]{:S(2)}, u32[]{:S(2)}) collective-permute-start(bf16[128,1024]{1,0:T(8,128)(2,1)S(1)} %bitcast.21), channel_id=1, source_target_pairs={{0,64},{64,0},{128,192},{192,128},{256,320},{320,256},{384,448},{4... | collective-permute-start | bytes 786440 | tf_op jit(solution)/shard_map/ppermute | solution.py:349
  41.9 20.4 %collective-permute-start.7 = (bf16[256,1024]{1,0:T(8,128)(2,1)S(1)}, bf16[256,1024]{1,0:T(8,128)(2,1)S(1)}, u32[]{:S(2)}, u32[]{:S(2)}) collective-permute-start(bf16[256,1024]{1,0:T(8,128)(2,1)S(1)} %constant_dynamic-update-slice_fusion.refs_0_), channel_id=1, source_target_pairs={{0,896},{64,960},{128,768},{192,832},{256,640},{320,704},{384,512}... | collective-permute-start | bytes 1572872 | tf_op jit(solution)/shard_map/ppermute | solution.py:350
  49.0 35.7 %collective-permute-start.6 = (bf16[256,1024]{1,0:T(8,128)(2,1)S(1)}, bf16[256,1024]{1,0:T(8,128)(2,1)S(1)}, u32[]{:S(2)}, u32[]{:S(2)}) collective-permute-start(bf16[256,1024]{1,0:T(8,128)(2,1)S(1)} %constant_dynamic-update-slice_fusion.refs_0_), channel_id=1, source_target_pairs={{0,768},{64,832},{128,896},{192,960},{256,512},{320,576},{384,640}... | collective-permute-start | bytes 1572872 | tf_op jit(solution)/shard_map/ppermute | solution.py:350
  50.9 74.6 %collective-permute-start.5 = (bf16[256,1024]{1,0:T(8,128)(2,1)S(1)}, bf16[256,1024]{1,0:T(8,128)(2,1)S(1)}, u32[]{:S(2)}, u32[]{:S(2)}) collective-permute-start(bf16[256,1024]{1,0:T(8,128)(2,1)S(1)} %constant_dynamic-update-slice_fusion.refs_0_), channel_id=1, source_target_pairs={{0,640},{64,704},{128,512},{192,576},{256,896},{320,960},{384,768}... | collective-permute-start | bytes 1572872 | tf_op jit(solution)/shard_map/ppermute | solution.py:350
  54.4 71.2 %collective-permute-start.4 = (bf16[256,1024]{1,0:T(8,128)(2,1)S(1)}, bf16[256,1024]{1,0:T(8,128)(2,1)}, u32[]{:S(2)}, u32[]{:S(2)}) collective-permute-start(bf16[256,1024]{1,0:T(8,128)(2,1)S(1)} %constant_dynamic-update-slice_fusion.refs_0_), channel_id=1, source_target_pairs={{0,512},{64,576},{128,640},{192,704},{256,768},{320,832},{384,896}... | collective-permute-start | bytes 1572872 | tf_op jit(solution)/shard_map/ppermute | solution.py:350
  57.7 67.9 %collective-permute-start.3 = (bf16[256,1024]{1,0:T(8,128)(2,1)S(1)}, bf16[256,1024]{1,0:T(8,128)(2,1)}, u32[]{:S(2)}, u32[]{:S(2)}) collective-permute-start(bf16[256,1024]{1,0:T(8,128)(2,1)S(1)} %constant_dynamic-update-slice_fusion.refs_0_), channel_id=1, source_target_pairs={{0,384},{64,448},{128,256},{192,320},{256,128},{320,192},{384,0},{... | collective-permute-start | bytes 1572872 | tf_op jit(solution)/shard_map/ppermute | solution.py:350
  62.4 63.3 %collective-permute-start.2 = (bf16[256,1024]{1,0:T(8,128)(2,1)S(1)}, bf16[256,1024]{1,0:T(8,128)(2,1)}, u32[]{:S(2)}, u32[]{:S(2)}) collective-permute-start(bf16[256,1024]{1,0:T(8,128)(2,1)S(1)} %constant_dynamic-update-slice_fusion.refs_0_), channel_id=1, source_target_pairs={{0,256},{64,320},{128,384},{192,448},{256,0},{320,64},{384,128},{4... | collective-permute-start | bytes 1572872 | tf_op jit(solution)/shard_map/ppermute | solution.py:350
  85.6 40.1 %collective-permute-start.1 = (bf16[256,1024]{1,0:T(8,128)(2,1)S(1)}, bf16[256,1024]{1,0:T(8,128)(2,1)}, u32[]{:S(2)}, u32[]{:S(2)}) collective-permute-start(bf16[256,1024]{1,0:T(8,128)(2,1)S(1)} %constant_dynamic-update-slice_fusion.refs_0_), channel_id=1, source_target_pairs={{0,128},{64,192},{128,0},{192,64},{256,384},{320,448},{384,256},{4... | collective-permute-start | bytes 1572872 | tf_op jit(solution)/shard_map/ppermute | solution.py:350
  125.7 17.2 %collective-permute-start.10 = (bf16[8,128,128]{2,1,0:T(8,128)(2,1)S(1)}, bf16[8,128,128]{2,1,0:T(8,128)(2,1)S(1)}, u32[]{:S(2)}, u32[]{:S(2)}) collective-permute-start(bf16[8,128,128]{2,1,0:T(8,128)(2,1)S(1)} %get-tuple-element.45), channel_id=1, source_target_pairs={{0,2},{1,3},{2,0},{3,1},{4,6},{5,7},{6,4},{7,5},{8,10},{9,11},{10,... | collective-permute-start | bytes 786440 | tf_op jit(solution)/shard_map/ppermute | solution.py:339
  132.5 12.8 %collective-permute-start.9 = (bf16[8,128,128]{2,1,0:T(8,128)(2,1)S(1)}, bf16[8,128,128]{2,1,0:T(8,128)(2,1)}, u32[]{:S(2)}, u32[]{:S(2)}) collective-permute-start(bf16[8,128,128]{2,1,0:T(8,128)(2,1)S(1)} %get-tuple-element.46), channel_id=1, source_target_pairs={{0,2},{1,3},{2,0},{3,1},{4,6},{5,7},{6,4},{7,5},{8,10},{9,11},{10,... | collective-permute-start | bytes 786440 | tf_op jit(solution)/shard_map/ppermute | solution.py:339
  134.4 16.4 %collective-permute-start.8 = (bf16[16,128,128]{2,1,0:T(8,128)(2,1)S(1)}, bf16[16,128,128]{2,1,0:T(8,128)(2,1)}, u32[]{:S(2)}, u32[]{:S(2)}) collective-permute-start(bf16[16,128,128]{2,1,0:T(8,128)(2,1)S(1)} %slice.24.refs_0_), channel_id=1, source_target_pairs={{0,1},{1,0},{2,3},{3,2},{4,5},{5,4},{6,7},{7,6},{8,9},{9,8},{10,11... | collective-permute-start | bytes 1572872 | tf_op jit(solution)/shard_map/ppermute | solution.py:339
  142.9 6.7 %collective-permute-start.12 = (bf16[8,128,128]{2,1,0:T(8,128)(2,1)S(1)}, bf16[8,128,128]{2,1,0:T(8,128)(2,1)}, u32[]{:S(2)}, u32[]{:S(2)}) collective-permute-start(bf16[8,128,128]{2,1,0:T(8,128)(2,1)S(1)} %collective-permute-done.10.refs_3_), channel_id=1, source_target_pairs={{0,1},{1,0},{2,3},{3,2},{4,5},{5,4},{6,7},{7,6},{8,9},{9,8},{10,11... | collective-permute-start | bytes 786440 | tf_op jit(solution)/shard_map/ppermute | solution.py:339
  145.3 5.5 %collective-permute-start.11 = (bf16[8,128,128]{2,1,0:T(8,128)(2,1)}, bf16[8,128,128]{2,1,0:T(8,128)(2,1)}, u32[]{:S(2)}, u32[]{:S(2)}) collective-permute-start(bf16[8,128,128]{2,1,0:T(8,128)(2,1)} %collective-permute-done.9.refs_2_), channel_id=1, source_target_pairs={{0,1},{1,0},{2,3},{3,2},{4,5},{5,4},{6,7},{7,6},{8,9},{9,8},{10,11... | collective-permute-start | bytes 786440 | tf_op jit(solution)/shard_map/ppermute | solution.py:339
  156.1 63.8 %all-to-all-start.1 = ((bf16[256,4,128]{2,1,0:T(4,128)(2,1)}), bf16[256,4,128]{2,1,0:T(4,128)(2,1)S(1)}, u32[]{:S(2)}, u32[]{:S(2)}) async-start(bf16[256,4,128]{2,1,0:T(4,128)(2,1)} %bitcast.26), calls=%async_computation.1 | async-start | bytes 524288 | tf_op jit(solution)/shard_map/all_to_all | solution.py:358
  185.1 34.8 %copy-start.3 = (bf16[256,1024]{1,0:T(8,128)(2,1)S(1)}, bf16[256,1024]{1,0:T(8,128)(2,1)}, u32[]{:S(2)}) copy-start(bf16[256,1024]{1,0:T(8,128)(2,1)} %copy-done.2) | copy-start | bytes 1572868
  185.1 34.8 %copy-start.5 = (bf16[256,1024]{1,0:T(8,128)(2,1)S(1)}, bf16[256,1024]{1,0:T(8,128)(2,1)}, u32[]{:S(2)}) copy-start(bf16[256,1024]{1,0:T(8,128)(2,1)} %copy-done.4) | copy-start | bytes 1572868
  185.1 4.2 %collective-permute-start.13 = (bf16[2,32,32,128]{3,2,1,0:T(8,128)(2,1)S(1)}, bf16[2,32,32,128]{3,2,1,0:T(8,128)(2,1)S(1)}, u32[]{:S(2)}, u32[]{:S(2)}) collective-permute-start(bf16[2,32,32,128]{3,2,1,0:T(8,128)(2,1)S(1)} %get-tuple-element.28), channel_id=1, source_target_pairs={{0,1},{1,0},{2,3},{3,2},{4,5},{5,4},{6,7},{7,6},{8,9},{9,8},{10,11... | collective-permute-start | bytes 1572872 | tf_op jit(solution)/shard_map/ppermute | solution.py:339
  189.5 40.4 %collective-permute-start.14 = (bf16[32,32,128]{2,1,0:T(8,128)(2,1)S(1)}, bf16[32,32,128]{2,1,0:T(8,128)(2,1)S(1)}, u32[]{:S(2)}, u32[]{:S(2)}) collective-permute-start(bf16[32,32,128]{2,1,0:T(8,128)(2,1)S(1)} %get-tuple-element.43), channel_id=1, source_target_pairs={{0,2},{1,3},{2,0},{3,1},{4,6},{5,7},{6,4},{7,5},{8,10},{9,11},{10,... | collective-permute-start | bytes 786440 | tf_op jit(solution)/shard_map/ppermute | solution.py:339
  222.4 8.4 %collective-permute-start.15 = (f32[32,8,128]{2,1,0:T(8,128)S(1)}, f32[32,8,128]{2,1,0:T(8,128)S(1)}, u32[]{:S(2)}, u32[]{:S(2)}) collective-permute-start(f32[32,8,128]{2,1,0:T(8,128)S(1)} %get-tuple-element.40), channel_id=1, source_target_pairs={{0,1},{1,0},{2,3},{3,2},{4,5},{5,4},{6,7},{7,6},{8,9},{9,8},{10,11... | collective-permute-start | bytes 393224 | tf_op jit(solution)/shard_map/ppermute | solution.py:339
  230.9 63.7 %copy-start = (bf16[1024,1024]{1,0:T(8,128)(2,1)S(1)}, bf16[1024,1024]{1,0:T(8,128)(2,1)}, u32[]{:S(2)}) copy-start(bf16[1024,1024]{1,0:T(8,128)(2,1)} %w_ref.3) | copy-start | bytes 6291460
  283.1 11.5 %all-to-all-start.3 = ((bf16[16,80,128]{2,1,0:T(8,128)(2,1)}), bf16[16,80,128]{2,1,0:T(8,128)(2,1)S(1)}, u32[]{:S(2)}, u32[]{:S(2)}) async-start(bf16[16,80,128]{2,1,0:T(8,128)(2,1)} %gather_send.1), calls=%async_computation.3 | async-start | bytes 655360 | tf_op jit(solution)/shard_map/all_to_all | solution.py:367
  (4 other events, 65.3 us)

commit v11 on v10

--- a/solution.py
+++ b/solution.py
@@ -68,18 +68,21 @@
 def forward_kernel(site_ref, blk_ref, cnt_ref, q_ref, *refs):
     parts, (att_ref, prob_ref, kv_ref, wide_ref, sems) = refs[:-5], refs[-5:]
 
-    @pl.when(pl.program_id(0) == 0)
-    def _():
-        copies = []
-        row = 0
+    def copies(kind):
+        row, made = 0, []
         for t, part in enumerate(parts):
             member, first = divmod(row, kv_ref.shape[1])
-            to = kv_ref.at[member, pl.ds(first, part.shape[0])]
-            copies.append(pltpu.make_async_copy(part, to, sems.at[t]))
+            lines = pl.ds(kind * 64, 64)
+            to = kv_ref.at[member, pl.ds(first, part.shape[0]), lines]
+            made.append(pltpu.make_async_copy(part.at[:, lines], to, sems.at[kind, t]))
             row += part.shape[0]
-        for copy in copies:
+        return made
+
+    @pl.when(pl.program_id(0) == 0)
+    def _():
+        for copy in copies(0) + copies(1):
             copy.start()
-        for copy in copies:
+        for copy in copies(0):
             copy.wait()
 
     count = q_ref.shape[0]
@@ -101,6 +104,12 @@
             s = jnp.dot(keys, both, preferred_element_type=F32)
             mine.append(s if j == 0 else jnp.where(j < number, s, -1e30))
         scores.append(jnp.concatenate(mine, axis=0))
+
+    @pl.when(pl.program_id(0) == 0)
+    def _():
+        for copy in copies(1):
+            copy.wait()
+
     for u in range(count):
         s = scores[u]
         top = jnp.max(s, axis=0, keepdims=True)
@@ -139,7 +148,7 @@
             scratch_shapes=[
                 pltpu.VMEM((SITE, n) + parts[0].shape[1:], BF),
                 pltpu.VMEM((ROWS * HD, CSIZE), F32),
-                pltpu.SemaphoreType.DMA((len(parts),)),
+                pltpu.SemaphoreType.DMA((2, len(parts))),
             ],
         ),
         out_shape=[
@@ -349,9 +358,9 @@
         cot = jnp.concatenate([cot, lax.ppermute(cot, "dp", [(i, i ^ 1) for i in range(ndp)])], axis=0)
         cots = [cot] + [lax.ppermute(cot, "dp", [(i, i ^ t) for i in range(ndp)]) for t in range(2, ndp, 2)]
     recv = lax.all_to_all(sent, "seq", split_axis=0, concat_axis=0, tiled=True, axis_index_groups=same_site)
-    half = H // 2
+    most = 3 * H // 4
     kv, cots = lax.optimization_barrier((recv[:, :128], cots))
-    kv_z = [swap(x, 2) for x in (kv[:half], kv[half:])]
+    kv_z = [swap(x, 2) for x in (kv[:most], kv[most:])]
     kvs = [[kv], [swap(kv, 1)], kv_z, [swap(x, 1) for x in kv_z]]
     att, probs = forward(site, blk, cnt, recv, kvs, ndp)
     sent_att = att.reshape(ndp * H, HD // ndp, CSIZE)

time: 297 us -> 304 us (1.024)
  starting transfers between devices: 124 us -> 128 us
  waiting for transfers between devices: 99.3 us -> 103 us
    ppermute x8, starting transfers between devices: 35.9 us -> 39.5 us  [swap(): return lax.ppermute(x, 'seq', [(i, i ^ bit) for i in range(nseq)])]
    ppermute x8, waiting for transfers between devices: 3.72 us -> 7.05 us  [swap(): return lax.ppermute(x, 'seq', [(i, i ^ bit) for i in range(nseq)])]
  transfers between devices with their start and end apart: 19 -> 19, of which waited for: 8 -> 9; matrix products, arithmetic and copies ran while one was open for 0% -> 0% of each run, Pallas kernels for 2% -> 2%
where the time goes in v11:
time: 304 us; the launch traced here: 302 us
  starting transfers between devices  128 us (42%)
  waiting for transfers between devices  103 us (34%)
  blocking collectives  51.3 us (17%)
  Pallas kernels  17 us (6%)
    all_to_all x1, blocking collectives, body(): lax.all_to_all(last, 'seq', split_axis=0, concat_axis=0, tiled=True, axis...  51.3 us
    ppermute x8, starting transfers between devices, swap(): return lax.ppermute(x, 'seq', [(i, i ^ bit) for i in range(nseq)])  39.5 us
    all_to_all x1, waiting for transfers between devices, body(): lax.all_to_all(sent, 'seq', split_axis=0, concat_axis=0, tiled=True, axis...  35.4 us
    all_to_all x1, starting transfers between devices, body(): lax.all_to_all(sent, 'seq', split_axis=0, concat_axis=0, tiled=True, axis...  29 us
    all_to_all x1, waiting for transfers between devices, body(): lax.all_to_all(sent_att, ('dp', 'seq'), split_axis=0, concat_axis=0, tile...  28.1 us
    ppermute x7, starting transfers between devices, body(): lax.ppermute(cot, 'dp', [(i, i ^ t) for i in range(ndp)])  28 us
    all_to_all x1, starting transfers between devices, body(): lax.all_to_all(sent_att, ('dp', 'seq'), split_axis=0, concat_axis=0, tile...  24.3 us
    ppermute x7, waiting for transfers between devices, body(): lax.ppermute(cot, 'dp', [(i, i ^ t) for i in range(ndp)])  19.3 us
  transfers between devices with their start and end apart: 19, of which 9 were waited for; matrix products, arithmetic and copies ran while one was open for 0% of the time, Pallas kernels for 2%

profile of v11, /device:TPU:1, one launch (start us, length us, event | category | flops | bytes accessed | tf_op | source)
XLA Modules:
  0.0 302.5 jit_solution(10541890373770767073)
XLA Ops:
  0.6 3.4 %pack.1 = bf16[16,256,128]{2,1,0:T(8,128)(2,1)} custom-call(bf16[128,1024]{1,0:T(8,128)(2,1)} %bitcast.23, bf16[128,1024]{1,0:T(8,128)(2,1)} %bitcast.24, bf16[128,1024]{1,0:T(8,128)(2,1)} %bitcast.25, bf16[128,1024]{1,0:T(8,128)(2,1)} %bitcast.20, bf16[1024,1024]{1,0:T(8,128)(2,1)} %w_ref.3), custom_call_target="tpu_custom_call" | custom-call | flops 268435456 | bytes 3407872 | tf_op jit(solution)/shard_map/pack/pallas_call | solution.py:47
  4.1 29.0 %all-to-all-start = ((bf16[16,256,128]{2,1,0:T(8,128)(2,1)}), bf16[16,256,128]{2,1,0:T(8,128)(2,1)S(1)}, u32[]{:S(2)}, u32[]{:S(2)}) async-start(bf16[16,256,128]{2,1,0:T(8,128)(2,1)} %pack.1), calls=%async_computation | async-start | bytes 2097152 | tf_op jit(solution)/shard_map/all_to_all | solution.py:360
  33.1 3.1 %collective-permute-start = (bf16[128,1024]{1,0:T(8,128)(2,1)S(1)}, bf16[128,1024]{1,0:T(8,128)(2,1)S(1)}, u32[]{:S(2)}, u32[]{:S(2)}) collective-permute-start(bf16[128,1024]{1,0:T(8,128)(2,1)S(1)} %bitcast.21), channel_id=1, source_target_pairs={{0,64},{64,0},{128,192},{192,128},{256,320},{320,256},{384,448},{4... | collective-permute-start | bytes 786440 | tf_op jit(solution)/shard_map/ppermute | solution.py:358
  36.3 5.6 %collective-permute-done = bf16[128,1024]{1,0:T(8,128)(2,1)S(1)} collective-permute-done((bf16[128,1024]{1,0:T(8,128)(2,1)S(1)}, bf16[128,1024]{1,0:T(8,128)(2,1)S(1)}, u32[]{:S(2)}, u32[]{:S(2)}) %collective-permute-start) | collective-permute-done | bytes 262176 | tf_op jit(solution)/shard_map/ppermute | solution.py:358
  41.9 7.1 %collective-permute-start.7 = (bf16[256,1024]{1,0:T(8,128)(2,1)S(1)}, bf16[256,1024]{1,0:T(8,128)(2,1)S(1)}, u32[]{:S(2)}, u32[]{:S(2)}) collective-permute-start(bf16[256,1024]{1,0:T(8,128)(2,1)S(1)} %constant_dynamic-update-slice_fusion.refs_0_), channel_id=1, source_target_pairs={{0,896},{64,960},{128,768},{192,832},{256,640},{320,704},{384,512}... | collective-permute-start | bytes 1572872 | tf_op jit(solution)/shard_map/ppermute | solution.py:359
  50.9 3.5 %collective-permute-start.5 = (bf16[256,1024]{1,0:T(8,128)(2,1)S(1)}, bf16[256,1024]{1,0:T(8,128)(2,1)S(1)}, u32[]{:S(2)}, u32[]{:S(2)}) collective-permute-start(bf16[256,1024]{1,0:T(8,128)(2,1)S(1)} %constant_dynamic-update-slice_fusion.refs_0_), channel_id=1, source_target_pairs={{0,640},{64,704},{128,512},{192,576},{256,896},{320,960},{384,768}... | collective-permute-start | bytes 1572872 | tf_op jit(solution)/shard_map/ppermute | solution.py:359
  54.4 3.3 %collective-permute-start.4 = (bf16[256,1024]{1,0:T(8,128)(2,1)S(1)}, bf16[256,1024]{1,0:T(8,128)(2,1)}, u32[]{:S(2)}, u32[]{:S(2)}) collective-permute-start(bf16[256,1024]{1,0:T(8,128)(2,1)S(1)} %constant_dynamic-update-slice_fusion.refs_0_), channel_id=1, source_target_pairs={{0,512},{64,576},{128,640},{192,704},{256,768},{320,832},{384,896}... | collective-permute-start | bytes 1572872 | tf_op jit(solution)/shard_map/ppermute | solution.py:359
  57.7 4.6 %collective-permute-start.3 = (bf16[256,1024]{1,0:T(8,128)(2,1)S(1)}, bf16[256,1024]{1,0:T(8,128)(2,1)}, u32[]{:S(2)}, u32[]{:S(2)}) collective-permute-start(bf16[256,1024]{1,0:T(8,128)(2,1)S(1)} %constant_dynamic-update-slice_fusion.refs_0_), channel_id=1, source_target_pairs={{0,384},{64,448},{128,256},{192,320},{256,128},{320,192},{384,0},{... | collective-permute-start | bytes 1572872 | tf_op jit(solution)/shard_map/ppermute | solution.py:359
  62.4 3.1 %collective-permute-start.2 = (bf16[256,1024]{1,0:T(8,128)(2,1)S(1)}, bf16[256,1024]{1,0:T(8,128)(2,1)}, u32[]{:S(2)}, u32[]{:S(2)}) collective-permute-start(bf16[256,1024]{1,0:T(8,128)(2,1)S(1)} %constant_dynamic-update-slice_fusion.refs_0_), channel_id=1, source_target_pairs={{0,256},{64,320},{128,384},{192,448},{256,0},{320,64},{384,128},{4... | collective-permute-start | bytes 1572872 | tf_op jit(solution)/shard_map/ppermute | solution.py:359
  65.5 19.3 %collective-permute-done.6.refs_6_ = bf16[256,1024]{1,0:T(8,128)(2,1)S(1)} collective-permute-done((bf16[256,1024]{1,0:T(8,128)(2,1)S(1)}, bf16[256,1024]{1,0:T(8,128)(2,1)S(1)}, u32[]{:S(2)}, u32[]{:S(2)}) %collective-permute-start.6) | collective-permute-done | bytes 524320 | tf_op jit(solution)/shard_map/ppermute | solution.py:359
  85.6 4.5 %collective-permute-start.1 = (bf16[256,1024]{1,0:T(8,128)(2,1)S(1)}, bf16[256,1024]{1,0:T(8,128)(2,1)}, u32[]{:S(2)}, u32[]{:S(2)}) collective-permute-start(bf16[256,1024]{1,0:T(8,128)(2,1)S(1)} %constant_dynamic-update-slice_fusion.refs_0_), channel_id=1, source_target_pairs={{0,128},{64,192},{128,0},{192,64},{256,384},{320,448},{384,256},{4... | collective-permute-start | bytes 1572872 | tf_op jit(solution)/shard_map/ppermute | solution.py:359
  90.1 35.4 %all-to-all-done.q_ref.g_ref = bf16[16,256,128]{2,1,0:T(8,128)(2,1)S(1)} async-done(((bf16[16,256,128]{2,1,0:T(8,128)(2,1)}), bf16[16,256,128]{2,1,0:T(8,128)(2,1)S(1)}, u32[]{:S(2)}, u32[]{:S(2)}) %all-to-all-start) | async-done | bytes 1048608 | tf_op jit(solution)/shard_map/all_to_all | solution.py:360
  125.7 6.8 %collective-permute-start.9 = (bf16[12,128,128]{2,1,0:T(8,128)(2,1)S(1)}, bf16[12,128,128]{2,1,0:T(8,128)(2,1)}, u32[]{:S(2)}, u32[]{:S(2)}) collective-permute-start(bf16[12,128,128]{2,1,0:T(8,128)(2,1)S(1)} %slice.19), channel_id=1, source_target_pairs={{0,2},{1,3},{2,0},{3,1},{4,6},{5,7},{6,4},{7,5},{8,10},{9,11},{10,... | collective-permute-start | bytes 1179656 | tf_op jit(solution)/shard_map/ppermute | solution.py:348
  132.4 8.5 %collective-permute-start.8 = (bf16[16,128,128]{2,1,0:T(8,128)(2,1)S(1)}, bf16[16,128,128]{2,1,0:T(8,128)(2,1)}, u32[]{:S(2)}, u32[]{:S(2)}) collective-permute-start(bf16[16,128,128]{2,1,0:T(8,128)(2,1)S(1)} %slice.24.refs_0_), channel_id=1, source_target_pairs={{0,1},{1,0},{2,3},{3,2},{4,5},{5,4},{6,7},{7,6},{8,9},{9,8},{10,11... | collective-permute-start | bytes 1572872 | tf_op jit(solution)/shard_map/ppermute | solution.py:348
  140.9 5.8 %collective-permute-start.11 = (bf16[12,128,128]{2,1,0:T(8,128)(2,1)}, bf16[12,128,128]{2,1,0:T(8,128)(2,1)}, u32[]{:S(2)}, u32[]{:S(2)}) collective-permute-start(bf16[12,128,128]{2,1,0:T(8,128)(2,1)} %collective-permute-done.9.refs_2_), channel_id=1, source_target_pairs={{0,1},{1,0},{2,3},{3,2},{4,5},{5,4},{6,7},{7,6},{8,9},{9,8},{10,11... | collective-permute-start | bytes 1179656 | tf_op jit(solution)/shard_map/ppermute | solution.py:348
  146.8 3.6 %collective-permute-start.10 = (bf16[4,128,128]{2,1,0:T(8,128)(2,1)S(1)}, bf16[4,128,128]{2,1,0:T(8,128)(2,1)S(1)}, u32[]{:S(2)}, u32[]{:S(2)}) collective-permute-start(bf16[4,128,128]{2,1,0:T(8,128)(2,1)S(1)} %slice.20), channel_id=1, source_target_pairs={{0,2},{1,3},{2,0},{3,1},{4,6},{5,7},{6,4},{7,5},{8,10},{9,11},{10,... | collective-permute-start | bytes 393224 | tf_op jit(solution)/shard_map/ppermute | solution.py:348
  150.4 3.8 %collective-permute-done.10.refs_3_ = bf16[4,128,128]{2,1,0:T(8,128)(2,1)S(1)} collective-permute-done((bf16[4,128,128]{2,1,0:T(8,128)(2,1)S(1)}, bf16[4,128,128]{2,1,0:T(8,128)(2,1)S(1)}, u32[]{:S(2)}, u32[]{:S(2)}) %collective-permute-start.10) | collective-permute-done | bytes 131104 | tf_op jit(solution)/shard_map/ppermute | solution.py:348
  157.7 5.5 %attend.1 = (bf16[16,64,128]{2,1,0:T(8,128)(2,1)}, bf16[16,4,128,128]{3,2,1,0:T(8,128)(2,1)}) custom-call(s32[1]{0:T(128)} %bitcast.site_ref, s32[256]{0:T(256)S(1)} %reshape_squeeze.3.blk_ref, s32[64]{0:T(128)S(1)} %bitcast.19, bf16[16,256,128]{2,1,0:T(8,128)(2,1)S(1)} %all-to-all-done.q_ref.g_ref, bf16[16,128,128]{2,1,0:T(8,128)(2,1)S(1)} %slice.24.refs_0_, ...), custom_call_target="tpu_custom_call" | custom-call | flops 268435456 | bytes 5242880 | tf_op jit(solution)/shard_map/attend/pallas_call | solution.py:135
  163.2 24.3 %all-to-all-start.1 = ((bf16[256,4,128]{2,1,0:T(4,128)(2,1)}), bf16[256,4,128]{2,1,0:T(4,128)(2,1)S(1)}, u32[]{:S(2)}, u32[]{:S(2)}) async-start(bf16[256,4,128]{2,1,0:T(4,128)(2,1)} %bitcast.26), calls=%async_computation.1 | async-start | bytes 524288 | tf_op jit(solution)/shard_map/all_to_all | solution.py:367
  198.3 28.1 %all-to-all-done.1 = bf16[256,4,128]{2,1,0:T(4,128)(2,1)S(1)} async-done(((bf16[256,4,128]{2,1,0:T(4,128)(2,1)}), bf16[256,4,128]{2,1,0:T(4,128)(2,1)S(1)}, u32[]{:S(2)}, u32[]{:S(2)}) %all-to-all-start.1) | async-done | bytes 262176 | tf_op jit(solution)/shard_map/all_to_all | solution.py:367
  229.0 7.5 %collective-permute-start.15 = (f32[32,8,128]{2,1,0:T(8,128)S(1)}, f32[32,8,128]{2,1,0:T(8,128)S(1)}, u32[]{:S(2)}, u32[]{:S(2)}) collective-permute-start(f32[32,8,128]{2,1,0:T(8,128)S(1)} %get-tuple-element.40), channel_id=1, source_target_pairs={{0,1},{1,0},{2,3},{3,2},{4,5},{5,4},{6,7},{7,6},{8,9},{9,8},{10,11... | collective-permute-start | bytes 393224 | tf_op jit(solution)/shard_map/ppermute | solution.py:348
  237.5 51.3 %all_to_all.20.back_ref = bf16[32,40,128]{2,1,0:T(8,128)(2,1)S(1)} all-to-all(bf16[32,40,128]{2,1,0:T(8,128)(2,1)S(1)} %merge.1), channel_id=1, replica_groups={{0,2,4,6,8,10,12,14,16,18,20,22,24,26,28,30,32,34,36,38,40,42,44,46,48,..., dimensions={0} | all-to-all | bytes 655360 | tf_op jit(solution)/shard_map/all_to_all | solution.py:375
  289.6 3.5 %all-to-all-start.3 = ((bf16[16,80,128]{2,1,0:T(8,128)(2,1)}), bf16[16,80,128]{2,1,0:T(8,128)(2,1)S(1)}, u32[]{:S(2)}, u32[]{:S(2)}) async-start(bf16[16,80,128]{2,1,0:T(8,128)(2,1)} %gather_send.1), calls=%async_computation.3 | async-start | bytes 655360 | tf_op jit(solution)/shard_map/all_to_all | solution.py:376
  294.1 7.1 %all-to-all-done.3.got_ref = bf16[16,80,128]{2,1,0:T(8,128)(2,1)S(1)} async-done(((bf16[16,80,128]{2,1,0:T(8,128)(2,1)}), bf16[16,80,128]{2,1,0:T(8,128)(2,1)S(1)}, u32[]{:S(2)}, u32[]{:S(2)}) %all-to-all-start.3) | async-done | bytes 327712 | tf_op jit(solution)/shard_map/all_to_all | solution.py:376
  (51 shorter events, 23.6 us)
Async XLA Ops:
  4.1 121.4 %all-to-all-start = ((bf16[16,256,128]{2,1,0:T(8,128)(2,1)}), bf16[16,256,128]{2,1,0:T(8,128)(2,1)S(1)}, u32[]{:S(2)}, u32[]{:S(2)}) async-start(bf16[16,256,128]{2,1,0:T(8,128)(2,1)} %pack.1), calls=%async_computation | async-start | bytes 2097152 | tf_op jit(solution)/shard_map/all_to_all | solution.py:360
  33.1 123.7 %copy-start.8 = (s32[1,64,4]{1,2,0:T(4,128)S(1)}, s32[1,64,4]{1,2,0:T(4,128)}, u32[]{:S(2)}) copy-start(s32[1,64,4]{1,2,0:T(4,128)} %param.12) | copy-start | bytes 3076
  33.1 124.6 %copy-start.6 = (s32[1,64]{1,0:T(1,128)S(1)}, s32[1,64]{1,0:T(1,128)}, u32[]{:S(2)}) copy-start(s32[1,64]{1,0:T(1,128)} %param.13) | copy-start | bytes 772
  33.1 8.8 %collective-permute-start = (bf16[128,1024]{1,0:T(8,128)(2,1)S(1)}, bf16[128,1024]{1,0:T(8,128)(2,1)S(1)}, u32[]{:S(2)}, u32[]{:S(2)}) collective-permute-start(bf16[128,1024]{1,0:T(8,128)(2,1)S(1)} %bitcast.21), channel_id=1, source_target_pairs={{0,64},{64,0},{128,192},{192,128},{256,320},{320,256},{384,448},{4... | collective-permute-start | bytes 786440 | tf_op jit(solution)/shard_map/ppermute | solution.py:358
  41.9 20.4 %collective-permute-start.7 = (bf16[256,1024]{1,0:T(8,128)(2,1)S(1)}, bf16[256,1024]{1,0:T(8,128)(2,1)S(1)}, u32[]{:S(2)}, u32[]{:S(2)}) collective-permute-start(bf16[256,1024]{1,0:T(8,128)(2,1)S(1)} %constant_dynamic-update-slice_fusion.refs_0_), channel_id=1, source_target_pairs={{0,896},{64,960},{128,768},{192,832},{256,640},{320,704},{384,512}... | collective-permute-start | bytes 1572872 | tf_op jit(solution)/shard_map/ppermute | solution.py:359
  49.0 35.7 %collective-permute-start.6 = (bf16[256,1024]{1,0:T(8,128)(2,1)S(1)}, bf16[256,1024]{1,0:T(8,128)(2,1)S(1)}, u32[]{:S(2)}, u32[]{:S(2)}) collective-permute-start(bf16[256,1024]{1,0:T(8,128)(2,1)S(1)} %constant_dynamic-update-slice_fusion.refs_0_), channel_id=1, source_target_pairs={{0,768},{64,832},{128,896},{192,960},{256,512},{320,576},{384,640}... | collective-permute-start | bytes 1572872 | tf_op jit(solution)/shard_map/ppermute | solution.py:359
  50.9 74.6 %collective-permute-start.5 = (bf16[256,1024]{1,0:T(8,128)(2,1)S(1)}, bf16[256,1024]{1,0:T(8,128)(2,1)S(1)}, u32[]{:S(2)}, u32[]{:S(2)}) collective-permute-start(bf16[256,1024]{1,0:T(8,128)(2,1)S(1)} %constant_dynamic-update-slice_fusion.refs_0_), channel_id=1, source_target_pairs={{0,640},{64,704},{128,512},{192,576},{256,896},{320,960},{384,768}... | collective-permute-start | bytes 1572872 | tf_op jit(solution)/shard_map/ppermute | solution.py:359
  54.4 71.2 %collective-permute-start.4 = (bf16[256,1024]{1,0:T(8,128)(2,1)S(1)}, bf16[256,1024]{1,0:T(8,128)(2,1)}, u32[]{:S(2)}, u32[]{:S(2)}) collective-permute-start(bf16[256,1024]{1,0:T(8,128)(2,1)S(1)} %constant_dynamic-update-slice_fusion.refs_0_), channel_id=1, source_target_pairs={{0,512},{64,576},{128,640},{192,704},{256,768},{320,832},{384,896}... | collective-permute-start | bytes 1572872 | tf_op jit(solution)/shard_map/ppermute | solution.py:359
  57.7 67.9 %collective-permute-start.3 = (bf16[256,1024]{1,0:T(8,128)(2,1)S(1)}, bf16[256,1024]{1,0:T(8,128)(2,1)}, u32[]{:S(2)}, u32[]{:S(2)}) collective-permute-start(bf16[256,1024]{1,0:T(8,128)(2,1)S(1)} %constant_dynamic-update-slice_fusion.refs_0_), channel_id=1, source_target_pairs={{0,384},{64,448},{128,256},{192,320},{256,128},{320,192},{384,0},{... | collective-permute-start | bytes 1572872 | tf_op jit(solution)/shard_map/ppermute | solution.py:359
  62.4 63.3 %collective-permute-start.2 = (bf16[256,1024]{1,0:T(8,128)(2,1)S(1)}, bf16[256,1024]{1,0:T(8,128)(2,1)}, u32[]{:S(2)}, u32[]{:S(2)}) collective-permute-start(bf16[256,1024]{1,0:T(8,128)(2,1)S(1)} %constant_dynamic-update-slice_fusion.refs_0_), channel_id=1, source_target_pairs={{0,256},{64,320},{128,384},{192,448},{256,0},{320,64},{384,128},{4... | collective-permute-start | bytes 1572872 | tf_op jit(solution)/shard_map/ppermute | solution.py:359
  85.6 40.1 %collective-permute-start.1 = (bf16[256,1024]{1,0:T(8,128)(2,1)S(1)}, bf16[256,1024]{1,0:T(8,128)(2,1)}, u32[]{:S(2)}, u32[]{:S(2)}) collective-permute-start(bf16[256,1024]{1,0:T(8,128)(2,1)S(1)} %constant_dynamic-update-slice_fusion.refs_0_), channel_id=1, source_target_pairs={{0,128},{64,192},{128,0},{192,64},{256,384},{320,448},{384,256},{4... | collective-permute-start | bytes 1572872 | tf_op jit(solution)/shard_map/ppermute | solution.py:359
  125.6 37.6 %copy-start.4 = (bf16[256,1024]{1,0:T(8,128)(2,1)}, bf16[256,1024]{1,0:T(8,128)(2,1)S(1)}, u32[]{:S(2)}) copy-start(bf16[256,1024]{1,0:T(8,128)(2,1)S(1)} %collective-permute-done.5.refs_5_) | copy-start | bytes 1572868
  125.7 15.2 %collective-permute-start.9 = (bf16[12,128,128]{2,1,0:T(8,128)(2,1)S(1)}, bf16[12,128,128]{2,1,0:T(8,128)(2,1)}, u32[]{:S(2)}, u32[]{:S(2)}) collective-permute-start(bf16[12,128,128]{2,1,0:T(8,128)(2,1)S(1)} %slice.19), channel_id=1, source_target_pairs={{0,2},{1,3},{2,0},{3,1},{4,6},{5,7},{6,4},{7,5},{8,10},{9,11},{10,... | collective-permute-start | bytes 1179656 | tf_op jit(solution)/shard_map/ppermute | solution.py:348
  132.4 25.3 %collective-permute-start.8 = (bf16[16,128,128]{2,1,0:T(8,128)(2,1)S(1)}, bf16[16,128,128]{2,1,0:T(8,128)(2,1)}, u32[]{:S(2)}, u32[]{:S(2)}) collective-permute-start(bf16[16,128,128]{2,1,0:T(8,128)(2,1)S(1)} %slice.24.refs_0_), channel_id=1, source_target_pairs={{0,1},{1,0},{2,3},{3,2},{4,5},{5,4},{6,7},{7,6},{8,9},{9,8},{10,11... | collective-permute-start | bytes 1572872 | tf_op jit(solution)/shard_map/ppermute | solution.py:348
  140.9 16.8 %collective-permute-start.11 = (bf16[12,128,128]{2,1,0:T(8,128)(2,1)}, bf16[12,128,128]{2,1,0:T(8,128)(2,1)}, u32[]{:S(2)}, u32[]{:S(2)}) collective-permute-start(bf16[12,128,128]{2,1,0:T(8,128)(2,1)} %collective-permute-done.9.refs_2_), channel_id=1, source_target_pairs={{0,1},{1,0},{2,3},{3,2},{4,5},{5,4},{6,7},{7,6},{8,9},{9,8},{10,11... | collective-permute-start | bytes 1179656 | tf_op jit(solution)/shard_map/ppermute | solution.py:348
  146.8 7.5 %collective-permute-start.10 = (bf16[4,128,128]{2,1,0:T(8,128)(2,1)S(1)}, bf16[4,128,128]{2,1,0:T(8,128)(2,1)S(1)}, u32[]{:S(2)}, u32[]{:S(2)}) collective-permute-start(bf16[4,128,128]{2,1,0:T(8,128)(2,1)S(1)} %slice.20), channel_id=1, source_target_pairs={{0,2},{1,3},{2,0},{3,1},{4,6},{5,7},{6,4},{7,5},{8,10},{9,11},{10,... | collective-permute-start | bytes 393224 | tf_op jit(solution)/shard_map/ppermute | solution.py:348
  154.3 3.5 %collective-permute-start.12 = (bf16[4,128,128]{2,1,0:T(8,128)(2,1)S(1)}, bf16[4,128,128]{2,1,0:T(8,128)(2,1)S(1)}, u32[]{:S(2)}, u32[]{:S(2)}) collective-permute-start(bf16[4,128,128]{2,1,0:T(8,128)(2,1)S(1)} %collective-permute-done.10.refs_3_), channel_id=1, source_target_pairs={{0,1},{1,0},{2,3},{3,2},{4,5},{5,4},{6,7},{7,6},{8,9},{9,8},{10,11... | collective-permute-start | bytes 393224 | tf_op jit(solution)/shard_map/ppermute | solution.py:348
  163.2 63.2 %all-to-all-start.1 = ((bf16[256,4,128]{2,1,0:T(4,128)(2,1)}), bf16[256,4,128]{2,1,0:T(4,128)(2,1)S(1)}, u32[]{:S(2)}, u32[]{:S(2)}) async-start(bf16[256,4,128]{2,1,0:T(4,128)(2,1)} %bitcast.26), calls=%async_computation.1 | async-start | bytes 524288 | tf_op jit(solution)/shard_map/all_to_all | solution.py:367
  191.7 34.8 %copy-start.3 = (bf16[256,1024]{1,0:T(8,128)(2,1)S(1)}, bf16[256,1024]{1,0:T(8,128)(2,1)}, u32[]{:S(2)}) copy-start(bf16[256,1024]{1,0:T(8,128)(2,1)} %copy-done.2) | copy-start | bytes 1572868
  191.7 4.2 %collective-permute-start.13 = (bf16[2,32,32,128]{3,2,1,0:T(8,128)(2,1)S(1)}, bf16[2,32,32,128]{3,2,1,0:T(8,128)(2,1)S(1)}, u32[]{:S(2)}, u32[]{:S(2)}) collective-permute-start(bf16[2,32,32,128]{3,2,1,0:T(8,128)(2,1)S(1)} %get-tuple-element.28), channel_id=1, source_target_pairs={{0,1},{1,0},{2,3},{3,2},{4,5},{5,4},{6,7},{7,6},{8,9},{9,8},{10,11... | collective-permute-start | bytes 1572872 | tf_op jit(solution)/shard_map/ppermute | solution.py:348
  196.1 40.4 %collective-permute-start.14 = (bf16[32,32,128]{2,1,0:T(8,128)(2,1)S(1)}, bf16[32,32,128]{2,1,0:T(8,128)(2,1)S(1)}, u32[]{:S(2)}, u32[]{:S(2)}) collective-permute-start(bf16[32,32,128]{2,1,0:T(8,128)(2,1)S(1)} %get-tuple-element.43), channel_id=1, source_target_pairs={{0,2},{1,3},{2,0},{3,1},{4,6},{5,7},{6,4},{7,5},{8,10},{9,11},{10,... | collective-permute-start | bytes 786440 | tf_op jit(solution)/shard_map/ppermute | solution.py:348
  229.0 8.5 %collective-permute-start.15 = (f32[32,8,128]{2,1,0:T(8,128)S(1)}, f32[32,8,128]{2,1,0:T(8,128)S(1)}, u32[]{:S(2)}, u32[]{:S(2)}) collective-permute-start(f32[32,8,128]{2,1,0:T(8,128)S(1)} %get-tuple-element.40), channel_id=1, source_target_pairs={{0,1},{1,0},{2,3},{3,2},{4,5},{5,4},{6,7},{7,6},{8,9},{9,8},{10,11... | collective-permute-start | bytes 393224 | tf_op jit(solution)/shard_map/ppermute | solution.py:348
  237.5 63.7 %copy-start = (bf16[1024,1024]{1,0:T(8,128)(2,1)S(1)}, bf16[1024,1024]{1,0:T(8,128)(2,1)}, u32[]{:S(2)}) copy-start(bf16[1024,1024]{1,0:T(8,128)(2,1)} %w_ref.3) | copy-start | bytes 6291460
  289.6 11.5 %all-to-all-start.3 = ((bf16[16,80,128]{2,1,0:T(8,128)(2,1)}), bf16[16,80,128]{2,1,0:T(8,128)(2,1)S(1)}, u32[]{:S(2)}, u32[]{:S(2)}) async-start(bf16[16,80,128]{2,1,0:T(8,128)(2,1)} %gather_send.1), calls=%async_computation.3 | async-start | bytes 655360 | tf_op jit(solution)/shard_map/all_to_all | solution.py:376
  (4 other events, 69.6 us)

commit v12 on v9

--- a/solution.py
+++ b/solution.py
@@ -221,14 +221,17 @@
 
 
 def weight_kernel(me_ref, site_ref, att_ref, *refs):
-    cots, (keep_ref, swap_ref, acc_ref, wide_ref) = refs[:-4], refs[-4:]
+    cots, (keep_ref, swap_ref, wide_ref) = refs[:-3], refs[-3:]
     each = att_ref.shape[0] // len(cots)
-    for t, cot_ref in enumerate(cots):
-        att = jnp.concatenate([att_ref[me_ref[0] ^ (each * t + i)] for i in range(each)], axis=1)
-        term = jnp.dot(att, cot_ref[...], preferred_element_type=F32)
-        acc_ref[...] = term if t == 0 else acc_ref[...] + term
-    for i in range(wide_ref.shape[1]):
-        wide_ref[:, i, :] = acc_ref[:, CSIZE * i : CSIZE * (i + 1)]
+    atts = [
+        jnp.concatenate([att_ref[me_ref[0] ^ (each * t + i)] for i in range(each)], axis=1)
+        for t in range(len(cots))
+    ]
+    for i in range(0, wide_ref.shape[1], 2):
+        block = slice(CSIZE * i, CSIZE * (i + 2))
+        total = sum(jnp.dot(att, cot[:, block], preferred_element_type=F32) for att, cot in zip(atts, cots))
+        wide_ref[:, i, :] = total[:, :CSIZE]
+        wide_ref[:, i + 1, :] = total[:, CSIZE:]
     core = site_ref[0] % 2
     half, piece, _ = keep_ref.shape
     rows = wide_ref.shape[0] // half // 2
@@ -245,7 +248,7 @@
         weight_kernel,
         in_specs=[pl.BlockSpec(memory_space=pltpu.SMEM)] * 2 + [pl.BlockSpec(memory_space=pltpu.VMEM)] * (1 + len(cots)),
         out_shape=[jax.ShapeDtypeStruct(piece, F32)] * 2,
-        scratch_shapes=[pltpu.VMEM((rows, width), F32), pltpu.VMEM((rows, width // CSIZE, CSIZE), F32)],
+        scratch_shapes=[pltpu.VMEM((rows, width // CSIZE, CSIZE), F32)],
         compiler_params=params(16),
         cost_estimate=pl.CostEstimate(
             flops=2 * n * rows * nodes * width, bytes_accessed=2 * n * nodes * width, transcendentals=0

time: 297 us -> 297 us (level)
  no operation moved by 1% of the time
where the time goes in v12:
time: 297 us; the launch traced here: 296 us
  starting transfers between devices  125 us (42%)
  waiting for transfers between devices  98.8 us (33%)
  blocking collectives  51.2 us (17%)
  Pallas kernels  16.8 us (6%)
  local copies, waits for them, and re-layouts  3.45 us (1%)
    all_to_all x1, blocking collectives, body(): lax.all_to_all(last, 'seq', split_axis=0, concat_axis=0, tiled=True, axis...  51.2 us
    ppermute x9, starting transfers between devices, swap(): return lax.ppermute(x, 'seq', [(i, i ^ bit) for i in range(nseq)])  36.1 us
    all_to_all x1, waiting for transfers between devices, body(): lax.all_to_all(sent, 'seq', split_axis=0, concat_axis=0, tiled=True, axis...  35.5 us
    all_to_all x1, starting transfers between devices, body(): lax.all_to_all(sent, 'seq', split_axis=0, concat_axis=0, tiled=True, axis...  29.1 us
    ppermute x7, starting transfers between devices, body(): lax.ppermute(cot, 'dp', [(i, i ^ t) for i in range(ndp)])  28 us
    all_to_all x1, waiting for transfers between devices, body(): lax.all_to_all(sent_att, ('dp', 'seq'), split_axis=0, concat_axis=0, tile...  27.4 us
    all_to_all x1, starting transfers between devices, body(): lax.all_to_all(sent_att, ('dp', 'seq'), split_axis=0, concat_axis=0, tile...  24.7 us
    ppermute x7, waiting for transfers between devices, body(): lax.ppermute(cot, 'dp', [(i, i ^ t) for i in range(ndp)])  19.3 us
  transfers between devices with their start and end apart: 20, of which 8 were waited for; matrix products, arithmetic and copies ran while one was open for 0% of the time, Pallas kernels for 2%

profile of v12, /device:TPU:1, one launch (start us, length us, event | category | flops | bytes accessed | tf_op | source)
XLA Modules:
  0.0 296.0 jit_solution(10306544971489759140)
XLA Ops:
  0.6 3.4 %pack.1 = bf16[16,256,128]{2,1,0:T(8,128)(2,1)} custom-call(bf16[128,1024]{1,0:T(8,128)(2,1)} %bitcast.23, bf16[128,1024]{1,0:T(8,128)(2,1)} %bitcast.24, bf16[128,1024]{1,0:T(8,128)(2,1)} %bitcast.25, bf16[128,1024]{1,0:T(8,128)(2,1)} %bitcast.20, bf16[1024,1024]{1,0:T(8,128)(2,1)} %w_ref.3), custom_call_target="tpu_custom_call" | custom-call | flops 268435456 | bytes 3407872 | tf_op jit(solution)/shard_map/pack/pallas_call | solution.py:47
  4.1 29.1 %all-to-all-start = ((bf16[16,256,128]{2,1,0:T(8,128)(2,1)}), bf16[16,256,128]{2,1,0:T(8,128)(2,1)S(1)}, u32[]{:S(2)}, u32[]{:S(2)}) async-start(bf16[16,256,128]{2,1,0:T(8,128)(2,1)} %pack.1), calls=%async_computation | async-start | bytes 2097152 | tf_op jit(solution)/shard_map/all_to_all | solution.py:353
  33.2 3.1 %collective-permute-start = (bf16[128,1024]{1,0:T(8,128)(2,1)S(1)}, bf16[128,1024]{1,0:T(8,128)(2,1)S(1)}, u32[]{:S(2)}, u32[]{:S(2)}) collective-permute-start(bf16[128,1024]{1,0:T(8,128)(2,1)S(1)} %bitcast.21), channel_id=1, source_target_pairs={{0,64},{64,0},{128,192},{192,128},{256,320},{320,256},{384,448},{4... | collective-permute-start | bytes 786440 | tf_op jit(solution)/shard_map/ppermute | solution.py:351
  36.4 5.6 %collective-permute-done = bf16[128,1024]{1,0:T(8,128)(2,1)S(1)} collective-permute-done((bf16[128,1024]{1,0:T(8,128)(2,1)S(1)}, bf16[128,1024]{1,0:T(8,128)(2,1)S(1)}, u32[]{:S(2)}, u32[]{:S(2)}) %collective-permute-start) | collective-permute-done | bytes 262176 | tf_op jit(solution)/shard_map/ppermute | solution.py:351
  42.0 7.1 %collective-permute-start.7 = (bf16[256,1024]{1,0:T(8,128)(2,1)S(1)}, bf16[256,1024]{1,0:T(8,128)(2,1)S(1)}, u32[]{:S(2)}, u32[]{:S(2)}) collective-permute-start(bf16[256,1024]{1,0:T(8,128)(2,1)S(1)} %constant_dynamic-update-slice_fusion.refs_0_), channel_id=1, source_target_pairs={{0,896},{64,960},{128,768},{192,832},{256,640},{320,704},{384,512}... | collective-permute-start | bytes 1572872 | tf_op jit(solution)/shard_map/ppermute | solution.py:352
  51.1 3.5 %collective-permute-start.5 = (bf16[256,1024]{1,0:T(8,128)(2,1)S(1)}, bf16[256,1024]{1,0:T(8,128)(2,1)S(1)}, u32[]{:S(2)}, u32[]{:S(2)}) collective-permute-start(bf16[256,1024]{1,0:T(8,128)(2,1)S(1)} %constant_dynamic-update-slice_fusion.refs_0_), channel_id=1, source_target_pairs={{0,640},{64,704},{128,512},{192,576},{256,896},{320,960},{384,768}... | collective-permute-start | bytes 1572872 | tf_op jit(solution)/shard_map/ppermute | solution.py:352
  54.5 3.3 %collective-permute-start.4 = (bf16[256,1024]{1,0:T(8,128)(2,1)S(1)}, bf16[256,1024]{1,0:T(8,128)(2,1)}, u32[]{:S(2)}, u32[]{:S(2)}) collective-permute-start(bf16[256,1024]{1,0:T(8,128)(2,1)S(1)} %constant_dynamic-update-slice_fusion.refs_0_), channel_id=1, source_target_pairs={{0,512},{64,576},{128,640},{192,704},{256,768},{320,832},{384,896}... | collective-permute-start | bytes 1572872 | tf_op jit(solution)/shard_map/ppermute | solution.py:352
  57.9 4.6 %collective-permute-start.3 = (bf16[256,1024]{1,0:T(8,128)(2,1)S(1)}, bf16[256,1024]{1,0:T(8,128)(2,1)}, u32[]{:S(2)}, u32[]{:S(2)}) collective-permute-start(bf16[256,1024]{1,0:T(8,128)(2,1)S(1)} %constant_dynamic-update-slice_fusion.refs_0_), channel_id=1, source_target_pairs={{0,384},{64,448},{128,256},{192,320},{256,128},{320,192},{384,0},{... | collective-permute-start | bytes 1572872 | tf_op jit(solution)/shard_map/ppermute | solution.py:352
  62.5 3.1 %collective-permute-start.2 = (bf16[256,1024]{1,0:T(8,128)(2,1)S(1)}, bf16[256,1024]{1,0:T(8,128)(2,1)}, u32[]{:S(2)}, u32[]{:S(2)}) collective-permute-start(bf16[256,1024]{1,0:T(8,128)(2,1)S(1)} %constant_dynamic-update-slice_fusion.refs_0_), channel_id=1, source_target_pairs={{0,256},{64,320},{128,384},{192,448},{256,0},{320,64},{384,128},{4... | collective-permute-start | bytes 1572872 | tf_op jit(solution)/shard_map/ppermute | solution.py:352
  65.6 19.3 %collective-permute-done.6.refs_6_ = bf16[256,1024]{1,0:T(8,128)(2,1)S(1)} collective-permute-done((bf16[256,1024]{1,0:T(8,128)(2,1)S(1)}, bf16[256,1024]{1,0:T(8,128)(2,1)S(1)}, u32[]{:S(2)}, u32[]{:S(2)}) %collective-permute-start.6) | collective-permute-done | bytes 524320 | tf_op jit(solution)/shard_map/ppermute | solution.py:352
  85.7 4.5 %collective-permute-start.1 = (bf16[256,1024]{1,0:T(8,128)(2,1)S(1)}, bf16[256,1024]{1,0:T(8,128)(2,1)}, u32[]{:S(2)}, u32[]{:S(2)}) collective-permute-start(bf16[256,1024]{1,0:T(8,128)(2,1)S(1)} %constant_dynamic-update-slice_fusion.refs_0_), channel_id=1, source_target_pairs={{0,128},{64,192},{128,0},{192,64},{256,384},{320,448},{384,256},{4... | collective-permute-start | bytes 1572872 | tf_op jit(solution)/shard_map/ppermute | solution.py:352
  90.2 35.5 %all-to-all-done.q_ref.g_ref = bf16[16,256,128]{2,1,0:T(8,128)(2,1)S(1)} async-done(((bf16[16,256,128]{2,1,0:T(8,128)(2,1)}), bf16[16,256,128]{2,1,0:T(8,128)(2,1)S(1)}, u32[]{:S(2)}, u32[]{:S(2)}) %all-to-all-start) | async-done | bytes 1048608 | tf_op jit(solution)/shard_map/all_to_all | solution.py:353
  125.8 6.8 %collective-permute-start.10 = (bf16[8,128,128]{2,1,0:T(8,128)(2,1)S(1)}, bf16[8,128,128]{2,1,0:T(8,128)(2,1)S(1)}, u32[]{:S(2)}, u32[]{:S(2)}) collective-permute-start(bf16[8,128,128]{2,1,0:T(8,128)(2,1)S(1)} %get-tuple-element.26.refs_0_), channel_id=1, source_target_pairs={{0,2},{1,3},{2,0},{3,1},{4,6},{5,7},{6,4},{7,5},{8,10},{9,11},{10,... | collective-permute-start | bytes 786440 | tf_op jit(solution)/shard_map/ppermute | solution.py:341
  134.5 8.5 %collective-permute-start.8 = (bf16[8,128,128]{2,1,0:T(8,128)(2,1)S(1)}, bf16[8,128,128]{2,1,0:T(8,128)(2,1)}, u32[]{:S(2)}, u32[]{:S(2)}) collective-permute-start(bf16[8,128,128]{2,1,0:T(8,128)(2,1)S(1)} %get-tuple-element.26.refs_0_), channel_id=1, source_target_pairs={{0,1},{1,0},{2,3},{3,2},{4,5},{5,4},{6,7},{7,6},{8,9},{9,8},{10,11... | collective-permute-start | bytes 786440 | tf_op jit(solution)/shard_map/ppermute | solution.py:341
  151.1 5.3 %attend.1 = (bf16[16,64,128]{2,1,0:T(8,128)(2,1)}, bf16[16,4,128,128]{3,2,1,0:T(8,128)(2,1)}) custom-call(s32[1]{0:T(128)} %bitcast.site_ref, s32[256]{0:T(256)S(1)} %reshape_squeeze.3.blk_ref, s32[64]{0:T(128)S(1)} %bitcast.19, bf16[16,256,128]{2,1,0:T(8,128)(2,1)S(1)} %all-to-all-done.q_ref.g_ref, bf16[8,128,128]{2,1,0:T(8,128)(2,1)S(1)} %get-tuple-element.26.refs_0_, ...), custom_call_target="tpu_custom_call" | custom-call | flops 268435456 | bytes 5242880 | tf_op jit(solution)/shard_map/attend/pallas_call | solution.py:125
  156.4 24.7 %all-to-all-start.1 = ((bf16[256,4,128]{2,1,0:T(4,128)(2,1)}), bf16[256,4,128]{2,1,0:T(4,128)(2,1)S(1)}, u32[]{:S(2)}, u32[]{:S(2)}) async-start(bf16[256,4,128]{2,1,0:T(4,128)(2,1)} %bitcast.26), calls=%async_computation.1 | async-start | bytes 524288 | tf_op jit(solution)/shard_map/all_to_all | solution.py:360
  182.7 2.5 value_contrib.1
  185.2 2.7 collective-permute-start.14
  192.6 27.4 %all-to-all-done.1 = bf16[256,4,128]{2,1,0:T(4,128)(2,1)S(1)} async-done(((bf16[256,4,128]{2,1,0:T(4,128)(2,1)}), bf16[256,4,128]{2,1,0:T(4,128)(2,1)S(1)}, u32[]{:S(2)}, u32[]{:S(2)}) %all-to-all-start.1) | async-done | bytes 262176 | tf_op jit(solution)/shard_map/all_to_all | solution.py:360
  220.0 2.5 weight_part.1
  222.5 7.6 %collective-permute-start.16 = (f32[32,8,128]{2,1,0:T(8,128)S(1)}, f32[32,8,128]{2,1,0:T(8,128)S(1)}, u32[]{:S(2)}, u32[]{:S(2)}) collective-permute-start(f32[32,8,128]{2,1,0:T(8,128)S(1)} %get-tuple-element.42), channel_id=1, source_target_pairs={{0,1},{1,0},{2,3},{3,2},{4,5},{5,4},{6,7},{7,6},{8,9},{9,8},{10,11... | collective-permute-start | bytes 393224 | tf_op jit(solution)/shard_map/ppermute | solution.py:341
  231.2 51.2 %all_to_all.20.back_ref = bf16[32,40,128]{2,1,0:T(8,128)(2,1)S(1)} all-to-all(bf16[32,40,128]{2,1,0:T(8,128)(2,1)S(1)} %merge.1), channel_id=1, replica_groups={{0,2,4,6,8,10,12,14,16,18,20,22,24,26,28,30,32,34,36,38,40,42,44,46,48,..., dimensions={0} | all-to-all | bytes 655360 | tf_op jit(solution)/shard_map/all_to_all | solution.py:368
  283.2 3.5 %all-to-all-start.3 = ((bf16[16,80,128]{2,1,0:T(8,128)(2,1)}), bf16[16,80,128]{2,1,0:T(8,128)(2,1)S(1)}, u32[]{:S(2)}, u32[]{:S(2)}) async-start(bf16[16,80,128]{2,1,0:T(8,128)(2,1)} %gather_send.1), calls=%async_computation.3 | async-start | bytes 655360 | tf_op jit(solution)/shard_map/all_to_all | solution.py:369
  287.6 7.1 %all-to-all-done.3.got_ref = bf16[16,80,128]{2,1,0:T(8,128)(2,1)S(1)} async-done(((bf16[16,80,128]{2,1,0:T(8,128)(2,1)}), bf16[16,80,128]{2,1,0:T(8,128)(2,1)S(1)}, u32[]{:S(2)}, u32[]{:S(2)}) %all-to-all-start.3) | async-done | bytes 327712 | tf_op jit(solution)/shard_map/all_to_all | solution.py:369
  (51 shorter events, 23.0 us)
Async XLA Ops:
  4.1 145.3 %copy-start.8 = (s32[1,64,4]{1,2,0:T(4,128)S(1)}, s32[1,64,4]{1,2,0:T(4,128)}, u32[]{:S(2)}) copy-start(s32[1,64,4]{1,2,0:T(4,128)} %param.12) | copy-start | bytes 3076
  4.1 147.0 %copy-start.6 = (s32[1,64]{1,0:T(1,128)S(1)}, s32[1,64]{1,0:T(1,128)}, u32[]{:S(2)}) copy-start(s32[1,64]{1,0:T(1,128)} %param.13) | copy-start | bytes 772
  4.1 121.6 %all-to-all-start = ((bf16[16,256,128]{2,1,0:T(8,128)(2,1)}), bf16[16,256,128]{2,1,0:T(8,128)(2,1)S(1)}, u32[]{:S(2)}, u32[]{:S(2)}) async-start(bf16[16,256,128]{2,1,0:T(8,128)(2,1)} %pack.1), calls=%async_computation | async-start | bytes 2097152 | tf_op jit(solution)/shard_map/all_to_all | solution.py:353
  33.2 8.8 %collective-permute-start = (bf16[128,1024]{1,0:T(8,128)(2,1)S(1)}, bf16[128,1024]{1,0:T(8,128)(2,1)S(1)}, u32[]{:S(2)}, u32[]{:S(2)}) collective-permute-start(bf16[128,1024]{1,0:T(8,128)(2,1)S(1)} %bitcast.21), channel_id=1, source_target_pairs={{0,64},{64,0},{128,192},{192,128},{256,320},{320,256},{384,448},{4... | collective-permute-start | bytes 786440 | tf_op jit(solution)/shard_map/ppermute | solution.py:351
  42.0 20.4 %collective-permute-start.7 = (bf16[256,1024]{1,0:T(8,128)(2,1)S(1)}, bf16[256,1024]{1,0:T(8,128)(2,1)S(1)}, u32[]{:S(2)}, u32[]{:S(2)}) collective-permute-start(bf16[256,1024]{1,0:T(8,128)(2,1)S(1)} %constant_dynamic-update-slice_fusion.refs_0_), channel_id=1, source_target_pairs={{0,896},{64,960},{128,768},{192,832},{256,640},{320,704},{384,512}... | collective-permute-start | bytes 1572872 | tf_op jit(solution)/shard_map/ppermute | solution.py:352
  49.1 35.7 %collective-permute-start.6 = (bf16[256,1024]{1,0:T(8,128)(2,1)S(1)}, bf16[256,1024]{1,0:T(8,128)(2,1)S(1)}, u32[]{:S(2)}, u32[]{:S(2)}) collective-permute-start(bf16[256,1024]{1,0:T(8,128)(2,1)S(1)} %constant_dynamic-update-slice_fusion.refs_0_), channel_id=1, source_target_pairs={{0,768},{64,832},{128,896},{192,960},{256,512},{320,576},{384,640}... | collective-permute-start | bytes 1572872 | tf_op jit(solution)/shard_map/ppermute | solution.py:352
  51.1 74.7 %collective-permute-start.5 = (bf16[256,1024]{1,0:T(8,128)(2,1)S(1)}, bf16[256,1024]{1,0:T(8,128)(2,1)S(1)}, u32[]{:S(2)}, u32[]{:S(2)}) collective-permute-start(bf16[256,1024]{1,0:T(8,128)(2,1)S(1)} %constant_dynamic-update-slice_fusion.refs_0_), channel_id=1, source_target_pairs={{0,640},{64,704},{128,512},{192,576},{256,896},{320,960},{384,768}... | collective-permute-start | bytes 1572872 | tf_op jit(solution)/shard_map/ppermute | solution.py:352
  54.5 71.2 %collective-permute-start.4 = (bf16[256,1024]{1,0:T(8,128)(2,1)S(1)}, bf16[256,1024]{1,0:T(8,128)(2,1)}, u32[]{:S(2)}, u32[]{:S(2)}) collective-permute-start(bf16[256,1024]{1,0:T(8,128)(2,1)S(1)} %constant_dynamic-update-slice_fusion.refs_0_), channel_id=1, source_target_pairs={{0,512},{64,576},{128,640},{192,704},{256,768},{320,832},{384,896}... | collective-permute-start | bytes 1572872 | tf_op jit(solution)/shard_map/ppermute | solution.py:352
  57.9 67.9 %collective-permute-start.3 = (bf16[256,1024]{1,0:T(8,128)(2,1)S(1)}, bf16[256,1024]{1,0:T(8,128)(2,1)}, u32[]{:S(2)}, u32[]{:S(2)}) collective-permute-start(bf16[256,1024]{1,0:T(8,128)(2,1)S(1)} %constant_dynamic-update-slice_fusion.refs_0_), channel_id=1, source_target_pairs={{0,384},{64,448},{128,256},{192,320},{256,128},{320,192},{384,0},{... | collective-permute-start | bytes 1572872 | tf_op jit(solution)/shard_map/ppermute | solution.py:352
  62.5 63.3 %collective-permute-start.2 = (bf16[256,1024]{1,0:T(8,128)(2,1)S(1)}, bf16[256,1024]{1,0:T(8,128)(2,1)}, u32[]{:S(2)}, u32[]{:S(2)}) collective-permute-start(bf16[256,1024]{1,0:T(8,128)(2,1)S(1)} %constant_dynamic-update-slice_fusion.refs_0_), channel_id=1, source_target_pairs={{0,256},{64,320},{128,384},{192,448},{256,0},{320,64},{384,128},{4... | collective-permute-start | bytes 1572872 | tf_op jit(solution)/shard_map/ppermute | solution.py:352
  85.7 40.1 %collective-permute-start.1 = (bf16[256,1024]{1,0:T(8,128)(2,1)S(1)}, bf16[256,1024]{1,0:T(8,128)(2,1)}, u32[]{:S(2)}, u32[]{:S(2)}) collective-permute-start(bf16[256,1024]{1,0:T(8,128)(2,1)S(1)} %constant_dynamic-update-slice_fusion.refs_0_), channel_id=1, source_target_pairs={{0,128},{64,192},{128,0},{192,64},{256,384},{320,448},{384,256},{4... | collective-permute-start | bytes 1572872 | tf_op jit(solution)/shard_map/ppermute | solution.py:352
  125.8 19.1 %collective-permute-start.10 = (bf16[8,128,128]{2,1,0:T(8,128)(2,1)S(1)}, bf16[8,128,128]{2,1,0:T(8,128)(2,1)S(1)}, u32[]{:S(2)}, u32[]{:S(2)}) collective-permute-start(bf16[8,128,128]{2,1,0:T(8,128)(2,1)S(1)} %get-tuple-element.26.refs_0_), channel_id=1, source_target_pairs={{0,2},{1,3},{2,0},{3,1},{4,6},{5,7},{6,4},{7,5},{8,10},{9,11},{10,... | collective-permute-start | bytes 786440 | tf_op jit(solution)/shard_map/ppermute | solution.py:341
  132.6 14.8 %collective-permute-start.11 = (bf16[8,128,128]{2,1,0:T(8,128)(2,1)S(1)}, bf16[8,128,128]{2,1,0:T(8,128)(2,1)}, u32[]{:S(2)}, u32[]{:S(2)}) collective-permute-start(bf16[8,128,128]{2,1,0:T(8,128)(2,1)S(1)} %get-tuple-element.27.refs_1_), channel_id=1, source_target_pairs={{0,2},{1,3},{2,0},{3,1},{4,6},{5,7},{6,4},{7,5},{8,10},{9,11},{10,... | collective-permute-start | bytes 786440 | tf_op jit(solution)/shard_map/ppermute | solution.py:341
  134.5 15.1 %collective-permute-start.8 = (bf16[8,128,128]{2,1,0:T(8,128)(2,1)S(1)}, bf16[8,128,128]{2,1,0:T(8,128)(2,1)}, u32[]{:S(2)}, u32[]{:S(2)}) collective-permute-start(bf16[8,128,128]{2,1,0:T(8,128)(2,1)S(1)} %get-tuple-element.26.refs_0_), channel_id=1, source_target_pairs={{0,1},{1,0},{2,3},{3,2},{4,5},{5,4},{6,7},{7,6},{8,9},{9,8},{10,11... | collective-permute-start | bytes 786440 | tf_op jit(solution)/shard_map/ppermute | solution.py:341
  142.9 6.7 %collective-permute-start.9 = (bf16[8,128,128]{2,1,0:T(8,128)(2,1)S(1)}, bf16[8,128,128]{2,1,0:T(8,128)(2,1)}, u32[]{:S(2)}, u32[]{:S(2)}) collective-permute-start(bf16[8,128,128]{2,1,0:T(8,128)(2,1)S(1)} %get-tuple-element.27.refs_1_), channel_id=1, source_target_pairs={{0,1},{1,0},{2,3},{3,2},{4,5},{5,4},{6,7},{7,6},{8,9},{9,8},{10,11... | collective-permute-start | bytes 786440 | tf_op jit(solution)/shard_map/ppermute | solution.py:341
  144.9 4.7 %collective-permute-start.12 = (bf16[8,128,128]{2,1,0:T(8,128)(2,1)S(1)}, bf16[8,128,128]{2,1,0:T(8,128)(2,1)}, u32[]{:S(2)}, u32[]{:S(2)}) collective-permute-start(bf16[8,128,128]{2,1,0:T(8,128)(2,1)S(1)} %collective-permute-done.10.refs_4_), channel_id=1, source_target_pairs={{0,1},{1,0},{2,3},{3,2},{4,5},{5,4},{6,7},{7,6},{8,9},{9,8},{10,11... | collective-permute-start | bytes 786440 | tf_op jit(solution)/shard_map/ppermute | solution.py:341
  147.3 3.8 %collective-permute-start.13 = (bf16[8,128,128]{2,1,0:T(8,128)(2,1)}, bf16[8,128,128]{2,1,0:T(8,128)(2,1)}, u32[]{:S(2)}, u32[]{:S(2)}) collective-permute-start(bf16[8,128,128]{2,1,0:T(8,128)(2,1)} %collective-permute-done.11.refs_5_), channel_id=1, source_target_pairs={{0,1},{1,0},{2,3},{3,2},{4,5},{5,4},{6,7},{7,6},{8,9},{9,8},{10,11... | collective-permute-start | bytes 786440 | tf_op jit(solution)/shard_map/ppermute | solution.py:341
  156.4 63.6 %all-to-all-start.1 = ((bf16[256,4,128]{2,1,0:T(4,128)(2,1)}), bf16[256,4,128]{2,1,0:T(4,128)(2,1)S(1)}, u32[]{:S(2)}, u32[]{:S(2)}) async-start(bf16[256,4,128]{2,1,0:T(4,128)(2,1)} %bitcast.26), calls=%async_computation.1 | async-start | bytes 524288 | tf_op jit(solution)/shard_map/all_to_all | solution.py:360
  185.2 34.8 %copy-start.3 = (bf16[256,1024]{1,0:T(8,128)(2,1)S(1)}, bf16[256,1024]{1,0:T(8,128)(2,1)}, u32[]{:S(2)}) copy-start(bf16[256,1024]{1,0:T(8,128)(2,1)} %copy-done.2) | copy-start | bytes 1572868
  185.2 4.2 %collective-permute-start.14 = (bf16[2,32,32,128]{3,2,1,0:T(8,128)(2,1)S(1)}, bf16[2,32,32,128]{3,2,1,0:T(8,128)(2,1)S(1)}, u32[]{:S(2)}, u32[]{:S(2)}) collective-permute-start(bf16[2,32,32,128]{3,2,1,0:T(8,128)(2,1)S(1)} %get-tuple-element.30), channel_id=1, source_target_pairs={{0,1},{1,0},{2,3},{3,2},{4,5},{5,4},{6,7},{7,6},{8,9},{9,8},{10,11... | collective-permute-start | bytes 1572872 | tf_op jit(solution)/shard_map/ppermute | solution.py:341
  190.3 39.8 %collective-permute-start.15 = (bf16[32,32,128]{2,1,0:T(8,128)(2,1)}, bf16[32,32,128]{2,1,0:T(8,128)(2,1)S(1)}, u32[]{:S(2)}, u32[]{:S(2)}) collective-permute-start(bf16[32,32,128]{2,1,0:T(8,128)(2,1)} %get-tuple-element.47), channel_id=1, source_target_pairs={{0,2},{1,3},{2,0},{3,1},{4,6},{5,7},{6,4},{7,5},{8,10},{9,11},{10,... | collective-permute-start | bytes 786440 | tf_op jit(solution)/shard_map/ppermute | solution.py:341
  222.5 8.6 %collective-permute-start.16 = (f32[32,8,128]{2,1,0:T(8,128)S(1)}, f32[32,8,128]{2,1,0:T(8,128)S(1)}, u32[]{:S(2)}, u32[]{:S(2)}) collective-permute-start(f32[32,8,128]{2,1,0:T(8,128)S(1)} %get-tuple-element.42), channel_id=1, source_target_pairs={{0,1},{1,0},{2,3},{3,2},{4,5},{5,4},{6,7},{7,6},{8,9},{9,8},{10,11... | collective-permute-start | bytes 393224 | tf_op jit(solution)/shard_map/ppermute | solution.py:341
  231.1 63.5 %copy-start = (bf16[1024,1024]{1,0:T(8,128)(2,1)S(1)}, bf16[1024,1024]{1,0:T(8,128)(2,1)}, u32[]{:S(2)}) copy-start(bf16[1024,1024]{1,0:T(8,128)(2,1)} %w_ref.3) | copy-start | bytes 6291460
  283.2 11.5 %all-to-all-start.3 = ((bf16[16,80,128]{2,1,0:T(8,128)(2,1)}), bf16[16,80,128]{2,1,0:T(8,128)(2,1)S(1)}, u32[]{:S(2)}, u32[]{:S(2)}) async-start(bf16[16,80,128]{2,1,0:T(8,128)(2,1)} %gather_send.1), calls=%async_computation.3 | async-start | bytes 655360 | tf_op jit(solution)/shard_map/all_to_all | solution.py:369
  (5 other events, 100.4 us)
